TPU v7x, 32 devices: a whole 2x2x4 slice. The times are simulated.
32 devices in a mesh: dp: 16 (over z, y, core), tensor: 2 (over x).
Axes of the slice: x: 2, y: 2, z: 4, core: 2. Of those that a mesh axis runs over, the one named last changes fastest.
Arguments:
- tokens: bfloat16 [8192, 768], P(('dp', 'tensor')), may hold values from -6 to 6
- cotangent: bfloat16 [8192, 768], P(('dp', 'tensor')), may hold values from -6 to 6
- lengths: int32 [16, 3], P('dp'), may hold values from 0 to 512, as said below
- w_qkv: float32 [3, 768, 768], P(None, 'dp', 'tensor'), may hold values from -0.21875 to 0.21875
- m_qkv: float32 [3, 768, 768], P(None, 'dp', 'tensor'), may hold values from -12 to 12
- v_qkv: float32 [3, 768, 768], P(None, 'dp', 'tensor'), may hold values from 0.16384 to 1.31072
- w_out: float32 [768, 768], P('tensor', 'dp'), may hold values from -2.5 to 2.5
- m_out: float32 [768, 768], P('tensor', 'dp'), may hold values from -4 to 4
- v_out: float32 [768, 768], P('tensor', 'dp'), may hold values from 0.01024 to 0.08192
- w_in: float32 [768, 3072], P('dp', 'tensor'), may hold values from -0.21875 to 0.21875
- m_in: float32 [768, 3072], P('dp', 'tensor'), may hold values from -32 to 32
- v_in: float32 [768, 3072], P('dp', 'tensor'), may hold values from 1.024 to 8.192
- w_back: float32 [3072, 768], P('tensor', 'dp'), may hold values from -0.109375 to 0.109375
- m_back: float32 [3072, 768], P('tensor', 'dp'), may hold values from -20 to 20
- v_back: float32 [3072, 768], P('tensor', 'dp'), may hold values from 0.49152 to 4.096
- vectors: float32 [12, 768], P(None, ('dp', 'tensor'))
- m_vectors: float32 [12, 768], P(None, ('dp', 'tensor')), may hold values from -40 to 40
- v_vectors: float32 [12, 768], P(None, ('dp', 'tensor')), may hold values from 2.048 to 16.384
Outputs:
- mixed: bfloat16 [8192, 768], P(('dp', 'tensor'))
- input_grad: float32 [8192, 768], P(('dp', 'tensor'))
- new_qkv: float32 [3, 768, 768], P(None, 'dp', 'tensor')
- moment_qkv: float32 [3, 768, 768], P(None, 'dp', 'tensor')
- square_qkv: float32 [3, 768, 768], P(None, 'dp', 'tensor')
- new_out: float32 [768, 768], P('tensor', 'dp')
- moment_out: float32 [768, 768], P('tensor', 'dp')
- square_out: float32 [768, 768], P('tensor', 'dp')
- new_in: float32 [768, 3072], P('dp', 'tensor')
- moment_in: float32 [768, 3072], P('dp', 'tensor')
- square_in: float32 [768, 3072], P('dp', 'tensor')
- new_back: float32 [3072, 768], P('tensor', 'dp')
- moment_back: float32 [3072, 768], P('tensor', 'dp')
- square_back: float32 [3072, 768], P('tensor', 'dp')
- new_vectors: float32 [12, 768], P(None, ('dp', 'tensor'))
- moment_vectors: float32 [12, 768], P(None, ('dp', 'tensor'))
- square_vectors: float32 [12, 768], P(None, ('dp', 'tensor'))
Inputs may be any that keep to these rules, and one draw needn't show every extreme that they name: In each group the lengths add up to more than 256 and at most 512; the first ends before slot 256 and the second after it; in one group a single sequence fills all 512 slots. Lengths may be 0.
All inputs are finite; a program needn't handle non-finite values.
Results may differ from a plain program's by a relative error of at most 0.015.
The roundings to bfloat16 on the way count: a program that leaves them out, or rounds other values in their place, can miss the bound.
Values may be sent and summed in bfloat16 or wider, within the bound.
No kernel may reach another device: no remote copies, remote signals or barrier semaphores. Data moves between devices by JAX's collectives and lax.ppermute only.
A program may use at most 128 MiB of HBM per device.

v0:
```python
import functools

import numpy as np

import jax
import jax.numpy as jnp
from jax import lax
from jax.experimental import pallas as pl
from jax.experimental.pallas import tpu as pltpu
from jax.sharding import PartitionSpec as P

HEAD_DIM = 64
LANES = 128
STEP = 10


EPS_NORM = 1e-05
BETA_ONE = 0.9
BETA_TWO = 0.999
EPS_ADAM = 1e-08
WEIGHT_DECAY = 0.01
NEG_FILL = -1000000000.0
LOW = jnp.bfloat16
F32 = jnp.float32


def normalize_fwd(values, gain_row, shift_row):
    row_mean = jnp.mean(values, axis=-1, keepdims=True)
    centered = values - row_mean
    variance = jnp.mean(centered * centered, axis=-1, keepdims=True)
    inv_std = lax.rsqrt(variance + EPS_NORM)
    normed = centered * inv_std
    return (normed * gain_row + shift_row, normed, inv_std)


def normalize_back(gradient, normed, inv_std, gain_row):
    grad_norm = gradient * gain_row
    grad_in = inv_std * (
        grad_norm
        - jnp.mean(grad_norm, axis=-1, keepdims=True)
        - normed * jnp.mean(grad_norm * normed, axis=-1, keepdims=True)
    )
    return (grad_in, jnp.sum(gradient * normed, axis=0), jnp.sum(gradient, axis=0))


def adamw(weight, moment, square, gradient, step_rate, decay_rate):
    moment = BETA_ONE * moment + (1.0 - BETA_ONE) * gradient
    square = BETA_TWO * square + (1.0 - BETA_TWO) * gradient * gradient
    direction = (
        moment / (1.0 - BETA_ONE**STEP) / (jnp.sqrt(square / (1.0 - BETA_TWO**STEP)) + EPS_ADAM)
    )
    return (weight - step_rate * (direction + decay_rate * weight), moment, square)


def swap_dp(values, mask):
    size = lax.axis_size("dp")
    return lax.ppermute(values, "dp", [(i, i ^ mask) for i in range(size)])


def swap_tensor(values):
    return lax.ppermute(values, "tensor", [(0, 1), (1, 0)])


def high_bits():
    return list(range(2, lax.axis_size("dp").bit_length() - 1))


def high_groups():
    bits = high_bits()
    return [[1 << bit for bit in bits[i : i + 2]] for i in range(0, len(bits), 2)]


def group_masks(group):
    return [0] + group + ([group[0] ^ group[1]] if len(group) == 2 else [])


def gather_high(shard):
    groups = high_groups()
    for place, group in enumerate(groups):
        pieces = [shard if mask == 0 else swap_dp(shard, mask) for mask in group_masks(group)]
        if place < len(groups) - 1:
            shard = jnp.concatenate(pieces, axis=0)
    return pieces


def send_high(parts):
    masks = group_masks(high_groups()[-1])
    return [parts[0]] + [swap_dp(part, mask) for part, mask in zip(parts[1:], masks[1:])]


def reduce_high(parts):
    total = sum(part.astype(F32) for part in parts)
    for group in reversed(high_groups()[:-1]):
        masks = group_masks(group)
        rows = total.shape[0] // len(masks)
        low = total.astype(LOW)
        total = total[:rows]
        for place, mask in enumerate(masks[1:], 1):
            total = total + swap_dp(low[place * rows : (place + 1) * rows], mask).astype(F32)
    return total


def relative_order(width):
    size = lax.axis_size("dp")
    rows = width // size
    inner_first = high_bits() + [1, 0]
    masks = np.zeros((size,), np.int32)
    for block in range(size):
        for place, bit in enumerate(inner_first):
            if (block >> place) & 1:
                masks[block] |= 1 << bit
    block_mask = jnp.asarray(np.repeat(masks, rows))
    offsets = jnp.asarray(np.tile(np.arange(rows, dtype=np.int32), size))
    return (lax.axis_index("dp") ^ block_mask) * rows + offsets


def dot(left, right):
    return jnp.dot(left, right, preferred_element_type=F32)


def dot_nt(left, right):
    return lax.dot_general(left, right, (((1,), (1,)), ((), ())), preferred_element_type=F32)


def dot_tn(left, right):
    return lax.dot_general(left, right, (((0,), (0,)), ((), ())), preferred_element_type=F32)


def shape_of(rows, columns, kind):
    return jax.ShapeDtypeStruct((rows, columns), kind)


def run(kernel, outs, operands, flops, after=(), grid=(), in_specs=None, out_specs=None, scratch=()):
    count = len(operands)

    def body(*refs):
        kernel(*refs[:count], *refs[count + len(after) :])

    whole = pl.BlockSpec(memory_space=pltpu.VMEM)
    in_specs = in_specs or [whole] * count
    size = sum(v.size * v.dtype.itemsize for v in list(operands) + list(outs))
    return pl.pallas_call(
        body,
        grid=grid,
        out_shape=list(outs),
        in_specs=list(in_specs) + [pl.BlockSpec(memory_space=pl.ANY)] * len(after),
        out_specs=list(out_specs or [whole] * len(outs)),
        scratch_shapes=list(scratch),
        compiler_params=pltpu.CompilerParams(
            vmem_limit_bytes=min(size + ((12 if flops else 4) << 20), 44 << 20)
        ),
        cost_estimate=pl.CostEstimate(flops=flops, bytes_accessed=size, transcendentals=0),
    )(*operands, *after)


def join_high_kernel(count, *refs):
    pieces, (first, second) = refs[:count], refs[count:]
    cut = first.shape[1]
    rows = pieces[0].shape[0]
    for place, piece in enumerate(pieces):
        to = slice(place * rows, (place + 1) * rows)
        first[to, :] = piece[:, :cut]
        second[to, :] = piece[:, cut:]


def join_high(pieces, cut, after=()):
    rows, columns = pieces[0].shape
    rows = rows * len(pieces)
    return run(
        functools.partial(join_high_kernel, len(pieces)),
        [shape_of(rows, cut, LOW), shape_of(rows, columns - cut, LOW)],
        pieces,
        0,
        after,
    )


def join_plane_kernel(across, down, across_far, down_far, across_all, down_all):
    columns, rows = across.shape[1], down.shape[0]
    across_all[:, :columns] = across[...]
    across_all[:, columns:] = across_far[...]
    down_all[:rows, :] = down[...]
    down_all[rows:, :] = down_far[...]


def join_plane(across, down, across_far, down_far, after=()):
    return run(
        join_plane_kernel,
        [
            shape_of(across.shape[0], 2 * across.shape[1], LOW),
            shape_of(2 * down.shape[0], down.shape[1], LOW),
        ],
        [across, down, across_far, down_far],
        0,
        after,
    )


def added(left, right, rows, columns):
    return (left[rows, columns].astype(F32) + right[rows, columns].astype(F32)).astype(LOW)


def split_core_kernel(keep, far, a_keep, a_send, b_keep, b_send):
    rows, cut = a_keep.shape
    half = b_keep.shape[1]
    every = slice(None)
    a_keep[...] = added(keep, far, slice(0, rows), slice(0, cut))
    a_send[...] = added(keep, far, slice(rows, 2 * rows), slice(0, cut))
    b_keep[...] = added(keep, far, every, slice(cut, cut + half))
    b_send[...] = added(keep, far, every, slice(cut + half, cut + 2 * half))


def split_core(keep, far, cut, after=()):
    rows, columns = keep.shape
    a_shape = shape_of(rows // 2, cut, LOW)
    b_shape = shape_of(rows, (columns - cut) // 2, LOW)
    return run(
        split_core_kernel, [a_shape, a_shape, b_shape, b_shape], [keep, far], 0, after
    )


def split_plane_kernel(a, a_far, b, b_far, a_keep, a_send, b_keep, b_send):
    half, rows = a_keep.shape[1], b_keep.shape[0]
    every = slice(None)
    a_keep[...] = added(a, a_far, every, slice(0, half))
    a_send[...] = added(a, a_far, every, slice(half, 2 * half))
    b_keep[...] = added(b, b_far, slice(0, rows), every)
    b_send[...] = added(b, b_far, slice(rows, 2 * rows), every)


def split_plane(a, a_far, b, b_far, after=()):
    a_shape = shape_of(a.shape[0], a.shape[1] // 2, LOW)
    b_shape = shape_of(b.shape[0] // 2, b.shape[1], LOW)
    return run(
        split_plane_kernel, [a_shape, a_shape, b_shape, b_shape], [a, a_far, b, b_far], 0, after
    )


def split_high_kernel(a, a_far, b, b_far, *parts):
    cut = a.shape[1]
    rows = parts[0].shape[0]
    for place, part in enumerate(parts):
        at = slice(place * rows, (place + 1) * rows)
        part[:, :cut] = added(a, a_far, at, slice(None))
        part[:, cut:] = added(b, b_far, at, slice(None))


def split_high(a, a_far, b, b_far, after=()):
    count = len(group_masks(high_groups()[-1]))
    part = shape_of(a.shape[0] // count, a.shape[1] + b.shape[1], LOW)
    return run(split_high_kernel, [part] * count, [a, a_far, b, b_far], 0, after)


def flip(rank, first, second):
    return jnp.where(rank == 0, first, second)


def vectors_kernel(rank_ref, permute, a_own, a_far, relative, bias_q, bias_v, bias_inner):
    rank = rank_ref[0]
    side = a_own.shape[1] // 2
    width = relative.shape[1]
    half = width // 2
    spread = jnp.concatenate(
        [
            (ref[:, side - LANES : side].astype(F32) + ref[:, 2 * side - LANES :].astype(F32))
            for ref in (a_own, a_far)
        ],
        axis=0,
    )
    parts = jnp.transpose(spread)
    parts = [parts[16 * i : 16 * (i + 1)] for i in range(3)]
    relative[...] = ((parts[0] + parts[1]) + parts[2])[2:8]
    natural = [dot_nt(part.astype(LOW), permute[...]) for part in parts]
    natural = (natural[0] + natural[1]) + natural[2]
    for row, target in ((0, bias_q), (1, bias_v)):
        first, second = natural[row : row + 1, :half], natural[row : row + 1, half:]
        target[:, :half] = flip(rank, first, second)
        target[:, half:] = flip(rank, second, first)
    for cut in range(2):
        for place in range(2):
            near, far = 8 + 2 * place + cut, 8 + 2 * (1 - place) + cut
            at = (2 * cut + place) * width
            bias_inner[:, at : at + width] = flip(
                rank, natural[near : near + 1], natural[far : far + 1]
            )


def vector_lanes(rank, permute, grad_q, grad_v, sums_one, sums_two, sums_inner, natural, relative):
    width = natural.shape[1]
    half = width // 2
    natural[...] = jnp.zeros_like(natural)
    relative[...] = jnp.zeros_like(relative)
    for row, source in ((0, grad_q), (1, grad_v)):
        total = jnp.sum(source[...].astype(F32), axis=0, keepdims=True)
        first, second = total[:, :half], total[:, half:]
        natural[row : row + 1, :half] = flip(rank, first, second)
        natural[row : row + 1, half:] = flip(rank, second, first)
    for cut in range(2):
        for place in range(2):
            near, far = (2 * cut + place) * width, (2 * cut + 1 - place) * width
            row = 8 + 2 * place + cut
            natural[row : row + 1, :] = flip(
                rank, sums_inner[:, near : near + width], sums_inner[:, far : far + width]
            )
    relative[:16, :] = dot(natural[...].astype(LOW), permute[...])
    relative[2:5, :] = sums_one[:3, :]
    relative[5:8, :] = sums_two[:3, :]
    return jnp.transpose(relative[...]).astype(LOW)


def cast_kernel(source, target):
    target[...] = source[...].astype(LOW)


def project_kernel(rows, a_own, a_far, b_own, b_far, bias_q, bias_v, q, k, v):
    half = a_own.shape[0]
    own_rows, width = q.shape
    part = width // 2
    low, high = rows[:, :half], rows[:, half:]
    a_half, b_half = a_own.shape[1] // 2, b_own.shape[1] // 2
    for side in range(2):
        cols = slice(side * part, (side + 1) * part)
        at = slice(side * a_half, side * a_half + part)
        q[:, cols] = (
            dot(low[:own_rows], a_own[:, at]) + dot(high[:own_rows], a_far[:, at]) + bias_q[:, cols]
        ).astype(LOW)
        at = slice(side * a_half + part, side * a_half + 2 * part)
        k[:, cols] = (dot(low, a_own[:, at]) + dot(high, a_far[:, at])).astype(LOW)
        at = slice(side * b_half, side * b_half + part)
        v[:, cols] = (dot(low, b_own[:, at]) + dot(high, b_far[:, at]) + bias_v[:, cols]).astype(
            LOW
        )


def softmax_down(seg_q, seg_k, key_rows, queries):
    scores = dot_nt(key_rows, queries) * 0.125
    scores = jnp.where(seg_k[...] == seg_q[...], scores, NEG_FILL)
    exp_scores = jnp.exp(scores - jnp.max(scores, axis=0, keepdims=True))
    return exp_scores * (1.0 / jnp.sum(exp_scores, axis=0, keepdims=True))


def two_heads(out):
    joined = jnp.concatenate([out[0][:HEAD_DIM], out[1][HEAD_DIM:]], axis=0)
    return jnp.transpose(joined).astype(LOW)


def attend_kernel(seg_q, seg_k, q, k, v, attended):
    queries, key_rows, value_rows = q[...], k[...], v[...]
    first = lax.broadcasted_iota(jnp.int32, queries.shape, 1) < HEAD_DIM
    out = []
    for mine in (first, jnp.logical_not(first)):
        prob = softmax_down(
            seg_q, seg_k, key_rows, jnp.where(mine, queries, jnp.zeros_like(queries))
        )
        out.append(dot_tn(value_rows, prob.astype(LOW)))
    attended[...] = two_heads(out)


def attend_back_kernel(seg_q, seg_k, q, k, v, grad, grad_q, grad_k, grad_v):
    queries, key_rows, value_rows, grad_rows = q[...], k[...], v[...], grad[...]
    first = lax.broadcasted_iota(jnp.int32, queries.shape, 1) < HEAD_DIM
    first_all = lax.broadcasted_iota(jnp.int32, key_rows.shape, 1) < HEAD_DIM
    blank = jnp.zeros_like(queries)
    out_q, out_k, out_v = [], [], []
    for mine in (first, jnp.logical_not(first)):
        prob = softmax_down(seg_q, seg_k, key_rows, jnp.where(mine, queries, blank))
        grad_prob = dot_nt(value_rows, jnp.where(mine, grad_rows, blank))
        delta = jnp.sum(grad_prob * prob, axis=0, keepdims=True)
        grad_score = (prob * (grad_prob - delta)).astype(LOW)
        out_q.append(dot_tn(key_rows, grad_score) * 0.125)
        out_k.append(dot(grad_score, queries) * 0.125)
        out_v.append(dot(prob.astype(LOW), grad_rows))
    grad_q[...] = two_heads(out_q)
    grad_k[...] = jnp.where(first_all, out_k[0], out_k[1]).astype(LOW)
    grad_v[...] = jnp.where(first_all, out_v[0], out_v[1]).astype(LOW)


def out_norm_kernel(attended, rows, b_own, b_far, vec, y, y_low, normed, inv):
    half = b_own.shape[0]
    own_rows, width = y.shape
    part = width // 2
    b_half = b_own.shape[1] // 2
    near, far = attended[:, :part], attended[:, part:]
    out = []
    for weights in (b_own, b_far):
        out.append(
            dot_nt(near, weights[:, part : 2 * part])
            + dot_nt(far, weights[:, b_half + part : b_half + 2 * part])
        )
    total = rows[:own_rows, :].astype(F32) + jnp.concatenate(out, axis=1) + vec[0:1]
    y_new, normed[...], inv[...] = normalize_fwd(total, vec[1:2], vec[2:3])
    y[...] = y_new
    y_low[...] = y_new.astype(LOW)


def hidden_kernel(y_low, a_own, a_far, b_own, b_far, bias, activation, slope):
    half = a_own.shape[0]
    low, high = y_low[:, :half], y_low[:, half:]
    columns = a_own.shape[1]
    step = columns // 4
    for place, (own, far) in enumerate(((a_own, a_far), (b_own, b_far))):
        for start in range(0, columns, step):
            at = slice(start, start + step)
            to = slice(place * columns + start, place * columns + start + step)
            pre = dot(low, own[:, at]) + dot(high, far[:, at]) + bias[:, to]
            cdf = 0.5 + 0.5 * lax.erf(pre * (0.5**0.5))
            activation[:, to] = (pre * cdf).astype(LOW)
            slope[:, to] = cdf + pre * jnp.exp(-0.5 * pre * pre) * ((2.0 * np.pi) ** -0.5)


def out_back_kernel(
    activation, a_own, a_far, b_own, b_far, y, cot, valid, vec, mixed, grad, grad_low, sums
):
    columns = a_own.shape[1]
    act_a, act_b = activation[:, :columns], activation[:, columns:]
    out = [dot_nt(act_a, wa[...]) + dot_nt(act_b, wb[...]) for wa, wb in ((a_own, b_own), (a_far, b_far))]
    total = y[...] + jnp.concatenate(out, axis=1) + vec[3:4]
    result, normed, inv_std = normalize_fwd(total, vec[4:5], vec[5:6])
    mixed[...] = result.astype(LOW)
    grad_in, gain_sum, shift_sum = normalize_back(
        cot[...] * valid[...], normed, inv_std, vec[4:5]
    )
    grad[...] = grad_in
    grad_low[...] = grad_in.astype(LOW)
    sums[0:1] = jnp.sum(grad_in, axis=0, keepdims=True)
    sums[1:2] = gain_sum[None]
    sums[2:3] = shift_sum[None]


def hidden_back_kernel(grad_low, a_own, a_far, b_own, b_far, slope, grad_pre, sums):
    half = a_own.shape[0]
    low, high = grad_low[:, :half], grad_low[:, half:]
    columns = a_own.shape[1]
    step = columns // 4
    for place, (own, far) in enumerate(((a_own, a_far), (b_own, b_far))):
        for start in range(0, columns, step):
            at = slice(start, start + step)
            to = slice(place * columns + start, place * columns + start + step)
            value = ((dot(low, own[:, at]) + dot(high, far[:, at])) * slope[:, to]).astype(LOW)
            grad_pre[:, to] = value
            sums[:, to] = jnp.sum(value.astype(F32), axis=0, keepdims=True)


def norm_back_kernel(
    grad_pre, a_own, a_far, b_own, b_far, grad_two, normed, inv, vec, o_own, o_far,
    grad, grad_low, grad_attn, sums,
):
    columns = a_own.shape[1]
    pre_a, pre_b = grad_pre[:, :columns], grad_pre[:, columns:]
    out = [dot_nt(pre_a, wa[...]) + dot_nt(pre_b, wb[...]) for wa, wb in ((a_own, b_own), (a_far, b_far))]
    grad_in, gain_sum, shift_sum = normalize_back(
        grad_two[...] + jnp.concatenate(out, axis=1), normed[...], inv[...], vec[1:2]
    )
    grad[...] = grad_in
    low = grad_in.astype(LOW)
    grad_low[...] = low
    sums[0:1] = jnp.sum(grad_in, axis=0, keepdims=True)
    sums[1:2] = gain_sum[None]
    sums[2:3] = shift_sum[None]
    half = o_own.shape[0]
    part = grad.shape[1] // 2
    o_half = o_own.shape[1] // 2
    for side in range(2):
        at = slice(side * o_half + part, side * o_half + 2 * part)
        grad_attn[:, side * part : (side + 1) * part] = (
            dot(low[:, :half], o_own[:, at]) + dot(low[:, half:], o_far[:, at])
        ).astype(LOW)


def rows_back_kernel(grad_q, grad_k, grad_v, a_own, a_far, b_own, b_far, grad_one, own, away):
    own_rows, width = own.shape
    part = width // 2
    a_half, b_half = a_own.shape[1] // 2, b_own.shape[1] // 2
    half = a_own.shape[0]
    for place, (wa, wb) in enumerate(((a_own, b_own), (a_far, b_far))):
        to = slice(place * half, (place + 1) * half)
        both = jnp.zeros((2 * own_rows, half), F32)
        mine = grad_one[:, to]
        for side in range(2):
            cols = slice(side * part, (side + 1) * part)
            at = side * a_half
            mine = mine + dot_nt(grad_q[:, cols], wa[:, at : at + part])
            both = both + dot_nt(grad_k[:, cols], wa[:, at + part : at + 2 * part])
            at = side * b_half
            both = both + dot_nt(grad_v[:, cols], wb[:, at : at + part])
        own[:, to] = mine + both[:own_rows]
        away[:, to] = both[own_rows:].astype(LOW)


def first_grads_kernel(
    a_half, rank_ref, permute, rows, grad_q, grad_k, grad_v, grad_low, attended,
    sums_one, sums_two, sums_inner, send, keep, natural, relative,
):
    half = keep.shape[0]
    own_rows, width = grad_q.shape
    part = width // 2
    extra = vector_lanes(
        rank_ref[0], permute, grad_q, grad_v, sums_one, sums_two, sums_inner, natural, relative
    )
    for place, to in ((1, send), (0, keep)):
        at = slice(place * half, (place + 1) * half)
        both = rows[:, at]
        mine = rows[:own_rows, at]
        low = grad_low[:, at]
        for side in range(2):
            cols = slice(side * part, (side + 1) * part)
            base = side * a_half
            to[:, base : base + part] = dot_tn(mine, grad_q[:, cols]).astype(LOW)
            to[:, base + part : base + 2 * part] = dot_tn(both, grad_k[:, cols]).astype(LOW)
            to[:, base + 2 * part : base + a_half] = extra[at, :]
            base = 2 * a_half + side * 2 * part
            to[:, base : base + part] = dot_tn(both, grad_v[:, cols]).astype(LOW)
            to[:, base + part : base + 2 * part] = dot_tn(low, attended[:, cols]).astype(LOW)


def on_device(
    tokens,
    cotangent,
    lengths,
    w_qkv,
    m_qkv,
    v_qkv,
    w_out,
    m_out,
    v_out,
    w_in,
    m_in,
    v_in,
    w_back,
    m_back,
    v_back,
    vectors,
    m_vectors,
    v_vectors,
):
    own_rows, width = tokens.shape
    tensor_rank = lax.axis_index("tensor")
    group_rows = 2 * own_rows
    shard_rows = w_qkv.shape[1]
    part = w_qkv.shape[2]
    hidden_half = w_in.shape[1]
    cut = hidden_half // 2
    full_inner = 2 * hidden_half
    half = width // 2
    count = vectors.shape[0]
    shard_width = vectors.shape[1]

    rest = vectors.T
    vec_parts = []
    for _ in range(3):
        vec_parts.append(jnp.pad(rest.astype(LOW), ((0, 0), (0, 16 - count))))
        rest = rest - rest.astype(LOW).astype(F32)
    vec_lanes = jnp.pad(jnp.concatenate(vec_parts, axis=1), ((0, 0), (0, LANES - 48)))
    blank = jnp.zeros_like(vec_lanes)
    vec_lanes = jnp.concatenate(
        [
            jnp.where(tensor_rank == 0, vec_lanes, blank),
            jnp.where(tensor_rank == 0, blank, vec_lanes),
        ],
        axis=0,
    )
    low_qkv = w_qkv.astype(LOW)
    shard_one = jnp.concatenate(
        [low_qkv[0], low_qkv[1], vec_lanes, low_qkv[2], w_out.T.astype(LOW)], axis=1
    )
    a_width = 2 * part + LANES
    low_shape = shape_of(shard_rows, hidden_half, LOW)
    rank = tensor_rank.astype(jnp.int32).reshape(1)
    scalar = pl.BlockSpec(memory_space=pltpu.SMEM)
    vmem = pl.BlockSpec(memory_space=pltpu.VMEM)

    tokens_far = swap_tensor(tokens)
    one_high = gather_high(shard_one)
    one = join_high(one_high, a_width)
    one_far = swap_tensor(one[0]), swap_dp(one[1], 2)
    shard_in = run(cast_kernel, [low_shape], [w_in], 0, after=one[:1])[0]
    inner_high = gather_high(shard_in)

    order = relative_order(width)
    permute = (jnp.arange(width, dtype=jnp.int32)[:, None] == order[None, :]).astype(LOW)
    permute_wide = permute.astype(F32)
    exact = lax.Precision.HIGHEST
    rows_all = jnp.concatenate([dot(tokens, permute), dot(tokens_far, permute)]).astype(LOW)
    cot = dot(cotangent, permute)

    one = join_plane(*one, *one_far, after=[shard_in])
    one_far = swap_dp(one[0], 2), swap_tensor(one[1])
    inner = join_high(inner_high, cut, after=one[:1])
    shard_back = run(cast_kernel, [low_shape], [w_back.T], 0, after=inner[:1])[0]
    outer_high = gather_high(shard_back)
    one = join_plane(one[1], one[0], one_far[1], one_far[0], after=inner[:1])[::-1]
    a_own, b_own = one
    a_far, b_far = swap_dp(a_own, 1), swap_dp(b_own, 1)
    inner_far = swap_tensor(inner[0]), swap_dp(inner[1], 2)

    vec, bias_query, bias_value, bias_inner = run(
        vectors_kernel,
        [
            shape_of(6, width, F32),
            shape_of(1, width, F32),
            shape_of(1, width, F32),
            shape_of(1, full_inner, F32),
        ],
        [rank, permute, a_own, a_far],
        1,
        after=[shard_back],
        in_specs=[scalar, vmem, vmem, vmem],
    )

    seq_ends = jnp.cumsum(lengths[0])
    local = jnp.arange(own_rows, dtype=jnp.int32)
    own_positions = tensor_rank * own_rows + local
    key_positions = jnp.concatenate([own_positions, (1 - tensor_rank) * own_rows + local])

    def segments(positions):
        return jnp.sum((positions[:, None] >= seq_ends[None, :]).astype(jnp.int32), axis=1)

    seg_own, seg_keys = segments(own_positions)[None, :], segments(key_positions)[:, None]
    valid = (own_positions < seq_ends[-1]).astype(F32)[:, None]

    wide_low = shape_of(own_rows, width, LOW)
    wide = shape_of(own_rows, width, F32)
    group_low = shape_of(group_rows, width, LOW)
    sums_shape = shape_of(8, width, F32)
    unit = 2 * own_rows * width * width
    queries, key_rows, value_rows = run(
        project_kernel,
        [wide_low, group_low, group_low],
        [rows_all, a_own, a_far, b_own, b_far, bias_query, bias_value],
        5 * unit,
    )
    inner = join_plane(*inner, *inner_far, after=[queries])
    inner_far = swap_dp(inner[0], 2), swap_tensor(inner[1])
    outer = join_high(outer_high, cut, after=[queries])
    pairs = width // LANES
    own_block = pl.BlockSpec((own_rows, LANES), lambda i: (0, i))
    all_block = pl.BlockSpec((group_rows, LANES), lambda i: (0, i))

    def fixed(shape):
        return pl.BlockSpec(shape, lambda i: (0, 0))

    attended = run(
        attend_kernel,
        [wide_low],
        [seg_own, seg_keys, queries, key_rows, value_rows],
        12 * unit,
        after=[inner[0], outer[0]],
        grid=(pairs,),
        in_specs=[fixed((1, own_rows)), fixed((group_rows, 1)), own_block, all_block, all_block],
        out_specs=[own_block],
    )[0]
    inner = join_plane(inner[1], inner[0], inner_far[1], inner_far[0], after=[attended])[::-1]
    c_own, d_own = inner
    c_far, d_far = swap_dp(c_own, 1), swap_dp(d_own, 1)
    outer_far = swap_tensor(outer[0]), swap_dp(outer[1], 2)
    first_norm, first_low, normed_one, inv_one = run(
        out_norm_kernel,
        [wide, wide_low, wide, shape_of(own_rows, 1, F32)],
        [attended, rows_all, b_own, b_far, vec],
        2 * unit,
        after=inner[:1],
    )
    outer = join_plane(*outer, *outer_far, after=[first_low])
    outer_far = swap_dp(outer[0], 2), swap_tensor(outer[1])
    activation, slope = run(
        hidden_kernel,
        [shape_of(own_rows, full_inner, LOW), shape_of(own_rows, full_inner, F32)],
        [first_low, c_own, c_far, d_own, d_far, bias_inner],
        8 * unit,
        after=outer[:1],
    )
    outer = join_plane(outer[1], outer[0], outer_far[1], outer_far[0], after=[activation])[::-1]
    e_own, f_own = outer
    e_far, f_far = swap_dp(e_own, 1), swap_dp(f_own, 1)
    mixed_rel, grad_two, grad_two_low, sums_two = run(
        out_back_kernel,
        [wide_low, wide, wide_low, sums_shape],
        [activation, e_own, e_far, f_own, f_far, first_norm, cot, valid, vec],
        5 * unit,
    )
    mixed = dot_nt(mixed_rel, permute).astype(LOW)

    def weight_grad(left, right):
        send = dot_tn(left[:, half:], right).astype(LOW)
        return dot_tn(left[:, :half], right).astype(LOW), swap_dp(send, 1)

    outer = weight_grad(grad_two_low, activation)
    grad_pre, sums_inner = run(
        hidden_back_kernel,
        [shape_of(own_rows, full_inner, LOW), shape_of(1, full_inner, F32)],
        [grad_two_low, e_own, e_far, f_own, f_far, slope],
        6 * unit,
    )
    a_keep, a_send, b_keep, b_send = split_core(*outer, hidden_half, after=[grad_pre])
    outer = a_keep, swap_dp(a_send, 2), b_keep, swap_tensor(b_send)
    inner = weight_grad(first_low, grad_pre)
    grad_one, grad_one_low, grad_attn, sums_one = run(
        norm_back_kernel,
        [wide, wide_low, wide_low, sums_shape],
        [grad_pre, c_own, c_far, d_own, d_far, grad_two, normed_one, inv_one, vec, b_own, b_far],
        6 * unit,
        after=[a_keep],
    )
    a_keep, a_send, b_keep, b_send = split_plane(*outer, after=[grad_attn])
    outer = a_keep, swap_tensor(a_send), b_keep, swap_dp(b_send, 2)
    inner_keep = split_core(*inner, hidden_half, after=[a_keep])
    grad_q, grad_k, grad_v = run(
        attend_back_kernel,
        [wide_low, group_low, group_low],
        [seg_own, seg_keys, queries, key_rows, value_rows, grad_attn],
        25 * unit,
        after=[a_keep, inner_keep[0]],
        grid=(pairs,),
        in_specs=[fixed((1, own_rows)), fixed((group_rows, 1))]
        + [own_block, all_block, all_block, own_block],
        out_specs=[own_block, all_block, all_block],
    )
    outer = send_high(split_high(*outer, after=[grad_q]))
    a_keep, a_send, b_keep, b_send = inner_keep
    inner = a_keep, swap_dp(a_send, 2), b_keep, swap_tensor(b_send)
    one_shape = shape_of(half, 2 * a_width + 4 * part, LOW)
    one_send, one_keep = run(
        functools.partial(first_grads_kernel, a_width),
        [one_shape, one_shape],
        [rank, permute, rows_all, grad_q, grad_k, grad_v, grad_one_low, attended]
        + [sums_one, sums_two, sums_inner],
        6 * unit,
        after=outer[:1],
        in_specs=[scalar] + [vmem] * 10,
        scratch=[pltpu.VMEM((16, width), F32), pltpu.VMEM((LANES, width), F32)],
    )
    one_far = swap_dp(one_send, 1)
    a_keep, a_send, b_keep, b_send = split_plane(*inner, after=[one_keep])
    inner = a_keep, swap_tensor(a_send), b_keep, swap_dp(b_send, 2)
    grad_own, grad_away = run(
        rows_back_kernel,
        [wide, wide_low],
        [grad_q, grad_k, grad_v, a_own, a_far, b_own, b_far, grad_one],
        5 * unit,
        after=[a_keep] + outer[1:],
    )
    grad_rel = grad_own + swap_tensor(grad_away).astype(F32)
    input_grad = lax.dot_general(
        grad_rel, permute_wide, (((1,), (1,)), ((), ())), precision=exact
    )
    summed_back = reduce_high(outer).T
    inner = send_high(split_high(*inner, after=[grad_own]))
    one_keep = split_core(one_keep, one_far, 2 * a_width, after=inner[:1])
    a_keep, a_send, b_keep, b_send = one_keep
    one = a_keep, swap_dp(a_send, 2), b_keep, swap_tensor(b_send)
    summed_in = reduce_high(inner)
    a_keep, a_send, b_keep, b_send = split_plane(*one)
    one = a_keep, swap_tensor(a_send), b_keep, swap_dp(b_send, 2)
    sum_one = reduce_high(send_high(split_high(*one, after=inner[1:])))

    summed_vectors = lax.dynamic_slice_in_dim(
        sum_one[:, 2 * part : a_width], tensor_rank * shard_width, shard_width, axis=0
    )[:, :count].T
    summed_qkv = jnp.stack(
        [
            sum_one[:, :part],
            sum_one[:, part : 2 * part],
            sum_one[:, a_width : a_width + part],
        ]
    )
    summed_out = sum_one[:, a_width + part :].T
    new_qkv, moment_qkv, square_qkv = adamw(
        w_qkv, m_qkv, v_qkv, summed_qkv, float(width) ** (-0.5), WEIGHT_DECAY
    )
    new_out, moment_out, square_out = adamw(
        w_out, m_out, v_out, summed_out, (4.0 * width / group_rows) ** (-0.5), WEIGHT_DECAY
    )
    new_in, moment_in, square_in = adamw(
        w_in, m_in, v_in, summed_in, float(width) ** (-0.5), WEIGHT_DECAY
    )
    new_back, moment_back, square_back = adamw(
        w_back, m_back, v_back, summed_back, float(full_inner) ** (-0.5), WEIGHT_DECAY
    )
    new_vectors, moment_vectors, square_vectors = adamw(
        vectors, m_vectors, v_vectors, summed_vectors, 0.1, 0.0
    )
    return (
        mixed,
        input_grad,
        new_qkv,
        moment_qkv,
        square_qkv,
        new_out,
        moment_out,
        square_out,
        new_in,
        moment_in,
        square_in,
        new_back,
        moment_back,
        square_back,
        new_vectors,
        moment_vectors,
        square_vectors,
    )


def solution(mesh):
    placed = (
        P(("dp", "tensor"), None),
        P(("dp", "tensor"), None),
        P("dp", None),
        P(None, "dp", "tensor"),
        P(None, "dp", "tensor"),
        P(None, "dp", "tensor"),
        P("tensor", "dp"),
        P("tensor", "dp"),
        P("tensor", "dp"),
        P("dp", "tensor"),
        P("dp", "tensor"),
        P("dp", "tensor"),
        P("tensor", "dp"),
        P("tensor", "dp"),
        P("tensor", "dp"),
        P(None, ("dp", "tensor")),
        P(None, ("dp", "tensor")),
        P(None, ("dp", "tensor")),
    )
    return jax.shard_map(
        on_device,
        mesh=mesh,
        in_specs=placed,
        out_specs=(
            P(("dp", "tensor"), None),
            P(("dp", "tensor"), None),
            P(None, "dp", "tensor"),
            P(None, "dp", "tensor"),
            P(None, "dp", "tensor"),
            P("tensor", "dp"),
            P("tensor", "dp"),
            P("tensor", "dp"),
            P("dp", "tensor"),
            P("dp", "tensor"),
            P("dp", "tensor"),
            P("tensor", "dp"),
            P("tensor", "dp"),
            P("tensor", "dp"),
            P(None, ("dp", "tensor")),
            P(None, ("dp", "tensor")),
            P(None, ("dp", "tensor")),
        ),
        check_vma=False,
    )
```

profile of v0, /device:TPU:0, one launch (start us, length us, event | category | flops | bytes accessed | tf_op | source)
XLA Modules:
  0.0 290.7 jit_solution(13877290359710627831)
XLA Ops:
  4.1 3.1 %collective-permute-start.1 = (bf16[48,1664]{1,0:T(8,128)(2,1)S(1)}, bf16[48,1664]{1,0:T(8,128)(2,1)S(1)}, u32[]{:S(2)}, u32[]{:S(2)}) collective-permute-start(bf16[48,1664]{1,0:T(8,128)(2,1)S(1)} %bitcast_dynamic-update-slice_fusion.refs_0_), channel_id=1, source_target_pairs={{0,8},{2,10},{4,12},{6,14},{8,0},{10,2},{12,4},{14,6},{16,24},{18,... | collective-permute-start | bytes 479240 | tf_op jit(solution)/shard_map/ppermute | solution.py:57
  7.2 2.6 collective-permute-start.2
  9.8 3.9 %collective-permute-done.1.refs_1_ = bf16[48,1664]{1,0:T(8,128)(2,1)S(1)} collective-permute-done((bf16[48,1664]{1,0:T(8,128)(2,1)S(1)}, bf16[48,1664]{1,0:T(8,128)(2,1)S(1)}, u32[]{:S(2)}, u32[]{:S(2)}) %collective-permute-start.1) | collective-permute-done | bytes 159776 | tf_op jit(solution)/shard_map/ppermute | solution.py:57
  13.7 8.3 %collective-permute-done.2.refs_2_ = bf16[48,1664]{1,0:T(8,128)(2,1)S(1)} collective-permute-done((bf16[48,1664]{1,0:T(8,128)(2,1)S(1)}, bf16[48,1664]{1,0:T(8,128)(2,1)S(1)}, u32[]{:S(2)}, u32[]{:S(2)}) %collective-permute-start.2) | collective-permute-done | bytes 159776 | tf_op jit(solution)/shard_map/ppermute | solution.py:57
  25.2 6.1 %collective-permute-done.5.refs_3_ = bf16[192,768]{1,0:T(8,128)(2,1)S(1)} collective-permute-done((bf16[192,768]{1,0:T(8,128)(2,1)S(1)}, bf16[192,768]{1,0:T(8,128)(2,1)S(1)}, u32[]{:S(2)}, u32[]{:S(2)}) %collective-permute-start.5) | collective-permute-done | bytes 294944 | tf_op jit(solution)/shard_map/ppermute | solution.py:57
  33.2 3.3 %collective-permute-start.8 = (bf16[48,1536]{1,0:T(8,128)(2,1)S(1)}, bf16[48,1536]{1,0:T(8,128)(2,1)S(1)}, u32[]{:S(2)}, u32[]{:S(2)}) collective-permute-start(bf16[48,1536]{1,0:T(8,128)(2,1)S(1)} %shard_map.324.refs_4_.refs_0_), channel_id=1, source_target_pairs={{0,8},{2,10},{4,12},{6,14},{8,0},{10,2},{12,4},{14,6},{16,24},{18,... | collective-permute-start | bytes 442376 | tf_op jit(solution)/shard_map/ppermute | solution.py:57
  40.2 7.9 %collective-permute-done.9.refs_2_ = bf16[48,1536]{1,0:T(8,128)(2,1)S(1)} collective-permute-done((bf16[48,1536]{1,0:T(8,128)(2,1)S(1)}, bf16[48,1536]{1,0:T(8,128)(2,1)S(1)}, u32[]{:S(2)}, u32[]{:S(2)}) %collective-permute-start.9) | collective-permute-done | bytes 147488 | tf_op jit(solution)/shard_map/ppermute | solution.py:57
  54.9 7.3 %collective-permute-done = bf16[256,768]{1,0:T(8,128)(2,1)S(1)} collective-permute-done((bf16[256,768]{1,0:T(8,128)(2,1)S(1)}, bf16[256,768]{1,0:T(8,128)(2,1)S(1)}, u32[]{:S(2)}, u32[]{:S(2)}) %collective-permute-start) | collective-permute-done | bytes 393248 | tf_op jit(solution)/shard_map/ppermute | solution.py:61
  62.9 2.9 shard_map.329
  66.4 4.3 %shard_map.330 = (bf16[256,768]{1,0:T(8,128)(2,1)S(1)}, bf16[512,768]{1,0:T(8,128)(2,1)S(1)}, bf16[512,768]{1,0:T(8,128)(2,1)S(1)}) custom-call(bf16[512,768]{1,0:T(8,128)(2,1)S(1)} %pad_maximum_fusion.refs_0_.refs_1_.refs_2_, bf16[384,1792]{1,0:T(8,128)(2,1)} %get-tuple-element.106.refs_2_.refs_1_.refs_3_, ...), custom_call_target="tpu_custom_call" | custom-call | flops 1509949440 | bytes 7870464 | tf_op jit(solution)/shard_map/pallas_call | solution.py:142
  70.8 2.6 shard_map.331
  85.5 7.1 %collective-permute-done.16.refs_2_ = bf16[48,1536]{1,0:T(8,128)(2,1)} collective-permute-done((bf16[48,1536]{1,0:T(8,128)(2,1)}, bf16[48,1536]{1,0:T(8,128)(2,1)}, u32[]{:S(2)}, u32[]{:S(2)}) %collective-permute-start.16) | collective-permute-done | bytes 147488 | tf_op jit(solution)/shard_map/ppermute | solution.py:57
  99.8 8.0 %shard_map.333.refs_4_.refs_0_.refs_7_ = bf16[256,768]{1,0:T(8,128)(2,1)S(1)} custom-call(s32[1,256]{1,0:T(1,128)S(1)} %bitcast.78, s32[512,1]{1,0:T(8,128)S(1)} %copy-done.20, bf16[256,768]{1,0:T(8,128)(2,1)S(1)} %copy-done.6, bf16[512,768]{1,0:T(8,128)(2,1)S(1)} %copy-done.27, bf16[512,768]{1,0:T(8,128)(2,1)S(1)} %copy-done.30, ...), custom_call_target="tpu_custom_call" | custom-call | flops 3623878656 | bytes 2362368 | tf_op jit(solution)/shard_map/pallas_call | solution.py:142
  114.1 5.0 %collective-permute-done.22.refs_2_ = bf16[192,768]{1,0:T(8,128)(2,1)S(1)} collective-permute-done((bf16[192,768]{1,0:T(8,128)(2,1)S(1)}, bf16[192,768]{1,0:T(8,128)(2,1)S(1)}, u32[]{:S(2)}, u32[]{:S(2)}) %collective-permute-start.22) | collective-permute-done | bytes 294944 | tf_op jit(solution)/shard_map/ppermute | solution.py:61
  122.6 2.5 shard_map.337
  125.1 9.5 %collective-permute-done.24.refs_2_ = bf16[384,768]{1,0:T(8,128)(2,1)S(1)} collective-permute-done((bf16[384,768]{1,0:T(8,128)(2,1)S(1)}, bf16[384,768]{1,0:T(8,128)(2,1)S(1)}, u32[]{:S(2)}, u32[]{:S(2)}) %collective-permute-start.24) | collective-permute-done | bytes 589856 | tf_op jit(solution)/shard_map/ppermute | solution.py:61
  139.7 2.4 shard_map.339
  147.6 12.7 %shard_map.341 = (bf16[192,1536]{1,0:T(8,128)(2,1)S(1)}, bf16[192,1536]{1,0:T(8,128)(2,1)S(1)}, bf16[384,768]{1,0:T(8,128)(2,1)S(1)}, bf16[384,768]{1,0:T(8,128)(2,1)S(1)}) custom-call(bf16[384,3072]{1,0:T(8,128)(2,1)S(1)} %convolution_convert_fusion.3.refs_0_, bf16[384,3072]{1,0:T(8,128)(2,1)S(1)} %collective-permute-done.28.refs_1_, ...), custom_call_target="tpu_custom_call" | custom-call | bytes 7077888 | tf_op jit(solution)/shard_map/pallas_call | solution.py:142
  164.2 2.7 shard_map.342
  166.8 9.0 %collective-permute-done.29.refs_1_ = bf16[192,1536]{1,0:T(8,128)(2,1)S(1)} collective-permute-done((bf16[192,1536]{1,0:T(8,128)(2,1)S(1)}, bf16[192,1536]{1,0:T(8,128)(2,1)S(1)}, u32[]{:S(2)}, u32[]{:S(2)}) %collective-permute-start.29) | collective-permute-done | bytes 589856 | tf_op jit(solution)/shard_map/ppermute | solution.py:57
  180.9 10.0 %shard_map.345 = (bf16[256,768]{1,0:T(8,128)(2,1)S(1)}, bf16[512,768]{1,0:T(8,128)(2,1)S(1)}, bf16[512,768]{1,0:T(8,128)(2,1)S(1)}) custom-call(s32[1,256]{1,0:T(1,128)S(1)} %bitcast.79, s32[512,1]{1,0:T(8,128)S(1)} %copy-done.21, bf16[256,768]{1,0:T(8,128)(2,1)S(1)} %copy-done.7, bf16[512,768]{1,0:T(8,128)(2,1)S(1)} %copy-done.28, ...), custom_call_target="tpu_custom_call" | custom-call | flops 7549747200 | bytes 4328448 | tf_op jit(solution)/shard_map/pallas_call | solution.py:142
  192.2 3.0 %shard_map.347 = (bf16[384,3328]{1,0:T(8,128)(2,1)S(1)}, bf16[384,3328]{1,0:T(8,128)(2,1)S(1)}) custom-call(s32[1]{0:T(128)} %bitcast.11.refs_0_, bf16[768,768]{1,0:T(8,128)(2,1)S(1)} %copy-done.3, bf16[512,768]{1,0:T(8,128)(2,1)S(1)} %pad_maximum_fusion.refs_0_.refs_1_.refs_2_, bf16[256,768]{1,0:T(8,128)(2,1)S(1)} %get-tuple-element.143.refs_4_.refs_3_.refs_0_, ...), custom_call_target="tpu_custom_call" | custom-call | flops 1811939328 | bytes 9891844 | tf_op jit(solution)/shard_map/pallas_call | solution.py:142
  199.6 11.4 %collective-permute-done.32.refs_1_ = bf16[192,1536]{1,0:T(8,128)(2,1)S(1)} collective-permute-done((bf16[192,1536]{1,0:T(8,128)(2,1)S(1)}, bf16[192,1536]{1,0:T(8,128)(2,1)S(1)}, u32[]{:S(2)}, u32[]{:S(2)}) %collective-permute-start.32) | collective-permute-done | bytes 589856 | tf_op jit(solution)/shard_map/ppermute | solution.py:57
  213.8 3.3 %collective-permute-start.37 = (bf16[48,1536]{1,0:T(8,128)(2,1)S(1)}, bf16[48,1536]{1,0:T(8,128)(2,1)S(1)}, u32[]{:S(2)}, u32[]{:S(2)}) collective-permute-start(bf16[48,1536]{1,0:T(8,128)(2,1)S(1)} %get-tuple-element.161), channel_id=1, source_target_pairs={{0,16},{2,18},{4,20},{6,22},{8,24},{10,26},{12,28},{14,30},{16,0},... | collective-permute-start | bytes 442376 | tf_op jit(solution)/shard_map/ppermute | solution.py:57
  218.3 9.1 %collective-permute-done.37.refs_10_ = bf16[48,1536]{1,0:T(8,128)(2,1)S(1)} collective-permute-done((bf16[48,1536]{1,0:T(8,128)(2,1)S(1)}, bf16[48,1536]{1,0:T(8,128)(2,1)S(1)}, u32[]{:S(2)}, u32[]{:S(2)}) %collective-permute-start.37) | collective-permute-done | bytes 147488 | tf_op jit(solution)/shard_map/ppermute | solution.py:57
  227.3 4.5 %shard_map.349 = (f32[256,768]{1,0:T(8,128)S(1)}, bf16[256,768]{1,0:T(8,128)(2,1)S(1)}) custom-call(bf16[256,768]{1,0:T(8,128)(2,1)S(1)} %get-tuple-element.143.refs_4_.refs_3_.refs_0_, bf16[512,768]{1,0:T(8,128)(2,1)S(1)} %get-tuple-element.144.refs_4_.refs_1_, bf16[512,768]{1,0:T(8,128)(2,1)S(1)} %get-tuple-element.145.refs_5_.refs_2_, ...), custom_call_target="tpu_custom_call" | custom-call | flops 1509949440 | bytes 9043968 | tf_op jit(solution)/shard_map/pallas_call | solution.py:142
  239.6 12.9 %collective-permute-done.44.refs_3_ = bf16[384,768]{1,0:T(8,128)(2,1)} collective-permute-done((bf16[384,768]{1,0:T(8,128)(2,1)}, bf16[384,768]{1,0:T(8,128)(2,1)}, u32[]{:S(2)}, u32[]{:S(2)}) %collective-permute-start.44) | collective-permute-done | bytes 589856 | tf_op jit(solution)/shard_map/ppermute | solution.py:61
  257.1 2.6 collective-permute-start.47
  266.0 4.6 %collective-permute-done.48.refs_5_ = bf16[48,1536]{1,0:T(8,128)(2,1)S(1)} collective-permute-done((bf16[48,1536]{1,0:T(8,128)(2,1)S(1)}, bf16[48,1536]{1,0:T(8,128)(2,1)S(1)}, u32[]{:S(2)}, u32[]{:S(2)}) %collective-permute-start.48) | collective-permute-done | bytes 147488 | tf_op jit(solution)/shard_map/ppermute | solution.py:57
  272.5 2.5 collective-permute-start.51
  276.7 2.9 collective-permute-done.52
  279.6 7.0 %collective-permute-done.51 = bf16[48,1664]{1,0:T(8,128)(2,1)S(1)} collective-permute-done((bf16[48,1664]{1,0:T(8,128)(2,1)S(1)}, bf16[48,1664]{1,0:T(8,128)(2,1)S(1)}, u32[]{:S(2)}, u32[]{:S(2)}) %collective-permute-start.51) | collective-permute-done | bytes 159776 | tf_op jit(solution)/shard_map/ppermute | solution.py:57
  (273 shorter events, 104.2 us)
Async XLA Ops:
  7.2 14.8 %collective-permute-start.2 = (bf16[48,1664]{1,0:T(8,128)(2,1)S(1)}, bf16[48,1664]{1,0:T(8,128)(2,1)S(1)}, u32[]{:S(2)}, u32[]{:S(2)}) collective-permute-start(bf16[48,1664]{1,0:T(8,128)(2,1)S(1)} %bitcast_dynamic-update-slice_fusion.refs_0_), channel_id=1, source_target_pairs={{0,16},{2,18},{4,20},{6,22},{8,24},{10,26},{12,28},{14,30},{16,0},... | collective-permute-start | bytes 479240 | tf_op jit(solution)/shard_map/ppermute | solution.py:57
  9.8 12.2 %collective-permute-start.3 = (bf16[48,1664]{1,0:T(8,128)(2,1)S(1)}, bf16[48,1664]{1,0:T(8,128)(2,1)S(1)}, u32[]{:S(2)}, u32[]{:S(2)}) collective-permute-start(bf16[48,1664]{1,0:T(8,128)(2,1)S(1)} %bitcast_dynamic-update-slice_fusion.refs_0_), channel_id=1, source_target_pairs={{0,24},{2,26},{4,28},{6,30},{8,16},{10,18},{12,20},{14,22},{16,8},... | collective-permute-start | bytes 479240 | tf_op jit(solution)/shard_map/ppermute | solution.py:57
  31.4 17.6 %collective-permute-start.7 = (bf16[192,1792]{1,0:T(8,128)(2,1)S(1)}, bf16[192,1792]{1,0:T(8,128)(2,1)S(1)}, u32[]{:S(2)}, u32[]{:S(2)}) collective-permute-start(bf16[192,1792]{1,0:T(8,128)(2,1)S(1)} %get-tuple-element.104.refs_4_.refs_1_), channel_id=1, source_target_pairs={{0,4},{2,6},{4,0},{6,2},{8,12},{10,14},{12,8},{14,10},{16,20},{18,... | collective-permute-start | bytes 2064392 | tf_op jit(solution)/shard_map/ppermute | solution.py:57
  33.0 16.0 %collective-permute-start.6 = (bf16[384,768]{1,0:T(8,128)(2,1)S(1)}, bf16[384,768]{1,0:T(8,128)(2,1)S(1)}, u32[]{:S(2)}, u32[]{:S(2)}) collective-permute-start(bf16[384,768]{1,0:T(8,128)(2,1)S(1)} %get-tuple-element.103.refs_0_), channel_id=1, source_target_pairs={{0,1},{1,0},{2,3},{3,2},{4,5},{5,4},{6,7},{7,6},{8,9},{9,8},{10,11... | collective-permute-start | bytes 1769480 | tf_op jit(solution)/shard_map/ppermute | solution.py:61
  50.2 12.7 %collective-permute-start.11 = (bf16[384,1792]{1,0:T(8,128)(2,1)}, bf16[384,1792]{1,0:T(8,128)(2,1)}, u32[]{:S(2)}, u32[]{:S(2)}) collective-permute-start(bf16[384,1792]{1,0:T(8,128)(2,1)} %get-tuple-element.106.refs_2_.refs_1_.refs_3_), channel_id=1, source_target_pairs={{0,2},{2,0},{4,6},{6,4},{8,10},{10,8},{12,14},{14,12},{16,18},{18,... | collective-permute-start | bytes 4128776 | tf_op jit(solution)/shard_map/ppermute | solution.py:57
  50.8 15.7 %collective-permute-start.12 = (bf16[384,1536]{1,0:T(8,128)(2,1)S(1)}, bf16[384,1536]{1,0:T(8,128)(2,1)S(1)}, u32[]{:S(2)}, u32[]{:S(2)}) collective-permute-start(bf16[384,1536]{1,0:T(8,128)(2,1)S(1)} %get-tuple-element.107.refs_3_.refs_2_.refs_9_.refs_5_), channel_id=1, source_target_pairs={{0,2},{2,0},{4,6},{6,4},{8,10},{10,8},{12,14},{14,12},{16,18},{18,... | collective-permute-start | bytes 3538952 | tf_op jit(solution)/shard_map/ppermute | solution.py:57
  52.8 17.9 %collective-permute-start.13 = (bf16[192,768]{1,0:T(8,128)(2,1)}, bf16[192,768]{1,0:T(8,128)(2,1)S(1)}, u32[]{:S(2)}, u32[]{:S(2)}) collective-permute-start(bf16[192,768]{1,0:T(8,128)(2,1)} %get-tuple-element.105.refs_4_.refs_1_.refs_0_), channel_id=1, source_target_pairs={{0,1},{1,0},{2,3},{3,2},{4,5},{5,4},{6,7},{7,6},{8,9},{9,8},{10,11... | collective-permute-start | bytes 884744 | tf_op jit(solution)/shard_map/ppermute | solution.py:61
  54.4 16.4 %collective-permute-start.14 = (bf16[192,768]{1,0:T(8,128)(2,1)}, bf16[192,768]{1,0:T(8,128)(2,1)S(1)}, u32[]{:S(2)}, u32[]{:S(2)}) collective-permute-start(bf16[192,768]{1,0:T(8,128)(2,1)} %get-tuple-element.113.refs_1_), channel_id=1, source_target_pairs={{0,4},{2,6},{4,0},{6,2},{8,12},{10,14},{12,8},{14,10},{16,20},{18,... | collective-permute-start | bytes 884744 | tf_op jit(solution)/shard_map/ppermute | solution.py:57
  74.1 33.7 %collective-permute-start.18 = (bf16[384,768]{1,0:T(8,128)(2,1)}, bf16[384,768]{1,0:T(8,128)(2,1)}, u32[]{:S(2)}, u32[]{:S(2)}) collective-permute-start(bf16[384,768]{1,0:T(8,128)(2,1)} %get-tuple-element.117.refs_0_), channel_id=1, source_target_pairs={{0,1},{1,0},{2,3},{3,2},{4,5},{5,4},{6,7},{7,6},{8,9},{9,8},{10,11... | collective-permute-start | bytes 1769480 | tf_op jit(solution)/shard_map/ppermute | solution.py:61
  74.6 33.2 %collective-permute-start.19 = (bf16[192,1536]{1,0:T(8,128)(2,1)}, bf16[192,1536]{1,0:T(8,128)(2,1)}, u32[]{:S(2)}, u32[]{:S(2)}) collective-permute-start(bf16[192,1536]{1,0:T(8,128)(2,1)} %get-tuple-element.114.refs_5_.refs_1_), channel_id=1, source_target_pairs={{0,4},{2,6},{4,0},{6,2},{8,12},{10,14},{12,8},{14,10},{16,20},{18,... | collective-permute-start | bytes 1769480 | tf_op jit(solution)/shard_map/ppermute | solution.py:57
  79.2 13.4 %collective-permute-start.16 = (bf16[48,1536]{1,0:T(8,128)(2,1)}, bf16[48,1536]{1,0:T(8,128)(2,1)}, u32[]{:S(2)}, u32[]{:S(2)}) collective-permute-start(bf16[48,1536]{1,0:T(8,128)(2,1)} %copy-done.8), channel_id=1, source_target_pairs={{0,16},{2,18},{4,20},{6,22},{8,24},{10,26},{12,28},{14,30},{16,0},... | collective-permute-start | bytes 442376 | tf_op jit(solution)/shard_map/ppermute | solution.py:57
  109.6 13.0 %collective-permute-start.20 = (bf16[384,1536]{1,0:T(8,128)(2,1)S(1)}, bf16[384,1536]{1,0:T(8,128)(2,1)S(1)}, u32[]{:S(2)}, u32[]{:S(2)}) collective-permute-start(bf16[384,1536]{1,0:T(8,128)(2,1)S(1)} %get-tuple-element.118.refs_5_.refs_1_), channel_id=1, source_target_pairs={{0,2},{2,0},{4,6},{6,4},{8,10},{10,8},{12,14},{14,12},{16,18},{18,... | collective-permute-start | bytes 3538952 | tf_op jit(solution)/shard_map/ppermute | solution.py:57
  109.7 12.9 %collective-permute-start.21 = (bf16[384,1536]{1,0:T(8,128)(2,1)S(1)}, bf16[384,1536]{1,0:T(8,128)(2,1)S(1)}, u32[]{:S(2)}, u32[]{:S(2)}) collective-permute-start(bf16[384,1536]{1,0:T(8,128)(2,1)S(1)} %get-tuple-element.120.refs_3_), channel_id=1, source_target_pairs={{0,2},{2,0},{4,6},{6,4},{8,10},{10,8},{12,14},{14,12},{16,18},{18,... | collective-permute-start | bytes 3538952 | tf_op jit(solution)/shard_map/ppermute | solution.py:57
  120.4 14.2 %collective-permute-start.24 = (bf16[384,768]{1,0:T(8,128)(2,1)S(1)}, bf16[384,768]{1,0:T(8,128)(2,1)S(1)}, u32[]{:S(2)}, u32[]{:S(2)}) collective-permute-start(bf16[384,768]{1,0:T(8,128)(2,1)S(1)} %get-tuple-element.125.refs_0_), channel_id=1, source_target_pairs={{0,1},{1,0},{2,3},{3,2},{4,5},{5,4},{6,7},{7,6},{8,9},{9,8},{10,11... | collective-permute-start | bytes 1769480 | tf_op jit(solution)/shard_map/ppermute | solution.py:61
  121.0 13.9 %collective-permute-start.25 = (bf16[192,1536]{1,0:T(8,128)(2,1)S(1)}, bf16[192,1536]{1,0:T(8,128)(2,1)S(1)}, u32[]{:S(2)}, u32[]{:S(2)}) collective-permute-start(bf16[192,1536]{1,0:T(8,128)(2,1)S(1)} %get-tuple-element.123.refs_6_.refs_1_), channel_id=1, source_target_pairs={{0,4},{2,6},{4,0},{6,2},{8,12},{10,14},{12,8},{14,10},{16,20},{18,... | collective-permute-start | bytes 1769480 | tf_op jit(solution)/shard_map/ppermute | solution.py:57
  146.1 33.1 %collective-permute-start.31 = (bf16[384,3072]{1,0:T(8,128)(2,1)S(1)}, bf16[384,3072]{1,0:T(8,128)(2,1)S(1)}, u32[]{:S(2)}, u32[]{:S(2)}) collective-permute-start(bf16[384,3072]{1,0:T(8,128)(2,1)S(1)} %convolution_convert_fusion), channel_id=1, source_target_pairs={{0,2},{2,0},{4,6},{6,4},{8,10},{10,8},{12,14},{14,12},{16,18},{18,... | collective-permute-start | bytes 7077896 | tf_op jit(solution)/shard_map/ppermute | solution.py:57
  160.3 15.4 %collective-permute-start.29 = (bf16[192,1536]{1,0:T(8,128)(2,1)S(1)}, bf16[192,1536]{1,0:T(8,128)(2,1)S(1)}, u32[]{:S(2)}, u32[]{:S(2)}) collective-permute-start(bf16[192,1536]{1,0:T(8,128)(2,1)S(1)} %get-tuple-element.138), channel_id=1, source_target_pairs={{0,4},{2,6},{4,0},{6,2},{8,12},{10,14},{12,8},{14,10},{16,20},{18,... | collective-permute-start | bytes 1769480 | tf_op jit(solution)/shard_map/ppermute | solution.py:57
  161.9 15.1 %collective-permute-start.30 = (bf16[384,768]{1,0:T(8,128)(2,1)S(1)}, bf16[384,768]{1,0:T(8,128)(2,1)S(1)}, u32[]{:S(2)}, u32[]{:S(2)}) collective-permute-start(bf16[384,768]{1,0:T(8,128)(2,1)S(1)} %get-tuple-element.140), channel_id=1, source_target_pairs={{0,1},{1,0},{2,3},{3,2},{4,5},{5,4},{6,7},{7,6},{8,9},{9,8},{10,11... | collective-permute-start | bytes 1769480 | tf_op jit(solution)/shard_map/ppermute | solution.py:61
  177.3 13.6 %collective-permute-start.34 = (bf16[192,768]{1,0:T(8,128)(2,1)S(1)}, bf16[192,768]{1,0:T(8,128)(2,1)S(1)}, u32[]{:S(2)}, u32[]{:S(2)}) collective-permute-start(bf16[192,768]{1,0:T(8,128)(2,1)S(1)} %get-tuple-element.154), channel_id=1, source_target_pairs={{0,1},{1,0},{2,3},{3,2},{4,5},{5,4},{6,7},{7,6},{8,9},{9,8},{10,11... | collective-permute-start | bytes 884744 | tf_op jit(solution)/shard_map/ppermute | solution.py:61
  195.2 37.5 %collective-permute-start.40 = (bf16[384,3328]{1,0:T(8,128)(2,1)S(1)}, bf16[384,3328]{1,0:T(8,128)(2,1)S(1)}, u32[]{:S(2)}, u32[]{:S(2)}) collective-permute-start(bf16[384,3328]{1,0:T(8,128)(2,1)S(1)} %get-tuple-element.165), channel_id=1, source_target_pairs={{0,2},{2,0},{4,6},{6,4},{8,10},{10,8},{12,14},{14,12},{16,18},{18,... | collective-permute-start | bytes 7667720 | tf_op jit(solution)/shard_map/ppermute | solution.py:57
  195.3 15.7 %collective-permute-start.32 = (bf16[192,1536]{1,0:T(8,128)(2,1)S(1)}, bf16[192,1536]{1,0:T(8,128)(2,1)S(1)}, u32[]{:S(2)}, u32[]{:S(2)}) collective-permute-start(bf16[192,1536]{1,0:T(8,128)(2,1)S(1)} %get-tuple-element.147), channel_id=1, source_target_pairs={{0,4},{2,6},{4,0},{6,2},{8,12},{10,14},{12,8},{14,10},{16,20},{18,... | collective-permute-start | bytes 1769480 | tf_op jit(solution)/shard_map/ppermute | solution.py:57
  196.9 15.4 %collective-permute-start.33 = (bf16[384,768]{1,0:T(8,128)(2,1)S(1)}, bf16[384,768]{1,0:T(8,128)(2,1)S(1)}, u32[]{:S(2)}, u32[]{:S(2)}) collective-permute-start(bf16[384,768]{1,0:T(8,128)(2,1)S(1)} %get-tuple-element.149), channel_id=1, source_target_pairs={{0,1},{1,0},{2,3},{3,2},{4,5},{5,4},{6,7},{7,6},{8,9},{9,8},{10,11... | collective-permute-start | bytes 1769480 | tf_op jit(solution)/shard_map/ppermute | solution.py:61
  197.5 19.6 %collective-permute-start.36 = (bf16[48,1536]{1,0:T(8,128)(2,1)S(1)}, bf16[48,1536]{1,0:T(8,128)(2,1)S(1)}, u32[]{:S(2)}, u32[]{:S(2)}) collective-permute-start(bf16[48,1536]{1,0:T(8,128)(2,1)S(1)} %get-tuple-element.160), channel_id=1, source_target_pairs={{0,8},{2,10},{4,12},{6,14},{8,0},{10,2},{12,4},{14,6},{16,24},{18,... | collective-permute-start | bytes 442376 | tf_op jit(solution)/shard_map/ppermute | solution.py:57
  212.6 19.3 %collective-permute-start.41 = (bf16[192,768]{1,0:T(8,128)(2,1)S(1)}, bf16[192,768]{1,0:T(8,128)(2,1)S(1)}, u32[]{:S(2)}, u32[]{:S(2)}) collective-permute-start(bf16[192,768]{1,0:T(8,128)(2,1)S(1)} %get-tuple-element.166), channel_id=1, source_target_pairs={{0,1},{1,0},{2,3},{3,2},{4,5},{5,4},{6,7},{7,6},{8,9},{9,8},{10,11... | collective-permute-start | bytes 884744 | tf_op jit(solution)/shard_map/ppermute | solution.py:61
  213.2 18.6 %collective-permute-start.42 = (bf16[192,768]{1,0:T(8,128)(2,1)S(1)}, bf16[192,768]{1,0:T(8,128)(2,1)S(1)}, u32[]{:S(2)}, u32[]{:S(2)}) collective-permute-start(bf16[192,768]{1,0:T(8,128)(2,1)S(1)} %get-tuple-element.168), channel_id=1, source_target_pairs={{0,4},{2,6},{4,0},{6,2},{8,12},{10,14},{12,8},{14,10},{16,20},{18,... | collective-permute-start | bytes 884744 | tf_op jit(solution)/shard_map/ppermute | solution.py:57
  213.8 13.6 %collective-permute-start.37 = (bf16[48,1536]{1,0:T(8,128)(2,1)S(1)}, bf16[48,1536]{1,0:T(8,128)(2,1)S(1)}, u32[]{:S(2)}, u32[]{:S(2)}) collective-permute-start(bf16[48,1536]{1,0:T(8,128)(2,1)S(1)} %get-tuple-element.161), channel_id=1, source_target_pairs={{0,16},{2,18},{4,20},{6,22},{8,24},{10,26},{12,28},{14,30},{16,0},... | collective-permute-start | bytes 442376 | tf_op jit(solution)/shard_map/ppermute | solution.py:57
  234.4 18.1 %collective-permute-start.43 = (bf16[192,1792]{1,0:T(8,128)(2,1)}, bf16[192,1792]{1,0:T(8,128)(2,1)S(1)}, u32[]{:S(2)}, u32[]{:S(2)}) collective-permute-start(bf16[192,1792]{1,0:T(8,128)(2,1)} %get-tuple-element.171), channel_id=1, source_target_pairs={{0,4},{2,6},{4,0},{6,2},{8,12},{10,14},{12,8},{14,10},{16,20},{18,... | collective-permute-start | bytes 2064392 | tf_op jit(solution)/shard_map/ppermute | solution.py:57
  235.9 16.6 %collective-permute-start.44 = (bf16[384,768]{1,0:T(8,128)(2,1)}, bf16[384,768]{1,0:T(8,128)(2,1)}, u32[]{:S(2)}, u32[]{:S(2)}) collective-permute-start(bf16[384,768]{1,0:T(8,128)(2,1)} %get-tuple-element.173), channel_id=1, source_target_pairs={{0,1},{1,0},{2,3},{3,2},{4,5},{5,4},{6,7},{7,6},{8,9},{9,8},{10,11... | collective-permute-start | bytes 1769480 | tf_op jit(solution)/shard_map/ppermute | solution.py:61
  238.9 21.9 %collective-permute-start.39 = (bf16[256,768]{1,0:T(8,128)(2,1)S(1)}, bf16[256,768]{1,0:T(8,128)(2,1)S(1)}, u32[]{:S(2)}, u32[]{:S(2)}) collective-permute-start(bf16[256,768]{1,0:T(8,128)(2,1)S(1)} %copy-done.35), channel_id=1, source_target_pairs={{0,1},{1,0},{2,3},{3,2},{4,5},{5,4},{6,7},{7,6},{8,9},{9,8},{10,11... | collective-permute-start | bytes 1179656 | tf_op jit(solution)/shard_map/ppermute | solution.py:61
  253.8 16.7 %collective-permute-start.45 = (bf16[192,896]{1,0:T(8,128)(2,1)S(1)}, bf16[192,896]{1,0:T(8,128)(2,1)S(1)}, u32[]{:S(2)}, u32[]{:S(2)}) collective-permute-start(bf16[192,896]{1,0:T(8,128)(2,1)S(1)} %get-tuple-element.175), channel_id=1, source_target_pairs={{0,1},{1,0},{2,3},{3,2},{4,5},{5,4},{6,7},{7,6},{8,9},{9,8},{10,11... | collective-permute-start | bytes 1032200 | tf_op jit(solution)/shard_map/ppermute | solution.py:61
  255.3 15.2 %collective-permute-start.46 = (bf16[192,768]{1,0:T(8,128)(2,1)S(1)}, bf16[192,768]{1,0:T(8,128)(2,1)S(1)}, u32[]{:S(2)}, u32[]{:S(2)}) collective-permute-start(bf16[192,768]{1,0:T(8,128)(2,1)S(1)} %get-tuple-element.177), channel_id=1, source_target_pairs={{0,4},{2,6},{4,0},{6,2},{8,12},{10,14},{12,8},{14,10},{16,20},{18,... | collective-permute-start | bytes 884744 | tf_op jit(solution)/shard_map/ppermute | solution.py:57
  272.5 14.1 %collective-permute-start.51 = (bf16[48,1664]{1,0:T(8,128)(2,1)S(1)}, bf16[48,1664]{1,0:T(8,128)(2,1)S(1)}, u32[]{:S(2)}, u32[]{:S(2)}) collective-permute-start(bf16[48,1664]{1,0:T(8,128)(2,1)S(1)} %get-tuple-element.183), channel_id=1, source_target_pairs={{0,16},{2,18},{4,20},{6,22},{8,24},{10,26},{12,28},{14,30},{16,0},... | collective-permute-start | bytes 479240 | tf_op jit(solution)/shard_map/ppermute | solution.py:57
  (83 other events, 763.9 us)
where the time goes:
time: 292 us; the launch traced here: 291 us
  waiting for transfers between devices  122 us (42%)
  Pallas kernels  68.5 us (23%)
  starting transfers between devices  61.9 us (21%)
  local copies, waits for them, and re-layouts  16.3 us (6%)
  other arithmetic  11.1 us (4%)
  matrix products  9.51 us (3%)
    ppermute x39, waiting for transfers between devices, swap_dp(): return lax.ppermute(values, 'dp', [(i, i ^ mask) for i in range(size)])  83.6 us
    pallas_call x31, Pallas kernels, run(): pl.pallas_call(body, grid=grid, out_shape=list(outs), in_specs=list(in_sp...  68.5 us
    ppermute x39, starting transfers between devices, swap_dp(): return lax.ppermute(values, 'dp', [(i, i ^ mask) for i in range(size)])  47.6 us
    ppermute x14, waiting for transfers between devices, swap_tensor(): return lax.ppermute(values, 'tensor', [(0, 1), (1, 0)])  38.2 us
    ppermute x14, starting transfers between devices, swap_tensor(): return lax.ppermute(values, 'tensor', [(0, 1), (1, 0)])  14.3 us
    unnamed x133, local copies, waits for them, and re-layouts  14.1 us
  transfers between devices with their start and end apart: 53, of which 25 were waited for; matrix products, arithmetic and copies ran while one was open for 6% of the time, Pallas kernels for 19%

commit v1 on v0

--- a/solution.py
+++ b/solution.py
@@ -583,15 +583,19 @@
     rows_all = jnp.concatenate([dot(tokens, permute), dot(tokens_far, permute)]).astype(LOW)
     cot = dot(cotangent, permute)
 
-    one = join_plane(*one, *one_far, after=[shard_in])
+    one = join_plane(*one, *one_far, after=[shard_in, rows_all])
     one_far = swap_dp(one[0], 2), swap_tensor(one[1])
     inner = join_high(inner_high, cut, after=one[:1])
     shard_back = run(cast_kernel, [low_shape], [w_back.T], 0, after=inner[:1])[0]
     outer_high = gather_high(shard_back)
-    one = join_plane(one[1], one[0], one_far[1], one_far[0], after=inner[:1])[::-1]
+    one = join_plane(one[1], one[0], one_far[1], one_far[0], after=[shard_back])[::-1]
     a_own, b_own = one
     a_far, b_far = swap_dp(a_own, 1), swap_dp(b_own, 1)
     inner_far = swap_tensor(inner[0]), swap_dp(inner[1], 2)
+    outer = join_high(outer_high, cut, after=[a_own])
+    inner = join_plane(*inner, *inner_far, after=[a_own])
+    inner_far = swap_dp(inner[0], 2), swap_tensor(inner[1])
+    outer_far = swap_tensor(outer[0]), swap_dp(outer[1], 2)
 
     vec, bias_query, bias_value, bias_inner = run(
         vectors_kernel,
@@ -603,7 +607,6 @@
         ],
         [rank, permute, a_own, a_far],
         1,
-        after=[shard_back],
         in_specs=[scalar, vmem, vmem, vmem],
     )
 
@@ -628,10 +631,8 @@
         [wide_low, group_low, group_low],
         [rows_all, a_own, a_far, b_own, b_far, bias_query, bias_value],
         5 * unit,
-    )
-    inner = join_plane(*inner, *inner_far, after=[queries])
-    inner_far = swap_dp(inner[0], 2), swap_tensor(inner[1])
-    outer = join_high(outer_high, cut, after=[queries])
+        after=[inner[0], outer[0]],
+    )
     pairs = width // LANES
     own_block = pl.BlockSpec((own_rows, LANES), lambda i: (0, i))
     all_block = pl.BlockSpec((group_rows, LANES), lambda i: (0, i))
@@ -643,8 +644,7 @@
         attend_kernel,
         [wide_low],
         [seg_own, seg_keys, queries, key_rows, value_rows],
-        12 * unit,
-        after=[inner[0], outer[0]],
+        3 * unit,
         grid=(pairs,),
         in_specs=[fixed((1, own_rows)), fixed((group_rows, 1)), own_block, all_block, all_block],
         out_specs=[own_block],
@@ -652,22 +652,20 @@
     inner = join_plane(inner[1], inner[0], inner_far[1], inner_far[0], after=[attended])[::-1]
     c_own, d_own = inner
     c_far, d_far = swap_dp(c_own, 1), swap_dp(d_own, 1)
-    outer_far = swap_tensor(outer[0]), swap_dp(outer[1], 2)
+    outer = join_plane(*outer, *outer_far, after=[attended])
+    outer_far = swap_dp(outer[0], 2), swap_tensor(outer[1])
     first_norm, first_low, normed_one, inv_one = run(
         out_norm_kernel,
         [wide, wide_low, wide, shape_of(own_rows, 1, F32)],
         [attended, rows_all, b_own, b_far, vec],
-        2 * unit,
-        after=inner[:1],
-    )
-    outer = join_plane(*outer, *outer_far, after=[first_low])
-    outer_far = swap_dp(outer[0], 2), swap_tensor(outer[1])
+        400 * unit,
+        after=[inner[0], outer[0]],
+    )
     activation, slope = run(
         hidden_kernel,
         [shape_of(own_rows, full_inner, LOW), shape_of(own_rows, full_inner, F32)],
         [first_low, c_own, c_far, d_own, d_far, bias_inner],
         8 * unit,
-        after=outer[:1],
     )
     outer = join_plane(outer[1], outer[0], outer_far[1], outer_far[0], after=[activation])[::-1]
     e_own, f_own = outer
@@ -694,6 +692,9 @@
     a_keep, a_send, b_keep, b_send = split_core(*outer, hidden_half, after=[grad_pre])
     outer = a_keep, swap_dp(a_send, 2), b_keep, swap_tensor(b_send)
     inner = weight_grad(first_low, grad_pre)
+    inner_keep = split_core(*inner, hidden_half, after=[a_keep])
+    a_keep, a_send, b_keep, b_send = inner_keep
+    inner = a_keep, swap_dp(a_send, 2), b_keep, swap_tensor(b_send)
     grad_one, grad_one_low, grad_attn, sums_one = run(
         norm_back_kernel,
         [wide, wide_low, wide_low, sums_shape],
@@ -701,23 +702,18 @@
         6 * unit,
         after=[a_keep],
     )
-    a_keep, a_send, b_keep, b_send = split_plane(*outer, after=[grad_attn])
-    outer = a_keep, swap_tensor(a_send), b_keep, swap_dp(b_send, 2)
-    inner_keep = split_core(*inner, hidden_half, after=[a_keep])
     grad_q, grad_k, grad_v = run(
         attend_back_kernel,
         [wide_low, group_low, group_low],
         [seg_own, seg_keys, queries, key_rows, value_rows, grad_attn],
         25 * unit,
-        after=[a_keep, inner_keep[0]],
         grid=(pairs,),
         in_specs=[fixed((1, own_rows)), fixed((group_rows, 1))]
         + [own_block, all_block, all_block, own_block],
         out_specs=[own_block, all_block, all_block],
     )
-    outer = send_high(split_high(*outer, after=[grad_q]))
-    a_keep, a_send, b_keep, b_send = inner_keep
-    inner = a_keep, swap_dp(a_send, 2), b_keep, swap_tensor(b_send)
+    a_keep, a_send, b_keep, b_send = split_plane(*outer, after=[grad_q])
+    outer = a_keep, swap_tensor(a_send), b_keep, swap_dp(b_send, 2)
     one_shape = shape_of(half, 2 * a_width + 4 * part, LOW)
     one_send, one_keep = run(
         functools.partial(first_grads_kernel, a_width),
@@ -725,7 +721,7 @@
         [rank, permute, rows_all, grad_q, grad_k, grad_v, grad_one_low, attended]
         + [sums_one, sums_two, sums_inner],
         6 * unit,
-        after=outer[:1],
+        after=[a_keep],
         in_specs=[scalar] + [vmem] * 10,
         scratch=[pltpu.VMEM((16, width), F32), pltpu.VMEM((LANES, width), F32)],
     )
@@ -736,20 +732,21 @@
         rows_back_kernel,
         [wide, wide_low],
         [grad_q, grad_k, grad_v, a_own, a_far, b_own, b_far, grad_one],
-        5 * unit,
-        after=[a_keep] + outer[1:],
+        400 * unit,
+        after=[a_keep],
     )
     grad_rel = grad_own + swap_tensor(grad_away).astype(F32)
     input_grad = lax.dot_general(
         grad_rel, permute_wide, (((1,), (1,)), ((), ())), precision=exact
     )
+    one_keep = split_core(one_keep, one_far, 2 * a_width, after=[grad_own])
+    outer = send_high(split_high(*outer, after=one_keep[:1]))
+    inner = send_high(split_high(*inner, after=outer[:1]))
     summed_back = reduce_high(outer).T
-    inner = send_high(split_high(*inner, after=[grad_own]))
-    one_keep = split_core(one_keep, one_far, 2 * a_width, after=inner[:1])
     a_keep, a_send, b_keep, b_send = one_keep
     one = a_keep, swap_dp(a_send, 2), b_keep, swap_tensor(b_send)
     summed_in = reduce_high(inner)
-    a_keep, a_send, b_keep, b_send = split_plane(*one)
+    a_keep, a_send, b_keep, b_send = split_plane(*one, after=inner[:1] + outer[1:])
     one = a_keep, swap_tensor(a_send), b_keep, swap_dp(b_send, 2)
     sum_one = reduce_high(send_high(split_high(*one, after=inner[1:])))
 

time: 292 us -> 247 us (0.85)
  waiting for transfers between devices: 122 us -> 80.6 us
  matrix products: 9.51 us -> 22.8 us
  Pallas kernels: 68.5 us -> 58.6 us
  local copies, waits for them, and re-layouts: 16.3 us -> 9.97 us
    ppermute x39, waiting for transfers between devices: 83.6 us -> 62.9 us  [swap_dp(): return lax.ppermute(values, 'dp', [(i, i ^ mask) for i in range(size)])]
    ppermute x14, waiting for transfers between devices: 38.2 us -> 17.7 us  [swap_tensor(): return lax.ppermute(values, 'tensor', [(0, 1), (1, 0)])]
    dot_general x4, matrix products: 3.23 us -> 15.3 us  [dot_tn(): lax.dot_general(left, right, (((0,), (0,)), ((), ())), preferred_element_...]
    pallas_call x31, Pallas kernels: 68.5 us -> 58.6 us  [run(): pl.pallas_call(body, grid=grid, out_shape=list(outs), in_specs=list(in_sp...]
    unnamed x133 -> x93, local copies, waits for them, and re-layouts: 14.1 us -> 8.55 us
  transfers between devices with their start and end apart: 53 -> 53, of which waited for: 25 -> 18; matrix products, arithmetic and copies ran while one was open for 6% -> 12% of each run, Pallas kernels for 19% -> 22%
where the time goes in v1:
time: 247 us; the launch traced here: 246 us
  waiting for transfers between devices  80.6 us (33%)
  starting transfers between devices  63.3 us (26%)
  Pallas kernels  58.6 us (24%)
  matrix products  22.8 us (9%)
  local copies, waits for them, and re-layouts  9.97 us (4%)
  other arithmetic  8.74 us (4%)
    ppermute x39, waiting for transfers between devices, swap_dp(): return lax.ppermute(values, 'dp', [(i, i ^ mask) for i in range(size)])  62.9 us
    pallas_call x31, Pallas kernels, run(): pl.pallas_call(body, grid=grid, out_shape=list(outs), in_specs=list(in_sp...  58.6 us
    ppermute x39, starting transfers between devices, swap_dp(): return lax.ppermute(values, 'dp', [(i, i ^ mask) for i in range(size)])  49.1 us
    ppermute x14, waiting for transfers between devices, swap_tensor(): return lax.ppermute(values, 'tensor', [(0, 1), (1, 0)])  17.7 us
    dot_general x4, matrix products, dot_tn(): lax.dot_general(left, right, (((0,), (0,)), ((), ())), preferred_element_...  15.3 us
    ppermute x14, starting transfers between devices, swap_tensor(): return lax.ppermute(values, 'tensor', [(0, 1), (1, 0)])  14.2 us
    unnamed x93, local copies, waits for them, and re-layouts  8.55 us
  transfers between devices with their start and end apart: 53, of which 18 were waited for; matrix products, arithmetic and copies ran while one was open for 12% of the time, Pallas kernels for 22%

profile of v1, /device:TPU:0, one launch (start us, length us, event | category | flops | bytes accessed | tf_op | source)
XLA Modules:
  0.0 245.6 jit_solution(5610846904504550996)
XLA Ops:
  4.2 3.1 %collective-permute-start.1 = (bf16[48,1664]{1,0:T(8,128)(2,1)S(1)}, bf16[48,1664]{1,0:T(8,128)(2,1)S(1)}, u32[]{:S(2)}, u32[]{:S(2)}) collective-permute-start(bf16[48,1664]{1,0:T(8,128)(2,1)S(1)} %bitcast_dynamic-update-slice_fusion.refs_0_), channel_id=1, source_target_pairs={{0,8},{2,10},{4,12},{6,14},{8,0},{10,2},{12,4},{14,6},{16,24},{18,... | collective-permute-start | bytes 479240 | tf_op jit(solution)/shard_map/ppermute | solution.py:57
  7.2 2.6 %collective-permute-start.2 = (bf16[48,1664]{1,0:T(8,128)(2,1)S(1)}, bf16[48,1664]{1,0:T(8,128)(2,1)S(1)}, u32[]{:S(2)}, u32[]{:S(2)}) collective-permute-start(bf16[48,1664]{1,0:T(8,128)(2,1)S(1)} %bitcast_dynamic-update-slice_fusion.refs_0_), channel_id=1, source_target_pairs={{0,16},{2,18},{4,20},{6,22},{8,24},{10,26},{12,28},{14,30},{16,0},... | collective-permute-start | bytes 479240 | tf_op jit(solution)/shard_map/ppermute | solution.py:57
  13.9 8.1 %collective-permute-done.2.refs_2_ = bf16[48,1664]{1,0:T(8,128)(2,1)S(1)} collective-permute-done((bf16[48,1664]{1,0:T(8,128)(2,1)S(1)}, bf16[48,1664]{1,0:T(8,128)(2,1)S(1)}, u32[]{:S(2)}, u32[]{:S(2)}) %collective-permute-start.2) | collective-permute-done | bytes 159776 | tf_op jit(solution)/shard_map/ppermute | solution.py:57
  25.9 5.4 %collective-permute-done.5.refs_3_ = bf16[192,768]{1,0:T(8,128)(2,1)S(1)} collective-permute-done((bf16[192,768]{1,0:T(8,128)(2,1)S(1)}, bf16[192,768]{1,0:T(8,128)(2,1)S(1)}, u32[]{:S(2)}, u32[]{:S(2)}) %collective-permute-start.5) | collective-permute-done | bytes 294944 | tf_op jit(solution)/shard_map/ppermute | solution.py:57
  33.2 3.3 %collective-permute-start.8 = (bf16[48,1536]{1,0:T(8,128)(2,1)S(1)}, bf16[48,1536]{1,0:T(8,128)(2,1)S(1)}, u32[]{:S(2)}, u32[]{:S(2)}) collective-permute-start(bf16[48,1536]{1,0:T(8,128)(2,1)S(1)} %shard_map.324.refs_4_.refs_0_), channel_id=1, source_target_pairs={{0,8},{2,10},{4,12},{6,14},{8,0},{10,2},{12,4},{14,6},{16,24},{18,... | collective-permute-start | bytes 442376 | tf_op jit(solution)/shard_map/ppermute | solution.py:57
  40.2 7.9 %collective-permute-done.9.refs_2_ = bf16[48,1536]{1,0:T(8,128)(2,1)S(1)} collective-permute-done((bf16[48,1536]{1,0:T(8,128)(2,1)S(1)}, bf16[48,1536]{1,0:T(8,128)(2,1)S(1)}, u32[]{:S(2)}, u32[]{:S(2)}) %collective-permute-start.9) | collective-permute-done | bytes 147488 | tf_op jit(solution)/shard_map/ppermute | solution.py:57
  51.0 2.4 collective-permute-start.15
  53.3 5.6 %collective-permute-done.13.refs_2_ = bf16[192,768]{1,0:T(8,128)(2,1)} collective-permute-done((bf16[192,768]{1,0:T(8,128)(2,1)S(1)}, bf16[192,768]{1,0:T(8,128)(2,1)}, u32[]{:S(2)}, u32[]{:S(2)}) %collective-permute-start.13) | collective-permute-done | bytes 294944 | tf_op jit(solution)/shard_map/ppermute | solution.py:61
  58.9 3.4 %collective-permute-start.16 = (bf16[48,1536]{1,0:T(8,128)(2,1)S(1)}, bf16[48,1536]{1,0:T(8,128)(2,1)}, u32[]{:S(2)}, u32[]{:S(2)}) collective-permute-start(bf16[48,1536]{1,0:T(8,128)(2,1)S(1)} %shard_map.327.refs_4_.refs_0_), channel_id=1, source_target_pairs={{0,16},{2,18},{4,20},{6,22},{8,24},{10,26},{12,28},{14,30},{16,0},... | collective-permute-start | bytes 442376 | tf_op jit(solution)/shard_map/ppermute | solution.py:57
  67.0 5.9 %collective-permute-done.16.refs_2_ = bf16[48,1536]{1,0:T(8,128)(2,1)} collective-permute-done((bf16[48,1536]{1,0:T(8,128)(2,1)S(1)}, bf16[48,1536]{1,0:T(8,128)(2,1)}, u32[]{:S(2)}, u32[]{:S(2)}) %collective-permute-start.16) | collective-permute-done | bytes 147488 | tf_op jit(solution)/shard_map/ppermute | solution.py:57
  77.5 2.4 shard_map.329
  79.9 4.6 %shard_map.332 = (bf16[256,768]{1,0:T(8,128)(2,1)S(1)}, bf16[512,768]{1,0:T(8,128)(2,1)S(1)}, bf16[512,768]{1,0:T(8,128)(2,1)S(1)}) custom-call(bf16[512,768]{1,0:T(8,128)(2,1)S(1)} %pad_maximum_fusion.refs_5_.refs_0_.refs_1_.refs_2_, bf16[384,1792]{1,0:T(8,128)(2,1)S(1)} %get-tuple-element.106.refs_2_.refs_4_.refs_1_.refs_3_, ...), custom_call_target="tpu_custom_call" | custom-call | flops 1509949440 | bytes 7870464 | tf_op jit(solution)/shard_map/pallas_call | solution.py:142
  84.5 8.0 %shard_map.333.refs_4_.refs_0_.refs_7_ = bf16[256,768]{1,0:T(8,128)(2,1)S(1)} custom-call(s32[1,256]{1,0:T(1,128)S(1)} %bitcast.78, s32[512,1]{1,0:T(8,128)S(1)} %copy.69.refs_1_, bf16[256,768]{1,0:T(8,128)(2,1)S(1)} %get-tuple-element.113.refs_2_, bf16[512,768]{1,0:T(8,128)(2,1)S(1)} %get-tuple-element.114.refs_3_, ...), custom_call_target="tpu_custom_call" | custom-call | flops 905969664 | bytes 2362368 | tf_op jit(solution)/shard_map/pallas_call | solution.py:142
  95.4 2.6 %shard_map.336 = (f32[256,768]{1,0:T(8,128)S(1)}, bf16[256,768]{1,0:T(8,128)(2,1)S(1)}, f32[256,768]{1,0:T(8,128)S(1)}, f32[256,1]{1,0:T(8,128)S(1)}) custom-call(bf16[256,768]{1,0:T(8,128)(2,1)S(1)} %shard_map.333.refs_4_.refs_0_.refs_7_, bf16[512,768]{1,0:T(8,128)(2,1)S(1)} %pad_maximum_fusion.refs_5_.refs_0_.refs_1_.refs_2_, ...), custom_call_target="tpu_custom_call" | custom-call | flops 120795955200 | bytes 5524480 | tf_op jit(solution)/shard_map/pallas_call | solution.py:142
  98.0 2.6 %shard_map.337 = (bf16[256,3072]{1,0:T(8,128)(2,1)S(1)}, f32[256,3072]{1,0:T(8,128)S(1)}) custom-call(bf16[256,768]{1,0:T(8,128)(2,1)S(1)} %get-tuple-element.121.refs_0_, bf16[384,1536]{1,0:T(8,128)(2,1)S(1)} %get-tuple-element.118.refs_5_.refs_1_, bf16[384,1536]{1,0:T(8,128)(2,1)S(1)} %collective-permute-done.22.refs_2_, ...), custom_call_target="tpu_custom_call" | custom-call | flops 2415919104 | bytes 9842688 | tf_op jit(solution)/shard_map/pallas_call | solution.py:142
  100.6 8.1 %collective-permute-done.24.refs_2_ = bf16[384,768]{1,0:T(8,128)(2,1)S(1)} collective-permute-done((bf16[384,768]{1,0:T(8,128)(2,1)S(1)}, bf16[384,768]{1,0:T(8,128)(2,1)S(1)}, u32[]{:S(2)}, u32[]{:S(2)}) %collective-permute-start.24) | collective-permute-done | bytes 589856 | tf_op jit(solution)/shard_map/ppermute | solution.py:61
  114.7 2.4 shard_map.339
  122.3 12.9 %convolution_convert_fusion.1.refs_0_ = bf16[384,3072]{1,0:T(8,128)(2,1)S(1)} fusion(bf16[256,3072]{1,0:T(8,128)(2,1)S(1)} %get-tuple-element.124.refs_4_.refs_0_, bf16[256,768]{1,0:T(8,128)(2,1)S(1)} %get-tuple-element.130.refs_0_), kind=kOutput, calls=%fused_computation.1 | convolution fusion | flops 605159424 | bytes 4128768 | tf_op jit(solution)/shard_map/dot_general | solution.py:126
  140.5 4.3 %shard_map.343 = (f32[256,768]{1,0:T(8,128)S(1)}, bf16[256,768]{1,0:T(8,128)(2,1)S(1)}, bf16[256,768]{1,0:T(8,128)(2,1)S(1)}, f32[8,768]{1,0:T(8,128)S(1)}) custom-call(bf16[256,3072]{1,0:T(8,128)(2,1)S(1)} %get-tuple-element.132.refs_2_.refs_0_, bf16[384,1536]{1,0:T(8,128)(2,1)S(1)} %get-tuple-element.118.refs_5_.refs_1_, ...), custom_call_target="tpu_custom_call" | custom-call | flops 1811939328 | bytes 11840512 | tf_op jit(solution)/shard_map/pallas_call | solution.py:142
  144.8 9.9 %shard_map.344 = (bf16[256,768]{1,0:T(8,128)(2,1)S(1)}, bf16[512,768]{1,0:T(8,128)(2,1)S(1)}, bf16[512,768]{1,0:T(8,128)(2,1)S(1)}) custom-call(s32[1,256]{1,0:T(1,128)S(1)} %bitcast.79, s32[512,1]{1,0:T(8,128)S(1)} %copy.69.refs_1_, bf16[256,768]{1,0:T(8,128)(2,1)S(1)} %get-tuple-element.113.refs_2_, bf16[512,768]{1,0:T(8,128)(2,1)S(1)} %get-tuple-element.114.refs_3_, ...), custom_call_target="tpu_custom_call" | custom-call | flops 7549747200 | bytes 4328448 | tf_op jit(solution)/shard_map/pallas_call | solution.py:142
  154.7 9.7 %collective-permute-done.32.refs_1_ = bf16[192,1536]{1,0:T(8,128)(2,1)S(1)} collective-permute-done((bf16[192,1536]{1,0:T(8,128)(2,1)S(1)}, bf16[192,1536]{1,0:T(8,128)(2,1)S(1)}, u32[]{:S(2)}, u32[]{:S(2)}) %collective-permute-start.32) | collective-permute-done | bytes 589856 | tf_op jit(solution)/shard_map/ppermute | solution.py:57
  165.7 3.0 %shard_map.346 = (bf16[384,3328]{1,0:T(8,128)(2,1)S(1)}, bf16[384,3328]{1,0:T(8,128)(2,1)S(1)}) custom-call(s32[1]{0:T(128)} %bitcast.12.refs_0_, bf16[768,768]{1,0:T(8,128)(2,1)S(1)} %copy-done.3, bf16[512,768]{1,0:T(8,128)(2,1)S(1)} %pad_maximum_fusion.refs_5_.refs_0_.refs_1_.refs_2_, bf16[256,768]{1,0:T(8,128)(2,1)S(1)} %get-tuple-element.139.refs_4_.refs_3_.refs_0_, ...), custom_call_target="tpu_custom_call" | custom-call | flops 1811939328 | bytes 9891844 | tf_op jit(solution)/shard_map/pallas_call | solution.py:142
  171.3 5.5 %shard_map.348 = (f32[256,768]{1,0:T(8,128)S(1)}, bf16[256,768]{1,0:T(8,128)(2,1)}) custom-call(bf16[256,768]{1,0:T(8,128)(2,1)S(1)} %get-tuple-element.139.refs_4_.refs_3_.refs_0_, bf16[512,768]{1,0:T(8,128)(2,1)S(1)} %get-tuple-element.140.refs_4_.refs_1_, bf16[512,768]{1,0:T(8,128)(2,1)S(1)} %get-tuple-element.141.refs_5_.refs_2_, ...), custom_call_target="tpu_custom_call" | custom-call | flops 120795955200 | bytes 9043968 | tf_op jit(solution)/shard_map/pallas_call | solution.py:142
  184.5 3.5 %collective-permute-done.41.refs_3_ = bf16[192,768]{1,0:T(8,128)(2,1)S(1)} collective-permute-done((bf16[192,768]{1,0:T(8,128)(2,1)S(1)}, bf16[192,768]{1,0:T(8,128)(2,1)S(1)}, u32[]{:S(2)}, u32[]{:S(2)}) %collective-permute-start.41) | collective-permute-done | bytes 294944 | tf_op jit(solution)/shard_map/ppermute | solution.py:57
  191.7 3.7 %collective-permute-done.38.refs_1_ = bf16[192,768]{1,0:T(8,128)(2,1)} collective-permute-done((bf16[192,768]{1,0:T(8,128)(2,1)}, bf16[192,768]{1,0:T(8,128)(2,1)}, u32[]{:S(2)}, u32[]{:S(2)}) %collective-permute-start.38) | collective-permute-done | bytes 294944 | tf_op jit(solution)/shard_map/ppermute | solution.py:61
  197.3 2.5 %collective-permute-start.44 = (bf16[48,1536]{1,0:T(8,128)(2,1)S(1)}, bf16[48,1536]{1,0:T(8,128)(2,1)S(1)}, u32[]{:S(2)}, u32[]{:S(2)}) collective-permute-start(bf16[48,1536]{1,0:T(8,128)(2,1)S(1)} %get-tuple-element.173), channel_id=1, source_target_pairs={{0,24},{2,26},{4,28},{6,30},{8,16},{10,18},{12,20},{14,22},{16,8},... | collective-permute-start | bytes 442376 | tf_op jit(solution)/shard_map/ppermute | solution.py:57
  203.3 7.3 %collective-permute-done.43.refs_6_ = bf16[48,1536]{1,0:T(8,128)(2,1)S(1)} collective-permute-done((bf16[48,1536]{1,0:T(8,128)(2,1)S(1)}, bf16[48,1536]{1,0:T(8,128)(2,1)S(1)}, u32[]{:S(2)}, u32[]{:S(2)}) %collective-permute-start.43) | collective-permute-done | bytes 147488 | tf_op jit(solution)/shard_map/ppermute | solution.py:57
  212.2 3.3 %fusion = f32[256,768]{1,0:T(8,128)} fusion(s32[768]{0:T(1024)S(1)} %copy-done.34, f32[256,768]{1,0:T(8,128)S(1)} %get-tuple-element.156.refs_2_, bf16[256,768]{1,0:T(8,128)(2,1)} %collective-permute-done.34), kind=kOutput, calls=%fused_computation.5 | convolution fusion | flops 1812922368 | bytes 1969152 | tf_op jit(solution)/shard_map/dot_general | solution.py:739
  218.9 2.7 %collective-permute-done.48.refs_5_ = bf16[48,1536]{1,0:T(8,128)(2,1)S(1)} collective-permute-done((bf16[48,1536]{1,0:T(8,128)(2,1)S(1)}, bf16[48,1536]{1,0:T(8,128)(2,1)S(1)}, u32[]{:S(2)}, u32[]{:S(2)}) %collective-permute-start.48) | collective-permute-done | bytes 147488 | tf_op jit(solution)/shard_map/ppermute | solution.py:57
  225.3 2.4 collective-permute-start.52
  227.7 7.1 %collective-permute-start.51 = (bf16[48,1664]{1,0:T(8,128)(2,1)S(1)}, bf16[48,1664]{1,0:T(8,128)(2,1)S(1)}, u32[]{:S(2)}, u32[]{:S(2)}) collective-permute-start(bf16[48,1664]{1,0:T(8,128)(2,1)S(1)} %get-tuple-element.183), channel_id=1, source_target_pairs={{0,16},{2,18},{4,20},{6,22},{8,24},{10,26},{12,28},{14,30},{16,0},... | collective-permute-start | bytes 479240 | tf_op jit(solution)/shard_map/ppermute | solution.py:57
  236.0 5.5 %collective-permute-done.51 = bf16[48,1664]{1,0:T(8,128)(2,1)S(1)} collective-permute-done((bf16[48,1664]{1,0:T(8,128)(2,1)S(1)}, bf16[48,1664]{1,0:T(8,128)(2,1)S(1)}, u32[]{:S(2)}, u32[]{:S(2)}) %collective-permute-start.51) | collective-permute-done | bytes 159776 | tf_op jit(solution)/shard_map/ppermute | solution.py:57
  (233 shorter events, 82.3 us)
Async XLA Ops:
  7.2 14.8 %collective-permute-start.2 = (bf16[48,1664]{1,0:T(8,128)(2,1)S(1)}, bf16[48,1664]{1,0:T(8,128)(2,1)S(1)}, u32[]{:S(2)}, u32[]{:S(2)}) collective-permute-start(bf16[48,1664]{1,0:T(8,128)(2,1)S(1)} %bitcast_dynamic-update-slice_fusion.refs_0_), channel_id=1, source_target_pairs={{0,16},{2,18},{4,20},{6,22},{8,24},{10,26},{12,28},{14,30},{16,0},... | collective-permute-start | bytes 479240 | tf_op jit(solution)/shard_map/ppermute | solution.py:57
  9.8 12.2 %collective-permute-start.3 = (bf16[48,1664]{1,0:T(8,128)(2,1)S(1)}, bf16[48,1664]{1,0:T(8,128)(2,1)S(1)}, u32[]{:S(2)}, u32[]{:S(2)}) collective-permute-start(bf16[48,1664]{1,0:T(8,128)(2,1)S(1)} %bitcast_dynamic-update-slice_fusion.refs_0_), channel_id=1, source_target_pairs={{0,24},{2,26},{4,28},{6,30},{8,16},{10,18},{12,20},{14,22},{16,8},... | collective-permute-start | bytes 479240 | tf_op jit(solution)/shard_map/ppermute | solution.py:57
  9.8 15.3 %collective-permute-start = (bf16[256,768]{1,0:T(8,128)(2,1)}, bf16[256,768]{1,0:T(8,128)(2,1)S(1)}, u32[]{:S(2)}, u32[]{:S(2)}) collective-permute-start(bf16[256,768]{1,0:T(8,128)(2,1)} %param.20), channel_id=1, source_target_pairs={{0,1},{1,0},{2,3},{3,2},{4,5},{5,4},{6,7},{7,6},{8,9},{9,8},{10,11... | collective-permute-start | bytes 1179656 | tf_op jit(solution)/shard_map/ppermute | solution.py:61
  31.4 16.8 %collective-permute-start.7 = (bf16[192,1792]{1,0:T(8,128)(2,1)S(1)}, bf16[192,1792]{1,0:T(8,128)(2,1)S(1)}, u32[]{:S(2)}, u32[]{:S(2)}) collective-permute-start(bf16[192,1792]{1,0:T(8,128)(2,1)S(1)} %get-tuple-element.104.refs_4_.refs_1_), channel_id=1, source_target_pairs={{0,4},{2,6},{4,0},{6,2},{8,12},{10,14},{12,8},{14,10},{16,20},{18,... | collective-permute-start | bytes 2064392 | tf_op jit(solution)/shard_map/ppermute | solution.py:57
  33.0 15.2 %collective-permute-start.6 = (bf16[384,768]{1,0:T(8,128)(2,1)S(1)}, bf16[384,768]{1,0:T(8,128)(2,1)S(1)}, u32[]{:S(2)}, u32[]{:S(2)}) collective-permute-start(bf16[384,768]{1,0:T(8,128)(2,1)S(1)} %get-tuple-element.103.refs_0_), channel_id=1, source_target_pairs={{0,1},{1,0},{2,3},{3,2},{4,5},{5,4},{6,7},{7,6},{8,9},{9,8},{10,11... | collective-permute-start | bytes 1769480 | tf_op jit(solution)/shard_map/ppermute | solution.py:61
  49.4 26.7 %collective-permute-start.11 = (bf16[384,1792]{1,0:T(8,128)(2,1)S(1)}, bf16[384,1792]{1,0:T(8,128)(2,1)}, u32[]{:S(2)}, u32[]{:S(2)}) collective-permute-start(bf16[384,1792]{1,0:T(8,128)(2,1)S(1)} %get-tuple-element.106.refs_2_.refs_4_.refs_1_.refs_3_), channel_id=1, source_target_pairs={{0,2},{2,0},{4,6},{6,4},{8,10},{10,8},{12,14},{14,12},{16,18},{18,... | collective-permute-start | bytes 4128776 | tf_op jit(solution)/shard_map/ppermute | solution.py:57
  49.4 30.5 %collective-permute-start.12 = (bf16[384,1536]{1,0:T(8,128)(2,1)}, bf16[384,1536]{1,0:T(8,128)(2,1)}, u32[]{:S(2)}, u32[]{:S(2)}) collective-permute-start(bf16[384,1536]{1,0:T(8,128)(2,1)} %get-tuple-element.107.refs_3_.refs_2_.refs_9_.refs_5_), channel_id=1, source_target_pairs={{0,2},{2,0},{4,6},{6,4},{8,10},{10,8},{12,14},{14,12},{16,18},{18,... | collective-permute-start | bytes 3538952 | tf_op jit(solution)/shard_map/ppermute | solution.py:57
  50.5 13.6 %collective-permute-start.14 = (bf16[192,768]{1,0:T(8,128)(2,1)S(1)}, bf16[192,768]{1,0:T(8,128)(2,1)}, u32[]{:S(2)}, u32[]{:S(2)}) collective-permute-start(bf16[192,768]{1,0:T(8,128)(2,1)S(1)} %get-tuple-element.110.refs_1_), channel_id=1, source_target_pairs={{0,4},{2,6},{4,0},{6,2},{8,12},{10,14},{12,8},{14,10},{16,20},{18,... | collective-permute-start | bytes 884744 | tf_op jit(solution)/shard_map/ppermute | solution.py:57
  51.0 15.4 %collective-permute-start.15 = (bf16[48,1536]{1,0:T(8,128)(2,1)S(1)}, bf16[48,1536]{1,0:T(8,128)(2,1)}, u32[]{:S(2)}, u32[]{:S(2)}) collective-permute-start(bf16[48,1536]{1,0:T(8,128)(2,1)S(1)} %shard_map.327.refs_4_.refs_0_), channel_id=1, source_target_pairs={{0,8},{2,10},{4,12},{6,14},{8,0},{10,2},{12,4},{14,6},{16,24},{18,... | collective-permute-start | bytes 442376 | tf_op jit(solution)/shard_map/ppermute | solution.py:57
  58.9 14.0 %collective-permute-start.16 = (bf16[48,1536]{1,0:T(8,128)(2,1)S(1)}, bf16[48,1536]{1,0:T(8,128)(2,1)}, u32[]{:S(2)}, u32[]{:S(2)}) collective-permute-start(bf16[48,1536]{1,0:T(8,128)(2,1)S(1)} %shard_map.327.refs_4_.refs_0_), channel_id=1, source_target_pairs={{0,16},{2,18},{4,20},{6,22},{8,24},{10,26},{12,28},{14,30},{16,0},... | collective-permute-start | bytes 442376 | tf_op jit(solution)/shard_map/ppermute | solution.py:57
  66.4 26.1 %collective-permute-start.18 = (bf16[384,768]{1,0:T(8,128)(2,1)S(1)}, bf16[384,768]{1,0:T(8,128)(2,1)S(1)}, u32[]{:S(2)}, u32[]{:S(2)}) collective-permute-start(bf16[384,768]{1,0:T(8,128)(2,1)S(1)} %get-tuple-element.117.refs_0_), channel_id=1, source_target_pairs={{0,1},{1,0},{2,3},{3,2},{4,5},{5,4},{6,7},{7,6},{8,9},{9,8},{10,11... | collective-permute-start | bytes 1769480 | tf_op jit(solution)/shard_map/ppermute | solution.py:61
  72.9 19.6 %collective-permute-start.19 = (bf16[192,1536]{1,0:T(8,128)(2,1)S(1)}, bf16[192,1536]{1,0:T(8,128)(2,1)S(1)}, u32[]{:S(2)}, u32[]{:S(2)}) collective-permute-start(bf16[192,1536]{1,0:T(8,128)(2,1)S(1)} %get-tuple-element.111.refs_7_.refs_1_), channel_id=1, source_target_pairs={{0,4},{2,6},{4,0},{6,2},{8,12},{10,14},{12,8},{14,10},{16,20},{18,... | collective-permute-start | bytes 1769480 | tf_op jit(solution)/shard_map/ppermute | solution.py:57
  75.2 18.0 %collective-permute-start.20 = (bf16[192,768]{1,0:T(8,128)(2,1)S(1)}, bf16[192,768]{1,0:T(8,128)(2,1)S(1)}, u32[]{:S(2)}, u32[]{:S(2)}) collective-permute-start(bf16[192,768]{1,0:T(8,128)(2,1)S(1)} %get-tuple-element.112.refs_8_.refs_0_), channel_id=1, source_target_pairs={{0,1},{1,0},{2,3},{3,2},{4,5},{5,4},{6,7},{7,6},{8,9},{9,8},{10,11... | collective-permute-start | bytes 884744 | tf_op jit(solution)/shard_map/ppermute | solution.py:61
  76.1 17.2 %collective-permute-start.21 = (bf16[192,768]{1,0:T(8,128)(2,1)S(1)}, bf16[192,768]{1,0:T(8,128)(2,1)S(1)}, u32[]{:S(2)}, u32[]{:S(2)}) collective-permute-start(bf16[192,768]{1,0:T(8,128)(2,1)S(1)} %get-tuple-element.119.refs_1_), channel_id=1, source_target_pairs={{0,4},{2,6},{4,0},{6,2},{8,12},{10,14},{12,8},{14,10},{16,20},{18,... | collective-permute-start | bytes 884744 | tf_op jit(solution)/shard_map/ppermute | solution.py:57
  93.3 15.4 %collective-permute-start.24 = (bf16[384,768]{1,0:T(8,128)(2,1)S(1)}, bf16[384,768]{1,0:T(8,128)(2,1)S(1)}, u32[]{:S(2)}, u32[]{:S(2)}) collective-permute-start(bf16[384,768]{1,0:T(8,128)(2,1)S(1)} %get-tuple-element.125.refs_0_), channel_id=1, source_target_pairs={{0,1},{1,0},{2,3},{3,2},{4,5},{5,4},{6,7},{7,6},{8,9},{9,8},{10,11... | collective-permute-start | bytes 1769480 | tf_op jit(solution)/shard_map/ppermute | solution.py:61
  94.9 15.0 %collective-permute-start.25 = (bf16[192,1536]{1,0:T(8,128)(2,1)S(1)}, bf16[192,1536]{1,0:T(8,128)(2,1)S(1)}, u32[]{:S(2)}, u32[]{:S(2)}) collective-permute-start(bf16[192,1536]{1,0:T(8,128)(2,1)S(1)} %get-tuple-element.120.refs_6_.refs_1_), channel_id=1, source_target_pairs={{0,4},{2,6},{4,0},{6,2},{8,12},{10,14},{12,8},{14,10},{16,20},{18,... | collective-permute-start | bytes 1769480 | tf_op jit(solution)/shard_map/ppermute | solution.py:57
  117.9 17.3 %collective-permute-start.29 = (bf16[384,3072]{1,0:T(8,128)(2,1)S(1)}, bf16[384,3072]{1,0:T(8,128)(2,1)S(1)}, u32[]{:S(2)}, u32[]{:S(2)}) collective-permute-start(bf16[384,3072]{1,0:T(8,128)(2,1)S(1)} %convolution_convert_fusion), channel_id=1, source_target_pairs={{0,2},{2,0},{4,6},{6,4},{8,10},{10,8},{12,14},{14,12},{16,18},{18,... | collective-permute-start | bytes 7077896 | tf_op jit(solution)/shard_map/ppermute | solution.py:57
  121.1 14.7 %collective-permute-start.28 = (bf16[384,3072]{1,0:T(8,128)(2,1)S(1)}, bf16[384,3072]{1,0:T(8,128)(2,1)S(1)}, u32[]{:S(2)}, u32[]{:S(2)}) collective-permute-start(bf16[384,3072]{1,0:T(8,128)(2,1)S(1)} %convolution_convert_fusion.2), channel_id=1, source_target_pairs={{0,2},{2,0},{4,6},{6,4},{8,10},{10,8},{12,14},{14,12},{16,18},{18,... | collective-permute-start | bytes 7077896 | tf_op jit(solution)/shard_map/ppermute | solution.py:57
  136.4 33.3 %collective-permute-start.30 = (bf16[192,1536]{1,0:T(8,128)(2,1)S(1)}, bf16[192,1536]{1,0:T(8,128)(2,1)S(1)}, u32[]{:S(2)}, u32[]{:S(2)}) collective-permute-start(bf16[192,1536]{1,0:T(8,128)(2,1)S(1)} %get-tuple-element.143), channel_id=1, source_target_pairs={{0,4},{2,6},{4,0},{6,2},{8,12},{10,14},{12,8},{14,10},{16,20},{18,... | collective-permute-start | bytes 1769480 | tf_op jit(solution)/shard_map/ppermute | solution.py:57
  136.9 32.7 %collective-permute-start.31 = (bf16[384,768]{1,0:T(8,128)(2,1)S(1)}, bf16[384,768]{1,0:T(8,128)(2,1)S(1)}, u32[]{:S(2)}, u32[]{:S(2)}) collective-permute-start(bf16[384,768]{1,0:T(8,128)(2,1)S(1)} %get-tuple-element.145), channel_id=1, source_target_pairs={{0,1},{1,0},{2,3},{3,2},{4,5},{5,4},{6,7},{7,6},{8,9},{9,8},{10,11... | collective-permute-start | bytes 1769480 | tf_op jit(solution)/shard_map/ppermute | solution.py:61
  137.7 26.7 %collective-permute-start.32 = (bf16[192,1536]{1,0:T(8,128)(2,1)S(1)}, bf16[192,1536]{1,0:T(8,128)(2,1)S(1)}, u32[]{:S(2)}, u32[]{:S(2)}) collective-permute-start(bf16[192,1536]{1,0:T(8,128)(2,1)S(1)} %get-tuple-element.150), channel_id=1, source_target_pairs={{0,4},{2,6},{4,0},{6,2},{8,12},{10,14},{12,8},{14,10},{16,20},{18,... | collective-permute-start | bytes 1769480 | tf_op jit(solution)/shard_map/ppermute | solution.py:57
  139.0 25.7 %collective-permute-start.33 = (bf16[384,768]{1,0:T(8,128)(2,1)S(1)}, bf16[384,768]{1,0:T(8,128)(2,1)S(1)}, u32[]{:S(2)}, u32[]{:S(2)}) collective-permute-start(bf16[384,768]{1,0:T(8,128)(2,1)S(1)} %get-tuple-element.152), channel_id=1, source_target_pairs={{0,1},{1,0},{2,3},{3,2},{4,5},{5,4},{6,7},{7,6},{8,9},{9,8},{10,11... | collective-permute-start | bytes 1769480 | tf_op jit(solution)/shard_map/ppermute | solution.py:61
  168.8 13.7 %collective-permute-start.40 = (bf16[192,768]{1,0:T(8,128)(2,1)S(1)}, bf16[192,768]{1,0:T(8,128)(2,1)S(1)}, u32[]{:S(2)}, u32[]{:S(2)}) collective-permute-start(bf16[192,768]{1,0:T(8,128)(2,1)S(1)} %get-tuple-element.166), channel_id=1, source_target_pairs={{0,1},{1,0},{2,3},{3,2},{4,5},{5,4},{6,7},{7,6},{8,9},{9,8},{10,11... | collective-permute-start | bytes 884744 | tf_op jit(solution)/shard_map/ppermute | solution.py:61
  176.8 20.5 %collective-permute-start.34 = (bf16[256,768]{1,0:T(8,128)(2,1)}, bf16[256,768]{1,0:T(8,128)(2,1)}, u32[]{:S(2)}, u32[]{:S(2)}) collective-permute-start(bf16[256,768]{1,0:T(8,128)(2,1)} %get-tuple-element.157), channel_id=1, source_target_pairs={{0,1},{1,0},{2,3},{3,2},{4,5},{5,4},{6,7},{7,6},{8,9},{9,8},{10,11... | collective-permute-start | bytes 1179656 | tf_op jit(solution)/shard_map/ppermute | solution.py:61
  179.6 15.8 %collective-permute-start.38 = (bf16[192,768]{1,0:T(8,128)(2,1)}, bf16[192,768]{1,0:T(8,128)(2,1)}, u32[]{:S(2)}, u32[]{:S(2)}) collective-permute-start(bf16[192,768]{1,0:T(8,128)(2,1)} %get-tuple-element.163), channel_id=1, source_target_pairs={{0,1},{1,0},{2,3},{3,2},{4,5},{5,4},{6,7},{7,6},{8,9},{9,8},{10,11... | collective-permute-start | bytes 884744 | tf_op jit(solution)/shard_map/ppermute | solution.py:61
  180.2 16.4 %collective-permute-start.39 = (bf16[192,768]{1,0:T(8,128)(2,1)}, bf16[192,768]{1,0:T(8,128)(2,1)}, u32[]{:S(2)}, u32[]{:S(2)}) collective-permute-start(bf16[192,768]{1,0:T(8,128)(2,1)} %get-tuple-element.165), channel_id=1, source_target_pairs={{0,4},{2,6},{4,0},{6,2},{8,12},{10,14},{12,8},{14,10},{16,20},{18,... | collective-permute-start | bytes 884744 | tf_op jit(solution)/shard_map/ppermute | solution.py:57
  183.2 32.3 %collective-permute-start.36 = (bf16[192,1792]{1,0:T(8,128)(2,1)}, bf16[192,1792]{1,0:T(8,128)(2,1)S(1)}, u32[]{:S(2)}, u32[]{:S(2)}) collective-permute-start(bf16[192,1792]{1,0:T(8,128)(2,1)} %get-tuple-element.160), channel_id=1, source_target_pairs={{0,4},{2,6},{4,0},{6,2},{8,12},{10,14},{12,8},{14,10},{16,20},{18,... | collective-permute-start | bytes 2064392 | tf_op jit(solution)/shard_map/ppermute | solution.py:57
  188.7 26.7 %collective-permute-start.37 = (bf16[384,768]{1,0:T(8,128)(2,1)}, bf16[384,768]{1,0:T(8,128)(2,1)}, u32[]{:S(2)}, u32[]{:S(2)}) collective-permute-start(bf16[384,768]{1,0:T(8,128)(2,1)} %get-tuple-element.162), channel_id=1, source_target_pairs={{0,1},{1,0},{2,3},{3,2},{4,5},{5,4},{6,7},{7,6},{8,9},{9,8},{10,11... | collective-permute-start | bytes 1769480 | tf_op jit(solution)/shard_map/ppermute | solution.py:61
  196.5 14.1 %collective-permute-start.43 = (bf16[48,1536]{1,0:T(8,128)(2,1)S(1)}, bf16[48,1536]{1,0:T(8,128)(2,1)S(1)}, u32[]{:S(2)}, u32[]{:S(2)}) collective-permute-start(bf16[48,1536]{1,0:T(8,128)(2,1)S(1)} %get-tuple-element.172), channel_id=1, source_target_pairs={{0,16},{2,18},{4,20},{6,22},{8,24},{10,26},{12,28},{14,30},{16,0},... | collective-permute-start | bytes 442376 | tf_op jit(solution)/shard_map/ppermute | solution.py:57
  197.3 13.3 %collective-permute-start.44 = (bf16[48,1536]{1,0:T(8,128)(2,1)S(1)}, bf16[48,1536]{1,0:T(8,128)(2,1)S(1)}, u32[]{:S(2)}, u32[]{:S(2)}) collective-permute-start(bf16[48,1536]{1,0:T(8,128)(2,1)S(1)} %get-tuple-element.173), channel_id=1, source_target_pairs={{0,24},{2,26},{4,28},{6,30},{8,16},{10,18},{12,20},{14,22},{16,8},... | collective-permute-start | bytes 442376 | tf_op jit(solution)/shard_map/ppermute | solution.py:57
  202.4 16.5 %collective-permute-start.47 = (bf16[48,1536]{1,0:T(8,128)(2,1)S(1)}, bf16[48,1536]{1,0:T(8,128)(2,1)S(1)}, u32[]{:S(2)}, u32[]{:S(2)}) collective-permute-start(bf16[48,1536]{1,0:T(8,128)(2,1)S(1)} %get-tuple-element.178), channel_id=1, source_target_pairs={{0,8},{2,10},{4,12},{6,14},{8,0},{10,2},{12,4},{14,6},{16,24},{18,... | collective-permute-start | bytes 442376 | tf_op jit(solution)/shard_map/ppermute | solution.py:57
  227.7 13.8 %collective-permute-start.51 = (bf16[48,1664]{1,0:T(8,128)(2,1)S(1)}, bf16[48,1664]{1,0:T(8,128)(2,1)S(1)}, u32[]{:S(2)}, u32[]{:S(2)}) collective-permute-start(bf16[48,1664]{1,0:T(8,128)(2,1)S(1)} %get-tuple-element.183), channel_id=1, source_target_pairs={{0,16},{2,18},{4,20},{6,22},{8,24},{10,26},{12,28},{14,30},{16,0},... | collective-permute-start | bytes 479240 | tf_op jit(solution)/shard_map/ppermute | solution.py:57
  (63 other events, 619.7 us)

commit v2 on v1

--- a/solution.py
+++ b/solution.py
@@ -200,22 +200,29 @@
     return (left[rows, columns].astype(F32) + right[rows, columns].astype(F32)).astype(LOW)
 
 
-def split_core_kernel(keep, far, a_keep, a_send, b_keep, b_send):
-    rows, cut = a_keep.shape
-    half = b_keep.shape[1]
+def split_core_kernel(cut, *refs):
+    count = len(refs) - 4
+    a_keep, a_send, b_keep, b_send = refs[count:]
+    a, a_far, b, b_far = refs[:4] if count == 4 else refs[:2] * 2
+    base = 0 if count == 4 else cut
+    rows, half = a_keep.shape[0], b_keep.shape[1]
     every = slice(None)
-    a_keep[...] = added(keep, far, slice(0, rows), slice(0, cut))
-    a_send[...] = added(keep, far, slice(rows, 2 * rows), slice(0, cut))
-    b_keep[...] = added(keep, far, every, slice(cut, cut + half))
-    b_send[...] = added(keep, far, every, slice(cut + half, cut + 2 * half))
-
-
-def split_core(keep, far, cut, after=()):
-    rows, columns = keep.shape
+    a_keep[...] = added(a, a_far, slice(0, rows), slice(0, cut))
+    a_send[...] = added(a, a_far, slice(rows, 2 * rows), slice(0, cut))
+    b_keep[...] = added(b, b_far, every, slice(base, base + half))
+    b_send[...] = added(b, b_far, every, slice(base + half, base + 2 * half))
+
+
+def split_core(arrays, cut, b_columns, after=()):
+    rows = arrays[0].shape[0]
     a_shape = shape_of(rows // 2, cut, LOW)
-    b_shape = shape_of(rows, (columns - cut) // 2, LOW)
+    b_shape = shape_of(rows, b_columns // 2, LOW)
     return run(
-        split_core_kernel, [a_shape, a_shape, b_shape, b_shape], [keep, far], 0, after
+        functools.partial(split_core_kernel, cut),
+        [a_shape, a_shape, b_shape, b_shape],
+        arrays,
+        0,
+        after,
     )
 
 
@@ -276,10 +283,10 @@
         first, second = natural[row : row + 1, :half], natural[row : row + 1, half:]
         target[:, :half] = flip(rank, first, second)
         target[:, half:] = flip(rank, second, first)
-    for cut in range(2):
-        for place in range(2):
+    for place in range(2):
+        for cut in range(2):
             near, far = 8 + 2 * place + cut, 8 + 2 * (1 - place) + cut
-            at = (2 * cut + place) * width
+            at = (2 * place + cut) * width
             bias_inner[:, at : at + width] = flip(
                 rank, natural[near : near + 1], natural[far : far + 1]
             )
@@ -295,9 +302,9 @@
         first, second = total[:, :half], total[:, half:]
         natural[row : row + 1, :half] = flip(rank, first, second)
         natural[row : row + 1, half:] = flip(rank, second, first)
-    for cut in range(2):
-        for place in range(2):
-            near, far = (2 * cut + place) * width, (2 * cut + 1 - place) * width
+    for place in range(2):
+        for cut in range(2):
+            near, far = (2 * place + cut) * width, (2 * (1 - place) + cut) * width
             row = 8 + 2 * place + cut
             natural[row : row + 1, :] = flip(
                 rank, sums_inner[:, near : near + width], sums_inner[:, far : far + width]
@@ -308,8 +315,10 @@
     return jnp.transpose(relative[...]).astype(LOW)
 
 
-def cast_kernel(source, target):
-    target[...] = source[...].astype(LOW)
+def cast_kernel(first, second, target):
+    columns = first.shape[1]
+    target[:, :columns] = first[...].astype(LOW)
+    target[:, columns:] = second[...].astype(LOW)
 
 
 def project_kernel(rows, a_own, a_far, b_own, b_far, bias_q, bias_v, q, k, v):
@@ -393,27 +402,21 @@
     y_low[...] = y_new.astype(LOW)
 
 
-def hidden_kernel(y_low, a_own, a_far, b_own, b_far, bias, activation, slope):
-    half = a_own.shape[0]
+def hidden_kernel(y_low, own, far, bias, activation, slope):
+    half = own.shape[0]
     low, high = y_low[:, :half], y_low[:, half:]
-    columns = a_own.shape[1]
-    step = columns // 4
-    for place, (own, far) in enumerate(((a_own, a_far), (b_own, b_far))):
-        for start in range(0, columns, step):
-            at = slice(start, start + step)
-            to = slice(place * columns + start, place * columns + start + step)
-            pre = dot(low, own[:, at]) + dot(high, far[:, at]) + bias[:, to]
-            cdf = 0.5 + 0.5 * lax.erf(pre * (0.5**0.5))
-            activation[:, to] = (pre * cdf).astype(LOW)
-            slope[:, to] = cdf + pre * jnp.exp(-0.5 * pre * pre) * ((2.0 * np.pi) ** -0.5)
-
-
-def out_back_kernel(
-    activation, a_own, a_far, b_own, b_far, y, cot, valid, vec, mixed, grad, grad_low, sums
-):
-    columns = a_own.shape[1]
-    act_a, act_b = activation[:, :columns], activation[:, columns:]
-    out = [dot_nt(act_a, wa[...]) + dot_nt(act_b, wb[...]) for wa, wb in ((a_own, b_own), (a_far, b_far))]
+    columns = own.shape[1]
+    step = columns // 8
+    for start in range(0, columns, step):
+        at = slice(start, start + step)
+        pre = dot(low, own[:, at]) + dot(high, far[:, at]) + bias[:, at]
+        cdf = 0.5 + 0.5 * lax.erf(pre * (0.5**0.5))
+        activation[:, at] = (pre * cdf).astype(LOW)
+        slope[:, at] = cdf + pre * jnp.exp(-0.5 * pre * pre) * ((2.0 * np.pi) ** -0.5)
+
+
+def out_back_kernel(activation, own, far, y, cot, valid, vec, mixed, grad, grad_low, sums):
+    out = [dot_nt(activation[...], weights[...]) for weights in (own, far)]
     total = y[...] + jnp.concatenate(out, axis=1) + vec[3:4]
     result, normed, inv_std = normalize_fwd(total, vec[4:5], vec[5:6])
     mixed[...] = result.astype(LOW)
@@ -427,27 +430,22 @@
     sums[2:3] = shift_sum[None]
 
 
-def hidden_back_kernel(grad_low, a_own, a_far, b_own, b_far, slope, grad_pre, sums):
-    half = a_own.shape[0]
+def hidden_back_kernel(grad_low, own, far, slope, grad_pre, sums):
+    half = own.shape[0]
     low, high = grad_low[:, :half], grad_low[:, half:]
-    columns = a_own.shape[1]
-    step = columns // 4
-    for place, (own, far) in enumerate(((a_own, a_far), (b_own, b_far))):
-        for start in range(0, columns, step):
-            at = slice(start, start + step)
-            to = slice(place * columns + start, place * columns + start + step)
-            value = ((dot(low, own[:, at]) + dot(high, far[:, at])) * slope[:, to]).astype(LOW)
-            grad_pre[:, to] = value
-            sums[:, to] = jnp.sum(value.astype(F32), axis=0, keepdims=True)
+    columns = own.shape[1]
+    step = columns // 8
+    for start in range(0, columns, step):
+        at = slice(start, start + step)
+        value = ((dot(low, own[:, at]) + dot(high, far[:, at])) * slope[:, at]).astype(LOW)
+        grad_pre[:, at] = value
+        sums[:, at] = jnp.sum(value.astype(F32), axis=0, keepdims=True)
 
 
 def norm_back_kernel(
-    grad_pre, a_own, a_far, b_own, b_far, grad_two, normed, inv, vec, o_own, o_far,
-    grad, grad_low, grad_attn, sums,
+    grad_pre, own, far, grad_two, normed, inv, vec, o_own, o_far, grad, grad_low, grad_attn, sums
 ):
-    columns = a_own.shape[1]
-    pre_a, pre_b = grad_pre[:, :columns], grad_pre[:, columns:]
-    out = [dot_nt(pre_a, wa[...]) + dot_nt(pre_b, wb[...]) for wa, wb in ((a_own, b_own), (a_far, b_far))]
+    out = [dot_nt(grad_pre[...], weights[...]) for weights in (own, far)]
     grad_in, gain_sum, shift_sum = normalize_back(
         grad_two[...] + jnp.concatenate(out, axis=1), normed[...], inv[...], vec[1:2]
     )
@@ -539,7 +537,6 @@
     shard_rows = w_qkv.shape[1]
     part = w_qkv.shape[2]
     hidden_half = w_in.shape[1]
-    cut = hidden_half // 2
     full_inner = 2 * hidden_half
     half = width // 2
     count = vectors.shape[0]
@@ -564,7 +561,6 @@
         [low_qkv[0], low_qkv[1], vec_lanes, low_qkv[2], w_out.T.astype(LOW)], axis=1
     )
     a_width = 2 * part + LANES
-    low_shape = shape_of(shard_rows, hidden_half, LOW)
     rank = tensor_rank.astype(jnp.int32).reshape(1)
     scalar = pl.BlockSpec(memory_space=pltpu.SMEM)
     vmem = pl.BlockSpec(memory_space=pltpu.VMEM)
@@ -573,8 +569,14 @@
     one_high = gather_high(shard_one)
     one = join_high(one_high, a_width)
     one_far = swap_tensor(one[0]), swap_dp(one[1], 2)
-    shard_in = run(cast_kernel, [low_shape], [w_in], 0, after=one[:1])[0]
-    inner_high = gather_high(shard_in)
+    shard_pair = run(
+        cast_kernel,
+        [shape_of(shard_rows, full_inner, LOW)],
+        [w_in, w_back.T],
+        0,
+        after=one[:1],
+    )[0]
+    pair_high = gather_high(shard_pair)
 
     order = relative_order(width)
     permute = (jnp.arange(width, dtype=jnp.int32)[:, None] == order[None, :]).astype(LOW)
@@ -583,19 +585,13 @@
     rows_all = jnp.concatenate([dot(tokens, permute), dot(tokens_far, permute)]).astype(LOW)
     cot = dot(cotangent, permute)
 
-    one = join_plane(*one, *one_far, after=[shard_in, rows_all])
+    one = join_plane(*one, *one_far, after=[rows_all, pair_high[1]])
     one_far = swap_dp(one[0], 2), swap_tensor(one[1])
-    inner = join_high(inner_high, cut, after=one[:1])
-    shard_back = run(cast_kernel, [low_shape], [w_back.T], 0, after=inner[:1])[0]
-    outer_high = gather_high(shard_back)
-    one = join_plane(one[1], one[0], one_far[1], one_far[0], after=[shard_back])[::-1]
+    one = join_plane(one[1], one[0], one_far[1], one_far[0], after=pair_high[2:])[::-1]
     a_own, b_own = one
     a_far, b_far = swap_dp(a_own, 1), swap_dp(b_own, 1)
-    inner_far = swap_tensor(inner[0]), swap_dp(inner[1], 2)
-    outer = join_high(outer_high, cut, after=[a_own])
-    inner = join_plane(*inner, *inner_far, after=[a_own])
-    inner_far = swap_dp(inner[0], 2), swap_tensor(inner[1])
-    outer_far = swap_tensor(outer[0]), swap_dp(outer[1], 2)
+    pair = join_high(pair_high, hidden_half, after=[a_own])
+    pair_far = swap_tensor(pair[0]), swap_dp(pair[1], 2)
 
     vec, bias_query, bias_value, bias_inner = run(
         vectors_kernel,
@@ -607,6 +603,7 @@
         ],
         [rank, permute, a_own, a_far],
         1,
+        after=pair[:1],
         in_specs=[scalar, vmem, vmem, vmem],
     )
 
@@ -631,8 +628,9 @@
         [wide_low, group_low, group_low],
         [rows_all, a_own, a_far, b_own, b_far, bias_query, bias_value],
         5 * unit,
-        after=[inner[0], outer[0]],
-    )
+    )
+    pair = join_plane(*pair, *pair_far, after=[queries])
+    pair_far = swap_dp(pair[0], 2), swap_tensor(pair[1])
     pairs = width // LANES
     own_block = pl.BlockSpec((own_rows, LANES), lambda i: (0, i))
     all_block = pl.BlockSpec((group_rows, LANES), lambda i: (0, i))
@@ -645,35 +643,30 @@
         [wide_low],
         [seg_own, seg_keys, queries, key_rows, value_rows],
         3 * unit,
+        after=pair[:1],
         grid=(pairs,),
         in_specs=[fixed((1, own_rows)), fixed((group_rows, 1)), own_block, all_block, all_block],
         out_specs=[own_block],
     )[0]
-    inner = join_plane(inner[1], inner[0], inner_far[1], inner_far[0], after=[attended])[::-1]
-    c_own, d_own = inner
-    c_far, d_far = swap_dp(c_own, 1), swap_dp(d_own, 1)
-    outer = join_plane(*outer, *outer_far, after=[attended])
-    outer_far = swap_dp(outer[0], 2), swap_tensor(outer[1])
     first_norm, first_low, normed_one, inv_one = run(
         out_norm_kernel,
         [wide, wide_low, wide, shape_of(own_rows, 1, F32)],
         [attended, rows_all, b_own, b_far, vec],
-        400 * unit,
-        after=[inner[0], outer[0]],
-    )
+        2 * unit,
+    )
+    pair = join_plane(pair[1], pair[0], pair_far[1], pair_far[0], after=[first_low])[::-1]
+    c_own, d_own = pair
+    c_far, d_far = swap_dp(c_own, 1), swap_dp(d_own, 1)
     activation, slope = run(
         hidden_kernel,
         [shape_of(own_rows, full_inner, LOW), shape_of(own_rows, full_inner, F32)],
-        [first_low, c_own, c_far, d_own, d_far, bias_inner],
+        [first_low, c_own, c_far, bias_inner],
         8 * unit,
     )
-    outer = join_plane(outer[1], outer[0], outer_far[1], outer_far[0], after=[activation])[::-1]
-    e_own, f_own = outer
-    e_far, f_far = swap_dp(e_own, 1), swap_dp(f_own, 1)
     mixed_rel, grad_two, grad_two_low, sums_two = run(
         out_back_kernel,
         [wide_low, wide, wide_low, sums_shape],
-        [activation, e_own, e_far, f_own, f_far, first_norm, cot, valid, vec],
+        [activation, d_own, d_far, first_norm, cot, valid, vec],
         5 * unit,
     )
     mixed = dot_nt(mixed_rel, permute).astype(LOW)
@@ -686,19 +679,16 @@
     grad_pre, sums_inner = run(
         hidden_back_kernel,
         [shape_of(own_rows, full_inner, LOW), shape_of(1, full_inner, F32)],
-        [grad_two_low, e_own, e_far, f_own, f_far, slope],
+        [grad_two_low, d_own, d_far, slope],
         6 * unit,
     )
-    a_keep, a_send, b_keep, b_send = split_core(*outer, hidden_half, after=[grad_pre])
-    outer = a_keep, swap_dp(a_send, 2), b_keep, swap_tensor(b_send)
     inner = weight_grad(first_low, grad_pre)
-    inner_keep = split_core(*inner, hidden_half, after=[a_keep])
-    a_keep, a_send, b_keep, b_send = inner_keep
-    inner = a_keep, swap_dp(a_send, 2), b_keep, swap_tensor(b_send)
+    a_keep, a_send, b_keep, b_send = split_core([*inner, *outer], full_inner, full_inner)
+    pair = a_keep, swap_dp(a_send, 2), b_keep, swap_tensor(b_send)
     grad_one, grad_one_low, grad_attn, sums_one = run(
         norm_back_kernel,
         [wide, wide_low, wide_low, sums_shape],
-        [grad_pre, c_own, c_far, d_own, d_far, grad_two, normed_one, inv_one, vec, b_own, b_far],
+        [grad_pre, c_own, c_far, grad_two, normed_one, inv_one, vec, b_own, b_far],
         6 * unit,
         after=[a_keep],
     )
@@ -706,14 +696,12 @@
         attend_back_kernel,
         [wide_low, group_low, group_low],
         [seg_own, seg_keys, queries, key_rows, value_rows, grad_attn],
-        25 * unit,
+        5 * unit,
         grid=(pairs,),
         in_specs=[fixed((1, own_rows)), fixed((group_rows, 1))]
         + [own_block, all_block, all_block, own_block],
         out_specs=[own_block, all_block, all_block],
     )
-    a_keep, a_send, b_keep, b_send = split_plane(*outer, after=[grad_q])
-    outer = a_keep, swap_tensor(a_send), b_keep, swap_dp(b_send, 2)
     one_shape = shape_of(half, 2 * a_width + 4 * part, LOW)
     one_send, one_keep = run(
         functools.partial(first_grads_kernel, a_width),
@@ -721,13 +709,12 @@
         [rank, permute, rows_all, grad_q, grad_k, grad_v, grad_one_low, attended]
         + [sums_one, sums_two, sums_inner],
         6 * unit,
-        after=[a_keep],
         in_specs=[scalar] + [vmem] * 10,
         scratch=[pltpu.VMEM((16, width), F32), pltpu.VMEM((LANES, width), F32)],
     )
     one_far = swap_dp(one_send, 1)
-    a_keep, a_send, b_keep, b_send = split_plane(*inner, after=[one_keep])
-    inner = a_keep, swap_tensor(a_send), b_keep, swap_dp(b_send, 2)
+    a_keep, a_send, b_keep, b_send = split_plane(*pair, after=[one_keep])
+    pair = a_keep, swap_tensor(a_send), b_keep, swap_dp(b_send, 2)
     grad_own, grad_away = run(
         rows_back_kernel,
         [wide, wide_low],
@@ -739,16 +726,16 @@
     input_grad = lax.dot_general(
         grad_rel, permute_wide, (((1,), (1,)), ((), ())), precision=exact
     )
-    one_keep = split_core(one_keep, one_far, 2 * a_width, after=[grad_own])
-    outer = send_high(split_high(*outer, after=one_keep[:1]))
-    inner = send_high(split_high(*inner, after=outer[:1]))
-    summed_back = reduce_high(outer).T
-    a_keep, a_send, b_keep, b_send = one_keep
+    a_keep, a_send, b_keep, b_send = split_core(
+        [one_keep, one_far], 2 * a_width, 4 * part, after=[grad_own, mixed]
+    )
     one = a_keep, swap_dp(a_send, 2), b_keep, swap_tensor(b_send)
-    summed_in = reduce_high(inner)
-    a_keep, a_send, b_keep, b_send = split_plane(*one, after=inner[:1] + outer[1:])
+    pair = send_high(split_high(*pair, after=[a_keep, input_grad]))
+    a_keep, a_send, b_keep, b_send = split_plane(*one, after=pair[:1])
     one = a_keep, swap_tensor(a_send), b_keep, swap_dp(b_send, 2)
-    sum_one = reduce_high(send_high(split_high(*one, after=inner[1:])))
+    sum_pair = reduce_high(pair)
+    summed_in, summed_back = sum_pair[:, :hidden_half], sum_pair[:, hidden_half:].T
+    sum_one = reduce_high(send_high(split_high(*one)))
 
     summed_vectors = lax.dynamic_slice_in_dim(
         sum_one[:, 2 * part : a_width], tensor_rank * shard_width, shard_width, axis=0

time: 247 us -> 256 us (1.036)
  waiting for transfers between devices: 80.6 us -> 123 us
  starting transfers between devices: 63.3 us -> 46.5 us
  matrix products: 22.8 us -> 8.14 us
    ppermute x39 -> x27, waiting for transfers between devices: 62.9 us -> 85 us  [swap_dp(): return lax.ppermute(values, 'dp', [(i, i ^ mask) for i in range(size)])]
    ppermute x14 -> x10, waiting for transfers between devices: 17.7 us -> 37.7 us  [swap_tensor(): return lax.ppermute(values, 'tensor', [(0, 1), (1, 0)])]
    ppermute x39 -> x27, starting transfers between devices: 49.1 us -> 34.9 us  [swap_dp(): return lax.ppermute(values, 'dp', [(i, i ^ mask) for i in range(size)])]
    dot_general x4, matrix products: 15.3 us -> 3.24 us  [dot_tn(): lax.dot_general(left, right, (((0,), (0,)), ((), ())), preferred_element_...]
    ppermute x14 -> x10, starting transfers between devices: 14.2 us -> 11.7 us  [swap_tensor(): return lax.ppermute(values, 'tensor', [(0, 1), (1, 0)])]
    unnamed x93 -> x89, local copies, waits for them, and re-layouts: 8.55 us -> 7.86 us
    pallas_call x31 -> x24, Pallas kernels: 58.6 us -> 58.3 us  [run(): pl.pallas_call(body, grid=grid, out_shape=list(outs), in_specs=list(in_sp...]
  transfers between devices with their start and end apart: 53 -> 37, of which waited for: 18 -> 22; matrix products, arithmetic and copies ran while one was open for 12% -> 5% of each run, Pallas kernels for 22% -> 14%
where the time goes in v2:
time: 256 us; the launch traced here: 255 us
  waiting for transfers between devices  123 us (48%)
  Pallas kernels  58.3 us (23%)
  starting transfers between devices  46.5 us (18%)
  other arithmetic  9.28 us (4%)
  local copies, waits for them, and re-layouts  8.61 us (3%)
  matrix products  8.14 us (3%)
    ppermute x27, waiting for transfers between devices, swap_dp(): return lax.ppermute(values, 'dp', [(i, i ^ mask) for i in range(size)])  85 us
    pallas_call x24, Pallas kernels, run(): pl.pallas_call(body, grid=grid, out_shape=list(outs), in_specs=list(in_sp...  58.3 us
    ppermute x10, waiting for transfers between devices, swap_tensor(): return lax.ppermute(values, 'tensor', [(0, 1), (1, 0)])  37.7 us
    ppermute x27, starting transfers between devices, swap_dp(): return lax.ppermute(values, 'dp', [(i, i ^ mask) for i in range(size)])  34.9 us
    ppermute x10, starting transfers between devices, swap_tensor(): return lax.ppermute(values, 'tensor', [(0, 1), (1, 0)])  11.7 us
    unnamed x89, local copies, waits for them, and re-layouts  7.86 us
  transfers between devices with their start and end apart: 37, of which 22 were waited for; matrix products, arithmetic and copies ran while one was open for 5% of the time, Pallas kernels for 14%

profile of v2, /device:TPU:0, one launch (start us, length us, event | category | flops | bytes accessed | tf_op | source)
XLA Modules:
  0.0 255.1 jit_solution(5746168016918841921)
XLA Ops:
  4.2 3.1 %collective-permute-start.1 = (bf16[48,1664]{1,0:T(8,128)(2,1)S(1)}, bf16[48,1664]{1,0:T(8,128)(2,1)S(1)}, u32[]{:S(2)}, u32[]{:S(2)}) collective-permute-start(bf16[48,1664]{1,0:T(8,128)(2,1)S(1)} %bitcast_dynamic-update-slice_fusion.refs_0_), channel_id=1, source_target_pairs={{0,8},{2,10},{4,12},{6,14},{8,0},{10,2},{12,4},{14,6},{16,24},{18,... | collective-permute-start | bytes 479240 | tf_op jit(solution)/shard_map/ppermute | solution.py:57
  7.3 2.6 %collective-permute-start.2 = (bf16[48,1664]{1,0:T(8,128)(2,1)S(1)}, bf16[48,1664]{1,0:T(8,128)(2,1)S(1)}, u32[]{:S(2)}, u32[]{:S(2)}) collective-permute-start(bf16[48,1664]{1,0:T(8,128)(2,1)S(1)} %bitcast_dynamic-update-slice_fusion.refs_0_), channel_id=1, source_target_pairs={{0,16},{2,18},{4,20},{6,22},{8,24},{10,26},{12,28},{14,30},{16,0},... | collective-permute-start | bytes 479240 | tf_op jit(solution)/shard_map/ppermute | solution.py:57
  13.9 8.1 %collective-permute-done.2.refs_2_ = bf16[48,1664]{1,0:T(8,128)(2,1)S(1)} collective-permute-done((bf16[48,1664]{1,0:T(8,128)(2,1)S(1)}, bf16[48,1664]{1,0:T(8,128)(2,1)S(1)}, u32[]{:S(2)}, u32[]{:S(2)}) %collective-permute-start.2) | collective-permute-done | bytes 159776 | tf_op jit(solution)/shard_map/ppermute | solution.py:57
  25.2 2.6 %collective-permute-start.6 = (bf16[48,3072]{1,0:T(8,128)(2,1)S(1)}, bf16[48,3072]{1,0:T(8,128)(2,1)S(1)}, u32[]{:S(2)}, u32[]{:S(2)}) collective-permute-start(bf16[48,3072]{1,0:T(8,128)(2,1)S(1)} %shard_map.324.refs_0_), channel_id=1, source_target_pairs={{0,8},{2,10},{4,12},{6,14},{8,0},{10,2},{12,4},{14,6},{16,24},{18,... | collective-permute-start | bytes 884744 | tf_op jit(solution)/shard_map/ppermute | solution.py:57
  30.4 2.8 %collective-permute-done.6.refs_5_.refs_1_ = bf16[48,3072]{1,0:T(8,128)(2,1)S(1)} collective-permute-done((bf16[48,3072]{1,0:T(8,128)(2,1)S(1)}, bf16[48,3072]{1,0:T(8,128)(2,1)S(1)}, u32[]{:S(2)}, u32[]{:S(2)}) %collective-permute-start.6) | collective-permute-done | bytes 294944 | tf_op jit(solution)/shard_map/ppermute | solution.py:57
  34.3 3.4 %collective-permute-start.9 = (bf16[48,3072]{1,0:T(8,128)(2,1)S(1)}, bf16[48,3072]{1,0:T(8,128)(2,1)S(1)}, u32[]{:S(2)}, u32[]{:S(2)}) collective-permute-start(bf16[48,3072]{1,0:T(8,128)(2,1)S(1)} %shard_map.324.refs_0_), channel_id=1, source_target_pairs={{0,16},{2,18},{4,20},{6,22},{8,24},{10,26},{12,28},{14,30},{16,0},... | collective-permute-start | bytes 884744 | tf_op jit(solution)/shard_map/ppermute | solution.py:57
  38.9 16.9 %collective-permute-done.9.refs_4_.refs_2_ = bf16[48,3072]{1,0:T(8,128)(2,1)S(1)} collective-permute-done((bf16[48,3072]{1,0:T(8,128)(2,1)S(1)}, bf16[48,3072]{1,0:T(8,128)(2,1)S(1)}, u32[]{:S(2)}, u32[]{:S(2)}) %collective-permute-start.9) | collective-permute-done | bytes 294944 | tf_op jit(solution)/shard_map/ppermute | solution.py:57
  60.9 2.5 shard_map.329
  63.5 8.5 %collective-permute-done.13.refs_2_ = bf16[192,1536]{1,0:T(8,128)(2,1)S(1)} collective-permute-done((bf16[192,1536]{1,0:T(8,128)(2,1)S(1)}, bf16[192,1536]{1,0:T(8,128)(2,1)S(1)}, u32[]{:S(2)}, u32[]{:S(2)}) %collective-permute-start.13) | collective-permute-done | bytes 589856 | tf_op jit(solution)/shard_map/ppermute | solution.py:61
  78.9 8.0 %shard_map.331.refs_0_.refs_7_ = bf16[256,768]{1,0:T(8,128)(2,1)S(1)} custom-call(s32[1,256]{1,0:T(1,128)S(1)} %bitcast.79, s32[512,1]{1,0:T(8,128)S(1)} %copy.69.refs_1_, bf16[256,768]{1,0:T(8,128)(2,1)S(1)} %get-tuple-element.92.refs_4_.refs_2_, bf16[512,768]{1,0:T(8,128)(2,1)S(1)} %copy-done.15, bf16[512,768]{1,0:T(8,128)(2,1)S(1)} %copy-done.18, ...), custom_call_target="tpu_custom_call" | custom-call | flops 905969664 | bytes 2362368 | tf_op jit(solution)/shard_map/pallas_call | solution.py:142
  87.8 13.3 %collective-permute-done.15.refs_2_ = bf16[384,1536]{1,0:T(8,128)(2,1)} collective-permute-done((bf16[384,1536]{1,0:T(8,128)(2,1)}, bf16[384,1536]{1,0:T(8,128)(2,1)}, u32[]{:S(2)}, u32[]{:S(2)}) %collective-permute-start.15) | collective-permute-done | bytes 1179680 | tf_op jit(solution)/shard_map/ppermute | solution.py:61
  102.2 2.6 %shard_map.333 = (bf16[384,3072]{1,0:T(8,128)(2,1)S(1)}, bf16[384,3072]{1,0:T(8,128)(2,1)S(1)}) custom-call(bf16[384,1536]{1,0:T(8,128)(2,1)} %get-tuple-element.99.refs_0_, bf16[192,3072]{1,0:T(8,128)(2,1)} %get-tuple-element.96.refs_5_.refs_1_, bf16[384,1536]{1,0:T(8,128)(2,1)} %collective-permute-done.15.refs_2_, ...), custom_call_target="tpu_custom_call" | custom-call | bytes 9437184 | tf_op jit(solution)/shard_map/pallas_call | solution.py:142
  109.5 2.8 %shard_map.334 = (bf16[256,3072]{1,0:T(8,128)(2,1)S(1)}, f32[256,3072]{1,0:T(8,128)S(1)}) custom-call(bf16[256,768]{1,0:T(8,128)(2,1)S(1)} %get-tuple-element.98.refs_4_.refs_0_, bf16[384,3072]{1,0:T(8,128)(2,1)S(1)} %get-tuple-element.100.refs_1_, bf16[384,3072]{1,0:T(8,128)(2,1)S(1)} %collective-permute-done.17.refs_2_, ...), custom_call_target="tpu_custom_call" | custom-call | flops 2415919104 | bytes 9842688 | tf_op jit(solution)/shard_map/pallas_call | solution.py:142
  112.9 2.4 shard_map.335
  116.1 2.1 shard_map.336
  121.2 2.4 collective-permute-done.19.refs_1_
  123.6 3.4 %collective-permute-done.20.refs_3_ = bf16[384,3072]{1,0:T(8,128)(2,1)S(1)} collective-permute-done((bf16[384,3072]{1,0:T(8,128)(2,1)S(1)}, bf16[384,3072]{1,0:T(8,128)(2,1)S(1)}, u32[]{:S(2)}, u32[]{:S(2)}) %collective-permute-start.20) | collective-permute-done | bytes 2359328 | tf_op jit(solution)/shard_map/ppermute | solution.py:57
  127.0 12.7 %shard_map.337 = (bf16[192,3072]{1,0:T(8,128)(2,1)S(1)}, bf16[192,3072]{1,0:T(8,128)(2,1)S(1)}, bf16[384,1536]{1,0:T(8,128)(2,1)S(1)}, bf16[384,1536]{1,0:T(8,128)(2,1)S(1)}) custom-call(bf16[384,3072]{1,0:T(8,128)(2,1)S(1)} %convolution_convert_fusion.3.refs_0_, bf16[384,3072]{1,0:T(8,128)(2,1)S(1)} %collective-permute-done.19.refs_1_, ...), custom_call_target="tpu_custom_call" | custom-call | bytes 14155776 | tf_op jit(solution)/shard_map/pallas_call | solution.py:142
  141.8 2.7 %shard_map.338 = (f32[256,768]{1,0:T(8,128)S(1)}, bf16[256,768]{1,0:T(8,128)(2,1)S(1)}, bf16[256,768]{1,0:T(8,128)(2,1)S(1)}, f32[8,768]{1,0:T(8,128)S(1)}) custom-call(bf16[256,3072]{1,0:T(8,128)(2,1)S(1)} %get-tuple-element.108.refs_0_, bf16[384,3072]{1,0:T(8,128)(2,1)S(1)} %get-tuple-element.100.refs_1_, ...), custom_call_target="tpu_custom_call" | custom-call | flops 1811939328 | bytes 11840512 | tf_op jit(solution)/shard_map/pallas_call | solution.py:142
  144.5 10.0 %shard_map.339 = (bf16[256,768]{1,0:T(8,128)(2,1)S(1)}, bf16[512,768]{1,0:T(8,128)(2,1)S(1)}, bf16[512,768]{1,0:T(8,128)(2,1)S(1)}) custom-call(s32[1,256]{1,0:T(1,128)S(1)} %bitcast.80, s32[512,1]{1,0:T(8,128)S(1)} %copy.69.refs_1_, bf16[256,768]{1,0:T(8,128)(2,1)S(1)} %get-tuple-element.92.refs_4_.refs_2_, bf16[512,768]{1,0:T(8,128)(2,1)S(1)} %copy-done.16, ...), custom_call_target="tpu_custom_call" | custom-call | flops 1509949440 | bytes 4328448 | tf_op jit(solution)/shard_map/pallas_call | solution.py:142
  154.5 3.1 %shard_map.340 = (bf16[384,3328]{1,0:T(8,128)(2,1)S(1)}, bf16[384,3328]{1,0:T(8,128)(2,1)S(1)}) custom-call(s32[1]{0:T(128)} %bitcast.12.refs_0_, bf16[768,768]{1,0:T(8,128)(2,1)S(1)} %copy-done.9, bf16[512,768]{1,0:T(8,128)(2,1)S(1)} %pad_maximum_fusion.refs_4_.refs_0_.refs_1_.refs_2_, bf16[256,768]{1,0:T(8,128)(2,1)S(1)} %get-tuple-element.114.refs_3_.refs_0_, ...), custom_call_target="tpu_custom_call" | custom-call | flops 1811939328 | bytes 9891844 | tf_op jit(solution)/shard_map/pallas_call | solution.py:142
  157.7 10.1 %collective-permute-done.21.refs_1_ = bf16[192,3072]{1,0:T(8,128)(2,1)S(1)} collective-permute-done((bf16[192,3072]{1,0:T(8,128)(2,1)S(1)}, bf16[192,3072]{1,0:T(8,128)(2,1)S(1)}, u32[]{:S(2)}, u32[]{:S(2)}) %collective-permute-start.21) | collective-permute-done | bytes 1179680 | tf_op jit(solution)/shard_map/ppermute | solution.py:57
  169.4 2.6 %shard_map.342 = (f32[256,768]{1,0:T(8,128)S(1)}, bf16[256,768]{1,0:T(8,128)(2,1)S(1)}) custom-call(bf16[256,768]{1,0:T(8,128)(2,1)S(1)} %get-tuple-element.114.refs_3_.refs_0_, bf16[512,768]{1,0:T(8,128)(2,1)S(1)} %get-tuple-element.115.refs_4_.refs_1_, bf16[512,768]{1,0:T(8,128)(2,1)S(1)} %get-tuple-element.116.refs_5_.refs_2_, ...), custom_call_target="tpu_custom_call" | custom-call | flops 120795955200 | bytes 9043968 | tf_op jit(solution)/shard_map/pallas_call | solution.py:142
  176.3 7.9 %collective-permute-done.23 = bf16[256,768]{1,0:T(8,128)(2,1)S(1)} collective-permute-done((bf16[256,768]{1,0:T(8,128)(2,1)S(1)}, bf16[256,768]{1,0:T(8,128)(2,1)S(1)}, u32[]{:S(2)}, u32[]{:S(2)}) %collective-permute-start.23) | collective-permute-done | bytes 393248 | tf_op jit(solution)/shard_map/ppermute | solution.py:61
  187.1 7.7 %collective-permute-done.27.refs_1_ = bf16[192,1536]{1,0:T(8,128)(2,1)S(1)} collective-permute-done((bf16[192,1536]{1,0:T(8,128)(2,1)S(1)}, bf16[192,1536]{1,0:T(8,128)(2,1)S(1)}, u32[]{:S(2)}, u32[]{:S(2)}) %collective-permute-start.27) | collective-permute-done | bytes 589856 | tf_op jit(solution)/shard_map/ppermute | solution.py:61
  195.9 2.9 %collective-permute-start.36 = (bf16[48,3072]{1,0:T(8,128)(2,1)}, bf16[48,3072]{1,0:T(8,128)(2,1)}, u32[]{:S(2)}, u32[]{:S(2)}) collective-permute-start(bf16[48,3072]{1,0:T(8,128)(2,1)} %get-tuple-element.148), channel_id=1, source_target_pairs={{0,24},{2,26},{4,28},{6,30},{8,16},{10,18},{12,20},{14,22},{16,8},... | collective-permute-start | bytes 884744 | tf_op jit(solution)/shard_map/ppermute | solution.py:57
  198.8 4.6 %collective-permute-start.35 = (bf16[48,3072]{1,0:T(8,128)(2,1)}, bf16[48,3072]{1,0:T(8,128)(2,1)}, u32[]{:S(2)}, u32[]{:S(2)}) collective-permute-start(bf16[48,3072]{1,0:T(8,128)(2,1)} %get-tuple-element.147), channel_id=1, source_target_pairs={{0,16},{2,18},{4,20},{6,22},{8,24},{10,26},{12,28},{14,30},{16,0},... | collective-permute-start | bytes 884744 | tf_op jit(solution)/shard_map/ppermute | solution.py:57
  205.9 18.1 %collective-permute-done.35 = bf16[48,3072]{1,0:T(8,128)(2,1)} collective-permute-done((bf16[48,3072]{1,0:T(8,128)(2,1)}, bf16[48,3072]{1,0:T(8,128)(2,1)}, u32[]{:S(2)}, u32[]{:S(2)}) %collective-permute-start.35) | collective-permute-done | bytes 294944 | tf_op jit(solution)/shard_map/ppermute | solution.py:57
  228.8 7.0 %collective-permute-done.30.refs_3_ = bf16[192,768]{1,0:T(8,128)(2,1)S(1)} collective-permute-done((bf16[192,768]{1,0:T(8,128)(2,1)S(1)}, bf16[192,768]{1,0:T(8,128)(2,1)S(1)}, u32[]{:S(2)}, u32[]{:S(2)}) %collective-permute-start.30) | collective-permute-done | bytes 294944 | tf_op jit(solution)/shard_map/ppermute | solution.py:57
  235.9 2.9 %collective-permute-start.33 = (bf16[48,1664]{1,0:T(8,128)(2,1)S(1)}, bf16[48,1664]{1,0:T(8,128)(2,1)S(1)}, u32[]{:S(2)}, u32[]{:S(2)}) collective-permute-start(bf16[48,1664]{1,0:T(8,128)(2,1)S(1)} %get-tuple-element.145), channel_id=1, source_target_pairs={{0,24},{2,26},{4,28},{6,30},{8,16},{10,18},{12,20},{14,22},{16,8},... | collective-permute-start | bytes 479240 | tf_op jit(solution)/shard_map/ppermute | solution.py:57
  241.5 3.4 %collective-permute-done.33 = bf16[48,1664]{1,0:T(8,128)(2,1)S(1)} collective-permute-done((bf16[48,1664]{1,0:T(8,128)(2,1)S(1)}, bf16[48,1664]{1,0:T(8,128)(2,1)S(1)}, u32[]{:S(2)}, u32[]{:S(2)}) %collective-permute-start.33) | collective-permute-done | bytes 159776 | tf_op jit(solution)/shard_map/ppermute | solution.py:57
  244.9 6.2 %collective-permute-done.32 = bf16[48,1664]{1,0:T(8,128)(2,1)S(1)} collective-permute-done((bf16[48,1664]{1,0:T(8,128)(2,1)S(1)}, bf16[48,1664]{1,0:T(8,128)(2,1)S(1)}, u32[]{:S(2)}, u32[]{:S(2)}) %collective-permute-start.32) | collective-permute-done | bytes 159776 | tf_op jit(solution)/shard_map/ppermute | solution.py:57
  (191 shorter events, 64.0 us)
Async XLA Ops:
  4.2 9.7 %collective-permute-start.1 = (bf16[48,1664]{1,0:T(8,128)(2,1)S(1)}, bf16[48,1664]{1,0:T(8,128)(2,1)S(1)}, u32[]{:S(2)}, u32[]{:S(2)}) collective-permute-start(bf16[48,1664]{1,0:T(8,128)(2,1)S(1)} %bitcast_dynamic-update-slice_fusion.refs_0_), channel_id=1, source_target_pairs={{0,8},{2,10},{4,12},{6,14},{8,0},{10,2},{12,4},{14,6},{16,24},{18,... | collective-permute-start | bytes 479240 | tf_op jit(solution)/shard_map/ppermute | solution.py:57
  7.3 14.8 %collective-permute-start.2 = (bf16[48,1664]{1,0:T(8,128)(2,1)S(1)}, bf16[48,1664]{1,0:T(8,128)(2,1)S(1)}, u32[]{:S(2)}, u32[]{:S(2)}) collective-permute-start(bf16[48,1664]{1,0:T(8,128)(2,1)S(1)} %bitcast_dynamic-update-slice_fusion.refs_0_), channel_id=1, source_target_pairs={{0,16},{2,18},{4,20},{6,22},{8,24},{10,26},{12,28},{14,30},{16,0},... | collective-permute-start | bytes 479240 | tf_op jit(solution)/shard_map/ppermute | solution.py:57
  9.8 12.2 %collective-permute-start.3 = (bf16[48,1664]{1,0:T(8,128)(2,1)S(1)}, bf16[48,1664]{1,0:T(8,128)(2,1)S(1)}, u32[]{:S(2)}, u32[]{:S(2)}) collective-permute-start(bf16[48,1664]{1,0:T(8,128)(2,1)S(1)} %bitcast_dynamic-update-slice_fusion.refs_0_), channel_id=1, source_target_pairs={{0,24},{2,26},{4,28},{6,30},{8,16},{10,18},{12,20},{14,22},{16,8},... | collective-permute-start | bytes 479240 | tf_op jit(solution)/shard_map/ppermute | solution.py:57
  9.8 18.0 %collective-permute-start = (bf16[256,768]{1,0:T(8,128)(2,1)}, bf16[256,768]{1,0:T(8,128)(2,1)S(1)}, u32[]{:S(2)}, u32[]{:S(2)}) collective-permute-start(bf16[256,768]{1,0:T(8,128)(2,1)} %param.20), channel_id=1, source_target_pairs={{0,1},{1,0},{2,3},{3,2},{4,5},{5,4},{6,7},{7,6},{8,9},{9,8},{10,11... | collective-permute-start | bytes 1179656 | tf_op jit(solution)/shard_map/ppermute | solution.py:61
  22.1 11.0 %collective-permute-start.4 = (bf16[192,896]{1,0:T(8,128)(2,1)S(1)}, bf16[192,896]{1,0:T(8,128)(2,1)S(1)}, u32[]{:S(2)}, u32[]{:S(2)}) collective-permute-start(bf16[192,896]{1,0:T(8,128)(2,1)S(1)} %get-tuple-element.83.refs_2_.refs_0_), channel_id=1, source_target_pairs={{0,1},{1,0},{2,3},{3,2},{4,5},{5,4},{6,7},{7,6},{8,9},{9,8},{10,11... | collective-permute-start | bytes 1032200 | tf_op jit(solution)/shard_map/ppermute | solution.py:61
  25.2 7.9 %collective-permute-start.6 = (bf16[48,3072]{1,0:T(8,128)(2,1)S(1)}, bf16[48,3072]{1,0:T(8,128)(2,1)S(1)}, u32[]{:S(2)}, u32[]{:S(2)}) collective-permute-start(bf16[48,3072]{1,0:T(8,128)(2,1)S(1)} %shard_map.324.refs_0_), channel_id=1, source_target_pairs={{0,8},{2,10},{4,12},{6,14},{8,0},{10,2},{12,4},{14,6},{16,24},{18,... | collective-permute-start | bytes 884744 | tf_op jit(solution)/shard_map/ppermute | solution.py:57
  33.2 22.6 %collective-permute-start.8 = (bf16[192,1792]{1,0:T(8,128)(2,1)S(1)}, bf16[192,1792]{1,0:T(8,128)(2,1)S(1)}, u32[]{:S(2)}, u32[]{:S(2)}) collective-permute-start(bf16[192,1792]{1,0:T(8,128)(2,1)S(1)} %get-tuple-element.86.refs_1_), channel_id=1, source_target_pairs={{0,4},{2,6},{4,0},{6,2},{8,12},{10,14},{12,8},{14,10},{16,20},{18,... | collective-permute-start | bytes 2064392 | tf_op jit(solution)/shard_map/ppermute | solution.py:57
  33.8 22.0 %collective-permute-start.7 = (bf16[384,768]{1,0:T(8,128)(2,1)S(1)}, bf16[384,768]{1,0:T(8,128)(2,1)S(1)}, u32[]{:S(2)}, u32[]{:S(2)}) collective-permute-start(bf16[384,768]{1,0:T(8,128)(2,1)S(1)} %get-tuple-element.85.refs_0_), channel_id=1, source_target_pairs={{0,1},{1,0},{2,3},{3,2},{4,5},{5,4},{6,7},{7,6},{8,9},{9,8},{10,11... | collective-permute-start | bytes 1769480 | tf_op jit(solution)/shard_map/ppermute | solution.py:61
  34.3 21.5 %collective-permute-start.9 = (bf16[48,3072]{1,0:T(8,128)(2,1)S(1)}, bf16[48,3072]{1,0:T(8,128)(2,1)S(1)}, u32[]{:S(2)}, u32[]{:S(2)}) collective-permute-start(bf16[48,3072]{1,0:T(8,128)(2,1)S(1)} %shard_map.324.refs_0_), channel_id=1, source_target_pairs={{0,16},{2,18},{4,20},{6,22},{8,24},{10,26},{12,28},{14,30},{16,0},... | collective-permute-start | bytes 884744 | tf_op jit(solution)/shard_map/ppermute | solution.py:57
  37.7 18.1 %collective-permute-start.10 = (bf16[48,3072]{1,0:T(8,128)(2,1)S(1)}, bf16[48,3072]{1,0:T(8,128)(2,1)S(1)}, u32[]{:S(2)}, u32[]{:S(2)}) collective-permute-start(bf16[48,3072]{1,0:T(8,128)(2,1)S(1)} %shard_map.324.refs_0_), channel_id=1, source_target_pairs={{0,24},{2,26},{4,28},{6,30},{8,16},{10,18},{12,20},{14,22},{16,8},... | collective-permute-start | bytes 884744 | tf_op jit(solution)/shard_map/ppermute | solution.py:57
  56.7 15.4 %collective-permute-start.13 = (bf16[192,1536]{1,0:T(8,128)(2,1)S(1)}, bf16[192,1536]{1,0:T(8,128)(2,1)S(1)}, u32[]{:S(2)}, u32[]{:S(2)}) collective-permute-start(bf16[192,1536]{1,0:T(8,128)(2,1)S(1)} %get-tuple-element.89.refs_4_.refs_0_), channel_id=1, source_target_pairs={{0,1},{1,0},{2,3},{3,2},{4,5},{5,4},{6,7},{7,6},{8,9},{9,8},{10,11... | collective-permute-start | bytes 1769480 | tf_op jit(solution)/shard_map/ppermute | solution.py:61
  57.3 15.0 %collective-permute-start.14 = (bf16[192,1536]{1,0:T(8,128)(2,1)S(1)}, bf16[192,1536]{1,0:T(8,128)(2,1)S(1)}, u32[]{:S(2)}, u32[]{:S(2)}) collective-permute-start(bf16[192,1536]{1,0:T(8,128)(2,1)S(1)} %get-tuple-element.95.refs_1_), channel_id=1, source_target_pairs={{0,4},{2,6},{4,0},{6,2},{8,12},{10,14},{12,8},{14,10},{16,20},{18,... | collective-permute-start | bytes 1769480 | tf_op jit(solution)/shard_map/ppermute | solution.py:57
  73.9 27.2 %collective-permute-start.15 = (bf16[384,1536]{1,0:T(8,128)(2,1)}, bf16[384,1536]{1,0:T(8,128)(2,1)}, u32[]{:S(2)}, u32[]{:S(2)}) collective-permute-start(bf16[384,1536]{1,0:T(8,128)(2,1)} %get-tuple-element.99.refs_0_), channel_id=1, source_target_pairs={{0,1},{1,0},{2,3},{3,2},{4,5},{5,4},{6,7},{7,6},{8,9},{9,8},{10,11... | collective-permute-start | bytes 3538952 | tf_op jit(solution)/shard_map/ppermute | solution.py:61
  75.4 26.8 %collective-permute-start.16 = (bf16[192,3072]{1,0:T(8,128)(2,1)}, bf16[192,3072]{1,0:T(8,128)(2,1)}, u32[]{:S(2)}, u32[]{:S(2)}) collective-permute-start(bf16[192,3072]{1,0:T(8,128)(2,1)} %get-tuple-element.96.refs_5_.refs_1_), channel_id=1, source_target_pairs={{0,4},{2,6},{4,0},{6,2},{8,12},{10,14},{12,8},{14,10},{16,20},{18,... | collective-permute-start | bytes 3538952 | tf_op jit(solution)/shard_map/ppermute | solution.py:57
  105.0 7.9 %collective-permute-start.18 = (bf16[384,3072]{1,0:T(8,128)(2,1)S(1)}, bf16[384,3072]{1,0:T(8,128)(2,1)S(1)}, u32[]{:S(2)}, u32[]{:S(2)}) collective-permute-start(bf16[384,3072]{1,0:T(8,128)(2,1)S(1)} %get-tuple-element.103.refs_1_), channel_id=1, source_target_pairs={{0,2},{2,0},{4,6},{6,4},{8,10},{10,8},{12,14},{14,12},{16,18},{18,... | collective-permute-start | bytes 7077896 | tf_op jit(solution)/shard_map/ppermute | solution.py:57
  119.2 7.8 %collective-permute-start.20 = (bf16[384,3072]{1,0:T(8,128)(2,1)S(1)}, bf16[384,3072]{1,0:T(8,128)(2,1)S(1)}, u32[]{:S(2)}, u32[]{:S(2)}) collective-permute-start(bf16[384,3072]{1,0:T(8,128)(2,1)S(1)} %convolution_convert_fusion), channel_id=1, source_target_pairs={{0,2},{2,0},{4,6},{6,4},{8,10},{10,8},{12,14},{14,12},{16,18},{18,... | collective-permute-start | bytes 7077896 | tf_op jit(solution)/shard_map/ppermute | solution.py:57
  139.7 28.1 %collective-permute-start.21 = (bf16[192,3072]{1,0:T(8,128)(2,1)S(1)}, bf16[192,3072]{1,0:T(8,128)(2,1)S(1)}, u32[]{:S(2)}, u32[]{:S(2)}) collective-permute-start(bf16[192,3072]{1,0:T(8,128)(2,1)S(1)} %get-tuple-element.118), channel_id=1, source_target_pairs={{0,4},{2,6},{4,0},{6,2},{8,12},{10,14},{12,8},{14,10},{16,20},{18,... | collective-permute-start | bytes 3538952 | tf_op jit(solution)/shard_map/ppermute | solution.py:57
  140.4 27.7 %collective-permute-start.22 = (bf16[384,1536]{1,0:T(8,128)(2,1)S(1)}, bf16[384,1536]{1,0:T(8,128)(2,1)S(1)}, u32[]{:S(2)}, u32[]{:S(2)}) collective-permute-start(bf16[384,1536]{1,0:T(8,128)(2,1)S(1)} %get-tuple-element.120), channel_id=1, source_target_pairs={{0,1},{1,0},{2,3},{3,2},{4,5},{5,4},{6,7},{7,6},{8,9},{9,8},{10,11... | collective-permute-start | bytes 3538952 | tf_op jit(solution)/shard_map/ppermute | solution.py:61
  157.6 28.0 %collective-permute-start.24 = (bf16[384,3328]{1,0:T(8,128)(2,1)S(1)}, bf16[384,3328]{1,0:T(8,128)(2,1)S(1)}, u32[]{:S(2)}, u32[]{:S(2)}) collective-permute-start(bf16[384,3328]{1,0:T(8,128)(2,1)S(1)} %get-tuple-element.129), channel_id=1, source_target_pairs={{0,2},{2,0},{4,6},{6,4},{8,10},{10,8},{12,14},{14,12},{16,18},{18,... | collective-permute-start | bytes 7667720 | tf_op jit(solution)/shard_map/ppermute | solution.py:57
  172.1 12.1 %collective-permute-start.23 = (bf16[256,768]{1,0:T(8,128)(2,1)S(1)}, bf16[256,768]{1,0:T(8,128)(2,1)S(1)}, u32[]{:S(2)}, u32[]{:S(2)}) collective-permute-start(bf16[256,768]{1,0:T(8,128)(2,1)S(1)} %get-tuple-element.128), channel_id=1, source_target_pairs={{0,1},{1,0},{2,3},{3,2},{4,5},{5,4},{6,7},{7,6},{8,9},{9,8},{10,11... | collective-permute-start | bytes 1179656 | tf_op jit(solution)/shard_map/ppermute | solution.py:61
  173.6 21.3 %collective-permute-start.27 = (bf16[192,1536]{1,0:T(8,128)(2,1)S(1)}, bf16[192,1536]{1,0:T(8,128)(2,1)S(1)}, u32[]{:S(2)}, u32[]{:S(2)}) collective-permute-start(bf16[192,1536]{1,0:T(8,128)(2,1)S(1)} %get-tuple-element.134), channel_id=1, source_target_pairs={{0,1},{1,0},{2,3},{3,2},{4,5},{5,4},{6,7},{7,6},{8,9},{9,8},{10,11... | collective-permute-start | bytes 1769480 | tf_op jit(solution)/shard_map/ppermute | solution.py:61
  174.2 20.7 %collective-permute-start.28 = (bf16[192,1536]{1,0:T(8,128)(2,1)S(1)}, bf16[192,1536]{1,0:T(8,128)(2,1)S(1)}, u32[]{:S(2)}, u32[]{:S(2)}) collective-permute-start(bf16[192,1536]{1,0:T(8,128)(2,1)S(1)} %get-tuple-element.136), channel_id=1, source_target_pairs={{0,4},{2,6},{4,0},{6,2},{8,12},{10,14},{12,8},{14,10},{16,20},{18,... | collective-permute-start | bytes 1769480 | tf_op jit(solution)/shard_map/ppermute | solution.py:57
  195.9 10.0 %collective-permute-start.36 = (bf16[48,3072]{1,0:T(8,128)(2,1)}, bf16[48,3072]{1,0:T(8,128)(2,1)}, u32[]{:S(2)}, u32[]{:S(2)}) collective-permute-start(bf16[48,3072]{1,0:T(8,128)(2,1)} %get-tuple-element.148), channel_id=1, source_target_pairs={{0,24},{2,26},{4,28},{6,30},{8,16},{10,18},{12,20},{14,22},{16,8},... | collective-permute-start | bytes 884744 | tf_op jit(solution)/shard_map/ppermute | solution.py:57
  198.8 25.2 %collective-permute-start.35 = (bf16[48,3072]{1,0:T(8,128)(2,1)}, bf16[48,3072]{1,0:T(8,128)(2,1)}, u32[]{:S(2)}, u32[]{:S(2)}) collective-permute-start(bf16[48,3072]{1,0:T(8,128)(2,1)} %get-tuple-element.147), channel_id=1, source_target_pairs={{0,16},{2,18},{4,20},{6,22},{8,24},{10,26},{12,28},{14,30},{16,0},... | collective-permute-start | bytes 884744 | tf_op jit(solution)/shard_map/ppermute | solution.py:57
  203.4 20.6 %collective-permute-start.34 = (bf16[48,3072]{1,0:T(8,128)(2,1)S(1)}, bf16[48,3072]{1,0:T(8,128)(2,1)}, u32[]{:S(2)}, u32[]{:S(2)}) collective-permute-start(bf16[48,3072]{1,0:T(8,128)(2,1)S(1)} %get-tuple-element.146), channel_id=1, source_target_pairs={{0,8},{2,10},{4,12},{6,14},{8,0},{10,2},{12,4},{14,6},{16,24},{18,... | collective-permute-start | bytes 884744 | tf_op jit(solution)/shard_map/ppermute | solution.py:57
  203.8 21.5 %collective-permute-start.25 = (bf16[192,1792]{1,0:T(8,128)(2,1)}, bf16[192,1792]{1,0:T(8,128)(2,1)S(1)}, u32[]{:S(2)}, u32[]{:S(2)}) collective-permute-start(bf16[192,1792]{1,0:T(8,128)(2,1)} %copy-done.22), channel_id=1, source_target_pairs={{0,4},{2,6},{4,0},{6,2},{8,12},{10,14},{12,8},{14,10},{16,20},{18,... | collective-permute-start | bytes 2064392 | tf_op jit(solution)/shard_map/ppermute | solution.py:57
  205.0 20.3 %collective-permute-start.26 = (bf16[384,768]{1,0:T(8,128)(2,1)S(1)}, bf16[384,768]{1,0:T(8,128)(2,1)S(1)}, u32[]{:S(2)}, u32[]{:S(2)}) collective-permute-start(bf16[384,768]{1,0:T(8,128)(2,1)S(1)} %copy-done.24), channel_id=1, source_target_pairs={{0,1},{1,0},{2,3},{3,2},{4,5},{5,4},{6,7},{7,6},{8,9},{9,8},{10,11... | collective-permute-start | bytes 1769480 | tf_op jit(solution)/shard_map/ppermute | solution.py:61
  225.7 10.1 %collective-permute-start.29 = (bf16[192,896]{1,0:T(8,128)(2,1)S(1)}, bf16[192,896]{1,0:T(8,128)(2,1)S(1)}, u32[]{:S(2)}, u32[]{:S(2)}) collective-permute-start(bf16[192,896]{1,0:T(8,128)(2,1)S(1)} %get-tuple-element.139), channel_id=1, source_target_pairs={{0,1},{1,0},{2,3},{3,2},{4,5},{5,4},{6,7},{7,6},{8,9},{9,8},{10,11... | collective-permute-start | bytes 1032200 | tf_op jit(solution)/shard_map/ppermute | solution.py:61
  227.1 8.6 %collective-permute-start.30 = (bf16[192,768]{1,0:T(8,128)(2,1)S(1)}, bf16[192,768]{1,0:T(8,128)(2,1)S(1)}, u32[]{:S(2)}, u32[]{:S(2)}) collective-permute-start(bf16[192,768]{1,0:T(8,128)(2,1)S(1)} %get-tuple-element.141), channel_id=1, source_target_pairs={{0,4},{2,6},{4,0},{6,2},{8,12},{10,14},{12,8},{14,10},{16,20},{18,... | collective-permute-start | bytes 884744 | tf_op jit(solution)/shard_map/ppermute | solution.py:57
  235.9 8.9 %collective-permute-start.33 = (bf16[48,1664]{1,0:T(8,128)(2,1)S(1)}, bf16[48,1664]{1,0:T(8,128)(2,1)S(1)}, u32[]{:S(2)}, u32[]{:S(2)}) collective-permute-start(bf16[48,1664]{1,0:T(8,128)(2,1)S(1)} %get-tuple-element.145), channel_id=1, source_target_pairs={{0,24},{2,26},{4,28},{6,30},{8,16},{10,18},{12,20},{14,22},{16,8},... | collective-permute-start | bytes 479240 | tf_op jit(solution)/shard_map/ppermute | solution.py:57
  238.9 12.2 %collective-permute-start.32 = (bf16[48,1664]{1,0:T(8,128)(2,1)S(1)}, bf16[48,1664]{1,0:T(8,128)(2,1)S(1)}, u32[]{:S(2)}, u32[]{:S(2)}) collective-permute-start(bf16[48,1664]{1,0:T(8,128)(2,1)S(1)} %get-tuple-element.144), channel_id=1, source_target_pairs={{0,16},{2,18},{4,20},{6,22},{8,24},{10,26},{12,28},{14,30},{16,0},... | collective-permute-start | bytes 479240 | tf_op jit(solution)/shard_map/ppermute | solution.py:57
  238.9 12.2 %collective-permute-start.31 = (bf16[48,1664]{1,0:T(8,128)(2,1)S(1)}, bf16[48,1664]{1,0:T(8,128)(2,1)S(1)}, u32[]{:S(2)}, u32[]{:S(2)}) collective-permute-start(bf16[48,1664]{1,0:T(8,128)(2,1)S(1)} %get-tuple-element.143), channel_id=1, source_target_pairs={{0,8},{2,10},{4,12},{6,14},{8,0},{10,2},{12,4},{14,6},{16,24},{18,... | collective-permute-start | bytes 479240 | tf_op jit(solution)/shard_map/ppermute | solution.py:57
  (45 other events, 615.0 us)

commit v3 on v2

--- a/solution.py
+++ b/solution.py
@@ -88,8 +88,7 @@
     return [parts[0]] + [swap_dp(part, mask) for part, mask in zip(parts[1:], masks[1:])]
 
 
-def reduce_high(parts):
-    total = sum(part.astype(F32) for part in parts)
+def reduce_rest(total):
     for group in reversed(high_groups()[:-1]):
         masks = group_masks(group)
         rows = total.shape[0] // len(masks)
@@ -163,14 +162,14 @@
         second[to, :] = piece[:, cut:]
 
 
-def join_high(pieces, cut, after=()):
+def join_high(pieces, cut, flops=0, after=()):
     rows, columns = pieces[0].shape
     rows = rows * len(pieces)
     return run(
         functools.partial(join_high_kernel, len(pieces)),
         [shape_of(rows, cut, LOW), shape_of(rows, columns - cut, LOW)],
         pieces,
-        0,
+        flops,
         after,
     )
 
@@ -200,30 +199,50 @@
     return (left[rows, columns].astype(F32) + right[rows, columns].astype(F32)).astype(LOW)
 
 
-def split_core_kernel(cut, *refs):
-    count = len(refs) - 4
-    a_keep, a_send, b_keep, b_send = refs[count:]
-    a, a_far, b, b_far = refs[:4] if count == 4 else refs[:2] * 2
-    base = 0 if count == 4 else cut
-    rows, half = a_keep.shape[0], b_keep.shape[1]
-    every = slice(None)
-    a_keep[...] = added(a, a_far, slice(0, rows), slice(0, cut))
-    a_send[...] = added(a, a_far, slice(rows, 2 * rows), slice(0, cut))
-    b_keep[...] = added(b, b_far, every, slice(base, base + half))
-    b_send[...] = added(b, b_far, every, slice(base + half, base + 2 * half))
-
-
-def split_core(arrays, cut, b_columns, after=()):
-    rows = arrays[0].shape[0]
-    a_shape = shape_of(rows // 2, cut, LOW)
-    b_shape = shape_of(rows, b_columns // 2, LOW)
+def split_rows_kernel(array, far, keep, send):
+    rows = keep.shape[0]
+    keep[...] = added(array, far, slice(0, rows), slice(None))
+    send[...] = added(array, far, slice(rows, 2 * rows), slice(None))
+
+
+def split_columns_kernel(array, far, keep, send):
+    columns = keep.shape[1]
+    keep[...] = added(array, far, slice(None), slice(0, columns))
+    send[...] = added(array, far, slice(None), slice(columns, 2 * columns))
+
+
+def split_rows(array, far, flops=0, after=()):
+    part = shape_of(array.shape[0] // 2, array.shape[1], LOW)
+    return run(split_rows_kernel, [part, part], [array, far], flops, after)
+
+
+def split_columns(array, far, flops=0, after=()):
+    part = shape_of(array.shape[0], array.shape[1] // 2, LOW)
+    return run(split_columns_kernel, [part, part], [array, far], flops, after)
+
+
+def split_core_kernel(a, a_far, b, b_far, a_keep, a_send, b_keep, b_send):
+    split_rows_kernel(a, a_far, a_keep, a_send)
+    split_columns_kernel(b, b_far, b_keep, b_send)
+
+
+def split_core(a, a_far, b, b_far, after=()):
+    a_shape = shape_of(a.shape[0] // 2, a.shape[1], LOW)
+    b_shape = shape_of(b.shape[0], b.shape[1] // 2, LOW)
     return run(
-        functools.partial(split_core_kernel, cut),
-        [a_shape, a_shape, b_shape, b_shape],
-        arrays,
-        0,
-        after,
-    )
+        split_core_kernel, [a_shape, a_shape, b_shape, b_shape], [a, a_far, b, b_far], 0, after
+    )
+
+
+def sum_kernel(*refs):
+    total = refs[0][...].astype(F32)
+    for ref in refs[1:-1]:
+        total = total + ref[...].astype(F32)
+    refs[-1][...] = total
+
+
+def sum_parts(parts, flops, after=()):
+    return run(sum_kernel, [shape_of(*parts[0].shape, F32)], parts, flops, after)
 
 
 def split_plane_kernel(a, a_far, b, b_far, a_keep, a_send, b_keep, b_send):
@@ -485,17 +504,28 @@
         away[:, to] = both[own_rows:].astype(LOW)
 
 
+def rows_out_kernel(own, away, permute, out):
+    rest = own[...] + away[...].astype(F32)
+    total = None
+    for _ in range(3):
+        part = rest.astype(LOW)
+        rest = rest - part.astype(F32)
+        moved = dot_nt(part, permute[...])
+        total = moved if total is None else total + moved
+    out[...] = total
+
+
 def first_grads_kernel(
     a_half, rank_ref, permute, rows, grad_q, grad_k, grad_v, grad_low, attended,
-    sums_one, sums_two, sums_inner, send, keep, natural, relative,
+    sums_one, sums_two, sums_inner, a_send, b_send, a_keep, b_keep, natural, relative,
 ):
-    half = keep.shape[0]
+    half = a_keep.shape[0]
     own_rows, width = grad_q.shape
     part = width // 2
     extra = vector_lanes(
         rank_ref[0], permute, grad_q, grad_v, sums_one, sums_two, sums_inner, natural, relative
     )
-    for place, to in ((1, send), (0, keep)):
+    for place, to, to_b in ((1, a_send, b_send), (0, a_keep, b_keep)):
         at = slice(place * half, (place + 1) * half)
         both = rows[:, at]
         mine = rows[:own_rows, at]
@@ -506,9 +536,9 @@
             to[:, base : base + part] = dot_tn(mine, grad_q[:, cols]).astype(LOW)
             to[:, base + part : base + 2 * part] = dot_tn(both, grad_k[:, cols]).astype(LOW)
             to[:, base + 2 * part : base + a_half] = extra[at, :]
-            base = 2 * a_half + side * 2 * part
-            to[:, base : base + part] = dot_tn(both, grad_v[:, cols]).astype(LOW)
-            to[:, base + part : base + 2 * part] = dot_tn(low, attended[:, cols]).astype(LOW)
+            base = side * 2 * part
+            to_b[:, base : base + part] = dot_tn(both, grad_v[:, cols]).astype(LOW)
+            to_b[:, base + part : base + 2 * part] = dot_tn(low, attended[:, cols]).astype(LOW)
 
 
 def on_device(
@@ -580,17 +610,16 @@
 
     order = relative_order(width)
     permute = (jnp.arange(width, dtype=jnp.int32)[:, None] == order[None, :]).astype(LOW)
-    permute_wide = permute.astype(F32)
-    exact = lax.Precision.HIGHEST
     rows_all = jnp.concatenate([dot(tokens, permute), dot(tokens_far, permute)]).astype(LOW)
     cot = dot(cotangent, permute)
 
-    one = join_plane(*one, *one_far, after=[rows_all, pair_high[1]])
+    one = join_plane(*one, *one_far, after=[rows_all])
     one_far = swap_dp(one[0], 2), swap_tensor(one[1])
-    one = join_plane(one[1], one[0], one_far[1], one_far[0], after=pair_high[2:])[::-1]
+    unit = 2 * own_rows * width * width
+    pair = join_high(pair_high, hidden_half, 400 * unit)
+    one = join_plane(one[1], one[0], one_far[1], one_far[0], after=pair[:1])[::-1]
     a_own, b_own = one
     a_far, b_far = swap_dp(a_own, 1), swap_dp(b_own, 1)
-    pair = join_high(pair_high, hidden_half, after=[a_own])
     pair_far = swap_tensor(pair[0]), swap_dp(pair[1], 2)
 
     vec, bias_query, bias_value, bias_inner = run(
@@ -603,7 +632,6 @@
         ],
         [rank, permute, a_own, a_far],
         1,
-        after=pair[:1],
         in_specs=[scalar, vmem, vmem, vmem],
     )
 
@@ -622,7 +650,6 @@
     wide = shape_of(own_rows, width, F32)
     group_low = shape_of(group_rows, width, LOW)
     sums_shape = shape_of(8, width, F32)
-    unit = 2 * own_rows * width * width
     queries, key_rows, value_rows = run(
         project_kernel,
         [wide_low, group_low, group_low],
@@ -683,7 +710,8 @@
         6 * unit,
     )
     inner = weight_grad(first_low, grad_pre)
-    a_keep, a_send, b_keep, b_send = split_core([*inner, *outer], full_inner, full_inner)
+    b_keep, b_send = split_columns(*outer, 400 * unit, after=[grad_pre])
+    a_keep, a_send = split_rows(*inner, after=[b_keep])
     pair = a_keep, swap_dp(a_send, 2), b_keep, swap_tensor(b_send)
     grad_one, grad_one_low, grad_attn, sums_one = run(
         norm_back_kernel,
@@ -702,18 +730,18 @@
         + [own_block, all_block, all_block, own_block],
         out_specs=[own_block, all_block, all_block],
     )
-    one_shape = shape_of(half, 2 * a_width + 4 * part, LOW)
-    one_send, one_keep = run(
+    a_shape, b_shape = shape_of(half, 2 * a_width, LOW), shape_of(half, 4 * part, LOW)
+    a_send, b_send, one_a, one_b = run(
         functools.partial(first_grads_kernel, a_width),
-        [one_shape, one_shape],
+        [a_shape, b_shape, a_shape, b_shape],
         [rank, permute, rows_all, grad_q, grad_k, grad_v, grad_one_low, attended]
         + [sums_one, sums_two, sums_inner],
         6 * unit,
         in_specs=[scalar] + [vmem] * 10,
         scratch=[pltpu.VMEM((16, width), F32), pltpu.VMEM((LANES, width), F32)],
     )
-    one_far = swap_dp(one_send, 1)
-    a_keep, a_send, b_keep, b_send = split_plane(*pair, after=[one_keep])
+    one = one_a, swap_dp(a_send, 1), one_b, swap_dp(b_send, 1)
+    a_keep, a_send, b_keep, b_send = split_plane(*pair, after=[one_a, mixed])
     pair = a_keep, swap_tensor(a_send), b_keep, swap_dp(b_send, 2)
     grad_own, grad_away = run(
         rows_back_kernel,
@@ -722,20 +750,23 @@
         400 * unit,
         after=[a_keep],
     )
-    grad_rel = grad_own + swap_tensor(grad_away).astype(F32)
-    input_grad = lax.dot_general(
-        grad_rel, permute_wide, (((1,), (1,)), ((), ())), precision=exact
-    )
-    a_keep, a_send, b_keep, b_send = split_core(
-        [one_keep, one_far], 2 * a_width, 4 * part, after=[grad_own, mixed]
-    )
+    a_keep, a_send, b_keep, b_send = split_core(*one, after=[grad_own])
     one = a_keep, swap_dp(a_send, 2), b_keep, swap_tensor(b_send)
-    pair = send_high(split_high(*pair, after=[a_keep, input_grad]))
+    pair = send_high(split_high(*pair, after=[a_keep]))
     a_keep, a_send, b_keep, b_send = split_plane(*one, after=pair[:1])
     one = a_keep, swap_tensor(a_send), b_keep, swap_dp(b_send, 2)
-    sum_pair = reduce_high(pair)
+    pair = sum_parts(pair, 400 * unit, after=[a_keep])
+    one = send_high(split_high(*one, after=pair))
+    input_grad = run(
+        rows_out_kernel,
+        [wide],
+        [grad_own, swap_tensor(grad_away), permute],
+        3 * unit,
+        after=one[:1],
+    )[0]
+    sum_pair = reduce_rest(pair[0])
     summed_in, summed_back = sum_pair[:, :hidden_half], sum_pair[:, hidden_half:].T
-    sum_one = reduce_high(send_high(split_high(*one)))
+    sum_one = reduce_rest(sum(part.astype(F32) for part in one))
 
     summed_vectors = lax.dynamic_slice_in_dim(
         sum_one[:, 2 * part : a_width], tensor_rank * shard_width, shard_width, axis=0

time: 256 us -> 225 us (0.88)
  waiting for transfers between devices: 123 us -> 82.5 us
  local copies, waits for them, and re-layouts: 8.61 us -> 13.3 us
  Pallas kernels: 58.3 us -> 62.3 us
    ppermute x27 -> x28, waiting for transfers between devices: 85 us -> 58.3 us  [swap_dp(): return lax.ppermute(values, 'dp', [(i, i ^ mask) for i in range(size)])]
    ppermute x10, waiting for transfers between devices: 37.7 us -> 24.2 us  [swap_tensor(): return lax.ppermute(values, 'tensor', [(0, 1), (1, 0)])]
    pallas_call x24 -> x27, Pallas kernels: 58.3 us -> 62.3 us  [run(): pl.pallas_call(body, grid=grid, out_shape=list(outs), in_specs=list(in_sp...]
    unnamed x89 -> x97, local copies, waits for them, and re-layouts: 7.86 us -> 11.2 us
    ppermute x27 -> x28, starting transfers between devices: 34.9 us -> 34.1 us  [swap_dp(): return lax.ppermute(values, 'dp', [(i, i ^ mask) for i in range(size)])]
  transfers between devices with their start and end apart: 37 -> 38, of which waited for: 22 -> 18; matrix products, arithmetic and copies ran while one was open for 5% -> 8% of each run, Pallas kernels for 14% -> 25%
where the time goes in v3:
time: 225 us; the launch traced here: 223 us
  waiting for transfers between devices  82.5 us (37%)
  Pallas kernels  62.3 us (28%)
  starting transfers between devices  45.6 us (20%)
  local copies, waits for them, and re-layouts  13.3 us (6%)
  other arithmetic  11.1 us (5%)
  matrix products  6.74 us (3%)
    pallas_call x27, Pallas kernels, run(): pl.pallas_call(body, grid=grid, out_shape=list(outs), in_specs=list(in_sp...  62.3 us
    ppermute x28, waiting for transfers between devices, swap_dp(): return lax.ppermute(values, 'dp', [(i, i ^ mask) for i in range(size)])  58.3 us
    ppermute x28, starting transfers between devices, swap_dp(): return lax.ppermute(values, 'dp', [(i, i ^ mask) for i in range(size)])  34.1 us
    ppermute x10, waiting for transfers between devices, swap_tensor(): return lax.ppermute(values, 'tensor', [(0, 1), (1, 0)])  24.2 us
    ppermute x10, starting transfers between devices, swap_tensor(): return lax.ppermute(values, 'tensor', [(0, 1), (1, 0)])  11.5 us
    unnamed x97, local copies, waits for them, and re-layouts  11.2 us
  transfers between devices with their start and end apart: 38, of which 18 were waited for; matrix products, arithmetic and copies ran while one was open for 8% of the time, Pallas kernels for 25%

profile of v3, /device:TPU:0, one launch (start us, length us, event | category | flops | bytes accessed | tf_op | source)
XLA Modules:
  0.0 223.1 jit_solution(6857185329989556460)
XLA Ops:
  4.2 3.1 %collective-permute-start.1 = (bf16[48,1664]{1,0:T(8,128)(2,1)S(1)}, bf16[48,1664]{1,0:T(8,128)(2,1)S(1)}, u32[]{:S(2)}, u32[]{:S(2)}) collective-permute-start(bf16[48,1664]{1,0:T(8,128)(2,1)S(1)} %bitcast_dynamic-update-slice_fusion.refs_0_), channel_id=1, source_target_pairs={{0,8},{2,10},{4,12},{6,14},{8,0},{10,2},{12,4},{14,6},{16,24},{18,... | collective-permute-start | bytes 479240 | tf_op jit(solution)/shard_map/ppermute | solution.py:57
  7.3 2.6 %collective-permute-start.2 = (bf16[48,1664]{1,0:T(8,128)(2,1)S(1)}, bf16[48,1664]{1,0:T(8,128)(2,1)S(1)}, u32[]{:S(2)}, u32[]{:S(2)}) collective-permute-start(bf16[48,1664]{1,0:T(8,128)(2,1)S(1)} %bitcast_dynamic-update-slice_fusion.refs_0_), channel_id=1, source_target_pairs={{0,16},{2,18},{4,20},{6,22},{8,24},{10,26},{12,28},{14,30},{16,0},... | collective-permute-start | bytes 479240 | tf_op jit(solution)/shard_map/ppermute | solution.py:57
  9.9 1.7 collective-permute-start
  12.3 1.6 fusion.10
  13.9 8.1 %collective-permute-done.2.refs_2_ = bf16[48,1664]{1,0:T(8,128)(2,1)S(1)} collective-permute-done((bf16[48,1664]{1,0:T(8,128)(2,1)S(1)}, bf16[48,1664]{1,0:T(8,128)(2,1)S(1)}, u32[]{:S(2)}, u32[]{:S(2)}) %collective-permute-start.2) | collective-permute-done | bytes 159776 | tf_op jit(solution)/shard_map/ppermute | solution.py:57
  23.7 2.6 %collective-permute-start.8 = (bf16[48,3072]{1,0:T(8,128)(2,1)S(1)}, bf16[48,3072]{1,0:T(8,128)(2,1)S(1)}, u32[]{:S(2)}, u32[]{:S(2)}) collective-permute-start(bf16[48,3072]{1,0:T(8,128)(2,1)S(1)} %shard_map.325.refs_0_), channel_id=1, source_target_pairs={{0,8},{2,10},{4,12},{6,14},{8,0},{10,2},{12,4},{14,6},{16,24},{18,... | collective-permute-start | bytes 884744 | tf_op jit(solution)/shard_map/ppermute | solution.py:57
  31.0 4.7 %collective-permute-done.5.refs_3_ = bf16[192,768]{1,0:T(8,128)(2,1)S(1)} collective-permute-done((bf16[192,768]{1,0:T(8,128)(2,1)S(1)}, bf16[192,768]{1,0:T(8,128)(2,1)S(1)}, u32[]{:S(2)}, u32[]{:S(2)}) %collective-permute-start.5) | collective-permute-done | bytes 294944 | tf_op jit(solution)/shard_map/ppermute | solution.py:57
  38.0 11.8 %collective-permute-done.9.refs_2_ = bf16[48,3072]{1,0:T(8,128)(2,1)S(1)} collective-permute-done((bf16[48,3072]{1,0:T(8,128)(2,1)S(1)}, bf16[48,3072]{1,0:T(8,128)(2,1)S(1)}, u32[]{:S(2)}, u32[]{:S(2)}) %collective-permute-start.9) | collective-permute-done | bytes 294944 | tf_op jit(solution)/shard_map/ppermute | solution.py:57
  56.6 2.5 %shard_map.329 = (bf16[256,768]{1,0:T(8,128)(2,1)S(1)}, bf16[512,768]{1,0:T(8,128)(2,1)S(1)}, bf16[512,768]{1,0:T(8,128)(2,1)S(1)}) custom-call(bf16[512,768]{1,0:T(8,128)(2,1)S(1)} %pad_maximum_fusion.refs_4_.refs_0_.refs_1_.refs_2_, bf16[384,1792]{1,0:T(8,128)(2,1)S(1)} %get-tuple-element.90.refs_2_.refs_1_.refs_3_, ...), custom_call_target="tpu_custom_call" | custom-call | flops 1509949440 | bytes 7870464 | tf_op jit(solution)/shard_map/pallas_call | solution.py:141
  59.2 7.5 %collective-permute-done.13.refs_2_ = bf16[192,1536]{1,0:T(8,128)(2,1)S(1)} collective-permute-done((bf16[192,1536]{1,0:T(8,128)(2,1)S(1)}, bf16[192,1536]{1,0:T(8,128)(2,1)S(1)}, u32[]{:S(2)}, u32[]{:S(2)}) %collective-permute-start.13) | collective-permute-done | bytes 589856 | tf_op jit(solution)/shard_map/ppermute | solution.py:61
  81.3 8.0 %shard_map.331.refs_0_.refs_7_ = bf16[256,768]{1,0:T(8,128)(2,1)S(1)} custom-call(s32[1,256]{1,0:T(1,128)S(1)} %bitcast.79, s32[512,1]{1,0:T(8,128)S(1)} %copy-done.16, bf16[256,768]{1,0:T(8,128)(2,1)S(1)} %copy-done.10, bf16[512,768]{1,0:T(8,128)(2,1)S(1)} %copy-done.18, bf16[512,768]{1,0:T(8,128)(2,1)S(1)} %copy-done.21, ...), custom_call_target="tpu_custom_call" | custom-call | flops 905969664 | bytes 2362368 | tf_op jit(solution)/shard_map/pallas_call | solution.py:141
  90.2 6.4 %collective-permute-done.15.refs_2_ = bf16[384,1536]{1,0:T(8,128)(2,1)} collective-permute-done((bf16[384,1536]{1,0:T(8,128)(2,1)}, bf16[384,1536]{1,0:T(8,128)(2,1)}, u32[]{:S(2)}, u32[]{:S(2)}) %collective-permute-start.15) | collective-permute-done | bytes 1179680 | tf_op jit(solution)/shard_map/ppermute | solution.py:61
  96.9 2.7 %shard_map.333 = (bf16[384,3072]{1,0:T(8,128)(2,1)S(1)}, bf16[384,3072]{1,0:T(8,128)(2,1)S(1)}) custom-call(bf16[384,1536]{1,0:T(8,128)(2,1)} %get-tuple-element.101.refs_0_, bf16[192,3072]{1,0:T(8,128)(2,1)} %get-tuple-element.98.refs_5_.refs_1_, bf16[384,1536]{1,0:T(8,128)(2,1)} %collective-permute-done.15.refs_2_, ...), custom_call_target="tpu_custom_call" | custom-call | bytes 9437184 | tf_op jit(solution)/shard_map/pallas_call | solution.py:141
  102.1 2.1 collective-permute-done.17.refs_2_
  104.2 2.8 %shard_map.334 = (bf16[256,3072]{1,0:T(8,128)(2,1)S(1)}, f32[256,3072]{1,0:T(8,128)S(1)}) custom-call(bf16[256,768]{1,0:T(8,128)(2,1)S(1)} %get-tuple-element.100.refs_4_.refs_0_, bf16[384,3072]{1,0:T(8,128)(2,1)S(1)} %get-tuple-element.102.refs_1_, bf16[384,3072]{1,0:T(8,128)(2,1)S(1)} %collective-permute-done.17.refs_2_, ...), custom_call_target="tpu_custom_call" | custom-call | flops 2415919104 | bytes 9842688 | tf_op jit(solution)/shard_map/pallas_call | solution.py:141
  107.5 2.4 %shard_map.335 = (bf16[256,768]{1,0:T(8,128)(2,1)S(1)}, f32[256,768]{1,0:T(8,128)S(1)}, bf16[256,768]{1,0:T(8,128)(2,1)S(1)}, f32[8,768]{1,0:T(8,128)S(1)}) custom-call(bf16[256,3072]{1,0:T(8,128)(2,1)S(1)} %get-tuple-element.104.refs_0_, bf16[384,3072]{1,0:T(8,128)(2,1)S(1)} %get-tuple-element.105.refs_1_, ...), custom_call_target="tpu_custom_call" | custom-call | flops 1509949440 | bytes 9481216 | tf_op jit(solution)/shard_map/pallas_call | solution.py:141
  111.0 2.2 shard_map.336
  116.1 12.0 %shard_map.337 = (bf16[384,1536]{1,0:T(8,128)(2,1)S(1)}, bf16[384,1536]{1,0:T(8,128)(2,1)S(1)}) custom-call(bf16[384,3072]{1,0:T(8,128)(2,1)S(1)} %convolution_convert_fusion.1.refs_0_, bf16[384,3072]{1,0:T(8,128)(2,1)S(1)} %collective-permute-done.20.refs_1_, bf16[256,3072]{1,0:T(8,128)(2,1)S(1)} %get-tuple-element.110.refs_2_.refs_0_), custom_call_target="tpu_custom_call" | custom-call | flops 120795955200 | bytes 7077888 | tf_op jit(solution)/shard_map/pallas_call | solution.py:141
  128.7 1.6 collective-permute-start.21
  132.4 2.6 %shard_map.339 = (f32[256,768]{1,0:T(8,128)S(1)}, bf16[256,768]{1,0:T(8,128)(2,1)S(1)}, bf16[256,768]{1,0:T(8,128)(2,1)S(1)}, f32[8,768]{1,0:T(8,128)S(1)}) custom-call(bf16[256,3072]{1,0:T(8,128)(2,1)S(1)} %get-tuple-element.110.refs_2_.refs_0_, bf16[384,3072]{1,0:T(8,128)(2,1)S(1)} %get-tuple-element.102.refs_1_, ...), custom_call_target="tpu_custom_call" | custom-call | flops 1811939328 | bytes 11840512 | tf_op jit(solution)/shard_map/pallas_call | solution.py:141
  135.1 10.0 %shard_map.340 = (bf16[256,768]{1,0:T(8,128)(2,1)S(1)}, bf16[512,768]{1,0:T(8,128)(2,1)S(1)}, bf16[512,768]{1,0:T(8,128)(2,1)S(1)}) custom-call(s32[1,256]{1,0:T(1,128)S(1)} %bitcast.80, s32[512,1]{1,0:T(8,128)S(1)} %copy-done.16, bf16[256,768]{1,0:T(8,128)(2,1)S(1)} %copy-done.11, bf16[512,768]{1,0:T(8,128)(2,1)S(1)} %copy-done.19, ...), custom_call_target="tpu_custom_call" | custom-call | flops 1509949440 | bytes 4328448 | tf_op jit(solution)/shard_map/pallas_call | solution.py:141
  145.1 3.1 %shard_map.341 = (bf16[384,1792]{1,0:T(8,128)(2,1)S(1)}, bf16[384,1536]{1,0:T(8,128)(2,1)S(1)}, bf16[384,1792]{1,0:T(8,128)(2,1)S(1)}, bf16[384,1536]{1,0:T(8,128)(2,1)S(1)}) custom-call(s32[1]{0:T(128)} %bitcast.12.refs_0_, bf16[768,768]{1,0:T(8,128)(2,1)S(1)} %copy-done.7, bf16[512,768]{1,0:T(8,128)(2,1)S(1)} %pad_maximum_fusion.refs_4_.refs_0_.refs_1_.refs_2_, ...), custom_call_target="tpu_custom_call" | custom-call | flops 1811939328 | bytes 9891844 | tf_op jit(solution)/shard_map/pallas_call | solution.py:141
  148.7 8.1 %collective-permute-done.21.refs_1_ = bf16[192,3072]{1,0:T(8,128)(2,1)S(1)} collective-permute-done((bf16[192,3072]{1,0:T(8,128)(2,1)S(1)}, bf16[192,3072]{1,0:T(8,128)(2,1)S(1)}, u32[]{:S(2)}, u32[]{:S(2)}) %collective-permute-start.21) | collective-permute-done | bytes 1179680 | tf_op jit(solution)/shard_map/ppermute | solution.py:57
  160.6 2.6 %shard_map.343 = (f32[256,768]{1,0:T(8,128)S(1)}, bf16[256,768]{1,0:T(8,128)(2,1)S(1)}) custom-call(bf16[256,768]{1,0:T(8,128)(2,1)S(1)} %get-tuple-element.117.refs_3_.refs_0_, bf16[512,768]{1,0:T(8,128)(2,1)S(1)} %get-tuple-element.118.refs_4_.refs_1_, bf16[512,768]{1,0:T(8,128)(2,1)S(1)} %get-tuple-element.119.refs_5_.refs_2_, ...), custom_call_target="tpu_custom_call" | custom-call | flops 120795955200 | bytes 9043968 | tf_op jit(solution)/shard_map/pallas_call | solution.py:141
  166.7 8.2 %collective-permute-done.28.refs_1_ = bf16[192,1536]{1,0:T(8,128)(2,1)S(1)} collective-permute-done((bf16[192,1536]{1,0:T(8,128)(2,1)S(1)}, bf16[192,1536]{1,0:T(8,128)(2,1)S(1)}, u32[]{:S(2)}, u32[]{:S(2)}) %collective-permute-start.28) | collective-permute-done | bytes 589856 | tf_op jit(solution)/shard_map/ppermute | solution.py:61
  177.4 2.4 %collective-permute-start.32 = (bf16[48,3072]{1,0:T(8,128)(2,1)}, bf16[48,3072]{1,0:T(8,128)(2,1)}, u32[]{:S(2)}, u32[]{:S(2)}) collective-permute-start(bf16[48,3072]{1,0:T(8,128)(2,1)} %get-tuple-element.146), channel_id=1, source_target_pairs={{0,8},{2,10},{4,12},{6,14},{8,0},{10,2},{12,4},{14,6},{16,24},{18,... | collective-permute-start | bytes 884744 | tf_op jit(solution)/shard_map/ppermute | solution.py:57
  187.0 1.8 collective-permute-done.26.refs_1_
  190.4 10.6 %collective-permute-done.33.refs_2_ = bf16[48,3072]{1,0:T(8,128)(2,1)} collective-permute-done((bf16[48,3072]{1,0:T(8,128)(2,1)}, bf16[48,3072]{1,0:T(8,128)(2,1)}, u32[]{:S(2)}, u32[]{:S(2)}) %collective-permute-start.33) | collective-permute-done | bytes 294944 | tf_op jit(solution)/shard_map/ppermute | solution.py:57
  203.7 2.2 collective-permute-start.37
  205.9 3.0 %collective-permute-start.36 = (bf16[48,1664]{1,0:T(8,128)(2,1)S(1)}, bf16[48,1664]{1,0:T(8,128)(2,1)S(1)}, u32[]{:S(2)}, u32[]{:S(2)}) collective-permute-start(bf16[48,1664]{1,0:T(8,128)(2,1)S(1)} %get-tuple-element.151), channel_id=1, source_target_pairs={{0,16},{2,18},{4,20},{6,22},{8,24},{10,26},{12,28},{14,30},{16,0},... | collective-permute-start | bytes 479240 | tf_op jit(solution)/shard_map/ppermute | solution.py:57
  210.4 2.0 shard_map.349
  212.4 6.6 %collective-permute-done.36 = bf16[48,1664]{1,0:T(8,128)(2,1)S(1)} collective-permute-done((bf16[48,1664]{1,0:T(8,128)(2,1)S(1)}, bf16[48,1664]{1,0:T(8,128)(2,1)S(1)}, u32[]{:S(2)}, u32[]{:S(2)}) %collective-permute-start.36) | collective-permute-done | bytes 159776 | tf_op jit(solution)/shard_map/ppermute | solution.py:57
  (202 shorter events, 71.7 us)
Async XLA Ops:
  4.2 9.7 %collective-permute-start.1 = (bf16[48,1664]{1,0:T(8,128)(2,1)S(1)}, bf16[48,1664]{1,0:T(8,128)(2,1)S(1)}, u32[]{:S(2)}, u32[]{:S(2)}) collective-permute-start(bf16[48,1664]{1,0:T(8,128)(2,1)S(1)} %bitcast_dynamic-update-slice_fusion.refs_0_), channel_id=1, source_target_pairs={{0,8},{2,10},{4,12},{6,14},{8,0},{10,2},{12,4},{14,6},{16,24},{18,... | collective-permute-start | bytes 479240 | tf_op jit(solution)/shard_map/ppermute | solution.py:57
  7.3 14.8 %collective-permute-start.2 = (bf16[48,1664]{1,0:T(8,128)(2,1)S(1)}, bf16[48,1664]{1,0:T(8,128)(2,1)S(1)}, u32[]{:S(2)}, u32[]{:S(2)}) collective-permute-start(bf16[48,1664]{1,0:T(8,128)(2,1)S(1)} %bitcast_dynamic-update-slice_fusion.refs_0_), channel_id=1, source_target_pairs={{0,16},{2,18},{4,20},{6,22},{8,24},{10,26},{12,28},{14,30},{16,0},... | collective-permute-start | bytes 479240 | tf_op jit(solution)/shard_map/ppermute | solution.py:57
  9.9 12.2 %collective-permute-start.3 = (bf16[48,1664]{1,0:T(8,128)(2,1)S(1)}, bf16[48,1664]{1,0:T(8,128)(2,1)S(1)}, u32[]{:S(2)}, u32[]{:S(2)}) collective-permute-start(bf16[48,1664]{1,0:T(8,128)(2,1)S(1)} %bitcast_dynamic-update-slice_fusion.refs_0_), channel_id=1, source_target_pairs={{0,24},{2,26},{4,28},{6,30},{8,16},{10,18},{12,20},{14,22},{16,8},... | collective-permute-start | bytes 479240 | tf_op jit(solution)/shard_map/ppermute | solution.py:57
  9.9 18.9 %collective-permute-start = (bf16[256,768]{1,0:T(8,128)(2,1)}, bf16[256,768]{1,0:T(8,128)(2,1)S(1)}, u32[]{:S(2)}, u32[]{:S(2)}) collective-permute-start(bf16[256,768]{1,0:T(8,128)(2,1)} %param.20), channel_id=1, source_target_pairs={{0,1},{1,0},{2,3},{3,2},{4,5},{5,4},{6,7},{7,6},{8,9},{9,8},{10,11... | collective-permute-start | bytes 1179656 | tf_op jit(solution)/shard_map/ppermute | solution.py:61
  22.1 13.7 %collective-permute-start.4 = (bf16[192,896]{1,0:T(8,128)(2,1)S(1)}, bf16[192,896]{1,0:T(8,128)(2,1)S(1)}, u32[]{:S(2)}, u32[]{:S(2)}) collective-permute-start(bf16[192,896]{1,0:T(8,128)(2,1)S(1)} %get-tuple-element.85.refs_0_.refs_2_), channel_id=1, source_target_pairs={{0,1},{1,0},{2,3},{3,2},{4,5},{5,4},{6,7},{7,6},{8,9},{9,8},{10,11... | collective-permute-start | bytes 1032200 | tf_op jit(solution)/shard_map/ppermute | solution.py:61
  23.7 14.3 %collective-permute-start.8 = (bf16[48,3072]{1,0:T(8,128)(2,1)S(1)}, bf16[48,3072]{1,0:T(8,128)(2,1)S(1)}, u32[]{:S(2)}, u32[]{:S(2)}) collective-permute-start(bf16[48,3072]{1,0:T(8,128)(2,1)S(1)} %shard_map.325.refs_0_), channel_id=1, source_target_pairs={{0,8},{2,10},{4,12},{6,14},{8,0},{10,2},{12,4},{14,6},{16,24},{18,... | collective-permute-start | bytes 884744 | tf_op jit(solution)/shard_map/ppermute | solution.py:57
  26.3 23.5 %collective-permute-start.9 = (bf16[48,3072]{1,0:T(8,128)(2,1)S(1)}, bf16[48,3072]{1,0:T(8,128)(2,1)S(1)}, u32[]{:S(2)}, u32[]{:S(2)}) collective-permute-start(bf16[48,3072]{1,0:T(8,128)(2,1)S(1)} %shard_map.325.refs_0_), channel_id=1, source_target_pairs={{0,16},{2,18},{4,20},{6,22},{8,24},{10,26},{12,28},{14,30},{16,0},... | collective-permute-start | bytes 884744 | tf_op jit(solution)/shard_map/ppermute | solution.py:57
  27.4 22.4 %collective-permute-start.10 = (bf16[48,3072]{1,0:T(8,128)(2,1)S(1)}, bf16[48,3072]{1,0:T(8,128)(2,1)S(1)}, u32[]{:S(2)}, u32[]{:S(2)}) collective-permute-start(bf16[48,3072]{1,0:T(8,128)(2,1)S(1)} %shard_map.325.refs_0_), channel_id=1, source_target_pairs={{0,24},{2,26},{4,28},{6,30},{8,16},{10,18},{12,20},{14,22},{16,8},... | collective-permute-start | bytes 884744 | tf_op jit(solution)/shard_map/ppermute | solution.py:57
  35.9 14.0 %collective-permute-start.6 = (bf16[384,768]{1,0:T(8,128)(2,1)S(1)}, bf16[384,768]{1,0:T(8,128)(2,1)S(1)}, u32[]{:S(2)}, u32[]{:S(2)}) collective-permute-start(bf16[384,768]{1,0:T(8,128)(2,1)S(1)} %get-tuple-element.87.refs_0_), channel_id=1, source_target_pairs={{0,1},{1,0},{2,3},{3,2},{4,5},{5,4},{6,7},{7,6},{8,9},{9,8},{10,11... | collective-permute-start | bytes 1769480 | tf_op jit(solution)/shard_map/ppermute | solution.py:61
  36.5 14.2 %collective-permute-start.7 = (bf16[192,1792]{1,0:T(8,128)(2,1)S(1)}, bf16[192,1792]{1,0:T(8,128)(2,1)S(1)}, u32[]{:S(2)}, u32[]{:S(2)}) collective-permute-start(bf16[192,1792]{1,0:T(8,128)(2,1)S(1)} %get-tuple-element.88.refs_1_), channel_id=1, source_target_pairs={{0,4},{2,6},{4,0},{6,2},{8,12},{10,14},{12,8},{14,10},{16,20},{18,... | collective-permute-start | bytes 2064392 | tf_op jit(solution)/shard_map/ppermute | solution.py:57
  51.4 15.3 %collective-permute-start.13 = (bf16[192,1536]{1,0:T(8,128)(2,1)S(1)}, bf16[192,1536]{1,0:T(8,128)(2,1)S(1)}, u32[]{:S(2)}, u32[]{:S(2)}) collective-permute-start(bf16[192,1536]{1,0:T(8,128)(2,1)S(1)} %get-tuple-element.89.refs_4_.refs_0_), channel_id=1, source_target_pairs={{0,1},{1,0},{2,3},{3,2},{4,5},{5,4},{6,7},{7,6},{8,9},{9,8},{10,11... | collective-permute-start | bytes 1769480 | tf_op jit(solution)/shard_map/ppermute | solution.py:61
  52.9 15.0 %collective-permute-start.14 = (bf16[192,1536]{1,0:T(8,128)(2,1)S(1)}, bf16[192,1536]{1,0:T(8,128)(2,1)S(1)}, u32[]{:S(2)}, u32[]{:S(2)}) collective-permute-start(bf16[192,1536]{1,0:T(8,128)(2,1)S(1)} %get-tuple-element.97.refs_1_), channel_id=1, source_target_pairs={{0,4},{2,6},{4,0},{6,2},{8,12},{10,14},{12,8},{14,10},{16,20},{18,... | collective-permute-start | bytes 1769480 | tf_op jit(solution)/shard_map/ppermute | solution.py:57
  69.5 27.1 %collective-permute-start.15 = (bf16[384,1536]{1,0:T(8,128)(2,1)}, bf16[384,1536]{1,0:T(8,128)(2,1)}, u32[]{:S(2)}, u32[]{:S(2)}) collective-permute-start(bf16[384,1536]{1,0:T(8,128)(2,1)} %get-tuple-element.101.refs_0_), channel_id=1, source_target_pairs={{0,1},{1,0},{2,3},{3,2},{4,5},{5,4},{6,7},{7,6},{8,9},{9,8},{10,11... | collective-permute-start | bytes 3538952 | tf_op jit(solution)/shard_map/ppermute | solution.py:61
  70.0 26.9 %collective-permute-start.16 = (bf16[192,3072]{1,0:T(8,128)(2,1)}, bf16[192,3072]{1,0:T(8,128)(2,1)}, u32[]{:S(2)}, u32[]{:S(2)}) collective-permute-start(bf16[192,3072]{1,0:T(8,128)(2,1)} %get-tuple-element.98.refs_5_.refs_1_), channel_id=1, source_target_pairs={{0,4},{2,6},{4,0},{6,2},{8,12},{10,14},{12,8},{14,10},{16,20},{18,... | collective-permute-start | bytes 3538952 | tf_op jit(solution)/shard_map/ppermute | solution.py:57
  114.0 14.1 %collective-permute-start.19 = (bf16[384,3072]{1,0:T(8,128)(2,1)S(1)}, bf16[384,3072]{1,0:T(8,128)(2,1)S(1)}, u32[]{:S(2)}, u32[]{:S(2)}) collective-permute-start(bf16[384,3072]{1,0:T(8,128)(2,1)S(1)} %convolution_convert_fusion.2), channel_id=1, source_target_pairs={{0,2},{2,0},{4,6},{6,4},{8,10},{10,8},{12,14},{14,12},{16,18},{18,... | collective-permute-start | bytes 7077896 | tf_op jit(solution)/shard_map/ppermute | solution.py:57
  128.7 28.1 %collective-permute-start.21 = (bf16[192,3072]{1,0:T(8,128)(2,1)S(1)}, bf16[192,3072]{1,0:T(8,128)(2,1)S(1)}, u32[]{:S(2)}, u32[]{:S(2)}) collective-permute-start(bf16[192,3072]{1,0:T(8,128)(2,1)S(1)} %get-tuple-element.121), channel_id=1, source_target_pairs={{0,4},{2,6},{4,0},{6,2},{8,12},{10,14},{12,8},{14,10},{16,20},{18,... | collective-permute-start | bytes 3538952 | tf_op jit(solution)/shard_map/ppermute | solution.py:57
  130.3 27.7 %collective-permute-start.22 = (bf16[384,1536]{1,0:T(8,128)(2,1)S(1)}, bf16[384,1536]{1,0:T(8,128)(2,1)S(1)}, u32[]{:S(2)}, u32[]{:S(2)}) collective-permute-start(bf16[384,1536]{1,0:T(8,128)(2,1)S(1)} %get-tuple-element.122), channel_id=1, source_target_pairs={{0,1},{1,0},{2,3},{3,2},{4,5},{5,4},{6,7},{7,6},{8,9},{9,8},{10,11... | collective-permute-start | bytes 3538952 | tf_op jit(solution)/shard_map/ppermute | solution.py:61
  148.1 15.2 %collective-permute-start.24 = (bf16[384,1792]{1,0:T(8,128)(2,1)S(1)}, bf16[384,1792]{1,0:T(8,128)(2,1)S(1)}, u32[]{:S(2)}, u32[]{:S(2)}) collective-permute-start(bf16[384,1792]{1,0:T(8,128)(2,1)S(1)} %get-tuple-element.131), channel_id=1, source_target_pairs={{0,2},{2,0},{4,6},{6,4},{8,10},{10,8},{12,14},{14,12},{16,18},{18,... | collective-permute-start | bytes 4128776 | tf_op jit(solution)/shard_map/ppermute | solution.py:57
  148.2 15.1 %collective-permute-start.25 = (bf16[384,1536]{1,0:T(8,128)(2,1)S(1)}, bf16[384,1536]{1,0:T(8,128)(2,1)S(1)}, u32[]{:S(2)}, u32[]{:S(2)}) collective-permute-start(bf16[384,1536]{1,0:T(8,128)(2,1)S(1)} %get-tuple-element.133), channel_id=1, source_target_pairs={{0,2},{2,0},{4,6},{6,4},{8,10},{10,8},{12,14},{14,12},{16,18},{18,... | collective-permute-start | bytes 3538952 | tf_op jit(solution)/shard_map/ppermute | solution.py:57
  158.6 16.3 %collective-permute-start.28 = (bf16[192,1536]{1,0:T(8,128)(2,1)S(1)}, bf16[192,1536]{1,0:T(8,128)(2,1)S(1)}, u32[]{:S(2)}, u32[]{:S(2)}) collective-permute-start(bf16[192,1536]{1,0:T(8,128)(2,1)S(1)} %get-tuple-element.138), channel_id=1, source_target_pairs={{0,1},{1,0},{2,3},{3,2},{4,5},{5,4},{6,7},{7,6},{8,9},{9,8},{10,11... | collective-permute-start | bytes 1769480 | tf_op jit(solution)/shard_map/ppermute | solution.py:61
  160.1 16.3 %collective-permute-start.29 = (bf16[192,1536]{1,0:T(8,128)(2,1)S(1)}, bf16[192,1536]{1,0:T(8,128)(2,1)S(1)}, u32[]{:S(2)}, u32[]{:S(2)}) collective-permute-start(bf16[192,1536]{1,0:T(8,128)(2,1)S(1)} %get-tuple-element.140), channel_id=1, source_target_pairs={{0,4},{2,6},{4,0},{6,2},{8,12},{10,14},{12,8},{14,10},{16,20},{18,... | collective-permute-start | bytes 1769480 | tf_op jit(solution)/shard_map/ppermute | solution.py:57
  164.6 24.2 %collective-permute-start.26 = (bf16[192,1792]{1,0:T(8,128)(2,1)S(1)}, bf16[192,1792]{1,0:T(8,128)(2,1)S(1)}, u32[]{:S(2)}, u32[]{:S(2)}) collective-permute-start(bf16[192,1792]{1,0:T(8,128)(2,1)S(1)} %get-tuple-element.135), channel_id=1, source_target_pairs={{0,4},{2,6},{4,0},{6,2},{8,12},{10,14},{12,8},{14,10},{16,20},{18,... | collective-permute-start | bytes 2064392 | tf_op jit(solution)/shard_map/ppermute | solution.py:57
  166.1 19.4 %collective-permute-start.27 = (bf16[384,768]{1,0:T(8,128)(2,1)}, bf16[384,768]{1,0:T(8,128)(2,1)S(1)}, u32[]{:S(2)}, u32[]{:S(2)}) collective-permute-start(bf16[384,768]{1,0:T(8,128)(2,1)} %get-tuple-element.137), channel_id=1, source_target_pairs={{0,1},{1,0},{2,3},{3,2},{4,5},{5,4},{6,7},{7,6},{8,9},{9,8},{10,11... | collective-permute-start | bytes 1769480 | tf_op jit(solution)/shard_map/ppermute | solution.py:61
  177.4 12.3 %collective-permute-start.32 = (bf16[48,3072]{1,0:T(8,128)(2,1)}, bf16[48,3072]{1,0:T(8,128)(2,1)}, u32[]{:S(2)}, u32[]{:S(2)}) collective-permute-start(bf16[48,3072]{1,0:T(8,128)(2,1)} %get-tuple-element.146), channel_id=1, source_target_pairs={{0,8},{2,10},{4,12},{6,14},{8,0},{10,2},{12,4},{14,6},{16,24},{18,... | collective-permute-start | bytes 884744 | tf_op jit(solution)/shard_map/ppermute | solution.py:57
  179.8 21.2 %collective-permute-start.33 = (bf16[48,3072]{1,0:T(8,128)(2,1)}, bf16[48,3072]{1,0:T(8,128)(2,1)}, u32[]{:S(2)}, u32[]{:S(2)}) collective-permute-start(bf16[48,3072]{1,0:T(8,128)(2,1)} %get-tuple-element.147), channel_id=1, source_target_pairs={{0,16},{2,18},{4,20},{6,22},{8,24},{10,26},{12,28},{14,30},{16,0},... | collective-permute-start | bytes 884744 | tf_op jit(solution)/shard_map/ppermute | solution.py:57
  181.1 20.0 %collective-permute-start.34 = (bf16[48,3072]{1,0:T(8,128)(2,1)}, bf16[48,3072]{1,0:T(8,128)(2,1)}, u32[]{:S(2)}, u32[]{:S(2)}) collective-permute-start(bf16[48,3072]{1,0:T(8,128)(2,1)} %get-tuple-element.148), channel_id=1, source_target_pairs={{0,24},{2,26},{4,28},{6,30},{8,16},{10,18},{12,20},{14,22},{16,8},... | collective-permute-start | bytes 884744 | tf_op jit(solution)/shard_map/ppermute | solution.py:57
  185.5 24.8 %collective-permute-start.23 = (bf16[256,768]{1,0:T(8,128)(2,1)}, bf16[256,768]{1,0:T(8,128)(2,1)S(1)}, u32[]{:S(2)}, u32[]{:S(2)}) collective-permute-start(bf16[256,768]{1,0:T(8,128)(2,1)} %copy-done.28), channel_id=1, source_target_pairs={{0,1},{1,0},{2,3},{3,2},{4,5},{5,4},{6,7},{7,6},{8,9},{9,8},{10,11... | collective-permute-start | bytes 1179656 | tf_op jit(solution)/shard_map/ppermute | solution.py:61
  189.1 14.4 %collective-permute-start.30 = (bf16[192,896]{1,0:T(8,128)(2,1)S(1)}, bf16[192,896]{1,0:T(8,128)(2,1)S(1)}, u32[]{:S(2)}, u32[]{:S(2)}) collective-permute-start(bf16[192,896]{1,0:T(8,128)(2,1)S(1)} %get-tuple-element.143), channel_id=1, source_target_pairs={{0,1},{1,0},{2,3},{3,2},{4,5},{5,4},{6,7},{7,6},{8,9},{9,8},{10,11... | collective-permute-start | bytes 1032200 | tf_op jit(solution)/shard_map/ppermute | solution.py:61
  189.8 13.7 %collective-permute-start.31 = (bf16[192,768]{1,0:T(8,128)(2,1)S(1)}, bf16[192,768]{1,0:T(8,128)(2,1)S(1)}, u32[]{:S(2)}, u32[]{:S(2)}) collective-permute-start(bf16[192,768]{1,0:T(8,128)(2,1)S(1)} %get-tuple-element.145), channel_id=1, source_target_pairs={{0,4},{2,6},{4,0},{6,2},{8,12},{10,14},{12,8},{14,10},{16,20},{18,... | collective-permute-start | bytes 884744 | tf_op jit(solution)/shard_map/ppermute | solution.py:57
  203.7 8.8 %collective-permute-start.37 = (bf16[48,1664]{1,0:T(8,128)(2,1)S(1)}, bf16[48,1664]{1,0:T(8,128)(2,1)S(1)}, u32[]{:S(2)}, u32[]{:S(2)}) collective-permute-start(bf16[48,1664]{1,0:T(8,128)(2,1)S(1)} %get-tuple-element.152), channel_id=1, source_target_pairs={{0,24},{2,26},{4,28},{6,30},{8,16},{10,18},{12,20},{14,22},{16,8},... | collective-permute-start | bytes 479240 | tf_op jit(solution)/shard_map/ppermute | solution.py:57
  205.9 13.2 %collective-permute-start.36 = (bf16[48,1664]{1,0:T(8,128)(2,1)S(1)}, bf16[48,1664]{1,0:T(8,128)(2,1)S(1)}, u32[]{:S(2)}, u32[]{:S(2)}) collective-permute-start(bf16[48,1664]{1,0:T(8,128)(2,1)S(1)} %get-tuple-element.151), channel_id=1, source_target_pairs={{0,16},{2,18},{4,20},{6,22},{8,24},{10,26},{12,28},{14,30},{16,0},... | collective-permute-start | bytes 479240 | tf_op jit(solution)/shard_map/ppermute | solution.py:57
  208.9 10.2 %collective-permute-start.35 = (bf16[48,1664]{1,0:T(8,128)(2,1)S(1)}, bf16[48,1664]{1,0:T(8,128)(2,1)S(1)}, u32[]{:S(2)}, u32[]{:S(2)}) collective-permute-start(bf16[48,1664]{1,0:T(8,128)(2,1)S(1)} %get-tuple-element.150), channel_id=1, source_target_pairs={{0,8},{2,10},{4,12},{6,14},{8,0},{10,2},{12,4},{14,6},{16,24},{18,... | collective-permute-start | bytes 479240 | tf_op jit(solution)/shard_map/ppermute | solution.py:57
  (50 other events, 415.6 us)

commit v4 on v3

--- a/solution.py
+++ b/solution.py
@@ -150,6 +150,18 @@
         ),
         cost_estimate=pl.CostEstimate(flops=flops, bytes_accessed=size, transcendentals=0),
     )(*operands, *after)
+
+
+def gate(values, after):
+    anywhere = pl.BlockSpec(memory_space=pl.ANY)
+    return pl.pallas_call(
+        lambda *refs: None,
+        out_shape=[shape_of(*value.shape, value.dtype) for value in values],
+        in_specs=[anywhere] * (len(values) + len(after)),
+        out_specs=[anywhere] * len(values),
+        input_output_aliases={place: place for place in range(len(values))},
+        cost_estimate=pl.CostEstimate(flops=0, bytes_accessed=0, transcendentals=0),
+    )(*values, *after)
 
 
 def join_high_kernel(count, *refs):
@@ -421,21 +433,32 @@
     y_low[...] = y_new.astype(LOW)
 
 
-def hidden_kernel(y_low, own, far, bias, activation, slope):
-    half = own.shape[0]
-    low, high = y_low[:, :half], y_low[:, half:]
-    columns = own.shape[1]
+def stacked(pieces, at=slice(None)):
+    return jnp.concatenate([piece[:, at] for piece in pieces], axis=0)
+
+
+def hidden_kernel(y_low, *refs):
+    pieces, (bias, activation, slope) = refs[:4], refs[4:]
+    rows = y_low[...]
+    columns = pieces[0].shape[1]
     step = columns // 8
     for start in range(0, columns, step):
         at = slice(start, start + step)
-        pre = dot(low, own[:, at]) + dot(high, far[:, at]) + bias[:, at]
+        pre = dot(rows, stacked(pieces, at)) + bias[:, at]
         cdf = 0.5 + 0.5 * lax.erf(pre * (0.5**0.5))
         activation[:, at] = (pre * cdf).astype(LOW)
         slope[:, at] = cdf + pre * jnp.exp(-0.5 * pre * pre) * ((2.0 * np.pi) ** -0.5)
 
 
-def out_back_kernel(activation, own, far, y, cot, valid, vec, mixed, grad, grad_low, sums):
-    out = [dot_nt(activation[...], weights[...]) for weights in (own, far)]
+def out_back_kernel(
+    activation, own, own_side, far, far_side, y, cot, valid, vec, mixed, grad, grad_low, sums
+):
+    columns = own.shape[1]
+    near, side = activation[:, :columns], activation[:, columns:]
+    out = [
+        dot_nt(near, first[...]) + dot_nt(side, second[...])
+        for first, second in ((own, own_side), (far, far_side))
+    ]
     total = y[...] + jnp.concatenate(out, axis=1) + vec[3:4]
     result, normed, inv_std = normalize_fwd(total, vec[4:5], vec[5:6])
     mixed[...] = result.astype(LOW)
@@ -449,22 +472,26 @@
     sums[2:3] = shift_sum[None]
 
 
-def hidden_back_kernel(grad_low, own, far, slope, grad_pre, sums):
-    half = own.shape[0]
-    low, high = grad_low[:, :half], grad_low[:, half:]
+def hidden_back_kernel(grad_low, own, own_side, far, far_side, slope, grad_pre, sums):
+    rows = grad_low[...]
     columns = own.shape[1]
-    step = columns // 8
-    for start in range(0, columns, step):
-        at = slice(start, start + step)
-        value = ((dot(low, own[:, at]) + dot(high, far[:, at])) * slope[:, at]).astype(LOW)
-        grad_pre[:, at] = value
-        sums[:, at] = jnp.sum(value.astype(F32), axis=0, keepdims=True)
+    step = columns // 4
+    for place, pieces in enumerate(((own, far), (own_side, far_side))):
+        for start in range(0, columns, step):
+            to = slice(place * columns + start, place * columns + start + step)
+            grad_act = dot(rows, stacked(pieces, slice(start, start + step)))
+            value = (grad_act * slope[:, to]).astype(LOW)
+            grad_pre[:, to] = value
+            sums[:, to] = jnp.sum(value.astype(F32), axis=0, keepdims=True)
 
 
 def norm_back_kernel(
-    grad_pre, own, far, grad_two, normed, inv, vec, o_own, o_far, grad, grad_low, grad_attn, sums
+    grad_pre, own, own_side, far, far_side, grad_two, normed, inv, vec, o_own, o_far,
+    grad, grad_low, grad_attn, sums,
 ):
-    out = [dot_nt(grad_pre[...], weights[...]) for weights in (own, far)]
+    out = [
+        dot_nt(grad_pre[...], stacked(pieces)) for pieces in ((own, own_side), (far, far_side))
+    ]
     grad_in, gain_sum, shift_sum = normalize_back(
         grad_two[...] + jnp.concatenate(out, axis=1), normed[...], inv[...], vec[1:2]
     )
@@ -539,6 +566,43 @@
             base = side * 2 * part
             to_b[:, base : base + part] = dot_tn(both, grad_v[:, cols]).astype(LOW)
             to_b[:, base + part : base + 2 * part] = dot_tn(low, attended[:, cols]).astype(LOW)
+
+
+def close_kernel(rates, rank_ref, *refs):
+    inputs, parts = refs[:9], refs[9:-10]
+    outs, turned = refs[-10:-1], refs[-1]
+    total = parts[0][...].astype(F32)
+    for part in parts[1:]:
+        total = total + part[...].astype(F32)
+    columns = outs[3].shape[1]
+    count, shard_width = outs[6].shape
+    a_width = 2 * columns + LANES
+    for place, start in enumerate((0, columns, a_width)):
+        values = adamw(
+            *[ref[place] for ref in inputs[:3]],
+            total[:, start : start + columns],
+            rates[0],
+            WEIGHT_DECAY,
+        )
+        for out, value in zip(outs[:3], values):
+            out[place] = value
+    values = adamw(
+        *[ref[...] for ref in inputs[3:6]],
+        total[:, a_width + columns :],
+        rates[1],
+        WEIGHT_DECAY,
+    )
+    for out, value in zip(outs[3:6], values):
+        out[...] = value
+    lanes = total[:, 2 * columns : a_width]
+    turned[...] = jnp.zeros_like(turned)
+    turned[:shard_width, :] = flip(
+        rank_ref[0], lanes[:shard_width], lanes[shard_width : 2 * shard_width]
+    )
+    gradient = jnp.transpose(turned[...])[:count, :shard_width]
+    values = adamw(*[ref[...] for ref in inputs[6:]], gradient, 0.1, 0.0)
+    for out, value in zip(outs[6:], values):
+        out[...] = value
 
 
 def on_device(
@@ -657,7 +721,9 @@
         5 * unit,
     )
     pair = join_plane(*pair, *pair_far, after=[queries])
-    pair_far = swap_dp(pair[0], 2), swap_tensor(pair[1])
+    in_near, in_side = pair[0], swap_dp(pair[0], 2)
+    back_near, back_side = pair[1], swap_tensor(pair[1])
+    in_far, back_far = swap_dp(in_near, 1), swap_dp(back_near, 1)
     pairs = width // LANES
     own_block = pl.BlockSpec((own_rows, LANES), lambda i: (0, i))
     all_block = pl.BlockSpec((group_rows, LANES), lambda i: (0, i))
@@ -680,20 +746,21 @@
         [wide, wide_low, wide, shape_of(own_rows, 1, F32)],
         [attended, rows_all, b_own, b_far, vec],
         2 * unit,
-    )
-    pair = join_plane(pair[1], pair[0], pair_far[1], pair_far[0], after=[first_low])[::-1]
-    c_own, d_own = pair
-    c_far, d_far = swap_dp(c_own, 1), swap_dp(d_own, 1)
+        after=[in_far, back_far],
+    )
+    in_side, back_side = gate([in_side, back_side], [first_low])
+    pieces_in = [in_near, in_side, in_far, swap_dp(in_side, 1)]
+    pieces_back = [back_near, back_side, back_far, swap_dp(back_side, 1)]
     activation, slope = run(
         hidden_kernel,
         [shape_of(own_rows, full_inner, LOW), shape_of(own_rows, full_inner, F32)],
-        [first_low, c_own, c_far, bias_inner],
+        [first_low, *pieces_in, bias_inner],
         8 * unit,
     )
     mixed_rel, grad_two, grad_two_low, sums_two = run(
         out_back_kernel,
         [wide_low, wide, wide_low, sums_shape],
-        [activation, d_own, d_far, first_norm, cot, valid, vec],
+        [activation, *pieces_back, first_norm, cot, valid, vec],
         5 * unit,
     )
     mixed = dot_nt(mixed_rel, permute).astype(LOW)
@@ -706,7 +773,7 @@
     grad_pre, sums_inner = run(
         hidden_back_kernel,
         [shape_of(own_rows, full_inner, LOW), shape_of(1, full_inner, F32)],
-        [grad_two_low, d_own, d_far, slope],
+        [grad_two_low, *pieces_back, slope],
         6 * unit,
     )
     inner = weight_grad(first_low, grad_pre)
@@ -716,7 +783,7 @@
     grad_one, grad_one_low, grad_attn, sums_one = run(
         norm_back_kernel,
         [wide, wide_low, wide_low, sums_shape],
-        [grad_pre, c_own, c_far, grad_two, normed_one, inv_one, vec, b_own, b_far],
+        [grad_pre, *pieces_in, grad_two, normed_one, inv_one, vec, b_own, b_far],
         6 * unit,
         after=[a_keep],
     )
@@ -766,33 +833,31 @@
     )[0]
     sum_pair = reduce_rest(pair[0])
     summed_in, summed_back = sum_pair[:, :hidden_half], sum_pair[:, hidden_half:].T
-    sum_one = reduce_rest(sum(part.astype(F32) for part in one))
-
-    summed_vectors = lax.dynamic_slice_in_dim(
-        sum_one[:, 2 * part : a_width], tensor_rank * shard_width, shard_width, axis=0
-    )[:, :count].T
-    summed_qkv = jnp.stack(
-        [
-            sum_one[:, :part],
-            sum_one[:, part : 2 * part],
-            sum_one[:, a_width : a_width + part],
-        ]
-    )
-    summed_out = sum_one[:, a_width + part :].T
-    new_qkv, moment_qkv, square_qkv = adamw(
-        w_qkv, m_qkv, v_qkv, summed_qkv, float(width) ** (-0.5), WEIGHT_DECAY
-    )
-    new_out, moment_out, square_out = adamw(
-        w_out, m_out, v_out, summed_out, (4.0 * width / group_rows) ** (-0.5), WEIGHT_DECAY
-    )
+    if len(high_groups()) > 1:
+        one = [reduce_rest(sum(piece.astype(F32) for piece in one))]
+    qkv_shape = jax.ShapeDtypeStruct(w_qkv.shape, F32)
+    out_shape = shape_of(shard_rows, part, F32)
+    vec_shape = shape_of(count, shard_width, F32)
+    done = run(
+        functools.partial(
+            close_kernel,
+            (float(width) ** (-0.5), (4.0 * width / group_rows) ** (-0.5)),
+        ),
+        [qkv_shape] * 3 + [out_shape] * 3 + [vec_shape] * 3,
+        [rank, w_qkv, m_qkv, v_qkv, w_out.T, m_out.T, v_out.T]
+        + [vectors, m_vectors, v_vectors, *one],
+        unit,
+        in_specs=[scalar] + [vmem] * (9 + len(one)),
+        scratch=[pltpu.VMEM((LANES, LANES), F32)],
+    )
+    new_qkv, moment_qkv, square_qkv = done[:3]
+    new_out, moment_out, square_out = [value.T for value in done[3:6]]
+    new_vectors, moment_vectors, square_vectors = done[6:]
     new_in, moment_in, square_in = adamw(
         w_in, m_in, v_in, summed_in, float(width) ** (-0.5), WEIGHT_DECAY
     )
     new_back, moment_back, square_back = adamw(
         w_back, m_back, v_back, summed_back, float(full_inner) ** (-0.5), WEIGHT_DECAY
-    )
-    new_vectors, moment_vectors, square_vectors = adamw(
-        vectors, m_vectors, v_vectors, summed_vectors, 0.1, 0.0
     )
     return (
         mixed,

time: 225 us -> 223 us (level)
  starting transfers between devices: 45.6 us -> 41.4 us
  Pallas kernels: 62.3 us -> 65.5 us
  other arithmetic: 11.1 us -> 8.72 us
    ppermute x28 -> x30, waiting for transfers between devices: 58.3 us -> 51.8 us  [swap_dp(): return lax.ppermute(values, 'dp', [(i, i ^ mask) for i in range(size)])]
    ppermute x10, waiting for transfers between devices: 24.2 us -> 30.5 us  [swap_tensor(): return lax.ppermute(values, 'tensor', [(0, 1), (1, 0)])]
    ppermute x28 -> x30, starting transfers between devices: 34.1 us -> 30.1 us  [swap_dp(): return lax.ppermute(values, 'dp', [(i, i ^ mask) for i in range(size)])]
    pallas_call x27, Pallas kernels: 62.3 us -> 65.5 us  [run(): pl.pallas_call(body, grid=grid, out_shape=list(outs), in_specs=list(in_sp...]
    unnamed x97 -> x114, local copies, waits for them, and re-layouts: 11.2 us -> 10.2 us
  transfers between devices with their start and end apart: 38 -> 40, of which waited for: 18 -> 19; matrix products, arithmetic and copies ran while one was open for 8% -> 7% of each run, Pallas kernels for 25% -> 26%
where the time goes in v4:
time: 223 us; the launch traced here: 220 us
  waiting for transfers between devices  82.4 us (37%)
  Pallas kernels  65.5 us (29%)
  starting transfers between devices  41.4 us (19%)
  local copies, waits for them, and re-layouts  12.9 us (6%)
  other arithmetic  8.72 us (4%)
  matrix products  7.42 us (3%)
    pallas_call x27, Pallas kernels, run(): pl.pallas_call(body, grid=grid, out_shape=list(outs), in_specs=list(in_sp...  65.5 us
    ppermute x30, waiting for transfers between devices, swap_dp(): return lax.ppermute(values, 'dp', [(i, i ^ mask) for i in range(size)])  51.8 us
    ppermute x10, waiting for transfers between devices, swap_tensor(): return lax.ppermute(values, 'tensor', [(0, 1), (1, 0)])  30.5 us
    ppermute x30, starting transfers between devices, swap_dp(): return lax.ppermute(values, 'dp', [(i, i ^ mask) for i in range(size)])  30.1 us
    ppermute x10, starting transfers between devices, swap_tensor(): return lax.ppermute(values, 'tensor', [(0, 1), (1, 0)])  11.3 us
    unnamed x114, local copies, waits for them, and re-layouts  10.2 us
  transfers between devices with their start and end apart: 40, of which 19 were waited for; matrix products, arithmetic and copies ran while one was open for 7% of the time, Pallas kernels for 26%

profile of v4, /device:TPU:0, one launch (start us, length us, event | category | flops | bytes accessed | tf_op | source)
XLA Modules:
  0.0 220.1 jit_solution(283060559840000381)
XLA Ops:
  3.6 5.1 %collective-permute-start.3 = (bf16[48,1664]{1,0:T(8,128)(2,1)S(1)}, bf16[48,1664]{1,0:T(8,128)(2,1)S(1)}, u32[]{:S(2)}, u32[]{:S(2)}) collective-permute-start(bf16[48,1664]{1,0:T(8,128)(2,1)S(1)} %convert_dynamic-update-slice_fusion.refs_0_), channel_id=1, source_target_pairs={{0,24},{2,26},{4,28},{6,30},{8,16},{10,18},{12,20},{14,22},{16,8},... | collective-permute-start | bytes 479240 | tf_op jit(solution)/shard_map/ppermute | solution.py:57
  9.4 1.6 collective-permute-start
  13.8 8.5 %collective-permute-done.2.refs_2_ = bf16[48,1664]{1,0:T(8,128)(2,1)S(1)} collective-permute-done((bf16[48,1664]{1,0:T(8,128)(2,1)S(1)}, bf16[48,1664]{1,0:T(8,128)(2,1)S(1)}, u32[]{:S(2)}, u32[]{:S(2)}) %collective-permute-start.2) | collective-permute-done | bytes 159776 | tf_op jit(solution)/shard_map/ppermute | solution.py:57
  22.4 2.6 %collective-permute-start.10 = (bf16[48,3072]{1,0:T(8,128)(2,1)S(1)}, bf16[48,3072]{1,0:T(8,128)(2,1)S(1)}, u32[]{:S(2)}, u32[]{:S(2)}) collective-permute-start(bf16[48,3072]{1,0:T(8,128)(2,1)S(1)} %shard_map.325.refs_0_), channel_id=1, source_target_pairs={{0,24},{2,26},{4,28},{6,30},{8,16},{10,18},{12,20},{14,22},{16,8},... | collective-permute-start | bytes 884744 | tf_op jit(solution)/shard_map/ppermute | solution.py:57
  25.0 1.9 collective-permute-start.8
  30.5 4.7 %collective-permute-done.5.refs_3_ = bf16[192,768]{1,0:T(8,128)(2,1)S(1)} collective-permute-done((bf16[192,768]{1,0:T(8,128)(2,1)S(1)}, bf16[192,768]{1,0:T(8,128)(2,1)S(1)}, u32[]{:S(2)}, u32[]{:S(2)}) %collective-permute-start.5) | collective-permute-done | bytes 294944 | tf_op jit(solution)/shard_map/ppermute | solution.py:57
  38.3 10.1 %collective-permute-done.9.refs_2_ = bf16[48,3072]{1,0:T(8,128)(2,1)S(1)} collective-permute-done((bf16[48,3072]{1,0:T(8,128)(2,1)S(1)}, bf16[48,3072]{1,0:T(8,128)(2,1)S(1)}, u32[]{:S(2)}, u32[]{:S(2)}) %collective-permute-start.9) | collective-permute-done | bytes 294944 | tf_op jit(solution)/shard_map/ppermute | solution.py:57
  48.5 2.7 %collective-permute-done.7.refs_3_ = bf16[192,1792]{1,0:T(8,128)(2,1)S(1)} collective-permute-done((bf16[192,1792]{1,0:T(8,128)(2,1)S(1)}, bf16[192,1792]{1,0:T(8,128)(2,1)S(1)}, u32[]{:S(2)}, u32[]{:S(2)}) %collective-permute-start.7) | collective-permute-done | bytes 688160 | tf_op jit(solution)/shard_map/ppermute | solution.py:57
  56.3 2.5 %shard_map.329 = (bf16[256,768]{1,0:T(8,128)(2,1)S(1)}, bf16[512,768]{1,0:T(8,128)(2,1)S(1)}, bf16[512,768]{1,0:T(8,128)(2,1)S(1)}) custom-call(bf16[512,768]{1,0:T(8,128)(2,1)S(1)} %pad_maximum_fusion.refs_4_.refs_0_.refs_1_.refs_2_, bf16[384,1792]{1,0:T(8,128)(2,1)S(1)} %get-tuple-element.99.refs_2_.refs_1_.refs_3_, ...), custom_call_target="tpu_custom_call" | custom-call | flops 1509949440 | bytes 7870464 | tf_op jit(solution)/shard_map/pallas_call | solution.py:141
  58.9 8.4 %collective-permute-done.14.refs_3_ = bf16[192,1536]{1,0:T(8,128)(2,1)S(1)} collective-permute-done((bf16[192,1536]{1,0:T(8,128)(2,1)S(1)}, bf16[192,1536]{1,0:T(8,128)(2,1)S(1)}, u32[]{:S(2)}, u32[]{:S(2)}) %collective-permute-start.14) | collective-permute-done | bytes 589856 | tf_op jit(solution)/shard_map/ppermute | solution.py:57
  80.2 8.0 %shard_map.331.refs_0_.refs_7_ = bf16[256,768]{1,0:T(8,128)(2,1)S(1)} custom-call(s32[1,256]{1,0:T(1,128)S(1)} %bitcast.65, s32[512,1]{1,0:T(8,128)S(1)} %copy-done.20, bf16[256,768]{1,0:T(8,128)(2,1)S(1)} %copy-done.14, bf16[512,768]{1,0:T(8,128)(2,1)S(1)} %copy-done.28, bf16[512,768]{1,0:T(8,128)(2,1)S(1)} %copy-done.31, ...), custom_call_target="tpu_custom_call" | custom-call | flops 905969664 | bytes 2362368 | tf_op jit(solution)/shard_map/pallas_call | solution.py:141
  92.4 6.5 %collective-permute-done.18.refs_1_ = bf16[384,1536]{1,0:T(8,128)(2,1)} collective-permute-done((bf16[384,1536]{1,0:T(8,128)(2,1)}, bf16[384,1536]{1,0:T(8,128)(2,1)}, u32[]{:S(2)}, u32[]{:S(2)}) %collective-permute-start.18) | collective-permute-done | bytes 1179680 | tf_op jit(solution)/shard_map/ppermute | solution.py:61
  103.0 4.8 %shard_map.334 = (bf16[256,3072]{1,0:T(8,128)(2,1)S(1)}, f32[256,3072]{1,0:T(8,128)S(1)}) custom-call(bf16[256,768]{1,0:T(8,128)(2,1)S(1)} %copy-done.10, bf16[192,3072]{1,0:T(8,128)(2,1)} %get-tuple-element.107.refs_5_.refs_1_, bf16[192,3072]{1,0:T(8,128)(2,1)} %get-tuple-element.111.refs_2_, bf16[192,3072]{1,0:T(8,128)(2,1)} %collective-permute-done.15.refs_5_.refs_3_, ...), custom_call_target="tpu_custom_call" | custom-call | flops 2415919104 | bytes 9842688 | tf_op jit(solution)/shard_map/pallas_call | solution.py:141
  107.9 4.4 %shard_map.335 = (bf16[256,768]{1,0:T(8,128)(2,1)S(1)}, f32[256,768]{1,0:T(8,128)S(1)}, bf16[256,768]{1,0:T(8,128)(2,1)S(1)}, f32[8,768]{1,0:T(8,128)S(1)}) custom-call(bf16[256,3072]{1,0:T(8,128)(2,1)S(1)} %get-tuple-element.113.refs_0_, bf16[384,1536]{1,0:T(8,128)(2,1)} %get-tuple-element.109.refs_1_, bf16[384,1536]{1,0:T(8,128)(2,1)} %get-tuple-element.114.refs_2_, ...), custom_call_target="tpu_custom_call" | custom-call | flops 1509949440 | bytes 9481216 | tf_op jit(solution)/shard_map/pallas_call | solution.py:141
  113.2 3.8 %shard_map.336 = (bf16[256,3072]{1,0:T(8,128)(2,1)S(1)}, f32[1,3072]{1,0:T(1,128)S(1)}) custom-call(bf16[256,768]{1,0:T(8,128)(2,1)S(1)} %get-tuple-element.117.refs_0_, bf16[384,1536]{1,0:T(8,128)(2,1)} %get-tuple-element.109.refs_1_, bf16[384,1536]{1,0:T(8,128)(2,1)} %get-tuple-element.114.refs_2_, ...), custom_call_target="tpu_custom_call" | custom-call | flops 1811939328 | bytes 9842688 | tf_op jit(solution)/shard_map/pallas_call | solution.py:141
  120.0 11.7 %shard_map.337 = (bf16[384,1536]{1,0:T(8,128)(2,1)S(1)}, bf16[384,1536]{1,0:T(8,128)(2,1)S(1)}) custom-call(bf16[384,3072]{1,0:T(8,128)(2,1)S(1)} %convolution_convert_fusion.1.refs_0_, bf16[384,3072]{1,0:T(8,128)(2,1)S(1)} %collective-permute-done.22.refs_1_, bf16[256,3072]{1,0:T(8,128)(2,1)S(1)} %get-tuple-element.119.refs_2_.refs_0_), custom_call_target="tpu_custom_call" | custom-call | flops 120795955200 | bytes 7077888 | tf_op jit(solution)/shard_map/pallas_call | solution.py:141
  135.1 4.8 %shard_map.339 = (f32[256,768]{1,0:T(8,128)S(1)}, bf16[256,768]{1,0:T(8,128)(2,1)S(1)}, bf16[256,768]{1,0:T(8,128)(2,1)S(1)}, f32[8,768]{1,0:T(8,128)S(1)}) custom-call(bf16[256,3072]{1,0:T(8,128)(2,1)S(1)} %get-tuple-element.119.refs_2_.refs_0_, bf16[192,3072]{1,0:T(8,128)(2,1)} %get-tuple-element.107.refs_5_.refs_1_, ...), custom_call_target="tpu_custom_call" | custom-call | flops 1811939328 | bytes 11840512 | tf_op jit(solution)/shard_map/pallas_call | solution.py:141
  140.0 10.0 %shard_map.340 = (bf16[256,768]{1,0:T(8,128)(2,1)S(1)}, bf16[512,768]{1,0:T(8,128)(2,1)S(1)}, bf16[512,768]{1,0:T(8,128)(2,1)S(1)}) custom-call(s32[1,256]{1,0:T(1,128)S(1)} %bitcast.66, s32[512,1]{1,0:T(8,128)S(1)} %copy-done.21, bf16[256,768]{1,0:T(8,128)(2,1)S(1)} %copy-done.15, bf16[512,768]{1,0:T(8,128)(2,1)S(1)} %copy-done.29, ...), custom_call_target="tpu_custom_call" | custom-call | flops 1509949440 | bytes 4328448 | tf_op jit(solution)/shard_map/pallas_call | solution.py:141
  150.0 3.0 %shard_map.341 = (bf16[384,1792]{1,0:T(8,128)(2,1)S(1)}, bf16[384,1536]{1,0:T(8,128)(2,1)S(1)}, bf16[384,1792]{1,0:T(8,128)(2,1)S(1)}, bf16[384,1536]{1,0:T(8,128)(2,1)S(1)}) custom-call(s32[1]{0:T(128)} %bitcast.12.refs_0_, bf16[768,768]{1,0:T(8,128)(2,1)S(1)} %copy-done.7, bf16[512,768]{1,0:T(8,128)(2,1)S(1)} %pad_maximum_fusion.refs_4_.refs_0_.refs_1_.refs_2_, ...), custom_call_target="tpu_custom_call" | custom-call | flops 1811939328 | bytes 9891844 | tf_op jit(solution)/shard_map/pallas_call | solution.py:141
  153.7 6.0 %collective-permute-done.24.refs_3_ = bf16[384,1536]{1,0:T(8,128)(2,1)S(1)} collective-permute-done((bf16[384,1536]{1,0:T(8,128)(2,1)S(1)}, bf16[384,1536]{1,0:T(8,128)(2,1)S(1)}, u32[]{:S(2)}, u32[]{:S(2)}) %collective-permute-start.24) | collective-permute-done | bytes 1179680 | tf_op jit(solution)/shard_map/ppermute | solution.py:61
  159.6 1.9 collective-permute-done.23.refs_1_
  163.3 2.6 %shard_map.343 = (f32[256,768]{1,0:T(8,128)S(1)}, bf16[256,768]{1,0:T(8,128)(2,1)S(1)}) custom-call(bf16[256,768]{1,0:T(8,128)(2,1)S(1)} %get-tuple-element.126.refs_3_.refs_0_, bf16[512,768]{1,0:T(8,128)(2,1)S(1)} %get-tuple-element.127.refs_4_.refs_1_, bf16[512,768]{1,0:T(8,128)(2,1)S(1)} %get-tuple-element.128.refs_5_.refs_2_, ...), custom_call_target="tpu_custom_call" | custom-call | flops 120795955200 | bytes 9043968 | tf_op jit(solution)/shard_map/pallas_call | solution.py:141
  169.5 8.9 %collective-permute-done.30.refs_1_ = bf16[192,1536]{1,0:T(8,128)(2,1)S(1)} collective-permute-done((bf16[192,1536]{1,0:T(8,128)(2,1)S(1)}, bf16[192,1536]{1,0:T(8,128)(2,1)S(1)}, u32[]{:S(2)}, u32[]{:S(2)}) %collective-permute-start.30) | collective-permute-done | bytes 589856 | tf_op jit(solution)/shard_map/ppermute | solution.py:61
  179.7 2.2 %collective-permute-start.35 = (bf16[48,3072]{1,0:T(8,128)(2,1)S(1)}, bf16[48,3072]{1,0:T(8,128)(2,1)S(1)}, u32[]{:S(2)}, u32[]{:S(2)}) collective-permute-start(bf16[48,3072]{1,0:T(8,128)(2,1)S(1)} %get-tuple-element.156), channel_id=1, source_target_pairs={{0,16},{2,18},{4,20},{6,22},{8,24},{10,26},{12,28},{14,30},{16,0},... | collective-permute-start | bytes 884744 | tf_op jit(solution)/shard_map/ppermute | solution.py:57
  181.9 1.8 collective-permute-start.36
  183.7 5.2 %collective-permute-done.29.refs_3_ = bf16[384,768]{1,0:T(8,128)(2,1)S(1)} collective-permute-done((bf16[384,768]{1,0:T(8,128)(2,1)S(1)}, bf16[384,768]{1,0:T(8,128)(2,1)S(1)}, u32[]{:S(2)}, u32[]{:S(2)}) %collective-permute-start.29) | collective-permute-done | bytes 589856 | tf_op jit(solution)/shard_map/ppermute | solution.py:61
  189.4 1.8 collective-permute-done.28.refs_1_
  193.6 6.6 %collective-permute-done.35.refs_2_ = bf16[48,3072]{1,0:T(8,128)(2,1)S(1)} collective-permute-done((bf16[48,3072]{1,0:T(8,128)(2,1)S(1)}, bf16[48,3072]{1,0:T(8,128)(2,1)S(1)}, u32[]{:S(2)}, u32[]{:S(2)}) %collective-permute-start.35) | collective-permute-done | bytes 294944 | tf_op jit(solution)/shard_map/ppermute | solution.py:57
  202.4 2.7 %collective-permute-done.32.refs_1_ = bf16[192,896]{1,0:T(8,128)(2,1)S(1)} collective-permute-done((bf16[192,896]{1,0:T(8,128)(2,1)S(1)}, bf16[192,896]{1,0:T(8,128)(2,1)S(1)}, u32[]{:S(2)}, u32[]{:S(2)}) %collective-permute-start.32) | collective-permute-done | bytes 344096 | tf_op jit(solution)/shard_map/ppermute | solution.py:61
  208.0 1.8 collective-permute-start.39
  211.0 2.0 shard_map.349
  213.0 5.7 %collective-permute-done.38.refs_12_ = bf16[48,1664]{1,0:T(8,128)(2,1)S(1)} collective-permute-done((bf16[48,1664]{1,0:T(8,128)(2,1)S(1)}, bf16[48,1664]{1,0:T(8,128)(2,1)S(1)}, u32[]{:S(2)}, u32[]{:S(2)}) %collective-permute-start.38) | collective-permute-done | bytes 159776 | tf_op jit(solution)/shard_map/ppermute | solution.py:57
  (218 shorter events, 63.9 us)
Async XLA Ops:
  3.6 10.2 %collective-permute-start.3 = (bf16[48,1664]{1,0:T(8,128)(2,1)S(1)}, bf16[48,1664]{1,0:T(8,128)(2,1)S(1)}, u32[]{:S(2)}, u32[]{:S(2)}) collective-permute-start(bf16[48,1664]{1,0:T(8,128)(2,1)S(1)} %convert_dynamic-update-slice_fusion.refs_0_), channel_id=1, source_target_pairs={{0,24},{2,26},{4,28},{6,30},{8,16},{10,18},{12,20},{14,22},{16,8},... | collective-permute-start | bytes 479240 | tf_op jit(solution)/shard_map/ppermute | solution.py:57
  8.7 13.5 %collective-permute-start.2 = (bf16[48,1664]{1,0:T(8,128)(2,1)S(1)}, bf16[48,1664]{1,0:T(8,128)(2,1)S(1)}, u32[]{:S(2)}, u32[]{:S(2)}) collective-permute-start(bf16[48,1664]{1,0:T(8,128)(2,1)S(1)} %convert_dynamic-update-slice_fusion.refs_0_), channel_id=1, source_target_pairs={{0,16},{2,18},{4,20},{6,22},{8,24},{10,26},{12,28},{14,30},{16,0},... | collective-permute-start | bytes 479240 | tf_op jit(solution)/shard_map/ppermute | solution.py:57
  8.7 13.5 %collective-permute-start.1 = (bf16[48,1664]{1,0:T(8,128)(2,1)S(1)}, bf16[48,1664]{1,0:T(8,128)(2,1)S(1)}, u32[]{:S(2)}, u32[]{:S(2)}) collective-permute-start(bf16[48,1664]{1,0:T(8,128)(2,1)S(1)} %convert_dynamic-update-slice_fusion.refs_0_), channel_id=1, source_target_pairs={{0,8},{2,10},{4,12},{6,14},{8,0},{10,2},{12,4},{14,6},{16,24},{18,... | collective-permute-start | bytes 479240 | tf_op jit(solution)/shard_map/ppermute | solution.py:57
  9.4 19.0 %collective-permute-start = (bf16[256,768]{1,0:T(8,128)(2,1)}, bf16[256,768]{1,0:T(8,128)(2,1)S(1)}, u32[]{:S(2)}, u32[]{:S(2)}) collective-permute-start(bf16[256,768]{1,0:T(8,128)(2,1)} %param.20), channel_id=1, source_target_pairs={{0,1},{1,0},{2,3},{3,2},{4,5},{5,4},{6,7},{7,6},{8,9},{9,8},{10,11... | collective-permute-start | bytes 1179656 | tf_op jit(solution)/shard_map/ppermute | solution.py:61
  22.4 15.9 %collective-permute-start.10 = (bf16[48,3072]{1,0:T(8,128)(2,1)S(1)}, bf16[48,3072]{1,0:T(8,128)(2,1)S(1)}, u32[]{:S(2)}, u32[]{:S(2)}) collective-permute-start(bf16[48,3072]{1,0:T(8,128)(2,1)S(1)} %shard_map.325.refs_0_), channel_id=1, source_target_pairs={{0,24},{2,26},{4,28},{6,30},{8,16},{10,18},{12,20},{14,22},{16,8},... | collective-permute-start | bytes 884744 | tf_op jit(solution)/shard_map/ppermute | solution.py:57
  24.9 23.4 %collective-permute-start.9 = (bf16[48,3072]{1,0:T(8,128)(2,1)S(1)}, bf16[48,3072]{1,0:T(8,128)(2,1)S(1)}, u32[]{:S(2)}, u32[]{:S(2)}) collective-permute-start(bf16[48,3072]{1,0:T(8,128)(2,1)S(1)} %shard_map.325.refs_0_), channel_id=1, source_target_pairs={{0,16},{2,18},{4,20},{6,22},{8,24},{10,26},{12,28},{14,30},{16,0},... | collective-permute-start | bytes 884744 | tf_op jit(solution)/shard_map/ppermute | solution.py:57
  25.0 23.4 %collective-permute-start.8 = (bf16[48,3072]{1,0:T(8,128)(2,1)S(1)}, bf16[48,3072]{1,0:T(8,128)(2,1)S(1)}, u32[]{:S(2)}, u32[]{:S(2)}) collective-permute-start(bf16[48,3072]{1,0:T(8,128)(2,1)S(1)} %shard_map.325.refs_0_), channel_id=1, source_target_pairs={{0,8},{2,10},{4,12},{6,14},{8,0},{10,2},{12,4},{14,6},{16,24},{18,... | collective-permute-start | bytes 884744 | tf_op jit(solution)/shard_map/ppermute | solution.py:57
  35.4 13.1 %collective-permute-start.6 = (bf16[384,768]{1,0:T(8,128)(2,1)S(1)}, bf16[384,768]{1,0:T(8,128)(2,1)S(1)}, u32[]{:S(2)}, u32[]{:S(2)}) collective-permute-start(bf16[384,768]{1,0:T(8,128)(2,1)S(1)} %get-tuple-element.96.refs_0_), channel_id=1, source_target_pairs={{0,1},{1,0},{2,3},{3,2},{4,5},{5,4},{6,7},{7,6},{8,9},{9,8},{10,11... | collective-permute-start | bytes 1769480 | tf_op jit(solution)/shard_map/ppermute | solution.py:61
  36.8 14.4 %collective-permute-start.7 = (bf16[192,1792]{1,0:T(8,128)(2,1)S(1)}, bf16[192,1792]{1,0:T(8,128)(2,1)S(1)}, u32[]{:S(2)}, u32[]{:S(2)}) collective-permute-start(bf16[192,1792]{1,0:T(8,128)(2,1)S(1)} %get-tuple-element.97.refs_1_), channel_id=1, source_target_pairs={{0,4},{2,6},{4,0},{6,2},{8,12},{10,14},{12,8},{14,10},{16,20},{18,... | collective-permute-start | bytes 2064392 | tf_op jit(solution)/shard_map/ppermute | solution.py:57
  52.0 15.3 %collective-permute-start.14 = (bf16[192,1536]{1,0:T(8,128)(2,1)S(1)}, bf16[192,1536]{1,0:T(8,128)(2,1)S(1)}, u32[]{:S(2)}, u32[]{:S(2)}) collective-permute-start(bf16[192,1536]{1,0:T(8,128)(2,1)S(1)} %get-tuple-element.106.refs_1_), channel_id=1, source_target_pairs={{0,4},{2,6},{4,0},{6,2},{8,12},{10,14},{12,8},{14,10},{16,20},{18,... | collective-permute-start | bytes 1769480 | tf_op jit(solution)/shard_map/ppermute | solution.py:57
  53.5 15.0 %collective-permute-start.13 = (bf16[192,1536]{1,0:T(8,128)(2,1)S(1)}, bf16[192,1536]{1,0:T(8,128)(2,1)S(1)}, u32[]{:S(2)}, u32[]{:S(2)}) collective-permute-start(bf16[192,1536]{1,0:T(8,128)(2,1)S(1)} %get-tuple-element.98.refs_4_.refs_0_), channel_id=1, source_target_pairs={{0,1},{1,0},{2,3},{3,2},{4,5},{5,4},{6,7},{7,6},{8,9},{9,8},{10,11... | collective-permute-start | bytes 1769480 | tf_op jit(solution)/shard_map/ppermute | solution.py:61
  70.1 18.1 %collective-permute-start.16 = (bf16[384,1536]{1,0:T(8,128)(2,1)}, bf16[384,1536]{1,0:T(8,128)(2,1)}, u32[]{:S(2)}, u32[]{:S(2)}) collective-permute-start(bf16[384,1536]{1,0:T(8,128)(2,1)} %get-tuple-element.109.refs_1_), channel_id=1, source_target_pairs={{0,2},{2,0},{4,6},{6,4},{8,10},{10,8},{12,14},{14,12},{16,18},{18,... | collective-permute-start | bytes 3538952 | tf_op jit(solution)/shard_map/ppermute | solution.py:57
  70.1 18.1 %collective-permute-start.15 = (bf16[192,3072]{1,0:T(8,128)(2,1)}, bf16[192,3072]{1,0:T(8,128)(2,1)}, u32[]{:S(2)}, u32[]{:S(2)}) collective-permute-start(bf16[192,3072]{1,0:T(8,128)(2,1)} %get-tuple-element.107.refs_5_.refs_1_), channel_id=1, source_target_pairs={{0,2},{2,0},{4,6},{6,4},{8,10},{10,8},{12,14},{14,12},{16,18},{18,... | collective-permute-start | bytes 3538952 | tf_op jit(solution)/shard_map/ppermute | solution.py:57
  70.6 28.3 %collective-permute-start.18 = (bf16[384,1536]{1,0:T(8,128)(2,1)}, bf16[384,1536]{1,0:T(8,128)(2,1)}, u32[]{:S(2)}, u32[]{:S(2)}) collective-permute-start(bf16[384,1536]{1,0:T(8,128)(2,1)} %get-tuple-element.109.refs_1_), channel_id=1, source_target_pairs={{0,1},{1,0},{2,3},{3,2},{4,5},{5,4},{6,7},{7,6},{8,9},{9,8},{10,11... | collective-permute-start | bytes 3538952 | tf_op jit(solution)/shard_map/ppermute | solution.py:61
  71.2 28.0 %collective-permute-start.17 = (bf16[192,3072]{1,0:T(8,128)(2,1)}, bf16[192,3072]{1,0:T(8,128)(2,1)}, u32[]{:S(2)}, u32[]{:S(2)}) collective-permute-start(bf16[192,3072]{1,0:T(8,128)(2,1)} %get-tuple-element.107.refs_5_.refs_1_), channel_id=1, source_target_pairs={{0,4},{2,6},{4,0},{6,2},{8,12},{10,14},{12,8},{14,10},{16,20},{18,... | collective-permute-start | bytes 3538952 | tf_op jit(solution)/shard_map/ppermute | solution.py:57
  117.8 15.4 %collective-permute-start.21 = (bf16[384,3072]{1,0:T(8,128)(2,1)S(1)}, bf16[384,3072]{1,0:T(8,128)(2,1)S(1)}, u32[]{:S(2)}, u32[]{:S(2)}) collective-permute-start(bf16[384,3072]{1,0:T(8,128)(2,1)S(1)} %convolution_convert_fusion.2), channel_id=1, source_target_pairs={{0,2},{2,0},{4,6},{6,4},{8,10},{10,8},{12,14},{14,12},{16,18},{18,... | collective-permute-start | bytes 7077896 | tf_op jit(solution)/shard_map/ppermute | solution.py:57
  131.7 28.0 %collective-permute-start.24 = (bf16[384,1536]{1,0:T(8,128)(2,1)S(1)}, bf16[384,1536]{1,0:T(8,128)(2,1)S(1)}, u32[]{:S(2)}, u32[]{:S(2)}) collective-permute-start(bf16[384,1536]{1,0:T(8,128)(2,1)S(1)} %get-tuple-element.131), channel_id=1, source_target_pairs={{0,1},{1,0},{2,3},{3,2},{4,5},{5,4},{6,7},{7,6},{8,9},{9,8},{10,11... | collective-permute-start | bytes 3538952 | tf_op jit(solution)/shard_map/ppermute | solution.py:61
  133.9 27.7 %collective-permute-start.23 = (bf16[192,3072]{1,0:T(8,128)(2,1)S(1)}, bf16[192,3072]{1,0:T(8,128)(2,1)S(1)}, u32[]{:S(2)}, u32[]{:S(2)}) collective-permute-start(bf16[192,3072]{1,0:T(8,128)(2,1)S(1)} %get-tuple-element.130), channel_id=1, source_target_pairs={{0,4},{2,6},{4,0},{6,2},{8,12},{10,14},{12,8},{14,10},{16,20},{18,... | collective-permute-start | bytes 3538952 | tf_op jit(solution)/shard_map/ppermute | solution.py:57
  153.1 12.8 %collective-permute-start.27 = (bf16[384,1536]{1,0:T(8,128)(2,1)S(1)}, bf16[384,1536]{1,0:T(8,128)(2,1)S(1)}, u32[]{:S(2)}, u32[]{:S(2)}) collective-permute-start(bf16[384,1536]{1,0:T(8,128)(2,1)S(1)} %get-tuple-element.142), channel_id=1, source_target_pairs={{0,2},{2,0},{4,6},{6,4},{8,10},{10,8},{12,14},{14,12},{16,18},{18,... | collective-permute-start | bytes 3538952 | tf_op jit(solution)/shard_map/ppermute | solution.py:57
  153.2 12.8 %collective-permute-start.26 = (bf16[384,1792]{1,0:T(8,128)(2,1)S(1)}, bf16[384,1792]{1,0:T(8,128)(2,1)S(1)}, u32[]{:S(2)}, u32[]{:S(2)}) collective-permute-start(bf16[384,1792]{1,0:T(8,128)(2,1)S(1)} %get-tuple-element.140), channel_id=1, source_target_pairs={{0,2},{2,0},{4,6},{6,4},{8,10},{10,8},{12,14},{14,12},{16,18},{18,... | collective-permute-start | bytes 4128776 | tf_op jit(solution)/shard_map/ppermute | solution.py:57
  162.1 16.3 %collective-permute-start.30 = (bf16[192,1536]{1,0:T(8,128)(2,1)S(1)}, bf16[192,1536]{1,0:T(8,128)(2,1)S(1)}, u32[]{:S(2)}, u32[]{:S(2)}) collective-permute-start(bf16[192,1536]{1,0:T(8,128)(2,1)S(1)} %get-tuple-element.147), channel_id=1, source_target_pairs={{0,1},{1,0},{2,3},{3,2},{4,5},{5,4},{6,7},{7,6},{8,9},{9,8},{10,11... | collective-permute-start | bytes 1769480 | tf_op jit(solution)/shard_map/ppermute | solution.py:61
  162.7 16.3 %collective-permute-start.31 = (bf16[192,1536]{1,0:T(8,128)(2,1)S(1)}, bf16[192,1536]{1,0:T(8,128)(2,1)S(1)}, u32[]{:S(2)}, u32[]{:S(2)}) collective-permute-start(bf16[192,1536]{1,0:T(8,128)(2,1)S(1)} %get-tuple-element.149), channel_id=1, source_target_pairs={{0,4},{2,6},{4,0},{6,2},{8,12},{10,14},{12,8},{14,10},{16,20},{18,... | collective-permute-start | bytes 1769480 | tf_op jit(solution)/shard_map/ppermute | solution.py:57
  166.5 24.7 %collective-permute-start.28 = (bf16[192,1792]{1,0:T(8,128)(2,1)S(1)}, bf16[192,1792]{1,0:T(8,128)(2,1)S(1)}, u32[]{:S(2)}, u32[]{:S(2)}) collective-permute-start(bf16[192,1792]{1,0:T(8,128)(2,1)S(1)} %get-tuple-element.144), channel_id=1, source_target_pairs={{0,4},{2,6},{4,0},{6,2},{8,12},{10,14},{12,8},{14,10},{16,20},{18,... | collective-permute-start | bytes 2064392 | tf_op jit(solution)/shard_map/ppermute | solution.py:57
  168.0 20.8 %collective-permute-start.29 = (bf16[384,768]{1,0:T(8,128)(2,1)S(1)}, bf16[384,768]{1,0:T(8,128)(2,1)S(1)}, u32[]{:S(2)}, u32[]{:S(2)}) collective-permute-start(bf16[384,768]{1,0:T(8,128)(2,1)S(1)} %get-tuple-element.146), channel_id=1, source_target_pairs={{0,1},{1,0},{2,3},{3,2},{4,5},{5,4},{6,7},{7,6},{8,9},{9,8},{10,11... | collective-permute-start | bytes 1769480 | tf_op jit(solution)/shard_map/ppermute | solution.py:61
  179.2 12.9 %collective-permute-start.34 = (bf16[48,3072]{1,0:T(8,128)(2,1)S(1)}, bf16[48,3072]{1,0:T(8,128)(2,1)S(1)}, u32[]{:S(2)}, u32[]{:S(2)}) collective-permute-start(bf16[48,3072]{1,0:T(8,128)(2,1)S(1)} %get-tuple-element.155), channel_id=1, source_target_pairs={{0,8},{2,10},{4,12},{6,14},{8,0},{10,2},{12,4},{14,6},{16,24},{18,... | collective-permute-start | bytes 884744 | tf_op jit(solution)/shard_map/ppermute | solution.py:57
  179.7 20.6 %collective-permute-start.35 = (bf16[48,3072]{1,0:T(8,128)(2,1)S(1)}, bf16[48,3072]{1,0:T(8,128)(2,1)S(1)}, u32[]{:S(2)}, u32[]{:S(2)}) collective-permute-start(bf16[48,3072]{1,0:T(8,128)(2,1)S(1)} %get-tuple-element.156), channel_id=1, source_target_pairs={{0,16},{2,18},{4,20},{6,22},{8,24},{10,26},{12,28},{14,30},{16,0},... | collective-permute-start | bytes 884744 | tf_op jit(solution)/shard_map/ppermute | solution.py:57
  181.9 18.3 %collective-permute-start.36 = (bf16[48,3072]{1,0:T(8,128)(2,1)S(1)}, bf16[48,3072]{1,0:T(8,128)(2,1)S(1)}, u32[]{:S(2)}, u32[]{:S(2)}) collective-permute-start(bf16[48,3072]{1,0:T(8,128)(2,1)S(1)} %get-tuple-element.157), channel_id=1, source_target_pairs={{0,24},{2,26},{4,28},{6,30},{8,16},{10,18},{12,20},{14,22},{16,8},... | collective-permute-start | bytes 884744 | tf_op jit(solution)/shard_map/ppermute | solution.py:57
  188.9 22.0 %collective-permute-start.25 = (bf16[256,768]{1,0:T(8,128)(2,1)S(1)}, bf16[256,768]{1,0:T(8,128)(2,1)S(1)}, u32[]{:S(2)}, u32[]{:S(2)}) collective-permute-start(bf16[256,768]{1,0:T(8,128)(2,1)S(1)} %get-tuple-element.139), channel_id=1, source_target_pairs={{0,1},{1,0},{2,3},{3,2},{4,5},{5,4},{6,7},{7,6},{8,9},{9,8},{10,11... | collective-permute-start | bytes 1179656 | tf_op jit(solution)/shard_map/ppermute | solution.py:61
  191.5 10.9 %collective-permute-start.33 = (bf16[192,768]{1,0:T(8,128)(2,1)S(1)}, bf16[192,768]{1,0:T(8,128)(2,1)S(1)}, u32[]{:S(2)}, u32[]{:S(2)}) collective-permute-start(bf16[192,768]{1,0:T(8,128)(2,1)S(1)} %get-tuple-element.154), channel_id=1, source_target_pairs={{0,4},{2,6},{4,0},{6,2},{8,12},{10,14},{12,8},{14,10},{16,20},{18,... | collective-permute-start | bytes 884744 | tf_op jit(solution)/shard_map/ppermute | solution.py:57
  192.1 13.1 %collective-permute-start.32 = (bf16[192,896]{1,0:T(8,128)(2,1)S(1)}, bf16[192,896]{1,0:T(8,128)(2,1)S(1)}, u32[]{:S(2)}, u32[]{:S(2)}) collective-permute-start(bf16[192,896]{1,0:T(8,128)(2,1)S(1)} %get-tuple-element.152), channel_id=1, source_target_pairs={{0,1},{1,0},{2,3},{3,2},{4,5},{5,4},{6,7},{7,6},{8,9},{9,8},{10,11... | collective-permute-start | bytes 1032200 | tf_op jit(solution)/shard_map/ppermute | solution.py:61
  206.4 12.2 %collective-permute-start.38 = (bf16[48,1664]{1,0:T(8,128)(2,1)S(1)}, bf16[48,1664]{1,0:T(8,128)(2,1)S(1)}, u32[]{:S(2)}, u32[]{:S(2)}) collective-permute-start(bf16[48,1664]{1,0:T(8,128)(2,1)S(1)} %get-tuple-element.160), channel_id=1, source_target_pairs={{0,16},{2,18},{4,20},{6,22},{8,24},{10,26},{12,28},{14,30},{16,0},... | collective-permute-start | bytes 479240 | tf_op jit(solution)/shard_map/ppermute | solution.py:57
  208.0 10.6 %collective-permute-start.39 = (bf16[48,1664]{1,0:T(8,128)(2,1)S(1)}, bf16[48,1664]{1,0:T(8,128)(2,1)S(1)}, u32[]{:S(2)}, u32[]{:S(2)}) collective-permute-start(bf16[48,1664]{1,0:T(8,128)(2,1)S(1)} %get-tuple-element.161), channel_id=1, source_target_pairs={{0,24},{2,26},{4,28},{6,30},{8,16},{10,18},{12,20},{14,22},{16,8},... | collective-permute-start | bytes 479240 | tf_op jit(solution)/shard_map/ppermute | solution.py:57
  (63 other events, 507.7 us)

commit v5 on v4

--- a/solution.py
+++ b/solution.py
@@ -138,6 +138,7 @@
     whole = pl.BlockSpec(memory_space=pltpu.VMEM)
     in_specs = in_specs or [whole] * count
     size = sum(v.size * v.dtype.itemsize for v in list(operands) + list(outs))
+    grant = 10 << 20 if grid else size + ((8 if flops else 2) << 20)
     return pl.pallas_call(
         body,
         grid=grid,
@@ -145,9 +146,7 @@
         in_specs=list(in_specs) + [pl.BlockSpec(memory_space=pl.ANY)] * len(after),
         out_specs=list(out_specs or [whole] * len(outs)),
         scratch_shapes=list(scratch),
-        compiler_params=pltpu.CompilerParams(
-            vmem_limit_bytes=min(size + ((12 if flops else 4) << 20), 44 << 20)
-        ),
+        compiler_params=pltpu.CompilerParams(vmem_limit_bytes=grant),
         cost_estimate=pl.CostEstimate(flops=flops, bytes_accessed=size, transcendentals=0),
     )(*operands, *after)
 
@@ -160,6 +159,7 @@
         in_specs=[anywhere] * (len(values) + len(after)),
         out_specs=[anywhere] * len(values),
         input_output_aliases={place: place for place in range(len(values))},
+        compiler_params=pltpu.CompilerParams(vmem_limit_bytes=1 << 20),
         cost_estimate=pl.CostEstimate(flops=0, bytes_accessed=0, transcendentals=0),
     )(*values, *after)
 
@@ -827,7 +827,7 @@
     input_grad = run(
         rows_out_kernel,
         [wide],
-        [grad_own, swap_tensor(grad_away), permute],
+        [grad_own, swap_tensor(gate([grad_away], one[:1])[0]), permute],
         3 * unit,
         after=one[:1],
     )[0]
@@ -847,6 +847,7 @@
         [rank, w_qkv, m_qkv, v_qkv, w_out.T, m_out.T, v_out.T]
         + [vectors, m_vectors, v_vectors, *one],
         unit,
+        after=[input_grad],
         in_specs=[scalar] + [vmem] * (9 + len(one)),
         scratch=[pltpu.VMEM((LANES, LANES), F32)],
     )

time: 223 us -> 224 us (level)
  local copies, waits for them, and re-layouts: 12.9 us -> 10.1 us
  starting transfers between devices: 41.4 us -> 44.1 us
    ppermute x10, waiting for transfers between devices: 30.5 us -> 35.3 us  [swap_tensor(): return lax.ppermute(values, 'tensor', [(0, 1), (1, 0)])]
    ppermute x30, waiting for transfers between devices: 51.8 us -> 48 us  [swap_dp(): return lax.ppermute(values, 'dp', [(i, i ^ mask) for i in range(size)])]
    unnamed x114 -> x90, local copies, waits for them, and re-layouts: 10.2 us -> 8 us
  transfers between devices with their start and end apart: 40 -> 40, of which waited for: 19 -> 20; matrix products, arithmetic and copies ran while one was open for 7% -> 7% of each run, Pallas kernels for 26% -> 26%
where the time goes in v5:
time: 224 us; the launch traced here: 221 us
  waiting for transfers between devices  83.3 us (37%)
  Pallas kernels  65.6 us (29%)
  starting transfers between devices  44.1 us (20%)
  local copies, waits for them, and re-layouts  10.1 us (5%)
  other arithmetic  9.39 us (4%)
  matrix products  6.73 us (3%)
    pallas_call x27, Pallas kernels, run(): pl.pallas_call(body, grid=grid, out_shape=list(outs), in_specs=list(in_sp...  65.5 us
    ppermute x30, waiting for transfers between devices, swap_dp(): return lax.ppermute(values, 'dp', [(i, i ^ mask) for i in range(size)])  48 us
    ppermute x10, waiting for transfers between devices, swap_tensor(): return lax.ppermute(values, 'tensor', [(0, 1), (1, 0)])  35.3 us
    ppermute x30, starting transfers between devices, swap_dp(): return lax.ppermute(values, 'dp', [(i, i ^ mask) for i in range(size)])  32 us
    ppermute x10, starting transfers between devices, swap_tensor(): return lax.ppermute(values, 'tensor', [(0, 1), (1, 0)])  12.1 us
    unnamed x90, local copies, waits for them, and re-layouts  8 us
  transfers between devices with their start and end apart: 40, of which 20 were waited for; matrix products, arithmetic and copies ran while one was open for 7% of the time, Pallas kernels for 26%

profile of v5, /device:TPU:0, one launch (start us, length us, event | category | flops | bytes accessed | tf_op | source)
XLA Modules:
  0.0 220.9 jit_solution(17205596875231206959)
XLA Ops:
  3.6 5.1 %collective-permute-start.3 = (bf16[48,1664]{1,0:T(8,128)(2,1)S(1)}, bf16[48,1664]{1,0:T(8,128)(2,1)S(1)}, u32[]{:S(2)}, u32[]{:S(2)}) collective-permute-start(bf16[48,1664]{1,0:T(8,128)(2,1)S(1)} %convert_dynamic-update-slice_fusion.refs_0_), channel_id=1, source_target_pairs={{0,24},{2,26},{4,28},{6,30},{8,16},{10,18},{12,20},{14,22},{16,8},... | collective-permute-start | bytes 479240 | tf_op jit(solution)/shard_map/ppermute | solution.py:57
  9.4 1.6 collective-permute-start
  13.8 8.5 %collective-permute-done.2.refs_2_ = bf16[48,1664]{1,0:T(8,128)(2,1)S(1)} collective-permute-done((bf16[48,1664]{1,0:T(8,128)(2,1)S(1)}, bf16[48,1664]{1,0:T(8,128)(2,1)S(1)}, u32[]{:S(2)}, u32[]{:S(2)}) %collective-permute-start.2) | collective-permute-done | bytes 159776 | tf_op jit(solution)/shard_map/ppermute | solution.py:57
  22.4 2.6 %collective-permute-start.10 = (bf16[48,3072]{1,0:T(8,128)(2,1)S(1)}, bf16[48,3072]{1,0:T(8,128)(2,1)S(1)}, u32[]{:S(2)}, u32[]{:S(2)}) collective-permute-start(bf16[48,3072]{1,0:T(8,128)(2,1)S(1)} %shard_map.325.refs_0_), channel_id=1, source_target_pairs={{0,24},{2,26},{4,28},{6,30},{8,16},{10,18},{12,20},{14,22},{16,8},... | collective-permute-start | bytes 884744 | tf_op jit(solution)/shard_map/ppermute | solution.py:57
  25.0 1.9 collective-permute-start.8
  30.5 4.7 %collective-permute-done.5.refs_3_ = bf16[192,768]{1,0:T(8,128)(2,1)S(1)} collective-permute-done((bf16[192,768]{1,0:T(8,128)(2,1)S(1)}, bf16[192,768]{1,0:T(8,128)(2,1)S(1)}, u32[]{:S(2)}, u32[]{:S(2)}) %collective-permute-start.5) | collective-permute-done | bytes 294944 | tf_op jit(solution)/shard_map/ppermute | solution.py:57
  38.3 10.1 %collective-permute-done.9.refs_2_ = bf16[48,3072]{1,0:T(8,128)(2,1)S(1)} collective-permute-done((bf16[48,3072]{1,0:T(8,128)(2,1)S(1)}, bf16[48,3072]{1,0:T(8,128)(2,1)S(1)}, u32[]{:S(2)}, u32[]{:S(2)}) %collective-permute-start.9) | collective-permute-done | bytes 294944 | tf_op jit(solution)/shard_map/ppermute | solution.py:57
  48.5 2.7 %collective-permute-done.7.refs_3_ = bf16[192,1792]{1,0:T(8,128)(2,1)S(1)} collective-permute-done((bf16[192,1792]{1,0:T(8,128)(2,1)S(1)}, bf16[192,1792]{1,0:T(8,128)(2,1)S(1)}, u32[]{:S(2)}, u32[]{:S(2)}) %collective-permute-start.7) | collective-permute-done | bytes 688160 | tf_op jit(solution)/shard_map/ppermute | solution.py:57
  56.3 2.6 %shard_map.329 = (bf16[256,768]{1,0:T(8,128)(2,1)S(1)}, bf16[512,768]{1,0:T(8,128)(2,1)S(1)}, bf16[512,768]{1,0:T(8,128)(2,1)S(1)}) custom-call(bf16[512,768]{1,0:T(8,128)(2,1)S(1)} %pad_maximum_fusion.refs_4_.refs_0_.refs_1_.refs_2_, bf16[384,1792]{1,0:T(8,128)(2,1)S(1)} %get-tuple-element.99.refs_2_.refs_1_.refs_3_, ...), custom_call_target="tpu_custom_call" | custom-call | flops 1509949440 | bytes 7870464 | tf_op jit(solution)/shard_map/pallas_call | solution.py:142
  58.9 8.4 %collective-permute-done.14.refs_3_ = bf16[192,1536]{1,0:T(8,128)(2,1)S(1)} collective-permute-done((bf16[192,1536]{1,0:T(8,128)(2,1)S(1)}, bf16[192,1536]{1,0:T(8,128)(2,1)S(1)}, u32[]{:S(2)}, u32[]{:S(2)}) %collective-permute-start.14) | collective-permute-done | bytes 589856 | tf_op jit(solution)/shard_map/ppermute | solution.py:57
  68.5 1.7 shard_map.330
  81.5 7.9 %shard_map.331.refs_0_.refs_7_ = bf16[256,768]{1,0:T(8,128)(2,1)S(1)} custom-call(s32[1,256]{1,0:T(1,128)S(1)} %bitcast.65, s32[512,1]{1,0:T(8,128)S(1)} %copy-done.16, bf16[256,768]{1,0:T(8,128)(2,1)S(1)} %copy-done.10, bf16[512,768]{1,0:T(8,128)(2,1)S(1)} %copy-done.21, bf16[512,768]{1,0:T(8,128)(2,1)S(1)} %copy-done.24, ...), custom_call_target="tpu_custom_call" | custom-call | flops 905969664 | bytes 2362368 | tf_op jit(solution)/shard_map/pallas_call | solution.py:142
  90.5 8.5 %collective-permute-done.18.refs_1_ = bf16[384,1536]{1,0:T(8,128)(2,1)} collective-permute-done((bf16[384,1536]{1,0:T(8,128)(2,1)}, bf16[384,1536]{1,0:T(8,128)(2,1)}, u32[]{:S(2)}, u32[]{:S(2)}) %collective-permute-start.18) | collective-permute-done | bytes 1179680 | tf_op jit(solution)/shard_map/ppermute | solution.py:61
  102.3 4.8 %shard_map.334 = (bf16[256,3072]{1,0:T(8,128)(2,1)S(1)}, f32[256,3072]{1,0:T(8,128)S(1)}) custom-call(bf16[256,768]{1,0:T(8,128)(2,1)S(1)} %get-tuple-element.110.refs_2_.refs_0_, bf16[192,3072]{1,0:T(8,128)(2,1)} %get-tuple-element.107.refs_5_.refs_1_, bf16[192,3072]{1,0:T(8,128)(2,1)} %get-tuple-element.111.refs_2_, ...), custom_call_target="tpu_custom_call" | custom-call | flops 2415919104 | bytes 9842688 | tf_op jit(solution)/shard_map/pallas_call | solution.py:142
  107.1 4.4 %shard_map.335 = (bf16[256,768]{1,0:T(8,128)(2,1)S(1)}, f32[256,768]{1,0:T(8,128)S(1)}, bf16[256,768]{1,0:T(8,128)(2,1)S(1)}, f32[8,768]{1,0:T(8,128)S(1)}) custom-call(bf16[256,3072]{1,0:T(8,128)(2,1)S(1)} %get-tuple-element.113.refs_0_, bf16[384,1536]{1,0:T(8,128)(2,1)} %get-tuple-element.109.refs_1_, bf16[384,1536]{1,0:T(8,128)(2,1)} %get-tuple-element.114.refs_2_, ...), custom_call_target="tpu_custom_call" | custom-call | flops 1509949440 | bytes 9481216 | tf_op jit(solution)/shard_map/pallas_call | solution.py:142
  112.5 3.8 %shard_map.336 = (bf16[256,3072]{1,0:T(8,128)(2,1)S(1)}, f32[1,3072]{1,0:T(1,128)S(1)}) custom-call(bf16[256,768]{1,0:T(8,128)(2,1)S(1)} %get-tuple-element.117.refs_0_, bf16[384,1536]{1,0:T(8,128)(2,1)} %get-tuple-element.109.refs_1_, bf16[384,1536]{1,0:T(8,128)(2,1)} %get-tuple-element.114.refs_2_, ...), custom_call_target="tpu_custom_call" | custom-call | flops 1811939328 | bytes 9842688 | tf_op jit(solution)/shard_map/pallas_call | solution.py:142
  119.2 11.6 %shard_map.337 = (bf16[384,1536]{1,0:T(8,128)(2,1)S(1)}, bf16[384,1536]{1,0:T(8,128)(2,1)S(1)}) custom-call(bf16[384,3072]{1,0:T(8,128)(2,1)S(1)} %convolution_convert_fusion.1.refs_0_, bf16[384,3072]{1,0:T(8,128)(2,1)S(1)} %collective-permute-done.22.refs_1_, bf16[256,3072]{1,0:T(8,128)(2,1)S(1)} %get-tuple-element.119.refs_2_.refs_0_), custom_call_target="tpu_custom_call" | custom-call | flops 120795955200 | bytes 7077888 | tf_op jit(solution)/shard_map/pallas_call | solution.py:142
  134.2 4.9 %shard_map.339 = (f32[256,768]{1,0:T(8,128)S(1)}, bf16[256,768]{1,0:T(8,128)(2,1)S(1)}, bf16[256,768]{1,0:T(8,128)(2,1)S(1)}, f32[8,768]{1,0:T(8,128)S(1)}) custom-call(bf16[256,3072]{1,0:T(8,128)(2,1)S(1)} %get-tuple-element.119.refs_2_.refs_0_, bf16[192,3072]{1,0:T(8,128)(2,1)} %get-tuple-element.107.refs_5_.refs_1_, ...), custom_call_target="tpu_custom_call" | custom-call | flops 1811939328 | bytes 11840512 | tf_op jit(solution)/shard_map/pallas_call | solution.py:142
  139.1 10.0 %shard_map.340 = (bf16[256,768]{1,0:T(8,128)(2,1)S(1)}, bf16[512,768]{1,0:T(8,128)(2,1)S(1)}, bf16[512,768]{1,0:T(8,128)(2,1)S(1)}) custom-call(s32[1,256]{1,0:T(1,128)S(1)} %bitcast.66, s32[512,1]{1,0:T(8,128)S(1)} %copy-done.17, bf16[256,768]{1,0:T(8,128)(2,1)S(1)} %copy-done.11, bf16[512,768]{1,0:T(8,128)(2,1)S(1)} %copy-done.22, ...), custom_call_target="tpu_custom_call" | custom-call | flops 1509949440 | bytes 4328448 | tf_op jit(solution)/shard_map/pallas_call | solution.py:142
  149.1 3.1 %shard_map.341 = (bf16[384,1792]{1,0:T(8,128)(2,1)S(1)}, bf16[384,1536]{1,0:T(8,128)(2,1)S(1)}, bf16[384,1792]{1,0:T(8,128)(2,1)S(1)}, bf16[384,1536]{1,0:T(8,128)(2,1)S(1)}) custom-call(s32[1]{0:T(128)} %bitcast.12.refs_0_, bf16[768,768]{1,0:T(8,128)(2,1)S(1)} %copy-done.7, bf16[512,768]{1,0:T(8,128)(2,1)S(1)} %pad_maximum_fusion.refs_4_.refs_0_.refs_1_.refs_2_, ...), custom_call_target="tpu_custom_call" | custom-call | flops 1811939328 | bytes 9891844 | tf_op jit(solution)/shard_map/pallas_call | solution.py:142
  152.8 6.1 %collective-permute-done.24.refs_3_ = bf16[384,1536]{1,0:T(8,128)(2,1)S(1)} collective-permute-done((bf16[384,1536]{1,0:T(8,128)(2,1)S(1)}, bf16[384,1536]{1,0:T(8,128)(2,1)S(1)}, u32[]{:S(2)}, u32[]{:S(2)}) %collective-permute-start.24) | collective-permute-done | bytes 1179680 | tf_op jit(solution)/shard_map/ppermute | solution.py:61
  158.9 1.8 collective-permute-done.23.refs_1_
  162.5 2.6 %shard_map.343 = (f32[256,768]{1,0:T(8,128)S(1)}, bf16[256,768]{1,0:T(8,128)(2,1)S(1)}) custom-call(bf16[256,768]{1,0:T(8,128)(2,1)S(1)} %get-tuple-element.126.refs_3_.refs_0_, bf16[512,768]{1,0:T(8,128)(2,1)S(1)} %get-tuple-element.127.refs_4_.refs_1_, bf16[512,768]{1,0:T(8,128)(2,1)S(1)} %get-tuple-element.128.refs_5_.refs_2_, ...), custom_call_target="tpu_custom_call" | custom-call | flops 120795955200 | bytes 9043968 | tf_op jit(solution)/shard_map/pallas_call | solution.py:142
  168.7 8.9 %collective-permute-done.29.refs_1_ = bf16[192,1536]{1,0:T(8,128)(2,1)S(1)} collective-permute-done((bf16[192,1536]{1,0:T(8,128)(2,1)S(1)}, bf16[192,1536]{1,0:T(8,128)(2,1)S(1)}, u32[]{:S(2)}, u32[]{:S(2)}) %collective-permute-start.29) | collective-permute-done | bytes 589856 | tf_op jit(solution)/shard_map/ppermute | solution.py:61
  178.9 2.2 %collective-permute-start.34 = (bf16[48,3072]{1,0:T(8,128)(2,1)S(1)}, bf16[48,3072]{1,0:T(8,128)(2,1)S(1)}, u32[]{:S(2)}, u32[]{:S(2)}) collective-permute-start(bf16[48,3072]{1,0:T(8,128)(2,1)S(1)} %get-tuple-element.156), channel_id=1, source_target_pairs={{0,16},{2,18},{4,20},{6,22},{8,24},{10,26},{12,28},{14,30},{16,0},... | collective-permute-start | bytes 884744 | tf_op jit(solution)/shard_map/ppermute | solution.py:57
  181.1 1.8 collective-permute-start.35
  182.9 5.3 %collective-permute-done.28.refs_3_ = bf16[384,768]{1,0:T(8,128)(2,1)S(1)} collective-permute-done((bf16[384,768]{1,0:T(8,128)(2,1)S(1)}, bf16[384,768]{1,0:T(8,128)(2,1)S(1)}, u32[]{:S(2)}, u32[]{:S(2)}) %collective-permute-start.28) | collective-permute-done | bytes 589856 | tf_op jit(solution)/shard_map/ppermute | solution.py:61
  188.2 2.3 %collective-permute-done.27.refs_1_ = bf16[192,1792]{1,0:T(8,128)(2,1)S(1)} collective-permute-done((bf16[192,1792]{1,0:T(8,128)(2,1)S(1)}, bf16[192,1792]{1,0:T(8,128)(2,1)S(1)}, u32[]{:S(2)}, u32[]{:S(2)}) %collective-permute-start.27) | collective-permute-done | bytes 688160 | tf_op jit(solution)/shard_map/ppermute | solution.py:57
  192.9 6.8 %collective-permute-done.34.refs_2_ = bf16[48,3072]{1,0:T(8,128)(2,1)S(1)} collective-permute-done((bf16[48,3072]{1,0:T(8,128)(2,1)S(1)}, bf16[48,3072]{1,0:T(8,128)(2,1)S(1)}, u32[]{:S(2)}, u32[]{:S(2)}) %collective-permute-start.34) | collective-permute-done | bytes 294944 | tf_op jit(solution)/shard_map/ppermute | solution.py:57
  202.1 3.9 %collective-permute-start.37 = (bf16[48,1664]{1,0:T(8,128)(2,1)S(1)}, bf16[48,1664]{1,0:T(8,128)(2,1)S(1)}, u32[]{:S(2)}, u32[]{:S(2)}) collective-permute-start(bf16[48,1664]{1,0:T(8,128)(2,1)S(1)} %get-tuple-element.159), channel_id=1, source_target_pairs={{0,8},{2,10},{4,12},{6,14},{8,0},{10,2},{12,4},{14,6},{16,24},{18,... | collective-permute-start | bytes 479240 | tf_op jit(solution)/shard_map/ppermute | solution.py:57
  211.0 5.2 %collective-permute-done.36.refs_1_ = bf16[256,768]{1,0:T(8,128)(2,1)S(1)} collective-permute-done((bf16[256,768]{1,0:T(8,128)(2,1)S(1)}, bf16[256,768]{1,0:T(8,128)(2,1)S(1)}, u32[]{:S(2)}, u32[]{:S(2)}) %collective-permute-start.36) | collective-permute-done | bytes 393248 | tf_op jit(solution)/shard_map/ppermute | solution.py:61
  216.2 2.1 shard_map.350.refs_14_
  (195 shorter events, 61.3 us)
Async XLA Ops:
  3.6 10.2 %collective-permute-start.3 = (bf16[48,1664]{1,0:T(8,128)(2,1)S(1)}, bf16[48,1664]{1,0:T(8,128)(2,1)S(1)}, u32[]{:S(2)}, u32[]{:S(2)}) collective-permute-start(bf16[48,1664]{1,0:T(8,128)(2,1)S(1)} %convert_dynamic-update-slice_fusion.refs_0_), channel_id=1, source_target_pairs={{0,24},{2,26},{4,28},{6,30},{8,16},{10,18},{12,20},{14,22},{16,8},... | collective-permute-start | bytes 479240 | tf_op jit(solution)/shard_map/ppermute | solution.py:57
  8.7 13.5 %collective-permute-start.2 = (bf16[48,1664]{1,0:T(8,128)(2,1)S(1)}, bf16[48,1664]{1,0:T(8,128)(2,1)S(1)}, u32[]{:S(2)}, u32[]{:S(2)}) collective-permute-start(bf16[48,1664]{1,0:T(8,128)(2,1)S(1)} %convert_dynamic-update-slice_fusion.refs_0_), channel_id=1, source_target_pairs={{0,16},{2,18},{4,20},{6,22},{8,24},{10,26},{12,28},{14,30},{16,0},... | collective-permute-start | bytes 479240 | tf_op jit(solution)/shard_map/ppermute | solution.py:57
  8.7 13.5 %collective-permute-start.1 = (bf16[48,1664]{1,0:T(8,128)(2,1)S(1)}, bf16[48,1664]{1,0:T(8,128)(2,1)S(1)}, u32[]{:S(2)}, u32[]{:S(2)}) collective-permute-start(bf16[48,1664]{1,0:T(8,128)(2,1)S(1)} %convert_dynamic-update-slice_fusion.refs_0_), channel_id=1, source_target_pairs={{0,8},{2,10},{4,12},{6,14},{8,0},{10,2},{12,4},{14,6},{16,24},{18,... | collective-permute-start | bytes 479240 | tf_op jit(solution)/shard_map/ppermute | solution.py:57
  9.4 19.0 %collective-permute-start = (bf16[256,768]{1,0:T(8,128)(2,1)}, bf16[256,768]{1,0:T(8,128)(2,1)S(1)}, u32[]{:S(2)}, u32[]{:S(2)}) collective-permute-start(bf16[256,768]{1,0:T(8,128)(2,1)} %param.20), channel_id=1, source_target_pairs={{0,1},{1,0},{2,3},{3,2},{4,5},{5,4},{6,7},{7,6},{8,9},{9,8},{10,11... | collective-permute-start | bytes 1179656 | tf_op jit(solution)/shard_map/ppermute | solution.py:61
  22.4 15.9 %collective-permute-start.10 = (bf16[48,3072]{1,0:T(8,128)(2,1)S(1)}, bf16[48,3072]{1,0:T(8,128)(2,1)S(1)}, u32[]{:S(2)}, u32[]{:S(2)}) collective-permute-start(bf16[48,3072]{1,0:T(8,128)(2,1)S(1)} %shard_map.325.refs_0_), channel_id=1, source_target_pairs={{0,24},{2,26},{4,28},{6,30},{8,16},{10,18},{12,20},{14,22},{16,8},... | collective-permute-start | bytes 884744 | tf_op jit(solution)/shard_map/ppermute | solution.py:57
  24.9 23.4 %collective-permute-start.9 = (bf16[48,3072]{1,0:T(8,128)(2,1)S(1)}, bf16[48,3072]{1,0:T(8,128)(2,1)S(1)}, u32[]{:S(2)}, u32[]{:S(2)}) collective-permute-start(bf16[48,3072]{1,0:T(8,128)(2,1)S(1)} %shard_map.325.refs_0_), channel_id=1, source_target_pairs={{0,16},{2,18},{4,20},{6,22},{8,24},{10,26},{12,28},{14,30},{16,0},... | collective-permute-start | bytes 884744 | tf_op jit(solution)/shard_map/ppermute | solution.py:57
  25.0 23.4 %collective-permute-start.8 = (bf16[48,3072]{1,0:T(8,128)(2,1)S(1)}, bf16[48,3072]{1,0:T(8,128)(2,1)S(1)}, u32[]{:S(2)}, u32[]{:S(2)}) collective-permute-start(bf16[48,3072]{1,0:T(8,128)(2,1)S(1)} %shard_map.325.refs_0_), channel_id=1, source_target_pairs={{0,8},{2,10},{4,12},{6,14},{8,0},{10,2},{12,4},{14,6},{16,24},{18,... | collective-permute-start | bytes 884744 | tf_op jit(solution)/shard_map/ppermute | solution.py:57
  35.4 13.1 %collective-permute-start.6 = (bf16[384,768]{1,0:T(8,128)(2,1)S(1)}, bf16[384,768]{1,0:T(8,128)(2,1)S(1)}, u32[]{:S(2)}, u32[]{:S(2)}) collective-permute-start(bf16[384,768]{1,0:T(8,128)(2,1)S(1)} %get-tuple-element.96.refs_0_), channel_id=1, source_target_pairs={{0,1},{1,0},{2,3},{3,2},{4,5},{5,4},{6,7},{7,6},{8,9},{9,8},{10,11... | collective-permute-start | bytes 1769480 | tf_op jit(solution)/shard_map/ppermute | solution.py:61
  36.8 14.4 %collective-permute-start.7 = (bf16[192,1792]{1,0:T(8,128)(2,1)S(1)}, bf16[192,1792]{1,0:T(8,128)(2,1)S(1)}, u32[]{:S(2)}, u32[]{:S(2)}) collective-permute-start(bf16[192,1792]{1,0:T(8,128)(2,1)S(1)} %get-tuple-element.97.refs_1_), channel_id=1, source_target_pairs={{0,4},{2,6},{4,0},{6,2},{8,12},{10,14},{12,8},{14,10},{16,20},{18,... | collective-permute-start | bytes 2064392 | tf_op jit(solution)/shard_map/ppermute | solution.py:57
  52.0 15.3 %collective-permute-start.14 = (bf16[192,1536]{1,0:T(8,128)(2,1)S(1)}, bf16[192,1536]{1,0:T(8,128)(2,1)S(1)}, u32[]{:S(2)}, u32[]{:S(2)}) collective-permute-start(bf16[192,1536]{1,0:T(8,128)(2,1)S(1)} %get-tuple-element.106.refs_1_), channel_id=1, source_target_pairs={{0,4},{2,6},{4,0},{6,2},{8,12},{10,14},{12,8},{14,10},{16,20},{18,... | collective-permute-start | bytes 1769480 | tf_op jit(solution)/shard_map/ppermute | solution.py:57
  53.5 15.0 %collective-permute-start.13 = (bf16[192,1536]{1,0:T(8,128)(2,1)S(1)}, bf16[192,1536]{1,0:T(8,128)(2,1)S(1)}, u32[]{:S(2)}, u32[]{:S(2)}) collective-permute-start(bf16[192,1536]{1,0:T(8,128)(2,1)S(1)} %get-tuple-element.98.refs_4_.refs_0_), channel_id=1, source_target_pairs={{0,1},{1,0},{2,3},{3,2},{4,5},{5,4},{6,7},{7,6},{8,9},{9,8},{10,11... | collective-permute-start | bytes 1769480 | tf_op jit(solution)/shard_map/ppermute | solution.py:61
  70.2 19.2 %collective-permute-start.16 = (bf16[384,1536]{1,0:T(8,128)(2,1)}, bf16[384,1536]{1,0:T(8,128)(2,1)}, u32[]{:S(2)}, u32[]{:S(2)}) collective-permute-start(bf16[384,1536]{1,0:T(8,128)(2,1)} %get-tuple-element.109.refs_1_), channel_id=1, source_target_pairs={{0,2},{2,0},{4,6},{6,4},{8,10},{10,8},{12,14},{14,12},{16,18},{18,... | collective-permute-start | bytes 3538952 | tf_op jit(solution)/shard_map/ppermute | solution.py:57
  70.2 19.2 %collective-permute-start.15 = (bf16[192,3072]{1,0:T(8,128)(2,1)}, bf16[192,3072]{1,0:T(8,128)(2,1)}, u32[]{:S(2)}, u32[]{:S(2)}) collective-permute-start(bf16[192,3072]{1,0:T(8,128)(2,1)} %get-tuple-element.107.refs_5_.refs_1_), channel_id=1, source_target_pairs={{0,2},{2,0},{4,6},{6,4},{8,10},{10,8},{12,14},{14,12},{16,18},{18,... | collective-permute-start | bytes 3538952 | tf_op jit(solution)/shard_map/ppermute | solution.py:57
  70.7 28.3 %collective-permute-start.18 = (bf16[384,1536]{1,0:T(8,128)(2,1)}, bf16[384,1536]{1,0:T(8,128)(2,1)}, u32[]{:S(2)}, u32[]{:S(2)}) collective-permute-start(bf16[384,1536]{1,0:T(8,128)(2,1)} %get-tuple-element.109.refs_1_), channel_id=1, source_target_pairs={{0,1},{1,0},{2,3},{3,2},{4,5},{5,4},{6,7},{7,6},{8,9},{9,8},{10,11... | collective-permute-start | bytes 3538952 | tf_op jit(solution)/shard_map/ppermute | solution.py:61
  71.2 28.0 %collective-permute-start.17 = (bf16[192,3072]{1,0:T(8,128)(2,1)}, bf16[192,3072]{1,0:T(8,128)(2,1)}, u32[]{:S(2)}, u32[]{:S(2)}) collective-permute-start(bf16[192,3072]{1,0:T(8,128)(2,1)} %get-tuple-element.107.refs_5_.refs_1_), channel_id=1, source_target_pairs={{0,4},{2,6},{4,0},{6,2},{8,12},{10,14},{12,8},{14,10},{16,20},{18,... | collective-permute-start | bytes 3538952 | tf_op jit(solution)/shard_map/ppermute | solution.py:57
  117.1 15.3 %collective-permute-start.21 = (bf16[384,3072]{1,0:T(8,128)(2,1)S(1)}, bf16[384,3072]{1,0:T(8,128)(2,1)S(1)}, u32[]{:S(2)}, u32[]{:S(2)}) collective-permute-start(bf16[384,3072]{1,0:T(8,128)(2,1)S(1)} %convolution_convert_fusion.2), channel_id=1, source_target_pairs={{0,2},{2,0},{4,6},{6,4},{8,10},{10,8},{12,14},{14,12},{16,18},{18,... | collective-permute-start | bytes 7077896 | tf_op jit(solution)/shard_map/ppermute | solution.py:57
  130.8 28.1 %collective-permute-start.24 = (bf16[384,1536]{1,0:T(8,128)(2,1)S(1)}, bf16[384,1536]{1,0:T(8,128)(2,1)S(1)}, u32[]{:S(2)}, u32[]{:S(2)}) collective-permute-start(bf16[384,1536]{1,0:T(8,128)(2,1)S(1)} %get-tuple-element.131), channel_id=1, source_target_pairs={{0,1},{1,0},{2,3},{3,2},{4,5},{5,4},{6,7},{7,6},{8,9},{9,8},{10,11... | collective-permute-start | bytes 3538952 | tf_op jit(solution)/shard_map/ppermute | solution.py:61
  132.9 27.8 %collective-permute-start.23 = (bf16[192,3072]{1,0:T(8,128)(2,1)S(1)}, bf16[192,3072]{1,0:T(8,128)(2,1)S(1)}, u32[]{:S(2)}, u32[]{:S(2)}) collective-permute-start(bf16[192,3072]{1,0:T(8,128)(2,1)S(1)} %get-tuple-element.130), channel_id=1, source_target_pairs={{0,4},{2,6},{4,0},{6,2},{8,12},{10,14},{12,8},{14,10},{16,20},{18,... | collective-permute-start | bytes 3538952 | tf_op jit(solution)/shard_map/ppermute | solution.py:57
  152.2 12.9 %collective-permute-start.26 = (bf16[384,1536]{1,0:T(8,128)(2,1)S(1)}, bf16[384,1536]{1,0:T(8,128)(2,1)S(1)}, u32[]{:S(2)}, u32[]{:S(2)}) collective-permute-start(bf16[384,1536]{1,0:T(8,128)(2,1)S(1)} %get-tuple-element.142), channel_id=1, source_target_pairs={{0,2},{2,0},{4,6},{6,4},{8,10},{10,8},{12,14},{14,12},{16,18},{18,... | collective-permute-start | bytes 3538952 | tf_op jit(solution)/shard_map/ppermute | solution.py:57
  152.3 12.9 %collective-permute-start.25 = (bf16[384,1792]{1,0:T(8,128)(2,1)S(1)}, bf16[384,1792]{1,0:T(8,128)(2,1)S(1)}, u32[]{:S(2)}, u32[]{:S(2)}) collective-permute-start(bf16[384,1792]{1,0:T(8,128)(2,1)S(1)} %get-tuple-element.140), channel_id=1, source_target_pairs={{0,2},{2,0},{4,6},{6,4},{8,10},{10,8},{12,14},{14,12},{16,18},{18,... | collective-permute-start | bytes 4128776 | tf_op jit(solution)/shard_map/ppermute | solution.py:57
  161.3 16.3 %collective-permute-start.29 = (bf16[192,1536]{1,0:T(8,128)(2,1)S(1)}, bf16[192,1536]{1,0:T(8,128)(2,1)S(1)}, u32[]{:S(2)}, u32[]{:S(2)}) collective-permute-start(bf16[192,1536]{1,0:T(8,128)(2,1)S(1)} %get-tuple-element.147), channel_id=1, source_target_pairs={{0,1},{1,0},{2,3},{3,2},{4,5},{5,4},{6,7},{7,6},{8,9},{9,8},{10,11... | collective-permute-start | bytes 1769480 | tf_op jit(solution)/shard_map/ppermute | solution.py:61
  161.9 16.3 %collective-permute-start.30 = (bf16[192,1536]{1,0:T(8,128)(2,1)S(1)}, bf16[192,1536]{1,0:T(8,128)(2,1)S(1)}, u32[]{:S(2)}, u32[]{:S(2)}) collective-permute-start(bf16[192,1536]{1,0:T(8,128)(2,1)S(1)} %get-tuple-element.149), channel_id=1, source_target_pairs={{0,4},{2,6},{4,0},{6,2},{8,12},{10,14},{12,8},{14,10},{16,20},{18,... | collective-permute-start | bytes 1769480 | tf_op jit(solution)/shard_map/ppermute | solution.py:57
  165.7 24.8 %collective-permute-start.27 = (bf16[192,1792]{1,0:T(8,128)(2,1)S(1)}, bf16[192,1792]{1,0:T(8,128)(2,1)S(1)}, u32[]{:S(2)}, u32[]{:S(2)}) collective-permute-start(bf16[192,1792]{1,0:T(8,128)(2,1)S(1)} %get-tuple-element.144), channel_id=1, source_target_pairs={{0,4},{2,6},{4,0},{6,2},{8,12},{10,14},{12,8},{14,10},{16,20},{18,... | collective-permute-start | bytes 2064392 | tf_op jit(solution)/shard_map/ppermute | solution.py:57
  167.2 21.0 %collective-permute-start.28 = (bf16[384,768]{1,0:T(8,128)(2,1)S(1)}, bf16[384,768]{1,0:T(8,128)(2,1)S(1)}, u32[]{:S(2)}, u32[]{:S(2)}) collective-permute-start(bf16[384,768]{1,0:T(8,128)(2,1)S(1)} %get-tuple-element.146), channel_id=1, source_target_pairs={{0,1},{1,0},{2,3},{3,2},{4,5},{5,4},{6,7},{7,6},{8,9},{9,8},{10,11... | collective-permute-start | bytes 1769480 | tf_op jit(solution)/shard_map/ppermute | solution.py:61
  178.4 14.5 %collective-permute-start.33 = (bf16[48,3072]{1,0:T(8,128)(2,1)S(1)}, bf16[48,3072]{1,0:T(8,128)(2,1)S(1)}, u32[]{:S(2)}, u32[]{:S(2)}) collective-permute-start(bf16[48,3072]{1,0:T(8,128)(2,1)S(1)} %get-tuple-element.155), channel_id=1, source_target_pairs={{0,8},{2,10},{4,12},{6,14},{8,0},{10,2},{12,4},{14,6},{16,24},{18,... | collective-permute-start | bytes 884744 | tf_op jit(solution)/shard_map/ppermute | solution.py:57
  178.9 20.8 %collective-permute-start.34 = (bf16[48,3072]{1,0:T(8,128)(2,1)S(1)}, bf16[48,3072]{1,0:T(8,128)(2,1)S(1)}, u32[]{:S(2)}, u32[]{:S(2)}) collective-permute-start(bf16[48,3072]{1,0:T(8,128)(2,1)S(1)} %get-tuple-element.156), channel_id=1, source_target_pairs={{0,16},{2,18},{4,20},{6,22},{8,24},{10,26},{12,28},{14,30},{16,0},... | collective-permute-start | bytes 884744 | tf_op jit(solution)/shard_map/ppermute | solution.py:57
  181.1 18.6 %collective-permute-start.35 = (bf16[48,3072]{1,0:T(8,128)(2,1)S(1)}, bf16[48,3072]{1,0:T(8,128)(2,1)S(1)}, u32[]{:S(2)}, u32[]{:S(2)}) collective-permute-start(bf16[48,3072]{1,0:T(8,128)(2,1)S(1)} %get-tuple-element.157), channel_id=1, source_target_pairs={{0,24},{2,26},{4,28},{6,30},{8,16},{10,18},{12,20},{14,22},{16,8},... | collective-permute-start | bytes 884744 | tf_op jit(solution)/shard_map/ppermute | solution.py:57
  190.8 11.1 %collective-permute-start.32 = (bf16[192,768]{1,0:T(8,128)(2,1)S(1)}, bf16[192,768]{1,0:T(8,128)(2,1)S(1)}, u32[]{:S(2)}, u32[]{:S(2)}) collective-permute-start(bf16[192,768]{1,0:T(8,128)(2,1)S(1)} %get-tuple-element.154), channel_id=1, source_target_pairs={{0,4},{2,6},{4,0},{6,2},{8,12},{10,14},{12,8},{14,10},{16,20},{18,... | collective-permute-start | bytes 884744 | tf_op jit(solution)/shard_map/ppermute | solution.py:57
  191.4 10.5 %collective-permute-start.31 = (bf16[192,896]{1,0:T(8,128)(2,1)S(1)}, bf16[192,896]{1,0:T(8,128)(2,1)S(1)}, u32[]{:S(2)}, u32[]{:S(2)}) collective-permute-start(bf16[192,896]{1,0:T(8,128)(2,1)S(1)} %get-tuple-element.152), channel_id=1, source_target_pairs={{0,1},{1,0},{2,3},{3,2},{4,5},{5,4},{6,7},{7,6},{8,9},{9,8},{10,11... | collective-permute-start | bytes 1032200 | tf_op jit(solution)/shard_map/ppermute | solution.py:61
  202.1 16.1 %collective-permute-start.37 = (bf16[48,1664]{1,0:T(8,128)(2,1)S(1)}, bf16[48,1664]{1,0:T(8,128)(2,1)S(1)}, u32[]{:S(2)}, u32[]{:S(2)}) collective-permute-start(bf16[48,1664]{1,0:T(8,128)(2,1)S(1)} %get-tuple-element.159), channel_id=1, source_target_pairs={{0,8},{2,10},{4,12},{6,14},{8,0},{10,2},{12,4},{14,6},{16,24},{18,... | collective-permute-start | bytes 479240 | tf_op jit(solution)/shard_map/ppermute | solution.py:57
  206.0 12.3 %collective-permute-start.38 = (bf16[48,1664]{1,0:T(8,128)(2,1)S(1)}, bf16[48,1664]{1,0:T(8,128)(2,1)S(1)}, u32[]{:S(2)}, u32[]{:S(2)}) collective-permute-start(bf16[48,1664]{1,0:T(8,128)(2,1)S(1)} %get-tuple-element.160), channel_id=1, source_target_pairs={{0,16},{2,18},{4,20},{6,22},{8,24},{10,26},{12,28},{14,30},{16,0},... | collective-permute-start | bytes 479240 | tf_op jit(solution)/shard_map/ppermute | solution.py:57
  206.9 11.4 %collective-permute-start.39 = (bf16[48,1664]{1,0:T(8,128)(2,1)S(1)}, bf16[48,1664]{1,0:T(8,128)(2,1)S(1)}, u32[]{:S(2)}, u32[]{:S(2)}) collective-permute-start(bf16[48,1664]{1,0:T(8,128)(2,1)S(1)} %get-tuple-element.161), channel_id=1, source_target_pairs={{0,24},{2,26},{4,28},{6,30},{8,16},{10,18},{12,20},{14,22},{16,8},... | collective-permute-start | bytes 479240 | tf_op jit(solution)/shard_map/ppermute | solution.py:57
  (51 other events, 430.4 us)

commit v6 on v5

--- a/solution.py
+++ b/solution.py
@@ -372,9 +372,24 @@
         )
 
 
-def softmax_down(seg_q, seg_k, key_rows, queries):
+def segment(lengths, positions):
+    end, total = 0, jnp.zeros_like(positions)
+    for place in range(lengths.shape[1]):
+        end = end + lengths[0, place]
+        total = total + (positions >= end).astype(jnp.int32)
+    return total
+
+
+def same_segment(rank, lengths, keys, queries):
+    own = lax.broadcasted_iota(jnp.int32, (1, queries), 1) + rank * queries
+    rows = lax.broadcasted_iota(jnp.int32, (keys, 1), 0)
+    rows = jnp.where(rows < queries, rows + rank * queries, rows - rank * queries)
+    return segment(lengths, rows) == segment(lengths, own)
+
+
+def softmax_down(same, key_rows, queries):
     scores = dot_nt(key_rows, queries) * 0.125
-    scores = jnp.where(seg_k[...] == seg_q[...], scores, NEG_FILL)
+    scores = jnp.where(same, scores, NEG_FILL)
     exp_scores = jnp.exp(scores - jnp.max(scores, axis=0, keepdims=True))
     return exp_scores * (1.0 / jnp.sum(exp_scores, axis=0, keepdims=True))
 
@@ -384,26 +399,26 @@
     return jnp.transpose(joined).astype(LOW)
 
 
-def attend_kernel(seg_q, seg_k, q, k, v, attended):
+def attend_kernel(rank_ref, lengths, q, k, v, attended):
     queries, key_rows, value_rows = q[...], k[...], v[...]
+    same = same_segment(rank_ref[0], lengths, k.shape[0], q.shape[0])
     first = lax.broadcasted_iota(jnp.int32, queries.shape, 1) < HEAD_DIM
     out = []
     for mine in (first, jnp.logical_not(first)):
-        prob = softmax_down(
-            seg_q, seg_k, key_rows, jnp.where(mine, queries, jnp.zeros_like(queries))
-        )
+        prob = softmax_down(same, key_rows, jnp.where(mine, queries, jnp.zeros_like(queries)))
         out.append(dot_tn(value_rows, prob.astype(LOW)))
     attended[...] = two_heads(out)
 
 
-def attend_back_kernel(seg_q, seg_k, q, k, v, grad, grad_q, grad_k, grad_v):
+def attend_back_kernel(rank_ref, lengths, q, k, v, grad, grad_q, grad_k, grad_v):
     queries, key_rows, value_rows, grad_rows = q[...], k[...], v[...], grad[...]
+    same = same_segment(rank_ref[0], lengths, k.shape[0], q.shape[0])
     first = lax.broadcasted_iota(jnp.int32, queries.shape, 1) < HEAD_DIM
     first_all = lax.broadcasted_iota(jnp.int32, key_rows.shape, 1) < HEAD_DIM
     blank = jnp.zeros_like(queries)
     out_q, out_k, out_v = [], [], []
     for mine in (first, jnp.logical_not(first)):
-        prob = softmax_down(seg_q, seg_k, key_rows, jnp.where(mine, queries, blank))
+        prob = softmax_down(same, key_rows, jnp.where(mine, queries, blank))
         grad_prob = dot_nt(value_rows, jnp.where(mine, grad_rows, blank))
         delta = jnp.sum(grad_prob * prob, axis=0, keepdims=True)
         grad_score = (prob * (grad_prob - delta)).astype(LOW)
@@ -451,7 +466,8 @@
 
 
 def out_back_kernel(
-    activation, own, own_side, far, far_side, y, cot, valid, vec, mixed, grad, grad_low, sums
+    rank_ref, lengths, activation, own, own_side, far, far_side, y, cot, vec,
+    mixed, grad, grad_low, sums,
 ):
     columns = own.shape[1]
     near, side = activation[:, :columns], activation[:, columns:]
@@ -462,9 +478,9 @@
     total = y[...] + jnp.concatenate(out, axis=1) + vec[3:4]
     result, normed, inv_std = normalize_fwd(total, vec[4:5], vec[5:6])
     mixed[...] = result.astype(LOW)
-    grad_in, gain_sum, shift_sum = normalize_back(
-        cot[...] * valid[...], normed, inv_std, vec[4:5]
-    )
+    rows = lax.broadcasted_iota(jnp.int32, (y.shape[0], 1), 0) + rank_ref[0] * y.shape[0]
+    valid = (segment(lengths, rows) < lengths.shape[1]).astype(F32)
+    grad_in, gain_sum, shift_sum = normalize_back(cot[...] * valid, normed, inv_std, vec[4:5])
     grad[...] = grad_in
     grad_low[...] = grad_in.astype(LOW)
     sums[0:1] = jnp.sum(grad_in, axis=0, keepdims=True)
@@ -699,17 +715,6 @@
         in_specs=[scalar, vmem, vmem, vmem],
     )
 
-    seq_ends = jnp.cumsum(lengths[0])
-    local = jnp.arange(own_rows, dtype=jnp.int32)
-    own_positions = tensor_rank * own_rows + local
-    key_positions = jnp.concatenate([own_positions, (1 - tensor_rank) * own_rows + local])
-
-    def segments(positions):
-        return jnp.sum((positions[:, None] >= seq_ends[None, :]).astype(jnp.int32), axis=1)
-
-    seg_own, seg_keys = segments(own_positions)[None, :], segments(key_positions)[:, None]
-    valid = (own_positions < seq_ends[-1]).astype(F32)[:, None]
-
     wide_low = shape_of(own_rows, width, LOW)
     wide = shape_of(own_rows, width, F32)
     group_low = shape_of(group_rows, width, LOW)
@@ -728,17 +733,14 @@
     own_block = pl.BlockSpec((own_rows, LANES), lambda i: (0, i))
     all_block = pl.BlockSpec((group_rows, LANES), lambda i: (0, i))
 
-    def fixed(shape):
-        return pl.BlockSpec(shape, lambda i: (0, 0))
-
     attended = run(
         attend_kernel,
         [wide_low],
-        [seg_own, seg_keys, queries, key_rows, value_rows],
+        [rank, lengths, queries, key_rows, value_rows],
         3 * unit,
         after=pair[:1],
         grid=(pairs,),
-        in_specs=[fixed((1, own_rows)), fixed((group_rows, 1)), own_block, all_block, all_block],
+        in_specs=[scalar, scalar, own_block, all_block, all_block],
         out_specs=[own_block],
     )[0]
     first_norm, first_low, normed_one, inv_one = run(
@@ -760,8 +762,9 @@
     mixed_rel, grad_two, grad_two_low, sums_two = run(
         out_back_kernel,
         [wide_low, wide, wide_low, sums_shape],
-        [activation, *pieces_back, first_norm, cot, valid, vec],
+        [rank, lengths, activation, *pieces_back, first_norm, cot, vec],
         5 * unit,
+        in_specs=[scalar, scalar] + [vmem] * 8,
     )
     mixed = dot_nt(mixed_rel, permute).astype(LOW)
 
@@ -790,11 +793,10 @@
     grad_q, grad_k, grad_v = run(
         attend_back_kernel,
         [wide_low, group_low, group_low],
-        [seg_own, seg_keys, queries, key_rows, value_rows, grad_attn],
+        [rank, lengths, queries, key_rows, value_rows, grad_attn],
         5 * unit,
         grid=(pairs,),
-        in_specs=[fixed((1, own_rows)), fixed((group_rows, 1))]
-        + [own_block, all_block, all_block, own_block],
+        in_specs=[scalar, scalar, own_block, all_block, all_block, own_block],
         out_specs=[own_block, all_block, all_block],
     )
     a_shape, b_shape = shape_of(half, 2 * a_width, LOW), shape_of(half, 4 * part, LOW)

time: 224 us -> 205 us (0.915); the launches traced: 221 us -> 205 us
  Pallas kernels: 65.6 us -> 46.4 us
  waiting for transfers between devices: 83.3 us -> 99.5 us
  local copies, waits for them, and re-layouts: 10.1 us -> 3.02 us
  other arithmetic: 9.39 us -> 5.29 us
    pallas_call x27, Pallas kernels: 65.5 us -> 46.4 us  [run(): pl.pallas_call(body, grid=grid, out_shape=list(outs), in_specs=list(in_sp...]
    ppermute x10, waiting for transfers between devices: 35.3 us -> 45.6 us  [swap_tensor(): return lax.ppermute(values, 'tensor', [(0, 1), (1, 0)])]
    ppermute x30, waiting for transfers between devices: 48 us -> 53.9 us  [swap_dp(): return lax.ppermute(values, 'dp', [(i, i ^ mask) for i in range(size)])]
    unnamed x90 -> x58, local copies, waits for them, and re-layouts: 8 us -> 3.02 us
  transfers between devices with their start and end apart: 40 -> 40, of which waited for: 20 -> 21; matrix products, arithmetic and copies ran while one was open for 7% -> 4% of each run, Pallas kernels for 26% -> 20%
where the time goes in v6:
time: 205 us
  waiting for transfers between devices  99.5 us (49%)
  Pallas kernels  46.4 us (23%)
  starting transfers between devices  42.6 us (21%)
  matrix products  6.75 us (3%)
  other arithmetic  5.29 us (3%)
  local copies, waits for them, and re-layouts  3.02 us (1%)
    ppermute x30, waiting for transfers between devices, swap_dp(): return lax.ppermute(values, 'dp', [(i, i ^ mask) for i in range(size)])  53.9 us
    pallas_call x27, Pallas kernels, run(): pl.pallas_call(body, grid=grid, out_shape=list(outs), in_specs=list(in_sp...  46.4 us
    ppermute x10, waiting for transfers between devices, swap_tensor(): return lax.ppermute(values, 'tensor', [(0, 1), (1, 0)])  45.6 us
    ppermute x30, starting transfers between devices, swap_dp(): return lax.ppermute(values, 'dp', [(i, i ^ mask) for i in range(size)])  32.1 us
    ppermute x10, starting transfers between devices, swap_tensor(): return lax.ppermute(values, 'tensor', [(0, 1), (1, 0)])  10.6 us
  transfers between devices with their start and end apart: 40, of which 21 were waited for; matrix products, arithmetic and copies ran while one was open for 4% of the time, Pallas kernels for 20%

profile of v6, /device:TPU:0, one launch (start us, length us, event | category | flops | bytes accessed | tf_op | source)
XLA Modules:
  0.0 205.1 jit_solution(7475457976744521340)
XLA Ops:
  3.6 5.1 %collective-permute-start.3 = (bf16[48,1664]{1,0:T(8,128)(2,1)S(1)}, bf16[48,1664]{1,0:T(8,128)(2,1)S(1)}, u32[]{:S(2)}, u32[]{:S(2)}) collective-permute-start(bf16[48,1664]{1,0:T(8,128)(2,1)S(1)} %convert_dynamic-update-slice_fusion.refs_0_), channel_id=1, source_target_pairs={{0,24},{2,26},{4,28},{6,30},{8,16},{10,18},{12,20},{14,22},{16,8},... | collective-permute-start | bytes 479240 | tf_op jit(solution)/shard_map/ppermute | solution.py:57
  9.4 1.6 collective-permute-start
  13.8 8.5 %collective-permute-done.2.refs_2_ = bf16[48,1664]{1,0:T(8,128)(2,1)S(1)} collective-permute-done((bf16[48,1664]{1,0:T(8,128)(2,1)S(1)}, bf16[48,1664]{1,0:T(8,128)(2,1)S(1)}, u32[]{:S(2)}, u32[]{:S(2)}) %collective-permute-start.2) | collective-permute-done | bytes 159776 | tf_op jit(solution)/shard_map/ppermute | solution.py:57
  22.4 2.6 %collective-permute-start.10 = (bf16[48,3072]{1,0:T(8,128)(2,1)S(1)}, bf16[48,3072]{1,0:T(8,128)(2,1)S(1)}, u32[]{:S(2)}, u32[]{:S(2)}) collective-permute-start(bf16[48,3072]{1,0:T(8,128)(2,1)S(1)} %shard_map.325.refs_0_), channel_id=1, source_target_pairs={{0,24},{2,26},{4,28},{6,30},{8,16},{10,18},{12,20},{14,22},{16,8},... | collective-permute-start | bytes 884744 | tf_op jit(solution)/shard_map/ppermute | solution.py:57
  25.0 1.9 collective-permute-start.8
  30.5 4.7 %collective-permute-done.5.refs_3_ = bf16[192,768]{1,0:T(8,128)(2,1)S(1)} collective-permute-done((bf16[192,768]{1,0:T(8,128)(2,1)S(1)}, bf16[192,768]{1,0:T(8,128)(2,1)S(1)}, u32[]{:S(2)}, u32[]{:S(2)}) %collective-permute-start.5) | collective-permute-done | bytes 294944 | tf_op jit(solution)/shard_map/ppermute | solution.py:57
  38.3 10.1 %collective-permute-done.9.refs_2_ = bf16[48,3072]{1,0:T(8,128)(2,1)S(1)} collective-permute-done((bf16[48,3072]{1,0:T(8,128)(2,1)S(1)}, bf16[48,3072]{1,0:T(8,128)(2,1)S(1)}, u32[]{:S(2)}, u32[]{:S(2)}) %collective-permute-start.9) | collective-permute-done | bytes 294944 | tf_op jit(solution)/shard_map/ppermute | solution.py:57
  48.5 2.7 %collective-permute-done.7.refs_3_ = bf16[192,1792]{1,0:T(8,128)(2,1)S(1)} collective-permute-done((bf16[192,1792]{1,0:T(8,128)(2,1)S(1)}, bf16[192,1792]{1,0:T(8,128)(2,1)S(1)}, u32[]{:S(2)}, u32[]{:S(2)}) %collective-permute-start.7) | collective-permute-done | bytes 688160 | tf_op jit(solution)/shard_map/ppermute | solution.py:57
  56.3 2.6 %shard_map.329 = (bf16[256,768]{1,0:T(8,128)(2,1)S(1)}, bf16[512,768]{1,0:T(8,128)(2,1)S(1)}, bf16[512,768]{1,0:T(8,128)(2,1)S(1)}) custom-call(bf16[512,768]{1,0:T(8,128)(2,1)S(1)} %pad_maximum_fusion.refs_4_.refs_0_.refs_1_.refs_2_, bf16[384,1792]{1,0:T(8,128)(2,1)S(1)} %get-tuple-element.99.refs_2_.refs_1_.refs_3_, ...), custom_call_target="tpu_custom_call" | custom-call | flops 1509949440 | bytes 7870464 | tf_op jit(solution)/shard_map/pallas_call | solution.py:142
  58.8 8.4 %collective-permute-done.14.refs_3_ = bf16[192,1536]{1,0:T(8,128)(2,1)S(1)} collective-permute-done((bf16[192,1536]{1,0:T(8,128)(2,1)S(1)}, bf16[192,1536]{1,0:T(8,128)(2,1)S(1)}, u32[]{:S(2)}, u32[]{:S(2)}) %collective-permute-start.14) | collective-permute-done | bytes 589856 | tf_op jit(solution)/shard_map/ppermute | solution.py:57
  70.3 8.4 %shard_map.331.refs_0_.refs_7_ = bf16[256,768]{1,0:T(8,128)(2,1)S(1)} custom-call(s32[1]{0:T(128)} %bitcast.refs_0_, s32[1,3]{1,0:T(1,128)S(1)} %copy-done.22, bf16[256,768]{1,0:T(8,128)(2,1)S(1)} %get-tuple-element.103.refs_4_.refs_2_, bf16[512,768]{1,0:T(8,128)(2,1)S(1)} %get-tuple-element.104.refs_3_, bf16[512,768]{1,0:T(8,128)(2,1)S(1)} %get-tuple-element.105.refs_4_, ...), custom_call_target="tpu_custom_call" | custom-call | flops 905969664 | bytes 2359312 | tf_op jit(solution)/shard_map/pallas_call | solution.py:142
  79.7 17.5 %collective-permute-done.18.refs_1_ = bf16[384,1536]{1,0:T(8,128)(2,1)S(1)} collective-permute-done((bf16[384,1536]{1,0:T(8,128)(2,1)S(1)}, bf16[384,1536]{1,0:T(8,128)(2,1)S(1)}, u32[]{:S(2)}, u32[]{:S(2)}) %collective-permute-start.18) | collective-permute-done | bytes 1179680 | tf_op jit(solution)/shard_map/ppermute | solution.py:61
  98.6 1.7 collective-permute-done.19.refs_4_
  100.3 2.8 %shard_map.334 = (bf16[256,3072]{1,0:T(8,128)(2,1)S(1)}, f32[256,3072]{1,0:T(8,128)S(1)}) custom-call(bf16[256,768]{1,0:T(8,128)(2,1)S(1)} %get-tuple-element.110.refs_2_.refs_0_, bf16[192,3072]{1,0:T(8,128)(2,1)S(1)} %get-tuple-element.107.refs_5_.refs_1_, bf16[192,3072]{1,0:T(8,128)(2,1)S(1)} %get-tuple-element.111.refs_2_, ...), custom_call_target="tpu_custom_call" | custom-call | flops 2415919104 | bytes 9842688 | tf_op jit(solution)/shard_map/pallas_call | solution.py:142
  103.1 3.0 %shard_map.335 = (bf16[256,768]{1,0:T(8,128)(2,1)S(1)}, f32[256,768]{1,0:T(8,128)S(1)}, bf16[256,768]{1,0:T(8,128)(2,1)S(1)}, f32[8,768]{1,0:T(8,128)S(1)}) custom-call(s32[1]{0:T(128)} %bitcast.refs_0_, s32[1,3]{1,0:T(1,128)S(1)} %copy-done.22, bf16[256,3072]{1,0:T(8,128)(2,1)S(1)} %get-tuple-element.113.refs_2_, ...), custom_call_target="tpu_custom_call" | custom-call | flops 1509949440 | bytes 9480208 | tf_op jit(solution)/shard_map/pallas_call | solution.py:142
  107.2 1.8 shard_map.336
  112.4 1.8 collective-permute-start.24
  116.7 2.7 %shard_map.339 = (f32[256,768]{1,0:T(8,128)S(1)}, bf16[256,768]{1,0:T(8,128)(2,1)S(1)}, bf16[256,768]{1,0:T(8,128)(2,1)S(1)}, f32[8,768]{1,0:T(8,128)S(1)}) custom-call(bf16[256,3072]{1,0:T(8,128)(2,1)S(1)} %get-tuple-element.119.refs_2_.refs_0_, bf16[192,3072]{1,0:T(8,128)(2,1)S(1)} %get-tuple-element.107.refs_5_.refs_1_, ...), custom_call_target="tpu_custom_call" | custom-call | flops 1811939328 | bytes 11840512 | tf_op jit(solution)/shard_map/pallas_call | solution.py:142
  119.4 10.5 %shard_map.340 = (bf16[256,768]{1,0:T(8,128)(2,1)S(1)}, bf16[512,768]{1,0:T(8,128)(2,1)S(1)}, bf16[512,768]{1,0:T(8,128)(2,1)S(1)}) custom-call(s32[1]{0:T(128)} %bitcast.refs_0_, s32[1,3]{1,0:T(1,128)S(1)} %copy-done.22, bf16[256,768]{1,0:T(8,128)(2,1)S(1)} %get-tuple-element.103.refs_4_.refs_2_, bf16[512,768]{1,0:T(8,128)(2,1)S(1)} %get-tuple-element.104.refs_3_, ...), custom_call_target="tpu_custom_call" | custom-call | flops 1509949440 | bytes 4325392 | tf_op jit(solution)/shard_map/pallas_call | solution.py:142
  130.0 3.1 %shard_map.341 = (bf16[384,1792]{1,0:T(8,128)(2,1)S(1)}, bf16[384,1536]{1,0:T(8,128)(2,1)S(1)}, bf16[384,1792]{1,0:T(8,128)(2,1)S(1)}, bf16[384,1536]{1,0:T(8,128)(2,1)S(1)}) custom-call(s32[1]{0:T(128)} %bitcast.refs_0_, bf16[768,768]{1,0:T(8,128)(2,1)S(1)} %copy-done.7, bf16[512,768]{1,0:T(8,128)(2,1)S(1)} %pad_maximum_fusion.refs_4_.refs_0_.refs_1_.refs_2_, ...), custom_call_target="tpu_custom_call" | custom-call | flops 1811939328 | bytes 9891844 | tf_op jit(solution)/shard_map/pallas_call | solution.py:142
  133.6 7.2 %collective-permute-done.24.refs_3_ = bf16[384,1536]{1,0:T(8,128)(2,1)S(1)} collective-permute-done((bf16[384,1536]{1,0:T(8,128)(2,1)S(1)}, bf16[384,1536]{1,0:T(8,128)(2,1)S(1)}, u32[]{:S(2)}, u32[]{:S(2)}) %collective-permute-start.24) | collective-permute-done | bytes 1179680 | tf_op jit(solution)/shard_map/ppermute | solution.py:61
  140.8 2.9 %collective-permute-done.23.refs_1_ = bf16[192,3072]{1,0:T(8,128)(2,1)S(1)} collective-permute-done((bf16[192,3072]{1,0:T(8,128)(2,1)S(1)}, bf16[192,3072]{1,0:T(8,128)(2,1)S(1)}, u32[]{:S(2)}, u32[]{:S(2)}) %collective-permute-start.23) | collective-permute-done | bytes 1179680 | tf_op jit(solution)/shard_map/ppermute | solution.py:57
  146.2 2.6 %shard_map.343 = (f32[256,768]{1,0:T(8,128)S(1)}, bf16[256,768]{1,0:T(8,128)(2,1)S(1)}) custom-call(bf16[256,768]{1,0:T(8,128)(2,1)S(1)} %get-tuple-element.126.refs_3_.refs_0_, bf16[512,768]{1,0:T(8,128)(2,1)S(1)} %get-tuple-element.127.refs_4_.refs_1_, bf16[512,768]{1,0:T(8,128)(2,1)S(1)} %get-tuple-element.128.refs_5_.refs_2_, ...), custom_call_target="tpu_custom_call" | custom-call | flops 120795955200 | bytes 9043968 | tf_op jit(solution)/shard_map/pallas_call | solution.py:142
  151.6 8.9 %collective-permute-done.29.refs_1_ = bf16[192,1536]{1,0:T(8,128)(2,1)S(1)} collective-permute-done((bf16[192,1536]{1,0:T(8,128)(2,1)S(1)}, bf16[192,1536]{1,0:T(8,128)(2,1)S(1)}, u32[]{:S(2)}, u32[]{:S(2)}) %collective-permute-start.29) | collective-permute-done | bytes 589856 | tf_op jit(solution)/shard_map/ppermute | solution.py:61
  162.7 2.2 %collective-permute-start.34 = (bf16[48,3072]{1,0:T(8,128)(2,1)S(1)}, bf16[48,3072]{1,0:T(8,128)(2,1)S(1)}, u32[]{:S(2)}, u32[]{:S(2)}) collective-permute-start(bf16[48,3072]{1,0:T(8,128)(2,1)S(1)} %get-tuple-element.156), channel_id=1, source_target_pairs={{0,16},{2,18},{4,20},{6,22},{8,24},{10,26},{12,28},{14,30},{16,0},... | collective-permute-start | bytes 884744 | tf_op jit(solution)/shard_map/ppermute | solution.py:57
  165.0 1.8 collective-permute-start.35
  166.7 4.7 %collective-permute-done.28.refs_3_ = bf16[384,768]{1,0:T(8,128)(2,1)S(1)} collective-permute-done((bf16[384,768]{1,0:T(8,128)(2,1)S(1)}, bf16[384,768]{1,0:T(8,128)(2,1)S(1)}, u32[]{:S(2)}, u32[]{:S(2)}) %collective-permute-start.28) | collective-permute-done | bytes 589856 | tf_op jit(solution)/shard_map/ppermute | solution.py:61
  171.4 3.3 %collective-permute-done.27.refs_1_ = bf16[192,1792]{1,0:T(8,128)(2,1)S(1)} collective-permute-done((bf16[192,1792]{1,0:T(8,128)(2,1)S(1)}, bf16[192,1792]{1,0:T(8,128)(2,1)S(1)}, u32[]{:S(2)}, u32[]{:S(2)}) %collective-permute-start.27) | collective-permute-done | bytes 688160 | tf_op jit(solution)/shard_map/ppermute | solution.py:57
  176.1 8.0 %collective-permute-done.34.refs_2_ = bf16[48,3072]{1,0:T(8,128)(2,1)S(1)} collective-permute-done((bf16[48,3072]{1,0:T(8,128)(2,1)S(1)}, bf16[48,3072]{1,0:T(8,128)(2,1)S(1)}, u32[]{:S(2)}, u32[]{:S(2)}) %collective-permute-start.34) | collective-permute-done | bytes 294944 | tf_op jit(solution)/shard_map/ppermute | solution.py:57
  186.5 3.8 %collective-permute-start.37 = (bf16[48,1664]{1,0:T(8,128)(2,1)S(1)}, bf16[48,1664]{1,0:T(8,128)(2,1)S(1)}, u32[]{:S(2)}, u32[]{:S(2)}) collective-permute-start(bf16[48,1664]{1,0:T(8,128)(2,1)S(1)} %get-tuple-element.159), channel_id=1, source_target_pairs={{0,8},{2,10},{4,12},{6,14},{8,0},{10,2},{12,4},{14,6},{16,24},{18,... | collective-permute-start | bytes 479240 | tf_op jit(solution)/shard_map/ppermute | solution.py:57
  194.4 6.1 %collective-permute-done.36.refs_1_ = bf16[256,768]{1,0:T(8,128)(2,1)S(1)} collective-permute-done((bf16[256,768]{1,0:T(8,128)(2,1)S(1)}, bf16[256,768]{1,0:T(8,128)(2,1)S(1)}, u32[]{:S(2)}, u32[]{:S(2)}) %collective-permute-start.36) | collective-permute-done | bytes 393248 | tf_op jit(solution)/shard_map/ppermute | solution.py:61
  200.5 2.0 shard_map.350.refs_14_
  (155 shorter events, 48.7 us)
Async XLA Ops:
  3.6 10.2 %collective-permute-start.3 = (bf16[48,1664]{1,0:T(8,128)(2,1)S(1)}, bf16[48,1664]{1,0:T(8,128)(2,1)S(1)}, u32[]{:S(2)}, u32[]{:S(2)}) collective-permute-start(bf16[48,1664]{1,0:T(8,128)(2,1)S(1)} %convert_dynamic-update-slice_fusion.refs_0_), channel_id=1, source_target_pairs={{0,24},{2,26},{4,28},{6,30},{8,16},{10,18},{12,20},{14,22},{16,8},... | collective-permute-start | bytes 479240 | tf_op jit(solution)/shard_map/ppermute | solution.py:57
  8.7 13.5 %collective-permute-start.2 = (bf16[48,1664]{1,0:T(8,128)(2,1)S(1)}, bf16[48,1664]{1,0:T(8,128)(2,1)S(1)}, u32[]{:S(2)}, u32[]{:S(2)}) collective-permute-start(bf16[48,1664]{1,0:T(8,128)(2,1)S(1)} %convert_dynamic-update-slice_fusion.refs_0_), channel_id=1, source_target_pairs={{0,16},{2,18},{4,20},{6,22},{8,24},{10,26},{12,28},{14,30},{16,0},... | collective-permute-start | bytes 479240 | tf_op jit(solution)/shard_map/ppermute | solution.py:57
  8.7 13.5 %collective-permute-start.1 = (bf16[48,1664]{1,0:T(8,128)(2,1)S(1)}, bf16[48,1664]{1,0:T(8,128)(2,1)S(1)}, u32[]{:S(2)}, u32[]{:S(2)}) collective-permute-start(bf16[48,1664]{1,0:T(8,128)(2,1)S(1)} %convert_dynamic-update-slice_fusion.refs_0_), channel_id=1, source_target_pairs={{0,8},{2,10},{4,12},{6,14},{8,0},{10,2},{12,4},{14,6},{16,24},{18,... | collective-permute-start | bytes 479240 | tf_op jit(solution)/shard_map/ppermute | solution.py:57
  9.4 19.0 %collective-permute-start = (bf16[256,768]{1,0:T(8,128)(2,1)}, bf16[256,768]{1,0:T(8,128)(2,1)S(1)}, u32[]{:S(2)}, u32[]{:S(2)}) collective-permute-start(bf16[256,768]{1,0:T(8,128)(2,1)} %param.20), channel_id=1, source_target_pairs={{0,1},{1,0},{2,3},{3,2},{4,5},{5,4},{6,7},{7,6},{8,9},{9,8},{10,11... | collective-permute-start | bytes 1179656 | tf_op jit(solution)/shard_map/ppermute | solution.py:61
  22.4 15.9 %collective-permute-start.10 = (bf16[48,3072]{1,0:T(8,128)(2,1)S(1)}, bf16[48,3072]{1,0:T(8,128)(2,1)S(1)}, u32[]{:S(2)}, u32[]{:S(2)}) collective-permute-start(bf16[48,3072]{1,0:T(8,128)(2,1)S(1)} %shard_map.325.refs_0_), channel_id=1, source_target_pairs={{0,24},{2,26},{4,28},{6,30},{8,16},{10,18},{12,20},{14,22},{16,8},... | collective-permute-start | bytes 884744 | tf_op jit(solution)/shard_map/ppermute | solution.py:57
  24.9 23.4 %collective-permute-start.9 = (bf16[48,3072]{1,0:T(8,128)(2,1)S(1)}, bf16[48,3072]{1,0:T(8,128)(2,1)S(1)}, u32[]{:S(2)}, u32[]{:S(2)}) collective-permute-start(bf16[48,3072]{1,0:T(8,128)(2,1)S(1)} %shard_map.325.refs_0_), channel_id=1, source_target_pairs={{0,16},{2,18},{4,20},{6,22},{8,24},{10,26},{12,28},{14,30},{16,0},... | collective-permute-start | bytes 884744 | tf_op jit(solution)/shard_map/ppermute | solution.py:57
  25.0 23.4 %collective-permute-start.8 = (bf16[48,3072]{1,0:T(8,128)(2,1)S(1)}, bf16[48,3072]{1,0:T(8,128)(2,1)S(1)}, u32[]{:S(2)}, u32[]{:S(2)}) collective-permute-start(bf16[48,3072]{1,0:T(8,128)(2,1)S(1)} %shard_map.325.refs_0_), channel_id=1, source_target_pairs={{0,8},{2,10},{4,12},{6,14},{8,0},{10,2},{12,4},{14,6},{16,24},{18,... | collective-permute-start | bytes 884744 | tf_op jit(solution)/shard_map/ppermute | solution.py:57
  26.8 8.4 %collective-permute-start.4 = (bf16[192,896]{1,0:T(8,128)(2,1)S(1)}, bf16[192,896]{1,0:T(8,128)(2,1)S(1)}, u32[]{:S(2)}, u32[]{:S(2)}) collective-permute-start(bf16[192,896]{1,0:T(8,128)(2,1)S(1)} %get-tuple-element.94.refs_0_.refs_2_), channel_id=1, source_target_pairs={{0,1},{1,0},{2,3},{3,2},{4,5},{5,4},{6,7},{7,6},{8,9},{9,8},{10,11... | collective-permute-start | bytes 1032200 | tf_op jit(solution)/shard_map/ppermute | solution.py:61
  35.4 13.1 %collective-permute-start.6 = (bf16[384,768]{1,0:T(8,128)(2,1)S(1)}, bf16[384,768]{1,0:T(8,128)(2,1)S(1)}, u32[]{:S(2)}, u32[]{:S(2)}) collective-permute-start(bf16[384,768]{1,0:T(8,128)(2,1)S(1)} %get-tuple-element.96.refs_0_), channel_id=1, source_target_pairs={{0,1},{1,0},{2,3},{3,2},{4,5},{5,4},{6,7},{7,6},{8,9},{9,8},{10,11... | collective-permute-start | bytes 1769480 | tf_op jit(solution)/shard_map/ppermute | solution.py:61
  36.8 14.4 %collective-permute-start.7 = (bf16[192,1792]{1,0:T(8,128)(2,1)S(1)}, bf16[192,1792]{1,0:T(8,128)(2,1)S(1)}, u32[]{:S(2)}, u32[]{:S(2)}) collective-permute-start(bf16[192,1792]{1,0:T(8,128)(2,1)S(1)} %get-tuple-element.97.refs_1_), channel_id=1, source_target_pairs={{0,4},{2,6},{4,0},{6,2},{8,12},{10,14},{12,8},{14,10},{16,20},{18,... | collective-permute-start | bytes 2064392 | tf_op jit(solution)/shard_map/ppermute | solution.py:57
  52.0 15.3 %collective-permute-start.14 = (bf16[192,1536]{1,0:T(8,128)(2,1)S(1)}, bf16[192,1536]{1,0:T(8,128)(2,1)S(1)}, u32[]{:S(2)}, u32[]{:S(2)}) collective-permute-start(bf16[192,1536]{1,0:T(8,128)(2,1)S(1)} %get-tuple-element.106.refs_1_), channel_id=1, source_target_pairs={{0,4},{2,6},{4,0},{6,2},{8,12},{10,14},{12,8},{14,10},{16,20},{18,... | collective-permute-start | bytes 1769480 | tf_op jit(solution)/shard_map/ppermute | solution.py:57
  53.5 15.0 %collective-permute-start.13 = (bf16[192,1536]{1,0:T(8,128)(2,1)S(1)}, bf16[192,1536]{1,0:T(8,128)(2,1)S(1)}, u32[]{:S(2)}, u32[]{:S(2)}) collective-permute-start(bf16[192,1536]{1,0:T(8,128)(2,1)S(1)} %get-tuple-element.98.refs_4_.refs_0_), channel_id=1, source_target_pairs={{0,1},{1,0},{2,3},{3,2},{4,5},{5,4},{6,7},{7,6},{8,9},{9,8},{10,11... | collective-permute-start | bytes 1769480 | tf_op jit(solution)/shard_map/ppermute | solution.py:61
  68.7 10.0 %collective-permute-start.16 = (bf16[384,1536]{1,0:T(8,128)(2,1)S(1)}, bf16[384,1536]{1,0:T(8,128)(2,1)S(1)}, u32[]{:S(2)}, u32[]{:S(2)}) collective-permute-start(bf16[384,1536]{1,0:T(8,128)(2,1)S(1)} %get-tuple-element.109.refs_3_.refs_1_), channel_id=1, source_target_pairs={{0,2},{2,0},{4,6},{6,4},{8,10},{10,8},{12,14},{14,12},{16,18},{18,... | collective-permute-start | bytes 3538952 | tf_op jit(solution)/shard_map/ppermute | solution.py:57
  68.7 10.0 %collective-permute-start.15 = (bf16[192,3072]{1,0:T(8,128)(2,1)S(1)}, bf16[192,3072]{1,0:T(8,128)(2,1)S(1)}, u32[]{:S(2)}, u32[]{:S(2)}) collective-permute-start(bf16[192,3072]{1,0:T(8,128)(2,1)S(1)} %get-tuple-element.107.refs_5_.refs_1_), channel_id=1, source_target_pairs={{0,2},{2,0},{4,6},{6,4},{8,10},{10,8},{12,14},{14,12},{16,18},{18,... | collective-permute-start | bytes 3538952 | tf_op jit(solution)/shard_map/ppermute | solution.py:57
  69.2 28.0 %collective-permute-start.18 = (bf16[384,1536]{1,0:T(8,128)(2,1)S(1)}, bf16[384,1536]{1,0:T(8,128)(2,1)S(1)}, u32[]{:S(2)}, u32[]{:S(2)}) collective-permute-start(bf16[384,1536]{1,0:T(8,128)(2,1)S(1)} %get-tuple-element.109.refs_3_.refs_1_), channel_id=1, source_target_pairs={{0,1},{1,0},{2,3},{3,2},{4,5},{5,4},{6,7},{7,6},{8,9},{9,8},{10,11... | collective-permute-start | bytes 3538952 | tf_op jit(solution)/shard_map/ppermute | solution.py:61
  69.8 27.7 %collective-permute-start.17 = (bf16[192,3072]{1,0:T(8,128)(2,1)S(1)}, bf16[192,3072]{1,0:T(8,128)(2,1)S(1)}, u32[]{:S(2)}, u32[]{:S(2)}) collective-permute-start(bf16[192,3072]{1,0:T(8,128)(2,1)S(1)} %get-tuple-element.107.refs_5_.refs_1_), channel_id=1, source_target_pairs={{0,4},{2,6},{4,0},{6,2},{8,12},{10,14},{12,8},{14,10},{16,20},{18,... | collective-permute-start | bytes 3538952 | tf_op jit(solution)/shard_map/ppermute | solution.py:57
  112.4 28.3 %collective-permute-start.24 = (bf16[384,1536]{1,0:T(8,128)(2,1)S(1)}, bf16[384,1536]{1,0:T(8,128)(2,1)S(1)}, u32[]{:S(2)}, u32[]{:S(2)}) collective-permute-start(bf16[384,1536]{1,0:T(8,128)(2,1)S(1)} %get-tuple-element.131), channel_id=1, source_target_pairs={{0,1},{1,0},{2,3},{3,2},{4,5},{5,4},{6,7},{7,6},{8,9},{9,8},{10,11... | collective-permute-start | bytes 3538952 | tf_op jit(solution)/shard_map/ppermute | solution.py:61
  115.5 28.1 %collective-permute-start.23 = (bf16[192,3072]{1,0:T(8,128)(2,1)S(1)}, bf16[192,3072]{1,0:T(8,128)(2,1)S(1)}, u32[]{:S(2)}, u32[]{:S(2)}) collective-permute-start(bf16[192,3072]{1,0:T(8,128)(2,1)S(1)} %get-tuple-element.130), channel_id=1, source_target_pairs={{0,4},{2,6},{4,0},{6,2},{8,12},{10,14},{12,8},{14,10},{16,20},{18,... | collective-permute-start | bytes 3538952 | tf_op jit(solution)/shard_map/ppermute | solution.py:57
  133.0 15.9 %collective-permute-start.26 = (bf16[384,1536]{1,0:T(8,128)(2,1)S(1)}, bf16[384,1536]{1,0:T(8,128)(2,1)S(1)}, u32[]{:S(2)}, u32[]{:S(2)}) collective-permute-start(bf16[384,1536]{1,0:T(8,128)(2,1)S(1)} %get-tuple-element.142), channel_id=1, source_target_pairs={{0,2},{2,0},{4,6},{6,4},{8,10},{10,8},{12,14},{14,12},{16,18},{18,... | collective-permute-start | bytes 3538952 | tf_op jit(solution)/shard_map/ppermute | solution.py:57
  133.1 15.8 %collective-permute-start.25 = (bf16[384,1792]{1,0:T(8,128)(2,1)S(1)}, bf16[384,1792]{1,0:T(8,128)(2,1)S(1)}, u32[]{:S(2)}, u32[]{:S(2)}) collective-permute-start(bf16[384,1792]{1,0:T(8,128)(2,1)S(1)} %get-tuple-element.140), channel_id=1, source_target_pairs={{0,2},{2,0},{4,6},{6,4},{8,10},{10,8},{12,14},{14,12},{16,18},{18,... | collective-permute-start | bytes 4128776 | tf_op jit(solution)/shard_map/ppermute | solution.py:57
  144.2 16.3 %collective-permute-start.29 = (bf16[192,1536]{1,0:T(8,128)(2,1)S(1)}, bf16[192,1536]{1,0:T(8,128)(2,1)S(1)}, u32[]{:S(2)}, u32[]{:S(2)}) collective-permute-start(bf16[192,1536]{1,0:T(8,128)(2,1)S(1)} %get-tuple-element.147), channel_id=1, source_target_pairs={{0,1},{1,0},{2,3},{3,2},{4,5},{5,4},{6,7},{7,6},{8,9},{9,8},{10,11... | collective-permute-start | bytes 1769480 | tf_op jit(solution)/shard_map/ppermute | solution.py:61
  145.7 16.3 %collective-permute-start.30 = (bf16[192,1536]{1,0:T(8,128)(2,1)S(1)}, bf16[192,1536]{1,0:T(8,128)(2,1)S(1)}, u32[]{:S(2)}, u32[]{:S(2)}) collective-permute-start(bf16[192,1536]{1,0:T(8,128)(2,1)S(1)} %get-tuple-element.149), channel_id=1, source_target_pairs={{0,4},{2,6},{4,0},{6,2},{8,12},{10,14},{12,8},{14,10},{16,20},{18,... | collective-permute-start | bytes 1769480 | tf_op jit(solution)/shard_map/ppermute | solution.py:57
  149.5 25.3 %collective-permute-start.27 = (bf16[192,1792]{1,0:T(8,128)(2,1)S(1)}, bf16[192,1792]{1,0:T(8,128)(2,1)S(1)}, u32[]{:S(2)}, u32[]{:S(2)}) collective-permute-start(bf16[192,1792]{1,0:T(8,128)(2,1)S(1)} %get-tuple-element.144), channel_id=1, source_target_pairs={{0,4},{2,6},{4,0},{6,2},{8,12},{10,14},{12,8},{14,10},{16,20},{18,... | collective-permute-start | bytes 2064392 | tf_op jit(solution)/shard_map/ppermute | solution.py:57
  151.1 20.4 %collective-permute-start.28 = (bf16[384,768]{1,0:T(8,128)(2,1)S(1)}, bf16[384,768]{1,0:T(8,128)(2,1)S(1)}, u32[]{:S(2)}, u32[]{:S(2)}) collective-permute-start(bf16[384,768]{1,0:T(8,128)(2,1)S(1)} %get-tuple-element.146), channel_id=1, source_target_pairs={{0,1},{1,0},{2,3},{3,2},{4,5},{5,4},{6,7},{7,6},{8,9},{9,8},{10,11... | collective-permute-start | bytes 1769480 | tf_op jit(solution)/shard_map/ppermute | solution.py:61
  162.3 13.9 %collective-permute-start.33 = (bf16[48,3072]{1,0:T(8,128)(2,1)S(1)}, bf16[48,3072]{1,0:T(8,128)(2,1)S(1)}, u32[]{:S(2)}, u32[]{:S(2)}) collective-permute-start(bf16[48,3072]{1,0:T(8,128)(2,1)S(1)} %get-tuple-element.155), channel_id=1, source_target_pairs={{0,8},{2,10},{4,12},{6,14},{8,0},{10,2},{12,4},{14,6},{16,24},{18,... | collective-permute-start | bytes 884744 | tf_op jit(solution)/shard_map/ppermute | solution.py:57
  162.7 21.4 %collective-permute-start.34 = (bf16[48,3072]{1,0:T(8,128)(2,1)S(1)}, bf16[48,3072]{1,0:T(8,128)(2,1)S(1)}, u32[]{:S(2)}, u32[]{:S(2)}) collective-permute-start(bf16[48,3072]{1,0:T(8,128)(2,1)S(1)} %get-tuple-element.156), channel_id=1, source_target_pairs={{0,16},{2,18},{4,20},{6,22},{8,24},{10,26},{12,28},{14,30},{16,0},... | collective-permute-start | bytes 884744 | tf_op jit(solution)/shard_map/ppermute | solution.py:57
  165.0 19.2 %collective-permute-start.35 = (bf16[48,3072]{1,0:T(8,128)(2,1)S(1)}, bf16[48,3072]{1,0:T(8,128)(2,1)S(1)}, u32[]{:S(2)}, u32[]{:S(2)}) collective-permute-start(bf16[48,3072]{1,0:T(8,128)(2,1)S(1)} %get-tuple-element.157), channel_id=1, source_target_pairs={{0,24},{2,26},{4,28},{6,30},{8,16},{10,18},{12,20},{14,22},{16,8},... | collective-permute-start | bytes 884744 | tf_op jit(solution)/shard_map/ppermute | solution.py:57
  175.0 11.3 %collective-permute-start.32 = (bf16[192,768]{1,0:T(8,128)(2,1)S(1)}, bf16[192,768]{1,0:T(8,128)(2,1)S(1)}, u32[]{:S(2)}, u32[]{:S(2)}) collective-permute-start(bf16[192,768]{1,0:T(8,128)(2,1)S(1)} %get-tuple-element.154), channel_id=1, source_target_pairs={{0,4},{2,6},{4,0},{6,2},{8,12},{10,14},{12,8},{14,10},{16,20},{18,... | collective-permute-start | bytes 884744 | tf_op jit(solution)/shard_map/ppermute | solution.py:57
  175.6 10.7 %collective-permute-start.31 = (bf16[192,896]{1,0:T(8,128)(2,1)S(1)}, bf16[192,896]{1,0:T(8,128)(2,1)S(1)}, u32[]{:S(2)}, u32[]{:S(2)}) collective-permute-start(bf16[192,896]{1,0:T(8,128)(2,1)S(1)} %get-tuple-element.152), channel_id=1, source_target_pairs={{0,1},{1,0},{2,3},{3,2},{4,5},{5,4},{6,7},{7,6},{8,9},{9,8},{10,11... | collective-permute-start | bytes 1032200 | tf_op jit(solution)/shard_map/ppermute | solution.py:61
  186.5 16.1 %collective-permute-start.37 = (bf16[48,1664]{1,0:T(8,128)(2,1)S(1)}, bf16[48,1664]{1,0:T(8,128)(2,1)S(1)}, u32[]{:S(2)}, u32[]{:S(2)}) collective-permute-start(bf16[48,1664]{1,0:T(8,128)(2,1)S(1)} %get-tuple-element.159), channel_id=1, source_target_pairs={{0,8},{2,10},{4,12},{6,14},{8,0},{10,2},{12,4},{14,6},{16,24},{18,... | collective-permute-start | bytes 479240 | tf_op jit(solution)/shard_map/ppermute | solution.py:57
  190.3 12.2 %collective-permute-start.38 = (bf16[48,1664]{1,0:T(8,128)(2,1)S(1)}, bf16[48,1664]{1,0:T(8,128)(2,1)S(1)}, u32[]{:S(2)}, u32[]{:S(2)}) collective-permute-start(bf16[48,1664]{1,0:T(8,128)(2,1)S(1)} %get-tuple-element.160), channel_id=1, source_target_pairs={{0,16},{2,18},{4,20},{6,22},{8,24},{10,26},{12,28},{14,30},{16,0},... | collective-permute-start | bytes 479240 | tf_op jit(solution)/shard_map/ppermute | solution.py:57
  191.1 11.4 %collective-permute-start.39 = (bf16[48,1664]{1,0:T(8,128)(2,1)S(1)}, bf16[48,1664]{1,0:T(8,128)(2,1)S(1)}, u32[]{:S(2)}, u32[]{:S(2)}) collective-permute-start(bf16[48,1664]{1,0:T(8,128)(2,1)S(1)} %get-tuple-element.161), channel_id=1, source_target_pairs={{0,24},{2,26},{4,28},{6,30},{8,16},{10,18},{12,20},{14,22},{16,8},... | collective-permute-start | bytes 479240 | tf_op jit(solution)/shard_map/ppermute | solution.py:57
  (35 other events, 351.6 us)

commit v7 on v6

--- a/solution.py
+++ b/solution.py
@@ -344,6 +344,30 @@
     relative[2:5, :] = sums_one[:3, :]
     relative[5:8, :] = sums_two[:3, :]
     return jnp.transpose(relative[...]).astype(LOW)
+
+
+def pack_kernel(rank_ref, w_qkv, w_out, vectors, target, turned):
+    columns = w_out.shape[1]
+    count, shard_width = vectors.shape
+    a_width = 2 * columns + LANES
+    turned[...] = jnp.zeros_like(turned)
+    for place in range(3):
+        turned[16 * place : 16 * place + count, :shard_width] = vectors[...]
+    values = jnp.transpose(turned[...])
+    lane = lax.broadcasted_iota(jnp.int32, values.shape, 1)
+    first = values.astype(LOW).astype(F32)
+    second = (values - first).astype(LOW).astype(F32)
+    third = values - first - second
+    values = jnp.where(lane < 16, first, jnp.where(lane < 32, second, third))[:shard_width]
+    blank = jnp.zeros_like(values)
+    values = jnp.concatenate(
+        [flip(rank_ref[0], values, blank), flip(rank_ref[0], blank, values)], axis=0
+    )
+    target[:, :columns] = w_qkv[0].astype(LOW)
+    target[:, columns : 2 * columns] = w_qkv[1].astype(LOW)
+    target[:, 2 * columns : a_width] = values.astype(LOW)
+    target[:, a_width : a_width + columns] = w_qkv[2].astype(LOW)
+    target[:, a_width + columns :] = w_out[...].astype(LOW)
 
 
 def cast_kernel(first, second, target):
@@ -652,28 +676,18 @@
     count = vectors.shape[0]
     shard_width = vectors.shape[1]
 
-    rest = vectors.T
-    vec_parts = []
-    for _ in range(3):
-        vec_parts.append(jnp.pad(rest.astype(LOW), ((0, 0), (0, 16 - count))))
-        rest = rest - rest.astype(LOW).astype(F32)
-    vec_lanes = jnp.pad(jnp.concatenate(vec_parts, axis=1), ((0, 0), (0, LANES - 48)))
-    blank = jnp.zeros_like(vec_lanes)
-    vec_lanes = jnp.concatenate(
-        [
-            jnp.where(tensor_rank == 0, vec_lanes, blank),
-            jnp.where(tensor_rank == 0, blank, vec_lanes),
-        ],
-        axis=0,
-    )
-    low_qkv = w_qkv.astype(LOW)
-    shard_one = jnp.concatenate(
-        [low_qkv[0], low_qkv[1], vec_lanes, low_qkv[2], w_out.T.astype(LOW)], axis=1
-    )
     a_width = 2 * part + LANES
     rank = tensor_rank.astype(jnp.int32).reshape(1)
     scalar = pl.BlockSpec(memory_space=pltpu.SMEM)
     vmem = pl.BlockSpec(memory_space=pltpu.VMEM)
+    shard_one = run(
+        pack_kernel,
+        [shape_of(shard_rows, a_width + 2 * part, LOW)],
+        [rank, w_qkv, w_out.T, vectors],
+        0,
+        in_specs=[scalar] + [vmem] * 3,
+        scratch=[pltpu.VMEM((LANES, LANES), F32)],
+    )[0]
 
     tokens_far = swap_tensor(tokens)
     one_high = gather_high(shard_one)
@@ -684,7 +698,7 @@
         [shape_of(shard_rows, full_inner, LOW)],
         [w_in, w_back.T],
         0,
-        after=one[:1],
+        after=one_high[1:2],
     )[0]
     pair_high = gather_high(shard_pair)
 
@@ -829,11 +843,11 @@
     input_grad = run(
         rows_out_kernel,
         [wide],
-        [grad_own, swap_tensor(gate([grad_away], one[:1])[0]), permute],
+        [grad_own, swap_tensor(gate([grad_away], pair)[0]), permute],
         3 * unit,
         after=one[:1],
     )[0]
-    sum_pair = reduce_rest(pair[0])
+    sum_pair = reduce_rest(gate(pair, one[:1])[0])
     summed_in, summed_back = sum_pair[:, :hidden_half], sum_pair[:, hidden_half:].T
     if len(high_groups()) > 1:
         one = [reduce_rest(sum(piece.astype(F32) for piece in one))]

time: 205 us -> 209 us (1.020)
  starting transfers between devices: 42.6 us -> 50.4 us
  waiting for transfers between devices: 99.5 us -> 96.5 us
    ppermute x10, waiting for transfers between devices: 45.6 us -> 35.6 us  [swap_tensor(): return lax.ppermute(values, 'tensor', [(0, 1), (1, 0)])]
    ppermute x30, waiting for transfers between devices: 53.9 us -> 60.9 us  [swap_dp(): return lax.ppermute(values, 'dp', [(i, i ^ mask) for i in range(size)])]
    ppermute x30, starting transfers between devices: 32.1 us -> 38.1 us  [swap_dp(): return lax.ppermute(values, 'dp', [(i, i ^ mask) for i in range(size)])]
    pallas_call x27 -> x28, Pallas kernels: 46.4 us -> 46.5 us  [run(): pl.pallas_call(body, grid=grid, out_shape=list(outs), in_specs=list(in_sp...]
  transfers between devices with their start and end apart: 40 -> 40, of which waited for: 21 -> 20; matrix products, arithmetic and copies ran while one was open for 4% -> 4% of each run, Pallas kernels for 20% -> 20%
where the time goes in v7:
time: 209 us
  waiting for transfers between devices  96.5 us (46%)
  starting transfers between devices  50.4 us (24%)
  Pallas kernels  46.5 us (22%)
  matrix products  6.75 us (3%)
  local copies, waits for them, and re-layouts  3.85 us (2%)
  other arithmetic  3.27 us (2%)
    ppermute x30, waiting for transfers between devices, swap_dp(): return lax.ppermute(values, 'dp', [(i, i ^ mask) for i in range(size)])  60.9 us
    pallas_call x28, Pallas kernels, run(): pl.pallas_call(body, grid=grid, out_shape=list(outs), in_specs=list(in_sp...  46.5 us
    ppermute x30, starting transfers between devices, swap_dp(): return lax.ppermute(values, 'dp', [(i, i ^ mask) for i in range(size)])  38.1 us
    ppermute x10, waiting for transfers between devices, swap_tensor(): return lax.ppermute(values, 'tensor', [(0, 1), (1, 0)])  35.6 us
    ppermute x10, starting transfers between devices, swap_tensor(): return lax.ppermute(values, 'tensor', [(0, 1), (1, 0)])  12.3 us
  transfers between devices with their start and end apart: 40, of which 20 were waited for; matrix products, arithmetic and copies ran while one was open for 4% of the time, Pallas kernels for 20%

profile of v7, /device:TPU:0, one launch (start us, length us, event | category | flops | bytes accessed | tf_op | source)
XLA Modules:
  0.0 208.8 jit_solution(8931641409796563921)
XLA Ops:
  3.4 5.1 %collective-permute-start.3 = (bf16[48,1664]{1,0:T(8,128)(2,1)S(1)}, bf16[48,1664]{1,0:T(8,128)(2,1)S(1)}, u32[]{:S(2)}, u32[]{:S(2)}) collective-permute-start(bf16[48,1664]{1,0:T(8,128)(2,1)S(1)} %shard_map.323.refs_0_), channel_id=1, source_target_pairs={{0,24},{2,26},{4,28},{6,30},{8,16},{10,18},{12,20},{14,22},{16,8},... | collective-permute-start | bytes 479240 | tf_op jit(solution)/shard_map/ppermute | solution.py:57
  9.1 1.6 collective-permute-start
  11.5 1.6 fusion.10
  13.1 5.7 %collective-permute-done.1.refs_1_.refs_2_ = bf16[48,1664]{1,0:T(8,128)(2,1)S(1)} collective-permute-done((bf16[48,1664]{1,0:T(8,128)(2,1)S(1)}, bf16[48,1664]{1,0:T(8,128)(2,1)S(1)}, u32[]{:S(2)}, u32[]{:S(2)}) %collective-permute-start.1) | collective-permute-done | bytes 159776 | tf_op jit(solution)/shard_map/ppermute | solution.py:57
  20.0 2.9 %collective-permute-start.9 = (bf16[48,3072]{1,0:T(8,128)(2,1)S(1)}, bf16[48,3072]{1,0:T(8,128)(2,1)S(1)}, u32[]{:S(2)}, u32[]{:S(2)}) collective-permute-start(bf16[48,3072]{1,0:T(8,128)(2,1)S(1)} %shard_map.326.refs_0_), channel_id=1, source_target_pairs={{0,16},{2,18},{4,20},{6,22},{8,24},{10,26},{12,28},{14,30},{16,0},... | collective-permute-start | bytes 884744 | tf_op jit(solution)/shard_map/ppermute | solution.py:57
  23.4 1.6 collective-permute-start.5
  27.1 3.4 %collective-permute-done.5.refs_3_ = bf16[192,768]{1,0:T(8,128)(2,1)S(1)} collective-permute-done((bf16[192,768]{1,0:T(8,128)(2,1)S(1)}, bf16[192,768]{1,0:T(8,128)(2,1)S(1)}, u32[]{:S(2)}, u32[]{:S(2)}) %collective-permute-start.5) | collective-permute-done | bytes 294944 | tf_op jit(solution)/shard_map/ppermute | solution.py:57
  30.5 2.5 %collective-permute-done.4.refs_2_ = bf16[192,896]{1,0:T(8,128)(2,1)S(1)} collective-permute-done((bf16[192,896]{1,0:T(8,128)(2,1)S(1)}, bf16[192,896]{1,0:T(8,128)(2,1)S(1)}, u32[]{:S(2)}, u32[]{:S(2)}) %collective-permute-start.4) | collective-permute-done | bytes 344096 | tf_op jit(solution)/shard_map/ppermute | solution.py:61
  33.1 1.6 collective-permute-start.6
  35.2 12.4 %collective-permute-done.9.refs_2_ = bf16[48,3072]{1,0:T(8,128)(2,1)S(1)} collective-permute-done((bf16[48,3072]{1,0:T(8,128)(2,1)S(1)}, bf16[48,3072]{1,0:T(8,128)(2,1)S(1)}, u32[]{:S(2)}, u32[]{:S(2)}) %collective-permute-start.9) | collective-permute-done | bytes 294944 | tf_op jit(solution)/shard_map/ppermute | solution.py:57
  53.6 2.6 %shard_map.330 = (bf16[256,768]{1,0:T(8,128)(2,1)S(1)}, bf16[512,768]{1,0:T(8,128)(2,1)S(1)}, bf16[512,768]{1,0:T(8,128)(2,1)S(1)}) custom-call(bf16[512,768]{1,0:T(8,128)(2,1)S(1)} %pad_maximum_fusion.refs_4_.refs_0_.refs_1_.refs_2_, bf16[384,1792]{1,0:T(8,128)(2,1)S(1)} %get-tuple-element.99.refs_2_.refs_1_.refs_3_, ...), custom_call_target="tpu_custom_call" | custom-call | flops 1509949440 | bytes 7870464 | tf_op jit(solution)/shard_map/pallas_call | solution.py:142
  56.1 8.4 %collective-permute-done.14.refs_3_ = bf16[192,1536]{1,0:T(8,128)(2,1)S(1)} collective-permute-done((bf16[192,1536]{1,0:T(8,128)(2,1)S(1)}, bf16[192,1536]{1,0:T(8,128)(2,1)S(1)}, u32[]{:S(2)}, u32[]{:S(2)}) %collective-permute-start.14) | collective-permute-done | bytes 589856 | tf_op jit(solution)/shard_map/ppermute | solution.py:57
  67.8 8.4 %shard_map.332.refs_0_.refs_7_ = bf16[256,768]{1,0:T(8,128)(2,1)S(1)} custom-call(s32[1]{0:T(128)} %bitcast.refs_0_, s32[1,3]{1,0:T(1,128)S(1)} %copy-done.25, bf16[256,768]{1,0:T(8,128)(2,1)S(1)} %get-tuple-element.103.refs_4_.refs_2_, bf16[512,768]{1,0:T(8,128)(2,1)S(1)} %get-tuple-element.104.refs_3_, bf16[512,768]{1,0:T(8,128)(2,1)S(1)} %get-tuple-element.105.refs_4_, ...), custom_call_target="tpu_custom_call" | custom-call | flops 905969664 | bytes 2359312 | tf_op jit(solution)/shard_map/pallas_call | solution.py:142
  77.2 16.5 %collective-permute-done.18.refs_1_ = bf16[384,1536]{1,0:T(8,128)(2,1)S(1)} collective-permute-done((bf16[384,1536]{1,0:T(8,128)(2,1)S(1)}, bf16[384,1536]{1,0:T(8,128)(2,1)S(1)}, u32[]{:S(2)}, u32[]{:S(2)}) %collective-permute-start.18) | collective-permute-done | bytes 1179680 | tf_op jit(solution)/shard_map/ppermute | solution.py:61
  96.1 1.7 collective-permute-done.19.refs_4_
  97.8 2.8 %shard_map.335 = (bf16[256,3072]{1,0:T(8,128)(2,1)S(1)}, f32[256,3072]{1,0:T(8,128)S(1)}) custom-call(bf16[256,768]{1,0:T(8,128)(2,1)S(1)} %get-tuple-element.110.refs_2_.refs_0_, bf16[192,3072]{1,0:T(8,128)(2,1)S(1)} %get-tuple-element.107.refs_5_.refs_1_, bf16[192,3072]{1,0:T(8,128)(2,1)S(1)} %get-tuple-element.111.refs_2_, ...), custom_call_target="tpu_custom_call" | custom-call | flops 2415919104 | bytes 9842688 | tf_op jit(solution)/shard_map/pallas_call | solution.py:142
  100.5 3.0 %shard_map.336 = (bf16[256,768]{1,0:T(8,128)(2,1)S(1)}, f32[256,768]{1,0:T(8,128)S(1)}, bf16[256,768]{1,0:T(8,128)(2,1)S(1)}, f32[8,768]{1,0:T(8,128)S(1)}) custom-call(s32[1]{0:T(128)} %bitcast.refs_0_, s32[1,3]{1,0:T(1,128)S(1)} %copy-done.25, bf16[256,3072]{1,0:T(8,128)(2,1)S(1)} %get-tuple-element.113.refs_2_, ...), custom_call_target="tpu_custom_call" | custom-call | flops 1509949440 | bytes 9480208 | tf_op jit(solution)/shard_map/pallas_call | solution.py:142
  104.6 1.8 shard_map.337
  110.7 1.6 collective-permute-done.21.refs_1_
  114.2 2.7 %shard_map.340 = (f32[256,768]{1,0:T(8,128)S(1)}, bf16[256,768]{1,0:T(8,128)(2,1)S(1)}, bf16[256,768]{1,0:T(8,128)(2,1)S(1)}, f32[8,768]{1,0:T(8,128)S(1)}) custom-call(bf16[256,3072]{1,0:T(8,128)(2,1)S(1)} %get-tuple-element.119.refs_2_.refs_0_, bf16[192,3072]{1,0:T(8,128)(2,1)S(1)} %get-tuple-element.107.refs_5_.refs_1_, ...), custom_call_target="tpu_custom_call" | custom-call | flops 1811939328 | bytes 11840512 | tf_op jit(solution)/shard_map/pallas_call | solution.py:142
  116.9 10.5 %shard_map.341 = (bf16[256,768]{1,0:T(8,128)(2,1)S(1)}, bf16[512,768]{1,0:T(8,128)(2,1)S(1)}, bf16[512,768]{1,0:T(8,128)(2,1)S(1)}) custom-call(s32[1]{0:T(128)} %bitcast.refs_0_, s32[1,3]{1,0:T(1,128)S(1)} %copy-done.25, bf16[256,768]{1,0:T(8,128)(2,1)S(1)} %get-tuple-element.103.refs_4_.refs_2_, bf16[512,768]{1,0:T(8,128)(2,1)S(1)} %get-tuple-element.104.refs_3_, ...), custom_call_target="tpu_custom_call" | custom-call | flops 1509949440 | bytes 4325392 | tf_op jit(solution)/shard_map/pallas_call | solution.py:142
  127.4 3.1 %shard_map.342 = (bf16[384,1792]{1,0:T(8,128)(2,1)S(1)}, bf16[384,1536]{1,0:T(8,128)(2,1)S(1)}, bf16[384,1792]{1,0:T(8,128)(2,1)S(1)}, bf16[384,1536]{1,0:T(8,128)(2,1)S(1)}) custom-call(s32[1]{0:T(128)} %bitcast.refs_0_, bf16[768,768]{1,0:T(8,128)(2,1)S(1)} %copy-done.7, bf16[512,768]{1,0:T(8,128)(2,1)S(1)} %pad_maximum_fusion.refs_4_.refs_0_.refs_1_.refs_2_, ...), custom_call_target="tpu_custom_call" | custom-call | flops 1811939328 | bytes 9891844 | tf_op jit(solution)/shard_map/pallas_call | solution.py:142
  131.1 7.1 %collective-permute-done.24.refs_3_ = bf16[384,1536]{1,0:T(8,128)(2,1)S(1)} collective-permute-done((bf16[384,1536]{1,0:T(8,128)(2,1)S(1)}, bf16[384,1536]{1,0:T(8,128)(2,1)S(1)}, u32[]{:S(2)}, u32[]{:S(2)}) %collective-permute-start.24) | collective-permute-done | bytes 1179680 | tf_op jit(solution)/shard_map/ppermute | solution.py:61
  138.2 2.9 %collective-permute-done.23.refs_1_ = bf16[192,3072]{1,0:T(8,128)(2,1)S(1)} collective-permute-done((bf16[192,3072]{1,0:T(8,128)(2,1)S(1)}, bf16[192,3072]{1,0:T(8,128)(2,1)S(1)}, u32[]{:S(2)}, u32[]{:S(2)}) %collective-permute-start.23) | collective-permute-done | bytes 1179680 | tf_op jit(solution)/shard_map/ppermute | solution.py:57
  143.5 2.6 %shard_map.344 = (f32[256,768]{1,0:T(8,128)S(1)}, bf16[256,768]{1,0:T(8,128)(2,1)S(1)}) custom-call(bf16[256,768]{1,0:T(8,128)(2,1)S(1)} %get-tuple-element.126.refs_3_.refs_0_, bf16[512,768]{1,0:T(8,128)(2,1)S(1)} %get-tuple-element.127.refs_4_.refs_1_, bf16[512,768]{1,0:T(8,128)(2,1)S(1)} %get-tuple-element.128.refs_5_.refs_2_, ...), custom_call_target="tpu_custom_call" | custom-call | flops 120795955200 | bytes 9043968 | tf_op jit(solution)/shard_map/pallas_call | solution.py:142
  149.1 8.9 %collective-permute-done.25.refs_1_ = bf16[192,1536]{1,0:T(8,128)(2,1)S(1)} collective-permute-done((bf16[192,1536]{1,0:T(8,128)(2,1)S(1)}, bf16[192,1536]{1,0:T(8,128)(2,1)S(1)}, u32[]{:S(2)}, u32[]{:S(2)}) %collective-permute-start.25) | collective-permute-done | bytes 589856 | tf_op jit(solution)/shard_map/ppermute | solution.py:61
  158.8 8.3 %collective-permute-start.29 = (bf16[48,3072]{1,0:T(8,128)(2,1)S(1)}, bf16[48,3072]{1,0:T(8,128)(2,1)S(1)}, u32[]{:S(2)}, u32[]{:S(2)}) collective-permute-start(bf16[48,3072]{1,0:T(8,128)(2,1)S(1)} %get-tuple-element.148), channel_id=1, source_target_pairs={{0,8},{2,10},{4,12},{6,14},{8,0},{10,2},{12,4},{14,6},{16,24},{18,... | collective-permute-start | bytes 884744 | tf_op jit(solution)/shard_map/ppermute | solution.py:57
  167.1 3.1 %collective-permute-start.30 = (bf16[48,3072]{1,0:T(8,128)(2,1)S(1)}, bf16[48,3072]{1,0:T(8,128)(2,1)S(1)}, u32[]{:S(2)}, u32[]{:S(2)}) collective-permute-start(bf16[48,3072]{1,0:T(8,128)(2,1)S(1)} %get-tuple-element.149), channel_id=1, source_target_pairs={{0,16},{2,18},{4,20},{6,22},{8,24},{10,26},{12,28},{14,30},{16,0},... | collective-permute-start | bytes 884744 | tf_op jit(solution)/shard_map/ppermute | solution.py:57
  174.5 14.5 %collective-permute-done.30.refs_2_ = bf16[48,3072]{1,0:T(8,128)(2,1)S(1)} collective-permute-done((bf16[48,3072]{1,0:T(8,128)(2,1)S(1)}, bf16[48,3072]{1,0:T(8,128)(2,1)S(1)}, u32[]{:S(2)}, u32[]{:S(2)}) %collective-permute-start.30) | collective-permute-done | bytes 294944 | tf_op jit(solution)/shard_map/ppermute | solution.py:57
  190.4 3.9 %collective-permute-start.37 = (bf16[48,1664]{1,0:T(8,128)(2,1)S(1)}, bf16[48,1664]{1,0:T(8,128)(2,1)S(1)}, u32[]{:S(2)}, u32[]{:S(2)}) collective-permute-start(bf16[48,1664]{1,0:T(8,128)(2,1)S(1)} %get-tuple-element.159), channel_id=1, source_target_pairs={{0,8},{2,10},{4,12},{6,14},{8,0},{10,2},{12,4},{14,6},{16,24},{18,... | collective-permute-start | bytes 479240 | tf_op jit(solution)/shard_map/ppermute | solution.py:57
  198.9 2.0 shard_map.351.refs_14_
  201.0 5.3 %collective-permute-done.38.refs_12_ = bf16[48,1664]{1,0:T(8,128)(2,1)S(1)} collective-permute-done((bf16[48,1664]{1,0:T(8,128)(2,1)S(1)}, bf16[48,1664]{1,0:T(8,128)(2,1)S(1)}, u32[]{:S(2)}, u32[]{:S(2)}) %collective-permute-start.38) | collective-permute-done | bytes 159776 | tf_op jit(solution)/shard_map/ppermute | solution.py:57
  (152 shorter events, 47.3 us)
Async XLA Ops:
  3.4 19.5 %collective-permute-start.3 = (bf16[48,1664]{1,0:T(8,128)(2,1)S(1)}, bf16[48,1664]{1,0:T(8,128)(2,1)S(1)}, u32[]{:S(2)}, u32[]{:S(2)}) collective-permute-start(bf16[48,1664]{1,0:T(8,128)(2,1)S(1)} %shard_map.323.refs_0_), channel_id=1, source_target_pairs={{0,24},{2,26},{4,28},{6,30},{8,16},{10,18},{12,20},{14,22},{16,8},... | collective-permute-start | bytes 479240 | tf_op jit(solution)/shard_map/ppermute | solution.py:57
  8.5 14.8 %collective-permute-start.2 = (bf16[48,1664]{1,0:T(8,128)(2,1)S(1)}, bf16[48,1664]{1,0:T(8,128)(2,1)S(1)}, u32[]{:S(2)}, u32[]{:S(2)}) collective-permute-start(bf16[48,1664]{1,0:T(8,128)(2,1)S(1)} %shard_map.323.refs_0_), channel_id=1, source_target_pairs={{0,16},{2,18},{4,20},{6,22},{8,24},{10,26},{12,28},{14,30},{16,0},... | collective-permute-start | bytes 479240 | tf_op jit(solution)/shard_map/ppermute | solution.py:57
  8.5 10.3 %collective-permute-start.1 = (bf16[48,1664]{1,0:T(8,128)(2,1)S(1)}, bf16[48,1664]{1,0:T(8,128)(2,1)S(1)}, u32[]{:S(2)}, u32[]{:S(2)}) collective-permute-start(bf16[48,1664]{1,0:T(8,128)(2,1)S(1)} %shard_map.323.refs_0_), channel_id=1, source_target_pairs={{0,8},{2,10},{4,12},{6,14},{8,0},{10,2},{12,4},{14,6},{16,24},{18,... | collective-permute-start | bytes 479240 | tf_op jit(solution)/shard_map/ppermute | solution.py:57
  9.1 15.8 %collective-permute-start = (bf16[256,768]{1,0:T(8,128)(2,1)}, bf16[256,768]{1,0:T(8,128)(2,1)S(1)}, u32[]{:S(2)}, u32[]{:S(2)}) collective-permute-start(bf16[256,768]{1,0:T(8,128)(2,1)} %param.20), channel_id=1, source_target_pairs={{0,1},{1,0},{2,3},{3,2},{4,5},{5,4},{6,7},{7,6},{8,9},{9,8},{10,11... | collective-permute-start | bytes 1179656 | tf_op jit(solution)/shard_map/ppermute | solution.py:61
  18.9 16.3 %collective-permute-start.10 = (bf16[48,3072]{1,0:T(8,128)(2,1)S(1)}, bf16[48,3072]{1,0:T(8,128)(2,1)S(1)}, u32[]{:S(2)}, u32[]{:S(2)}) collective-permute-start(bf16[48,3072]{1,0:T(8,128)(2,1)S(1)} %shard_map.326.refs_0_), channel_id=1, source_target_pairs={{0,24},{2,26},{4,28},{6,30},{8,16},{10,18},{12,20},{14,22},{16,8},... | collective-permute-start | bytes 884744 | tf_op jit(solution)/shard_map/ppermute | solution.py:57
  20.0 27.6 %collective-permute-start.9 = (bf16[48,3072]{1,0:T(8,128)(2,1)S(1)}, bf16[48,3072]{1,0:T(8,128)(2,1)S(1)}, u32[]{:S(2)}, u32[]{:S(2)}) collective-permute-start(bf16[48,3072]{1,0:T(8,128)(2,1)S(1)} %shard_map.326.refs_0_), channel_id=1, source_target_pairs={{0,16},{2,18},{4,20},{6,22},{8,24},{10,26},{12,28},{14,30},{16,0},... | collective-permute-start | bytes 884744 | tf_op jit(solution)/shard_map/ppermute | solution.py:57
  22.9 24.7 %collective-permute-start.8 = (bf16[48,3072]{1,0:T(8,128)(2,1)S(1)}, bf16[48,3072]{1,0:T(8,128)(2,1)S(1)}, u32[]{:S(2)}, u32[]{:S(2)}) collective-permute-start(bf16[48,3072]{1,0:T(8,128)(2,1)S(1)} %shard_map.326.refs_0_), channel_id=1, source_target_pairs={{0,8},{2,10},{4,12},{6,14},{8,0},{10,2},{12,4},{14,6},{16,24},{18,... | collective-permute-start | bytes 884744 | tf_op jit(solution)/shard_map/ppermute | solution.py:57
  33.1 14.6 %collective-permute-start.6 = (bf16[384,768]{1,0:T(8,128)(2,1)S(1)}, bf16[384,768]{1,0:T(8,128)(2,1)S(1)}, u32[]{:S(2)}, u32[]{:S(2)}) collective-permute-start(bf16[384,768]{1,0:T(8,128)(2,1)S(1)} %get-tuple-element.96.refs_0_), channel_id=1, source_target_pairs={{0,1},{1,0},{2,3},{3,2},{4,5},{5,4},{6,7},{7,6},{8,9},{9,8},{10,11... | collective-permute-start | bytes 1769480 | tf_op jit(solution)/shard_map/ppermute | solution.py:61
  34.7 13.8 %collective-permute-start.7 = (bf16[192,1792]{1,0:T(8,128)(2,1)S(1)}, bf16[192,1792]{1,0:T(8,128)(2,1)S(1)}, u32[]{:S(2)}, u32[]{:S(2)}) collective-permute-start(bf16[192,1792]{1,0:T(8,128)(2,1)S(1)} %get-tuple-element.97.refs_1_), channel_id=1, source_target_pairs={{0,4},{2,6},{4,0},{6,2},{8,12},{10,14},{12,8},{14,10},{16,20},{18,... | collective-permute-start | bytes 2064392 | tf_op jit(solution)/shard_map/ppermute | solution.py:57
  49.2 15.3 %collective-permute-start.14 = (bf16[192,1536]{1,0:T(8,128)(2,1)S(1)}, bf16[192,1536]{1,0:T(8,128)(2,1)S(1)}, u32[]{:S(2)}, u32[]{:S(2)}) collective-permute-start(bf16[192,1536]{1,0:T(8,128)(2,1)S(1)} %get-tuple-element.106.refs_1_), channel_id=1, source_target_pairs={{0,4},{2,6},{4,0},{6,2},{8,12},{10,14},{12,8},{14,10},{16,20},{18,... | collective-permute-start | bytes 1769480 | tf_op jit(solution)/shard_map/ppermute | solution.py:57
  50.0 15.0 %collective-permute-start.13 = (bf16[192,1536]{1,0:T(8,128)(2,1)S(1)}, bf16[192,1536]{1,0:T(8,128)(2,1)S(1)}, u32[]{:S(2)}, u32[]{:S(2)}) collective-permute-start(bf16[192,1536]{1,0:T(8,128)(2,1)S(1)} %get-tuple-element.98.refs_4_.refs_0_), channel_id=1, source_target_pairs={{0,1},{1,0},{2,3},{3,2},{4,5},{5,4},{6,7},{7,6},{8,9},{9,8},{10,11... | collective-permute-start | bytes 1769480 | tf_op jit(solution)/shard_map/ppermute | solution.py:61
  65.2 11.0 %collective-permute-start.16 = (bf16[384,1536]{1,0:T(8,128)(2,1)S(1)}, bf16[384,1536]{1,0:T(8,128)(2,1)S(1)}, u32[]{:S(2)}, u32[]{:S(2)}) collective-permute-start(bf16[384,1536]{1,0:T(8,128)(2,1)S(1)} %get-tuple-element.109.refs_3_.refs_1_), channel_id=1, source_target_pairs={{0,2},{2,0},{4,6},{6,4},{8,10},{10,8},{12,14},{14,12},{16,18},{18,... | collective-permute-start | bytes 3538952 | tf_op jit(solution)/shard_map/ppermute | solution.py:57
  65.3 10.9 %collective-permute-start.15 = (bf16[192,3072]{1,0:T(8,128)(2,1)S(1)}, bf16[192,3072]{1,0:T(8,128)(2,1)S(1)}, u32[]{:S(2)}, u32[]{:S(2)}) collective-permute-start(bf16[192,3072]{1,0:T(8,128)(2,1)S(1)} %get-tuple-element.107.refs_5_.refs_1_), channel_id=1, source_target_pairs={{0,2},{2,0},{4,6},{6,4},{8,10},{10,8},{12,14},{14,12},{16,18},{18,... | collective-permute-start | bytes 3538952 | tf_op jit(solution)/shard_map/ppermute | solution.py:57
  65.8 28.0 %collective-permute-start.18 = (bf16[384,1536]{1,0:T(8,128)(2,1)S(1)}, bf16[384,1536]{1,0:T(8,128)(2,1)S(1)}, u32[]{:S(2)}, u32[]{:S(2)}) collective-permute-start(bf16[384,1536]{1,0:T(8,128)(2,1)S(1)} %get-tuple-element.109.refs_3_.refs_1_), channel_id=1, source_target_pairs={{0,1},{1,0},{2,3},{3,2},{4,5},{5,4},{6,7},{7,6},{8,9},{9,8},{10,11... | collective-permute-start | bytes 3538952 | tf_op jit(solution)/shard_map/ppermute | solution.py:61
  67.2 27.7 %collective-permute-start.17 = (bf16[192,3072]{1,0:T(8,128)(2,1)S(1)}, bf16[192,3072]{1,0:T(8,128)(2,1)S(1)}, u32[]{:S(2)}, u32[]{:S(2)}) collective-permute-start(bf16[192,3072]{1,0:T(8,128)(2,1)S(1)} %get-tuple-element.107.refs_5_.refs_1_), channel_id=1, source_target_pairs={{0,4},{2,6},{4,0},{6,2},{8,12},{10,14},{12,8},{14,10},{16,20},{18,... | collective-permute-start | bytes 3538952 | tf_op jit(solution)/shard_map/ppermute | solution.py:57
  109.9 28.3 %collective-permute-start.24 = (bf16[384,1536]{1,0:T(8,128)(2,1)S(1)}, bf16[384,1536]{1,0:T(8,128)(2,1)S(1)}, u32[]{:S(2)}, u32[]{:S(2)}) collective-permute-start(bf16[384,1536]{1,0:T(8,128)(2,1)S(1)} %get-tuple-element.131), channel_id=1, source_target_pairs={{0,1},{1,0},{2,3},{3,2},{4,5},{5,4},{6,7},{7,6},{8,9},{9,8},{10,11... | collective-permute-start | bytes 3538952 | tf_op jit(solution)/shard_map/ppermute | solution.py:61
  113.0 28.1 %collective-permute-start.23 = (bf16[192,3072]{1,0:T(8,128)(2,1)S(1)}, bf16[192,3072]{1,0:T(8,128)(2,1)S(1)}, u32[]{:S(2)}, u32[]{:S(2)}) collective-permute-start(bf16[192,3072]{1,0:T(8,128)(2,1)S(1)} %get-tuple-element.130), channel_id=1, source_target_pairs={{0,4},{2,6},{4,0},{6,2},{8,12},{10,14},{12,8},{14,10},{16,20},{18,... | collective-permute-start | bytes 3538952 | tf_op jit(solution)/shard_map/ppermute | solution.py:57
  130.5 15.7 %collective-permute-start.28 = (bf16[384,1536]{1,0:T(8,128)(2,1)S(1)}, bf16[384,1536]{1,0:T(8,128)(2,1)S(1)}, u32[]{:S(2)}, u32[]{:S(2)}) collective-permute-start(bf16[384,1536]{1,0:T(8,128)(2,1)S(1)} %get-tuple-element.145), channel_id=1, source_target_pairs={{0,2},{2,0},{4,6},{6,4},{8,10},{10,8},{12,14},{14,12},{16,18},{18,... | collective-permute-start | bytes 3538952 | tf_op jit(solution)/shard_map/ppermute | solution.py:57
  130.6 15.6 %collective-permute-start.27 = (bf16[384,1792]{1,0:T(8,128)(2,1)S(1)}, bf16[384,1792]{1,0:T(8,128)(2,1)S(1)}, u32[]{:S(2)}, u32[]{:S(2)}) collective-permute-start(bf16[384,1792]{1,0:T(8,128)(2,1)S(1)} %get-tuple-element.143), channel_id=1, source_target_pairs={{0,2},{2,0},{4,6},{6,4},{8,10},{10,8},{12,14},{14,12},{16,18},{18,... | collective-permute-start | bytes 4128776 | tf_op jit(solution)/shard_map/ppermute | solution.py:57
  141.6 16.3 %collective-permute-start.25 = (bf16[192,1536]{1,0:T(8,128)(2,1)S(1)}, bf16[192,1536]{1,0:T(8,128)(2,1)S(1)}, u32[]{:S(2)}, u32[]{:S(2)}) collective-permute-start(bf16[192,1536]{1,0:T(8,128)(2,1)S(1)} %get-tuple-element.140), channel_id=1, source_target_pairs={{0,1},{1,0},{2,3},{3,2},{4,5},{5,4},{6,7},{7,6},{8,9},{9,8},{10,11... | collective-permute-start | bytes 1769480 | tf_op jit(solution)/shard_map/ppermute | solution.py:61
  142.2 16.3 %collective-permute-start.26 = (bf16[192,1536]{1,0:T(8,128)(2,1)S(1)}, bf16[192,1536]{1,0:T(8,128)(2,1)S(1)}, u32[]{:S(2)}, u32[]{:S(2)}) collective-permute-start(bf16[192,1536]{1,0:T(8,128)(2,1)S(1)} %get-tuple-element.142), channel_id=1, source_target_pairs={{0,4},{2,6},{4,0},{6,2},{8,12},{10,14},{12,8},{14,10},{16,20},{18,... | collective-permute-start | bytes 1769480 | tf_op jit(solution)/shard_map/ppermute | solution.py:57
  146.8 24.5 %collective-permute-start.32 = (bf16[192,1792]{1,0:T(8,128)(2,1)S(1)}, bf16[192,1792]{1,0:T(8,128)(2,1)S(1)}, u32[]{:S(2)}, u32[]{:S(2)}) collective-permute-start(bf16[192,1792]{1,0:T(8,128)(2,1)S(1)} %get-tuple-element.151), channel_id=1, source_target_pairs={{0,4},{2,6},{4,0},{6,2},{8,12},{10,14},{12,8},{14,10},{16,20},{18,... | collective-permute-start | bytes 2064392 | tf_op jit(solution)/shard_map/ppermute | solution.py:57
  147.6 22.6 %collective-permute-start.33 = (bf16[384,768]{1,0:T(8,128)(2,1)S(1)}, bf16[384,768]{1,0:T(8,128)(2,1)S(1)}, u32[]{:S(2)}, u32[]{:S(2)}) collective-permute-start(bf16[384,768]{1,0:T(8,128)(2,1)S(1)} %get-tuple-element.153), channel_id=1, source_target_pairs={{0,1},{1,0},{2,3},{3,2},{4,5},{5,4},{6,7},{7,6},{8,9},{9,8},{10,11... | collective-permute-start | bytes 1769480 | tf_op jit(solution)/shard_map/ppermute | solution.py:61
  158.8 15.8 %collective-permute-start.29 = (bf16[48,3072]{1,0:T(8,128)(2,1)S(1)}, bf16[48,3072]{1,0:T(8,128)(2,1)S(1)}, u32[]{:S(2)}, u32[]{:S(2)}) collective-permute-start(bf16[48,3072]{1,0:T(8,128)(2,1)S(1)} %get-tuple-element.148), channel_id=1, source_target_pairs={{0,8},{2,10},{4,12},{6,14},{8,0},{10,2},{12,4},{14,6},{16,24},{18,... | collective-permute-start | bytes 884744 | tf_op jit(solution)/shard_map/ppermute | solution.py:57
  167.1 21.9 %collective-permute-start.30 = (bf16[48,3072]{1,0:T(8,128)(2,1)S(1)}, bf16[48,3072]{1,0:T(8,128)(2,1)S(1)}, u32[]{:S(2)}, u32[]{:S(2)}) collective-permute-start(bf16[48,3072]{1,0:T(8,128)(2,1)S(1)} %get-tuple-element.149), channel_id=1, source_target_pairs={{0,16},{2,18},{4,20},{6,22},{8,24},{10,26},{12,28},{14,30},{16,0},... | collective-permute-start | bytes 884744 | tf_op jit(solution)/shard_map/ppermute | solution.py:57
  170.2 18.8 %collective-permute-start.31 = (bf16[48,3072]{1,0:T(8,128)(2,1)S(1)}, bf16[48,3072]{1,0:T(8,128)(2,1)S(1)}, u32[]{:S(2)}, u32[]{:S(2)}) collective-permute-start(bf16[48,3072]{1,0:T(8,128)(2,1)S(1)} %get-tuple-element.150), channel_id=1, source_target_pairs={{0,24},{2,26},{4,28},{6,30},{8,16},{10,18},{12,20},{14,22},{16,8},... | collective-permute-start | bytes 884744 | tf_op jit(solution)/shard_map/ppermute | solution.py:57
  171.6 18.7 %collective-permute-start.36 = (bf16[192,768]{1,0:T(8,128)(2,1)S(1)}, bf16[192,768]{1,0:T(8,128)(2,1)S(1)}, u32[]{:S(2)}, u32[]{:S(2)}) collective-permute-start(bf16[192,768]{1,0:T(8,128)(2,1)S(1)} %get-tuple-element.157), channel_id=1, source_target_pairs={{0,4},{2,6},{4,0},{6,2},{8,12},{10,14},{12,8},{14,10},{16,20},{18,... | collective-permute-start | bytes 884744 | tf_op jit(solution)/shard_map/ppermute | solution.py:57
  172.9 17.3 %collective-permute-start.35 = (bf16[192,896]{1,0:T(8,128)(2,1)S(1)}, bf16[192,896]{1,0:T(8,128)(2,1)S(1)}, u32[]{:S(2)}, u32[]{:S(2)}) collective-permute-start(bf16[192,896]{1,0:T(8,128)(2,1)S(1)} %get-tuple-element.155), channel_id=1, source_target_pairs={{0,1},{1,0},{2,3},{3,2},{4,5},{5,4},{6,7},{7,6},{8,9},{9,8},{10,11... | collective-permute-start | bytes 1032200 | tf_op jit(solution)/shard_map/ppermute | solution.py:61
  189.2 9.8 %collective-permute-start.34 = (bf16[256,768]{1,0:T(8,128)(2,1)S(1)}, bf16[256,768]{1,0:T(8,128)(2,1)S(1)}, u32[]{:S(2)}, u32[]{:S(2)}) collective-permute-start(bf16[256,768]{1,0:T(8,128)(2,1)S(1)} %shard_map.349), channel_id=1, source_target_pairs={{0,1},{1,0},{2,3},{3,2},{4,5},{5,4},{6,7},{7,6},{8,9},{9,8},{10,11... | collective-permute-start | bytes 1179656 | tf_op jit(solution)/shard_map/ppermute | solution.py:61
  190.4 10.5 %collective-permute-start.37 = (bf16[48,1664]{1,0:T(8,128)(2,1)S(1)}, bf16[48,1664]{1,0:T(8,128)(2,1)S(1)}, u32[]{:S(2)}, u32[]{:S(2)}) collective-permute-start(bf16[48,1664]{1,0:T(8,128)(2,1)S(1)} %get-tuple-element.159), channel_id=1, source_target_pairs={{0,8},{2,10},{4,12},{6,14},{8,0},{10,2},{12,4},{14,6},{16,24},{18,... | collective-permute-start | bytes 479240 | tf_op jit(solution)/shard_map/ppermute | solution.py:57
  194.3 11.9 %collective-permute-start.38 = (bf16[48,1664]{1,0:T(8,128)(2,1)S(1)}, bf16[48,1664]{1,0:T(8,128)(2,1)S(1)}, u32[]{:S(2)}, u32[]{:S(2)}) collective-permute-start(bf16[48,1664]{1,0:T(8,128)(2,1)S(1)} %get-tuple-element.160), channel_id=1, source_target_pairs={{0,16},{2,18},{4,20},{6,22},{8,24},{10,26},{12,28},{14,30},{16,0},... | collective-permute-start | bytes 479240 | tf_op jit(solution)/shard_map/ppermute | solution.py:57
  195.7 10.5 %collective-permute-start.39 = (bf16[48,1664]{1,0:T(8,128)(2,1)S(1)}, bf16[48,1664]{1,0:T(8,128)(2,1)S(1)}, u32[]{:S(2)}, u32[]{:S(2)}) collective-permute-start(bf16[48,1664]{1,0:T(8,128)(2,1)S(1)} %get-tuple-element.161), channel_id=1, source_target_pairs={{0,24},{2,26},{4,28},{6,30},{8,16},{10,18},{12,20},{14,22},{16,8},... | collective-permute-start | bytes 479240 | tf_op jit(solution)/shard_map/ppermute | solution.py:57
  (38 other events, 345.5 us)

commit v8 on v7

--- a/solution.py
+++ b/solution.py
@@ -698,7 +698,7 @@
         [shape_of(shard_rows, full_inner, LOW)],
         [w_in, w_back.T],
         0,
-        after=one_high[1:2],
+        after=one[:1],
     )[0]
     pair_high = gather_high(shard_pair)
 
@@ -833,7 +833,7 @@
         400 * unit,
         after=[a_keep],
     )
-    a_keep, a_send, b_keep, b_send = split_core(*one, after=[grad_own])
+    a_keep, a_send, b_keep, b_send = split_core(*one, after=[grad_own, pair[1], pair[3]])
     one = a_keep, swap_dp(a_send, 2), b_keep, swap_tensor(b_send)
     pair = send_high(split_high(*pair, after=[a_keep]))
     a_keep, a_send, b_keep, b_send = split_plane(*one, after=pair[:1])

time: 209 us -> 206 us (0.986)
  starting transfers between devices: 50.4 us -> 42.2 us
  waiting for transfers between devices: 96.5 us -> 101 us
    ppermute x10, waiting for transfers between devices: 35.6 us -> 44.1 us  [swap_tensor(): return lax.ppermute(values, 'tensor', [(0, 1), (1, 0)])]
    ppermute x30, starting transfers between devices: 38.1 us -> 30.6 us  [swap_dp(): return lax.ppermute(values, 'dp', [(i, i ^ mask) for i in range(size)])]
    ppermute x30, waiting for transfers between devices: 60.9 us -> 57.3 us  [swap_dp(): return lax.ppermute(values, 'dp', [(i, i ^ mask) for i in range(size)])]
  transfers between devices with their start and end apart: 40 -> 40, of which waited for: 20 -> 22; matrix products, arithmetic and copies ran while one was open for 4% -> 4% of each run, Pallas kernels for 20% -> 20%
where the time goes in v8:
time: 206 us; the launch traced here: 205 us
  waiting for transfers between devices  101 us (49%)
  Pallas kernels  46.6 us (23%)
  starting transfers between devices  42.2 us (20%)
  matrix products  6.74 us (3%)
  local copies, waits for them, and re-layouts  3.85 us (2%)
  other arithmetic  3.28 us (2%)
    ppermute x30, waiting for transfers between devices, swap_dp(): return lax.ppermute(values, 'dp', [(i, i ^ mask) for i in range(size)])  57.3 us
    pallas_call x28, Pallas kernels, run(): pl.pallas_call(body, grid=grid, out_shape=list(outs), in_specs=list(in_sp...  46.6 us
    ppermute x10, waiting for transfers between devices, swap_tensor(): return lax.ppermute(values, 'tensor', [(0, 1), (1, 0)])  44.1 us
    ppermute x30, starting transfers between devices, swap_dp(): return lax.ppermute(values, 'dp', [(i, i ^ mask) for i in range(size)])  30.6 us
    ppermute x10, starting transfers between devices, swap_tensor(): return lax.ppermute(values, 'tensor', [(0, 1), (1, 0)])  11.5 us
  transfers between devices with their start and end apart: 40, of which 22 were waited for; matrix products, arithmetic and copies ran while one was open for 4% of the time, Pallas kernels for 20%

profile of v8, /device:TPU:0, one launch (start us, length us, event | category | flops | bytes accessed | tf_op | source)
XLA Modules:
  0.0 205.4 jit_solution(8057882877408988980)
XLA Ops:
  3.4 5.1 %collective-permute-start.3 = (bf16[48,1664]{1,0:T(8,128)(2,1)S(1)}, bf16[48,1664]{1,0:T(8,128)(2,1)S(1)}, u32[]{:S(2)}, u32[]{:S(2)}) collective-permute-start(bf16[48,1664]{1,0:T(8,128)(2,1)S(1)} %shard_map.323.refs_0_), channel_id=1, source_target_pairs={{0,24},{2,26},{4,28},{6,30},{8,16},{10,18},{12,20},{14,22},{16,8},... | collective-permute-start | bytes 479240 | tf_op jit(solution)/shard_map/ppermute | solution.py:57
  9.1 1.6 collective-permute-start
  13.5 8.5 %collective-permute-done.2.refs_2_ = bf16[48,1664]{1,0:T(8,128)(2,1)S(1)} collective-permute-done((bf16[48,1664]{1,0:T(8,128)(2,1)S(1)}, bf16[48,1664]{1,0:T(8,128)(2,1)S(1)}, u32[]{:S(2)}, u32[]{:S(2)}) %collective-permute-start.2) | collective-permute-done | bytes 159776 | tf_op jit(solution)/shard_map/ppermute | solution.py:57
  22.2 2.6 %collective-permute-start.10 = (bf16[48,3072]{1,0:T(8,128)(2,1)S(1)}, bf16[48,3072]{1,0:T(8,128)(2,1)S(1)}, u32[]{:S(2)}, u32[]{:S(2)}) collective-permute-start(bf16[48,3072]{1,0:T(8,128)(2,1)S(1)} %shard_map.326.refs_0_), channel_id=1, source_target_pairs={{0,24},{2,26},{4,28},{6,30},{8,16},{10,18},{12,20},{14,22},{16,8},... | collective-permute-start | bytes 884744 | tf_op jit(solution)/shard_map/ppermute | solution.py:57
  24.7 1.9 collective-permute-start.8
  30.3 4.7 %collective-permute-done.5.refs_3_ = bf16[192,768]{1,0:T(8,128)(2,1)S(1)} collective-permute-done((bf16[192,768]{1,0:T(8,128)(2,1)S(1)}, bf16[192,768]{1,0:T(8,128)(2,1)S(1)}, u32[]{:S(2)}, u32[]{:S(2)}) %collective-permute-start.5) | collective-permute-done | bytes 294944 | tf_op jit(solution)/shard_map/ppermute | solution.py:57
  38.1 10.1 %collective-permute-done.9.refs_2_ = bf16[48,3072]{1,0:T(8,128)(2,1)S(1)} collective-permute-done((bf16[48,3072]{1,0:T(8,128)(2,1)S(1)}, bf16[48,3072]{1,0:T(8,128)(2,1)S(1)}, u32[]{:S(2)}, u32[]{:S(2)}) %collective-permute-start.9) | collective-permute-done | bytes 294944 | tf_op jit(solution)/shard_map/ppermute | solution.py:57
  48.2 2.7 %collective-permute-done.7.refs_3_ = bf16[192,1792]{1,0:T(8,128)(2,1)S(1)} collective-permute-done((bf16[192,1792]{1,0:T(8,128)(2,1)S(1)}, bf16[192,1792]{1,0:T(8,128)(2,1)S(1)}, u32[]{:S(2)}, u32[]{:S(2)}) %collective-permute-start.7) | collective-permute-done | bytes 688160 | tf_op jit(solution)/shard_map/ppermute | solution.py:57
  56.0 2.6 %shard_map.330 = (bf16[256,768]{1,0:T(8,128)(2,1)S(1)}, bf16[512,768]{1,0:T(8,128)(2,1)S(1)}, bf16[512,768]{1,0:T(8,128)(2,1)S(1)}) custom-call(bf16[512,768]{1,0:T(8,128)(2,1)S(1)} %pad_maximum_fusion.refs_4_.refs_0_.refs_1_.refs_2_, bf16[384,1792]{1,0:T(8,128)(2,1)S(1)} %get-tuple-element.99.refs_2_.refs_1_.refs_3_, ...), custom_call_target="tpu_custom_call" | custom-call | flops 1509949440 | bytes 7870464 | tf_op jit(solution)/shard_map/pallas_call | solution.py:142
  58.6 8.4 %collective-permute-done.14.refs_3_ = bf16[192,1536]{1,0:T(8,128)(2,1)S(1)} collective-permute-done((bf16[192,1536]{1,0:T(8,128)(2,1)S(1)}, bf16[192,1536]{1,0:T(8,128)(2,1)S(1)}, u32[]{:S(2)}, u32[]{:S(2)}) %collective-permute-start.14) | collective-permute-done | bytes 589856 | tf_op jit(solution)/shard_map/ppermute | solution.py:57
  70.1 8.4 %shard_map.332.refs_0_.refs_7_ = bf16[256,768]{1,0:T(8,128)(2,1)S(1)} custom-call(s32[1]{0:T(128)} %bitcast.refs_0_, s32[1,3]{1,0:T(1,128)S(1)} %copy-done.25, bf16[256,768]{1,0:T(8,128)(2,1)S(1)} %get-tuple-element.103.refs_4_.refs_2_, bf16[512,768]{1,0:T(8,128)(2,1)S(1)} %get-tuple-element.104.refs_3_, bf16[512,768]{1,0:T(8,128)(2,1)S(1)} %get-tuple-element.105.refs_4_, ...), custom_call_target="tpu_custom_call" | custom-call | flops 905969664 | bytes 2359312 | tf_op jit(solution)/shard_map/pallas_call | solution.py:142
  79.5 17.5 %collective-permute-done.18.refs_1_ = bf16[384,1536]{1,0:T(8,128)(2,1)S(1)} collective-permute-done((bf16[384,1536]{1,0:T(8,128)(2,1)S(1)}, bf16[384,1536]{1,0:T(8,128)(2,1)S(1)}, u32[]{:S(2)}, u32[]{:S(2)}) %collective-permute-start.18) | collective-permute-done | bytes 1179680 | tf_op jit(solution)/shard_map/ppermute | solution.py:61
  98.4 1.7 collective-permute-done.19.refs_4_
  100.1 2.8 %shard_map.335 = (bf16[256,3072]{1,0:T(8,128)(2,1)S(1)}, f32[256,3072]{1,0:T(8,128)S(1)}) custom-call(bf16[256,768]{1,0:T(8,128)(2,1)S(1)} %get-tuple-element.110.refs_2_.refs_0_, bf16[192,3072]{1,0:T(8,128)(2,1)S(1)} %get-tuple-element.107.refs_5_.refs_1_, bf16[192,3072]{1,0:T(8,128)(2,1)S(1)} %get-tuple-element.111.refs_2_, ...), custom_call_target="tpu_custom_call" | custom-call | flops 2415919104 | bytes 9842688 | tf_op jit(solution)/shard_map/pallas_call | solution.py:142
  102.9 3.0 %shard_map.336 = (bf16[256,768]{1,0:T(8,128)(2,1)S(1)}, f32[256,768]{1,0:T(8,128)S(1)}, bf16[256,768]{1,0:T(8,128)(2,1)S(1)}, f32[8,768]{1,0:T(8,128)S(1)}) custom-call(s32[1]{0:T(128)} %bitcast.refs_0_, s32[1,3]{1,0:T(1,128)S(1)} %copy-done.25, bf16[256,3072]{1,0:T(8,128)(2,1)S(1)} %get-tuple-element.113.refs_2_, ...), custom_call_target="tpu_custom_call" | custom-call | flops 1509949440 | bytes 9480208 | tf_op jit(solution)/shard_map/pallas_call | solution.py:142
  106.9 1.8 shard_map.337
  112.2 1.8 collective-permute-start.24
  116.5 2.7 %shard_map.340 = (f32[256,768]{1,0:T(8,128)S(1)}, bf16[256,768]{1,0:T(8,128)(2,1)S(1)}, bf16[256,768]{1,0:T(8,128)(2,1)S(1)}, f32[8,768]{1,0:T(8,128)S(1)}) custom-call(bf16[256,3072]{1,0:T(8,128)(2,1)S(1)} %get-tuple-element.119.refs_2_.refs_0_, bf16[192,3072]{1,0:T(8,128)(2,1)S(1)} %get-tuple-element.107.refs_5_.refs_1_, ...), custom_call_target="tpu_custom_call" | custom-call | flops 1811939328 | bytes 11840512 | tf_op jit(solution)/shard_map/pallas_call | solution.py:142
  119.2 10.5 %shard_map.341 = (bf16[256,768]{1,0:T(8,128)(2,1)S(1)}, bf16[512,768]{1,0:T(8,128)(2,1)S(1)}, bf16[512,768]{1,0:T(8,128)(2,1)S(1)}) custom-call(s32[1]{0:T(128)} %bitcast.refs_0_, s32[1,3]{1,0:T(1,128)S(1)} %copy-done.25, bf16[256,768]{1,0:T(8,128)(2,1)S(1)} %get-tuple-element.103.refs_4_.refs_2_, bf16[512,768]{1,0:T(8,128)(2,1)S(1)} %get-tuple-element.104.refs_3_, ...), custom_call_target="tpu_custom_call" | custom-call | flops 1509949440 | bytes 4325392 | tf_op jit(solution)/shard_map/pallas_call | solution.py:142
  129.7 3.1 %shard_map.342 = (bf16[384,1792]{1,0:T(8,128)(2,1)S(1)}, bf16[384,1536]{1,0:T(8,128)(2,1)S(1)}, bf16[384,1792]{1,0:T(8,128)(2,1)S(1)}, bf16[384,1536]{1,0:T(8,128)(2,1)S(1)}) custom-call(s32[1]{0:T(128)} %bitcast.refs_0_, bf16[768,768]{1,0:T(8,128)(2,1)S(1)} %copy-done.7, bf16[512,768]{1,0:T(8,128)(2,1)S(1)} %pad_maximum_fusion.refs_4_.refs_0_.refs_1_.refs_2_, ...), custom_call_target="tpu_custom_call" | custom-call | flops 1811939328 | bytes 9891844 | tf_op jit(solution)/shard_map/pallas_call | solution.py:142
  133.4 7.1 %collective-permute-done.24.refs_3_ = bf16[384,1536]{1,0:T(8,128)(2,1)S(1)} collective-permute-done((bf16[384,1536]{1,0:T(8,128)(2,1)S(1)}, bf16[384,1536]{1,0:T(8,128)(2,1)S(1)}, u32[]{:S(2)}, u32[]{:S(2)}) %collective-permute-start.24) | collective-permute-done | bytes 1179680 | tf_op jit(solution)/shard_map/ppermute | solution.py:61
  140.5 2.9 %collective-permute-done.23.refs_1_ = bf16[192,3072]{1,0:T(8,128)(2,1)S(1)} collective-permute-done((bf16[192,3072]{1,0:T(8,128)(2,1)S(1)}, bf16[192,3072]{1,0:T(8,128)(2,1)S(1)}, u32[]{:S(2)}, u32[]{:S(2)}) %collective-permute-start.23) | collective-permute-done | bytes 1179680 | tf_op jit(solution)/shard_map/ppermute | solution.py:57
  146.0 2.6 %shard_map.344 = (f32[256,768]{1,0:T(8,128)S(1)}, bf16[256,768]{1,0:T(8,128)(2,1)S(1)}) custom-call(bf16[256,768]{1,0:T(8,128)(2,1)S(1)} %get-tuple-element.126.refs_3_.refs_0_, bf16[512,768]{1,0:T(8,128)(2,1)S(1)} %get-tuple-element.127.refs_4_.refs_1_, bf16[512,768]{1,0:T(8,128)(2,1)S(1)} %get-tuple-element.128.refs_5_.refs_2_, ...), custom_call_target="tpu_custom_call" | custom-call | flops 120795955200 | bytes 9043968 | tf_op jit(solution)/shard_map/pallas_call | solution.py:142
  148.7 9.9 %collective-permute-done.25.refs_5_.refs_1_ = bf16[192,1536]{1,0:T(8,128)(2,1)S(1)} collective-permute-done((bf16[192,1536]{1,0:T(8,128)(2,1)S(1)}, bf16[192,1536]{1,0:T(8,128)(2,1)S(1)}, u32[]{:S(2)}, u32[]{:S(2)}) %collective-permute-start.25) | collective-permute-done | bytes 589856 | tf_op jit(solution)/shard_map/ppermute | solution.py:61
  162.3 2.2 %collective-permute-start.30 = (bf16[48,3072]{1,0:T(8,128)(2,1)S(1)}, bf16[48,3072]{1,0:T(8,128)(2,1)S(1)}, u32[]{:S(2)}, u32[]{:S(2)}) collective-permute-start(bf16[48,3072]{1,0:T(8,128)(2,1)S(1)} %get-tuple-element.149), channel_id=1, source_target_pairs={{0,16},{2,18},{4,20},{6,22},{8,24},{10,26},{12,28},{14,30},{16,0},... | collective-permute-start | bytes 884744 | tf_op jit(solution)/shard_map/ppermute | solution.py:57
  164.5 1.8 collective-permute-start.31
  166.2 7.8 %collective-permute-done.33.refs_3_ = bf16[384,768]{1,0:T(8,128)(2,1)S(1)} collective-permute-done((bf16[384,768]{1,0:T(8,128)(2,1)S(1)}, bf16[384,768]{1,0:T(8,128)(2,1)S(1)}, u32[]{:S(2)}, u32[]{:S(2)}) %collective-permute-start.33) | collective-permute-done | bytes 589856 | tf_op jit(solution)/shard_map/ppermute | solution.py:61
  174.0 1.9 collective-permute-done.32.refs_1_
  177.3 7.8 %collective-permute-done.30.refs_2_ = bf16[48,3072]{1,0:T(8,128)(2,1)S(1)} collective-permute-done((bf16[48,3072]{1,0:T(8,128)(2,1)S(1)}, bf16[48,3072]{1,0:T(8,128)(2,1)S(1)}, u32[]{:S(2)}, u32[]{:S(2)}) %collective-permute-start.30) | collective-permute-done | bytes 294944 | tf_op jit(solution)/shard_map/ppermute | solution.py:57
  187.6 3.4 %collective-permute-start.37 = (bf16[48,1664]{1,0:T(8,128)(2,1)S(1)}, bf16[48,1664]{1,0:T(8,128)(2,1)S(1)}, u32[]{:S(2)}, u32[]{:S(2)}) collective-permute-start(bf16[48,1664]{1,0:T(8,128)(2,1)S(1)} %get-tuple-element.159), channel_id=1, source_target_pairs={{0,8},{2,10},{4,12},{6,14},{8,0},{10,2},{12,4},{14,6},{16,24},{18,... | collective-permute-start | bytes 479240 | tf_op jit(solution)/shard_map/ppermute | solution.py:57
  195.6 2.0 shard_map.351.refs_14_
  197.6 5.3 %collective-permute-done.38.refs_12_ = bf16[48,1664]{1,0:T(8,128)(2,1)S(1)} collective-permute-done((bf16[48,1664]{1,0:T(8,128)(2,1)S(1)}, bf16[48,1664]{1,0:T(8,128)(2,1)S(1)}, u32[]{:S(2)}, u32[]{:S(2)}) %collective-permute-start.38) | collective-permute-done | bytes 159776 | tf_op jit(solution)/shard_map/ppermute | solution.py:57
  (152 shorter events, 47.9 us)
Async XLA Ops:
  3.4 10.2 %collective-permute-start.3 = (bf16[48,1664]{1,0:T(8,128)(2,1)S(1)}, bf16[48,1664]{1,0:T(8,128)(2,1)S(1)}, u32[]{:S(2)}, u32[]{:S(2)}) collective-permute-start(bf16[48,1664]{1,0:T(8,128)(2,1)S(1)} %shard_map.323.refs_0_), channel_id=1, source_target_pairs={{0,24},{2,26},{4,28},{6,30},{8,16},{10,18},{12,20},{14,22},{16,8},... | collective-permute-start | bytes 479240 | tf_op jit(solution)/shard_map/ppermute | solution.py:57
  8.5 13.5 %collective-permute-start.2 = (bf16[48,1664]{1,0:T(8,128)(2,1)S(1)}, bf16[48,1664]{1,0:T(8,128)(2,1)S(1)}, u32[]{:S(2)}, u32[]{:S(2)}) collective-permute-start(bf16[48,1664]{1,0:T(8,128)(2,1)S(1)} %shard_map.323.refs_0_), channel_id=1, source_target_pairs={{0,16},{2,18},{4,20},{6,22},{8,24},{10,26},{12,28},{14,30},{16,0},... | collective-permute-start | bytes 479240 | tf_op jit(solution)/shard_map/ppermute | solution.py:57
  8.5 13.5 %collective-permute-start.1 = (bf16[48,1664]{1,0:T(8,128)(2,1)S(1)}, bf16[48,1664]{1,0:T(8,128)(2,1)S(1)}, u32[]{:S(2)}, u32[]{:S(2)}) collective-permute-start(bf16[48,1664]{1,0:T(8,128)(2,1)S(1)} %shard_map.323.refs_0_), channel_id=1, source_target_pairs={{0,8},{2,10},{4,12},{6,14},{8,0},{10,2},{12,4},{14,6},{16,24},{18,... | collective-permute-start | bytes 479240 | tf_op jit(solution)/shard_map/ppermute | solution.py:57
  9.1 19.0 %collective-permute-start = (bf16[256,768]{1,0:T(8,128)(2,1)}, bf16[256,768]{1,0:T(8,128)(2,1)S(1)}, u32[]{:S(2)}, u32[]{:S(2)}) collective-permute-start(bf16[256,768]{1,0:T(8,128)(2,1)} %param.20), channel_id=1, source_target_pairs={{0,1},{1,0},{2,3},{3,2},{4,5},{5,4},{6,7},{7,6},{8,9},{9,8},{10,11... | collective-permute-start | bytes 1179656 | tf_op jit(solution)/shard_map/ppermute | solution.py:61
  22.2 15.9 %collective-permute-start.10 = (bf16[48,3072]{1,0:T(8,128)(2,1)S(1)}, bf16[48,3072]{1,0:T(8,128)(2,1)S(1)}, u32[]{:S(2)}, u32[]{:S(2)}) collective-permute-start(bf16[48,3072]{1,0:T(8,128)(2,1)S(1)} %shard_map.326.refs_0_), channel_id=1, source_target_pairs={{0,24},{2,26},{4,28},{6,30},{8,16},{10,18},{12,20},{14,22},{16,8},... | collective-permute-start | bytes 884744 | tf_op jit(solution)/shard_map/ppermute | solution.py:57
  24.7 23.4 %collective-permute-start.9 = (bf16[48,3072]{1,0:T(8,128)(2,1)S(1)}, bf16[48,3072]{1,0:T(8,128)(2,1)S(1)}, u32[]{:S(2)}, u32[]{:S(2)}) collective-permute-start(bf16[48,3072]{1,0:T(8,128)(2,1)S(1)} %shard_map.326.refs_0_), channel_id=1, source_target_pairs={{0,16},{2,18},{4,20},{6,22},{8,24},{10,26},{12,28},{14,30},{16,0},... | collective-permute-start | bytes 884744 | tf_op jit(solution)/shard_map/ppermute | solution.py:57
  24.7 23.4 %collective-permute-start.8 = (bf16[48,3072]{1,0:T(8,128)(2,1)S(1)}, bf16[48,3072]{1,0:T(8,128)(2,1)S(1)}, u32[]{:S(2)}, u32[]{:S(2)}) collective-permute-start(bf16[48,3072]{1,0:T(8,128)(2,1)S(1)} %shard_map.326.refs_0_), channel_id=1, source_target_pairs={{0,8},{2,10},{4,12},{6,14},{8,0},{10,2},{12,4},{14,6},{16,24},{18,... | collective-permute-start | bytes 884744 | tf_op jit(solution)/shard_map/ppermute | solution.py:57
  35.1 13.1 %collective-permute-start.6 = (bf16[384,768]{1,0:T(8,128)(2,1)S(1)}, bf16[384,768]{1,0:T(8,128)(2,1)S(1)}, u32[]{:S(2)}, u32[]{:S(2)}) collective-permute-start(bf16[384,768]{1,0:T(8,128)(2,1)S(1)} %get-tuple-element.96.refs_0_), channel_id=1, source_target_pairs={{0,1},{1,0},{2,3},{3,2},{4,5},{5,4},{6,7},{7,6},{8,9},{9,8},{10,11... | collective-permute-start | bytes 1769480 | tf_op jit(solution)/shard_map/ppermute | solution.py:61
  36.5 14.4 %collective-permute-start.7 = (bf16[192,1792]{1,0:T(8,128)(2,1)S(1)}, bf16[192,1792]{1,0:T(8,128)(2,1)S(1)}, u32[]{:S(2)}, u32[]{:S(2)}) collective-permute-start(bf16[192,1792]{1,0:T(8,128)(2,1)S(1)} %get-tuple-element.97.refs_1_), channel_id=1, source_target_pairs={{0,4},{2,6},{4,0},{6,2},{8,12},{10,14},{12,8},{14,10},{16,20},{18,... | collective-permute-start | bytes 2064392 | tf_op jit(solution)/shard_map/ppermute | solution.py:57
  51.7 15.3 %collective-permute-start.14 = (bf16[192,1536]{1,0:T(8,128)(2,1)S(1)}, bf16[192,1536]{1,0:T(8,128)(2,1)S(1)}, u32[]{:S(2)}, u32[]{:S(2)}) collective-permute-start(bf16[192,1536]{1,0:T(8,128)(2,1)S(1)} %get-tuple-element.106.refs_1_), channel_id=1, source_target_pairs={{0,4},{2,6},{4,0},{6,2},{8,12},{10,14},{12,8},{14,10},{16,20},{18,... | collective-permute-start | bytes 1769480 | tf_op jit(solution)/shard_map/ppermute | solution.py:57
  53.3 15.0 %collective-permute-start.13 = (bf16[192,1536]{1,0:T(8,128)(2,1)S(1)}, bf16[192,1536]{1,0:T(8,128)(2,1)S(1)}, u32[]{:S(2)}, u32[]{:S(2)}) collective-permute-start(bf16[192,1536]{1,0:T(8,128)(2,1)S(1)} %get-tuple-element.98.refs_4_.refs_0_), channel_id=1, source_target_pairs={{0,1},{1,0},{2,3},{3,2},{4,5},{5,4},{6,7},{7,6},{8,9},{9,8},{10,11... | collective-permute-start | bytes 1769480 | tf_op jit(solution)/shard_map/ppermute | solution.py:61
  68.4 10.0 %collective-permute-start.16 = (bf16[384,1536]{1,0:T(8,128)(2,1)S(1)}, bf16[384,1536]{1,0:T(8,128)(2,1)S(1)}, u32[]{:S(2)}, u32[]{:S(2)}) collective-permute-start(bf16[384,1536]{1,0:T(8,128)(2,1)S(1)} %get-tuple-element.109.refs_3_.refs_1_), channel_id=1, source_target_pairs={{0,2},{2,0},{4,6},{6,4},{8,10},{10,8},{12,14},{14,12},{16,18},{18,... | collective-permute-start | bytes 3538952 | tf_op jit(solution)/shard_map/ppermute | solution.py:57
  68.5 10.0 %collective-permute-start.15 = (bf16[192,3072]{1,0:T(8,128)(2,1)S(1)}, bf16[192,3072]{1,0:T(8,128)(2,1)S(1)}, u32[]{:S(2)}, u32[]{:S(2)}) collective-permute-start(bf16[192,3072]{1,0:T(8,128)(2,1)S(1)} %get-tuple-element.107.refs_5_.refs_1_), channel_id=1, source_target_pairs={{0,2},{2,0},{4,6},{6,4},{8,10},{10,8},{12,14},{14,12},{16,18},{18,... | collective-permute-start | bytes 3538952 | tf_op jit(solution)/shard_map/ppermute | solution.py:57
  69.0 28.0 %collective-permute-start.18 = (bf16[384,1536]{1,0:T(8,128)(2,1)S(1)}, bf16[384,1536]{1,0:T(8,128)(2,1)S(1)}, u32[]{:S(2)}, u32[]{:S(2)}) collective-permute-start(bf16[384,1536]{1,0:T(8,128)(2,1)S(1)} %get-tuple-element.109.refs_3_.refs_1_), channel_id=1, source_target_pairs={{0,1},{1,0},{2,3},{3,2},{4,5},{5,4},{6,7},{7,6},{8,9},{9,8},{10,11... | collective-permute-start | bytes 3538952 | tf_op jit(solution)/shard_map/ppermute | solution.py:61
  69.6 27.7 %collective-permute-start.17 = (bf16[192,3072]{1,0:T(8,128)(2,1)S(1)}, bf16[192,3072]{1,0:T(8,128)(2,1)S(1)}, u32[]{:S(2)}, u32[]{:S(2)}) collective-permute-start(bf16[192,3072]{1,0:T(8,128)(2,1)S(1)} %get-tuple-element.107.refs_5_.refs_1_), channel_id=1, source_target_pairs={{0,4},{2,6},{4,0},{6,2},{8,12},{10,14},{12,8},{14,10},{16,20},{18,... | collective-permute-start | bytes 3538952 | tf_op jit(solution)/shard_map/ppermute | solution.py:57
  112.2 28.3 %collective-permute-start.24 = (bf16[384,1536]{1,0:T(8,128)(2,1)S(1)}, bf16[384,1536]{1,0:T(8,128)(2,1)S(1)}, u32[]{:S(2)}, u32[]{:S(2)}) collective-permute-start(bf16[384,1536]{1,0:T(8,128)(2,1)S(1)} %get-tuple-element.131), channel_id=1, source_target_pairs={{0,1},{1,0},{2,3},{3,2},{4,5},{5,4},{6,7},{7,6},{8,9},{9,8},{10,11... | collective-permute-start | bytes 3538952 | tf_op jit(solution)/shard_map/ppermute | solution.py:61
  115.3 28.1 %collective-permute-start.23 = (bf16[192,3072]{1,0:T(8,128)(2,1)S(1)}, bf16[192,3072]{1,0:T(8,128)(2,1)S(1)}, u32[]{:S(2)}, u32[]{:S(2)}) collective-permute-start(bf16[192,3072]{1,0:T(8,128)(2,1)S(1)} %get-tuple-element.130), channel_id=1, source_target_pairs={{0,4},{2,6},{4,0},{6,2},{8,12},{10,14},{12,8},{14,10},{16,20},{18,... | collective-permute-start | bytes 3538952 | tf_op jit(solution)/shard_map/ppermute | solution.py:57
  132.8 15.8 %collective-permute-start.28 = (bf16[384,1536]{1,0:T(8,128)(2,1)S(1)}, bf16[384,1536]{1,0:T(8,128)(2,1)S(1)}, u32[]{:S(2)}, u32[]{:S(2)}) collective-permute-start(bf16[384,1536]{1,0:T(8,128)(2,1)S(1)} %get-tuple-element.145), channel_id=1, source_target_pairs={{0,2},{2,0},{4,6},{6,4},{8,10},{10,8},{12,14},{14,12},{16,18},{18,... | collective-permute-start | bytes 3538952 | tf_op jit(solution)/shard_map/ppermute | solution.py:57
  132.9 15.8 %collective-permute-start.27 = (bf16[384,1792]{1,0:T(8,128)(2,1)S(1)}, bf16[384,1792]{1,0:T(8,128)(2,1)S(1)}, u32[]{:S(2)}, u32[]{:S(2)}) collective-permute-start(bf16[384,1792]{1,0:T(8,128)(2,1)S(1)} %get-tuple-element.143), channel_id=1, source_target_pairs={{0,2},{2,0},{4,6},{6,4},{8,10},{10,8},{12,14},{14,12},{16,18},{18,... | collective-permute-start | bytes 4128776 | tf_op jit(solution)/shard_map/ppermute | solution.py:57
  144.0 14.6 %collective-permute-start.25 = (bf16[192,1536]{1,0:T(8,128)(2,1)S(1)}, bf16[192,1536]{1,0:T(8,128)(2,1)S(1)}, u32[]{:S(2)}, u32[]{:S(2)}) collective-permute-start(bf16[192,1536]{1,0:T(8,128)(2,1)S(1)} %get-tuple-element.140), channel_id=1, source_target_pairs={{0,1},{1,0},{2,3},{3,2},{4,5},{5,4},{6,7},{7,6},{8,9},{9,8},{10,11... | collective-permute-start | bytes 1769480 | tf_op jit(solution)/shard_map/ppermute | solution.py:61
  145.5 14.3 %collective-permute-start.26 = (bf16[192,1536]{1,0:T(8,128)(2,1)S(1)}, bf16[192,1536]{1,0:T(8,128)(2,1)S(1)}, u32[]{:S(2)}, u32[]{:S(2)}) collective-permute-start(bf16[192,1536]{1,0:T(8,128)(2,1)S(1)} %get-tuple-element.142), channel_id=1, source_target_pairs={{0,4},{2,6},{4,0},{6,2},{8,12},{10,14},{12,8},{14,10},{16,20},{18,... | collective-permute-start | bytes 1769480 | tf_op jit(solution)/shard_map/ppermute | solution.py:57
  160.4 15.5 %collective-permute-start.32 = (bf16[192,1792]{1,0:T(8,128)(2,1)S(1)}, bf16[192,1792]{1,0:T(8,128)(2,1)S(1)}, u32[]{:S(2)}, u32[]{:S(2)}) collective-permute-start(bf16[192,1792]{1,0:T(8,128)(2,1)S(1)} %get-tuple-element.151), channel_id=1, source_target_pairs={{0,4},{2,6},{4,0},{6,2},{8,12},{10,14},{12,8},{14,10},{16,20},{18,... | collective-permute-start | bytes 2064392 | tf_op jit(solution)/shard_map/ppermute | solution.py:57
  161.0 13.1 %collective-permute-start.33 = (bf16[384,768]{1,0:T(8,128)(2,1)S(1)}, bf16[384,768]{1,0:T(8,128)(2,1)S(1)}, u32[]{:S(2)}, u32[]{:S(2)}) collective-permute-start(bf16[384,768]{1,0:T(8,128)(2,1)S(1)} %get-tuple-element.153), channel_id=1, source_target_pairs={{0,1},{1,0},{2,3},{3,2},{4,5},{5,4},{6,7},{7,6},{8,9},{9,8},{10,11... | collective-permute-start | bytes 1769480 | tf_op jit(solution)/shard_map/ppermute | solution.py:61
  161.8 15.5 %collective-permute-start.29 = (bf16[48,3072]{1,0:T(8,128)(2,1)S(1)}, bf16[48,3072]{1,0:T(8,128)(2,1)S(1)}, u32[]{:S(2)}, u32[]{:S(2)}) collective-permute-start(bf16[48,3072]{1,0:T(8,128)(2,1)S(1)} %get-tuple-element.148), channel_id=1, source_target_pairs={{0,8},{2,10},{4,12},{6,14},{8,0},{10,2},{12,4},{14,6},{16,24},{18,... | collective-permute-start | bytes 884744 | tf_op jit(solution)/shard_map/ppermute | solution.py:57
  162.3 22.9 %collective-permute-start.30 = (bf16[48,3072]{1,0:T(8,128)(2,1)S(1)}, bf16[48,3072]{1,0:T(8,128)(2,1)S(1)}, u32[]{:S(2)}, u32[]{:S(2)}) collective-permute-start(bf16[48,3072]{1,0:T(8,128)(2,1)S(1)} %get-tuple-element.149), channel_id=1, source_target_pairs={{0,16},{2,18},{4,20},{6,22},{8,24},{10,26},{12,28},{14,30},{16,0},... | collective-permute-start | bytes 884744 | tf_op jit(solution)/shard_map/ppermute | solution.py:57
  164.5 20.6 %collective-permute-start.31 = (bf16[48,3072]{1,0:T(8,128)(2,1)S(1)}, bf16[48,3072]{1,0:T(8,128)(2,1)S(1)}, u32[]{:S(2)}, u32[]{:S(2)}) collective-permute-start(bf16[48,3072]{1,0:T(8,128)(2,1)S(1)} %get-tuple-element.150), channel_id=1, source_target_pairs={{0,24},{2,26},{4,28},{6,30},{8,16},{10,18},{12,20},{14,22},{16,8},... | collective-permute-start | bytes 884744 | tf_op jit(solution)/shard_map/ppermute | solution.py:57
  176.2 10.6 %collective-permute-start.36 = (bf16[192,768]{1,0:T(8,128)(2,1)S(1)}, bf16[192,768]{1,0:T(8,128)(2,1)S(1)}, u32[]{:S(2)}, u32[]{:S(2)}) collective-permute-start(bf16[192,768]{1,0:T(8,128)(2,1)S(1)} %get-tuple-element.157), channel_id=1, source_target_pairs={{0,4},{2,6},{4,0},{6,2},{8,12},{10,14},{12,8},{14,10},{16,20},{18,... | collective-permute-start | bytes 884744 | tf_op jit(solution)/shard_map/ppermute | solution.py:57
  176.8 10.6 %collective-permute-start.35 = (bf16[192,896]{1,0:T(8,128)(2,1)S(1)}, bf16[192,896]{1,0:T(8,128)(2,1)S(1)}, u32[]{:S(2)}, u32[]{:S(2)}) collective-permute-start(bf16[192,896]{1,0:T(8,128)(2,1)S(1)} %get-tuple-element.155), channel_id=1, source_target_pairs={{0,1},{1,0},{2,3},{3,2},{4,5},{5,4},{6,7},{7,6},{8,9},{9,8},{10,11... | collective-permute-start | bytes 1032200 | tf_op jit(solution)/shard_map/ppermute | solution.py:61
  185.3 10.3 %collective-permute-start.34 = (bf16[256,768]{1,0:T(8,128)(2,1)S(1)}, bf16[256,768]{1,0:T(8,128)(2,1)S(1)}, u32[]{:S(2)}, u32[]{:S(2)}) collective-permute-start(bf16[256,768]{1,0:T(8,128)(2,1)S(1)} %shard_map.349), channel_id=1, source_target_pairs={{0,1},{1,0},{2,3},{3,2},{4,5},{5,4},{6,7},{7,6},{8,9},{9,8},{10,11... | collective-permute-start | bytes 1179656 | tf_op jit(solution)/shard_map/ppermute | solution.py:61
  187.6 10.0 %collective-permute-start.37 = (bf16[48,1664]{1,0:T(8,128)(2,1)S(1)}, bf16[48,1664]{1,0:T(8,128)(2,1)S(1)}, u32[]{:S(2)}, u32[]{:S(2)}) collective-permute-start(bf16[48,1664]{1,0:T(8,128)(2,1)S(1)} %get-tuple-element.159), channel_id=1, source_target_pairs={{0,8},{2,10},{4,12},{6,14},{8,0},{10,2},{12,4},{14,6},{16,24},{18,... | collective-permute-start | bytes 479240 | tf_op jit(solution)/shard_map/ppermute | solution.py:57
  190.9 12.0 %collective-permute-start.38 = (bf16[48,1664]{1,0:T(8,128)(2,1)S(1)}, bf16[48,1664]{1,0:T(8,128)(2,1)S(1)}, u32[]{:S(2)}, u32[]{:S(2)}) collective-permute-start(bf16[48,1664]{1,0:T(8,128)(2,1)S(1)} %get-tuple-element.160), channel_id=1, source_target_pairs={{0,16},{2,18},{4,20},{6,22},{8,24},{10,26},{12,28},{14,30},{16,0},... | collective-permute-start | bytes 479240 | tf_op jit(solution)/shard_map/ppermute | solution.py:57
  191.8 11.1 %collective-permute-start.39 = (bf16[48,1664]{1,0:T(8,128)(2,1)S(1)}, bf16[48,1664]{1,0:T(8,128)(2,1)S(1)}, u32[]{:S(2)}, u32[]{:S(2)}) collective-permute-start(bf16[48,1664]{1,0:T(8,128)(2,1)S(1)} %get-tuple-element.161), channel_id=1, source_target_pairs={{0,24},{2,26},{4,28},{6,30},{8,16},{10,18},{12,20},{14,22},{16,8},... | collective-permute-start | bytes 479240 | tf_op jit(solution)/shard_map/ppermute | solution.py:57
  (38 other events, 353.5 us)

commit v9 on v8

--- a/solution.py
+++ b/solution.py
@@ -211,6 +211,14 @@
     return (left[rows, columns].astype(F32) + right[rows, columns].astype(F32)).astype(LOW)
 
 
+def add_kernel(array, far, total):
+    total[...] = added(array, far, slice(None), slice(None))
+
+
+def add_parts(array, far, flops=0, after=()):
+    return run(add_kernel, [shape_of(*array.shape, LOW)], [array, far], flops, after)[0]
+
+
 def split_rows_kernel(array, far, keep, send):
     rows = keep.shape[0]
     keep[...] = added(array, far, slice(0, rows), slice(None))
@@ -221,16 +229,6 @@
     columns = keep.shape[1]
     keep[...] = added(array, far, slice(None), slice(0, columns))
     send[...] = added(array, far, slice(None), slice(columns, 2 * columns))
-
-
-def split_rows(array, far, flops=0, after=()):
-    part = shape_of(array.shape[0] // 2, array.shape[1], LOW)
-    return run(split_rows_kernel, [part, part], [array, far], flops, after)
-
-
-def split_columns(array, far, flops=0, after=()):
-    part = shape_of(array.shape[0], array.shape[1] // 2, LOW)
-    return run(split_columns_kernel, [part, part], [array, far], flops, after)
 
 
 def split_core_kernel(a, a_far, b, b_far, a_keep, a_send, b_keep, b_send):
@@ -782,28 +780,38 @@
     )
     mixed = dot_nt(mixed_rel, permute).astype(LOW)
 
-    def weight_grad(left, right):
-        send = dot_tn(left[:, half:], right).astype(LOW)
-        return dot_tn(left[:, :half], right).astype(LOW), swap_dp(send, 1)
-
-    outer = weight_grad(grad_two_low, activation)
+    def gradient(left, right):
+        return dot_tn(left, right).astype(LOW)
+
+    back_parts = []
+    for columns in (activation[:, hidden_half:], activation[:, :hidden_half]):
+        sent = swap_dp(gradient(grad_two_low[:, half:], columns), 1)
+        back_parts.append((gradient(grad_two_low[:, :half], columns), sent))
     grad_pre, sums_inner = run(
         hidden_back_kernel,
         [shape_of(own_rows, full_inner, LOW), shape_of(1, full_inner, F32)],
         [grad_two_low, *pieces_back, slope],
         6 * unit,
     )
-    inner = weight_grad(first_low, grad_pre)
-    b_keep, b_send = split_columns(*outer, 400 * unit, after=[grad_pre])
-    a_keep, a_send = split_rows(*inner, after=[b_keep])
-    pair = a_keep, swap_dp(a_send, 2), b_keep, swap_tensor(b_send)
+    quarter = half // 2
+    in_parts = []
+    for start in (quarter, 0):
+        rows = slice(half + start, half + start + quarter)
+        sent = swap_dp(gradient(first_low[:, rows], grad_pre), 1)
+        in_parts.append((gradient(first_low[:, start : start + quarter], grad_pre), sent))
+    b_send = add_parts(*back_parts[0], 400 * unit, after=[grad_pre])
+    a_send = add_parts(*in_parts[0], after=[b_send])
+    a_far_sum, b_far_sum = swap_dp(a_send, 2), swap_tensor(b_send)
     grad_one, grad_one_low, grad_attn, sums_one = run(
         norm_back_kernel,
         [wide, wide_low, wide_low, sums_shape],
         [grad_pre, *pieces_in, grad_two, normed_one, inv_one, vec, b_own, b_far],
         6 * unit,
-        after=[a_keep],
-    )
+        after=[a_send],
+    )
+    b_keep = add_parts(*back_parts[1], after=[grad_one_low])
+    a_keep = add_parts(*in_parts[1], after=[b_keep])
+    pair = a_keep, a_far_sum, b_keep, b_far_sum
     grad_q, grad_k, grad_v = run(
         attend_back_kernel,
         [wide_low, group_low, group_low],
@@ -833,7 +841,7 @@
         400 * unit,
         after=[a_keep],
     )
-    a_keep, a_send, b_keep, b_send = split_core(*one, after=[grad_own, pair[1], pair[3]])
+    a_keep, a_send, b_keep, b_send = split_core(*one, after=[grad_own])
     one = a_keep, swap_dp(a_send, 2), b_keep, swap_tensor(b_send)
     pair = send_high(split_high(*pair, after=[a_keep]))
     a_keep, a_send, b_keep, b_send = split_plane(*one, after=pair[:1])

time: 206 us -> 216 us (1.049)
  between operations: 1.44 us -> 13 us
  waiting for transfers between devices: 101 us -> 93.9 us
  starting transfers between devices: 42.2 us -> 45.7 us
    ppermute x10, waiting for transfers between devices: 44.1 us -> 21.7 us  [swap_tensor(): return lax.ppermute(values, 'tensor', [(0, 1), (1, 0)])]
    ppermute x30 -> x32, waiting for transfers between devices: 57.3 us -> 72.2 us  [swap_dp(): return lax.ppermute(values, 'dp', [(i, i ^ mask) for i in range(size)])]
    ppermute x30 -> x32, starting transfers between devices: 30.6 us -> 35 us  [swap_dp(): return lax.ppermute(values, 'dp', [(i, i ^ mask) for i in range(size)])]
    pallas_call x28 -> x30, Pallas kernels: 46.6 us -> 46.5 us  [run(): pl.pallas_call(body, grid=grid, out_shape=list(outs), in_specs=list(in_sp...]
  transfers between devices with their start and end apart: 40 -> 42, of which waited for: 22 -> 16; matrix products, arithmetic and copies ran while one was open for 4% -> 5% of each run, Pallas kernels for 20% -> 20%
where the time goes in v9:
time: 216 us; the launch traced here: 215 us
  waiting for transfers between devices  93.9 us (43%)
  Pallas kernels  46.5 us (22%)
  starting transfers between devices  45.7 us (21%)
  between operations  13 us (6%)
  matrix products  7.68 us (4%)
  local copies, waits for them, and re-layouts  4.74 us (2%)
  other arithmetic  3.27 us (2%)
    ppermute x32, waiting for transfers between devices, swap_dp(): return lax.ppermute(values, 'dp', [(i, i ^ mask) for i in range(size)])  72.2 us
    pallas_call x30, Pallas kernels, run(): pl.pallas_call(body, grid=grid, out_shape=list(outs), in_specs=list(in_sp...  46.5 us
    ppermute x32, starting transfers between devices, swap_dp(): return lax.ppermute(values, 'dp', [(i, i ^ mask) for i in range(size)])  35 us
    ppermute x10, waiting for transfers between devices, swap_tensor(): return lax.ppermute(values, 'tensor', [(0, 1), (1, 0)])  21.7 us
    ppermute x10, starting transfers between devices, swap_tensor(): return lax.ppermute(values, 'tensor', [(0, 1), (1, 0)])  10.7 us
    unnamed x60, local copies, waits for them, and re-layouts  4.74 us
  transfers between devices with their start and end apart: 42, of which 16 were waited for; matrix products, arithmetic and copies ran while one was open for 5% of the time, Pallas kernels for 20%

profile of v9, /device:TPU:0, one launch (start us, length us, event | category | flops | bytes accessed | tf_op | source)
XLA Modules:
  0.0 214.9 jit_solution(18030835128601878057)
XLA Ops:
  3.4 3.1 %collective-permute-start.1 = (bf16[48,1664]{1,0:T(8,128)(2,1)S(1)}, bf16[48,1664]{1,0:T(8,128)(2,1)S(1)}, u32[]{:S(2)}, u32[]{:S(2)}) collective-permute-start(bf16[48,1664]{1,0:T(8,128)(2,1)S(1)} %shard_map.323.refs_0_), channel_id=1, source_target_pairs={{0,8},{2,10},{4,12},{6,14},{8,0},{10,2},{12,4},{14,6},{16,24},{18,... | collective-permute-start | bytes 479240 | tf_op jit(solution)/shard_map/ppermute | solution.py:57
  6.5 2.6 %collective-permute-start.2 = (bf16[48,1664]{1,0:T(8,128)(2,1)S(1)}, bf16[48,1664]{1,0:T(8,128)(2,1)S(1)}, u32[]{:S(2)}, u32[]{:S(2)}) collective-permute-start(bf16[48,1664]{1,0:T(8,128)(2,1)S(1)} %shard_map.323.refs_0_), channel_id=1, source_target_pairs={{0,16},{2,18},{4,20},{6,22},{8,24},{10,26},{12,28},{14,30},{16,0},... | collective-permute-start | bytes 479240 | tf_op jit(solution)/shard_map/ppermute | solution.py:57
  9.0 1.7 collective-permute-start
  11.5 1.6 fusion.10
  13.1 8.1 %collective-permute-done.2.refs_2_ = bf16[48,1664]{1,0:T(8,128)(2,1)S(1)} collective-permute-done((bf16[48,1664]{1,0:T(8,128)(2,1)S(1)}, bf16[48,1664]{1,0:T(8,128)(2,1)S(1)}, u32[]{:S(2)}, u32[]{:S(2)}) %collective-permute-start.2) | collective-permute-done | bytes 159776 | tf_op jit(solution)/shard_map/ppermute | solution.py:57
  21.3 1.6 collective-permute-start.4
  22.9 2.6 %collective-permute-start.8 = (bf16[48,3072]{1,0:T(8,128)(2,1)S(1)}, bf16[48,3072]{1,0:T(8,128)(2,1)S(1)}, u32[]{:S(2)}, u32[]{:S(2)}) collective-permute-start(bf16[48,3072]{1,0:T(8,128)(2,1)S(1)} %shard_map.326.refs_0_), channel_id=1, source_target_pairs={{0,8},{2,10},{4,12},{6,14},{8,0},{10,2},{12,4},{14,6},{16,24},{18,... | collective-permute-start | bytes 884744 | tf_op jit(solution)/shard_map/ppermute | solution.py:57
  30.2 4.7 %collective-permute-done.5.refs_3_ = bf16[192,768]{1,0:T(8,128)(2,1)S(1)} collective-permute-done((bf16[192,768]{1,0:T(8,128)(2,1)S(1)}, bf16[192,768]{1,0:T(8,128)(2,1)S(1)}, u32[]{:S(2)}, u32[]{:S(2)}) %collective-permute-start.5) | collective-permute-done | bytes 294944 | tf_op jit(solution)/shard_map/ppermute | solution.py:57
  37.2 11.8 %collective-permute-done.9.refs_2_ = bf16[48,3072]{1,0:T(8,128)(2,1)S(1)} collective-permute-done((bf16[48,3072]{1,0:T(8,128)(2,1)S(1)}, bf16[48,3072]{1,0:T(8,128)(2,1)S(1)}, u32[]{:S(2)}, u32[]{:S(2)}) %collective-permute-start.9) | collective-permute-done | bytes 294944 | tf_op jit(solution)/shard_map/ppermute | solution.py:57
  55.5 2.6 %shard_map.330 = (bf16[256,768]{1,0:T(8,128)(2,1)S(1)}, bf16[512,768]{1,0:T(8,128)(2,1)S(1)}, bf16[512,768]{1,0:T(8,128)(2,1)S(1)}) custom-call(bf16[512,768]{1,0:T(8,128)(2,1)S(1)} %pad_maximum_fusion.refs_4_.refs_0_.refs_1_.refs_2_, bf16[384,1792]{1,0:T(8,128)(2,1)S(1)} %get-tuple-element.95.refs_2_.refs_1_.refs_3_, ...), custom_call_target="tpu_custom_call" | custom-call | flops 1509949440 | bytes 7870464 | tf_op jit(solution)/shard_map/pallas_call | solution.py:142
  58.1 7.8 %collective-permute-done.13.refs_2_ = bf16[192,1536]{1,0:T(8,128)(2,1)S(1)} collective-permute-done((bf16[192,1536]{1,0:T(8,128)(2,1)S(1)}, bf16[192,1536]{1,0:T(8,128)(2,1)S(1)}, u32[]{:S(2)}, u32[]{:S(2)}) %collective-permute-start.13) | collective-permute-done | bytes 589856 | tf_op jit(solution)/shard_map/ppermute | solution.py:61
  69.9 8.5 %shard_map.332.refs_0_.refs_7_ = bf16[256,768]{1,0:T(8,128)(2,1)S(1)} custom-call(s32[1]{0:T(128)} %bitcast.refs_0_, s32[1,3]{1,0:T(1,128)S(1)} %copy-done.25, bf16[256,768]{1,0:T(8,128)(2,1)S(1)} %get-tuple-element.99.refs_4_.refs_2_, bf16[512,768]{1,0:T(8,128)(2,1)S(1)} %get-tuple-element.100.refs_3_, bf16[512,768]{1,0:T(8,128)(2,1)S(1)} %get-tuple-element.101.refs_4_, ...), custom_call_target="tpu_custom_call" | custom-call | flops 905969664 | bytes 2359312 | tf_op jit(solution)/shard_map/pallas_call | solution.py:142
  79.4 16.4 %collective-permute-done.17.refs_0_ = bf16[192,3072]{1,0:T(8,128)(2,1)S(1)} collective-permute-done((bf16[192,3072]{1,0:T(8,128)(2,1)S(1)}, bf16[192,3072]{1,0:T(8,128)(2,1)S(1)}, u32[]{:S(2)}, u32[]{:S(2)}) %collective-permute-start.17) | collective-permute-done | bytes 1179680 | tf_op jit(solution)/shard_map/ppermute | solution.py:57
  98.2 1.7 collective-permute-done.19.refs_4_
  99.9 2.8 %shard_map.335 = (bf16[256,3072]{1,0:T(8,128)(2,1)S(1)}, f32[256,3072]{1,0:T(8,128)S(1)}) custom-call(bf16[256,768]{1,0:T(8,128)(2,1)S(1)} %get-tuple-element.106.refs_2_.refs_0_, bf16[192,3072]{1,0:T(8,128)(2,1)S(1)} %get-tuple-element.103.refs_5_.refs_1_, bf16[192,3072]{1,0:T(8,128)(2,1)S(1)} %get-tuple-element.107.refs_2_, ...), custom_call_target="tpu_custom_call" | custom-call | flops 2415919104 | bytes 9842688 | tf_op jit(solution)/shard_map/pallas_call | solution.py:142
  102.7 3.0 %shard_map.336 = (bf16[256,768]{1,0:T(8,128)(2,1)S(1)}, f32[256,768]{1,0:T(8,128)S(1)}, bf16[256,768]{1,0:T(8,128)(2,1)S(1)}, f32[8,768]{1,0:T(8,128)S(1)}) custom-call(s32[1]{0:T(128)} %bitcast.refs_0_, s32[1,3]{1,0:T(1,128)S(1)} %copy-done.25, bf16[256,3072]{1,0:T(8,128)(2,1)S(1)} %get-tuple-element.109.refs_2_, ...), custom_call_target="tpu_custom_call" | custom-call | flops 1509949440 | bytes 9480208 | tf_op jit(solution)/shard_map/pallas_call | solution.py:142
  106.4 1.8 shard_map.337
  127.0 2.7 %shard_map.340 = (f32[256,768]{1,0:T(8,128)S(1)}, bf16[256,768]{1,0:T(8,128)(2,1)S(1)}, bf16[256,768]{1,0:T(8,128)(2,1)S(1)}, f32[8,768]{1,0:T(8,128)S(1)}) custom-call(bf16[256,3072]{1,0:T(8,128)(2,1)S(1)} %get-tuple-element.115.refs_2_.refs_0_, bf16[192,3072]{1,0:T(8,128)(2,1)S(1)} %get-tuple-element.103.refs_5_.refs_1_, ...), custom_call_target="tpu_custom_call" | custom-call | flops 1811939328 | bytes 11840512 | tf_op jit(solution)/shard_map/pallas_call | solution.py:142
  129.7 10.5 %shard_map.341 = (bf16[256,768]{1,0:T(8,128)(2,1)S(1)}, bf16[512,768]{1,0:T(8,128)(2,1)S(1)}, bf16[512,768]{1,0:T(8,128)(2,1)S(1)}) custom-call(s32[1]{0:T(128)} %bitcast.refs_0_, s32[1,3]{1,0:T(1,128)S(1)} %copy-done.25, bf16[256,768]{1,0:T(8,128)(2,1)S(1)} %get-tuple-element.99.refs_4_.refs_2_, bf16[512,768]{1,0:T(8,128)(2,1)S(1)} %get-tuple-element.100.refs_3_, ...), custom_call_target="tpu_custom_call" | custom-call | flops 1509949440 | bytes 4325392 | tf_op jit(solution)/shard_map/pallas_call | solution.py:142
  140.2 3.1 %shard_map.344 = (bf16[384,1792]{1,0:T(8,128)(2,1)S(1)}, bf16[384,1536]{1,0:T(8,128)(2,1)S(1)}, bf16[384,1792]{1,0:T(8,128)(2,1)S(1)}, bf16[384,1536]{1,0:T(8,128)(2,1)S(1)}) custom-call(s32[1]{0:T(128)} %bitcast.refs_0_, bf16[768,768]{1,0:T(8,128)(2,1)S(1)} %copy-done.7, bf16[512,768]{1,0:T(8,128)(2,1)S(1)} %pad_maximum_fusion.refs_4_.refs_0_.refs_1_.refs_2_, ...), custom_call_target="tpu_custom_call" | custom-call | flops 1811939328 | bytes 9891844 | tf_op jit(solution)/shard_map/pallas_call | solution.py:142
  144.4 8.1 %collective-permute-done.25.refs_1_ = bf16[192,3072]{1,0:T(8,128)(2,1)S(1)} collective-permute-done((bf16[192,3072]{1,0:T(8,128)(2,1)S(1)}, bf16[192,3072]{1,0:T(8,128)(2,1)S(1)}, u32[]{:S(2)}, u32[]{:S(2)}) %collective-permute-start.25) | collective-permute-done | bytes 1179680 | tf_op jit(solution)/shard_map/ppermute | solution.py:57
  153.1 1.6 collective-permute-start.27
  155.2 2.6 %shard_map.346 = (f32[256,768]{1,0:T(8,128)S(1)}, bf16[256,768]{1,0:T(8,128)(2,1)S(1)}) custom-call(bf16[256,768]{1,0:T(8,128)(2,1)S(1)} %get-tuple-element.120.refs_3_.refs_0_, bf16[512,768]{1,0:T(8,128)(2,1)S(1)} %get-tuple-element.121.refs_4_.refs_1_, bf16[512,768]{1,0:T(8,128)(2,1)S(1)} %get-tuple-element.122.refs_5_.refs_2_, ...), custom_call_target="tpu_custom_call" | custom-call | flops 120795955200 | bytes 9043968 | tf_op jit(solution)/shard_map/pallas_call | solution.py:142
  158.4 1.6 collective-permute-start.34
  160.6 8.9 %collective-permute-done.27.refs_1_ = bf16[192,1536]{1,0:T(8,128)(2,1)S(1)} collective-permute-done((bf16[192,1536]{1,0:T(8,128)(2,1)S(1)}, bf16[192,1536]{1,0:T(8,128)(2,1)S(1)}, u32[]{:S(2)}, u32[]{:S(2)}) %collective-permute-start.27) | collective-permute-done | bytes 589856 | tf_op jit(solution)/shard_map/ppermute | solution.py:61
  171.2 2.4 %collective-permute-start.31 = (bf16[48,3072]{1,0:T(8,128)(2,1)S(1)}, bf16[48,3072]{1,0:T(8,128)(2,1)S(1)}, u32[]{:S(2)}, u32[]{:S(2)}) collective-permute-start(bf16[48,3072]{1,0:T(8,128)(2,1)S(1)} %get-tuple-element.140), channel_id=1, source_target_pairs={{0,8},{2,10},{4,12},{6,14},{8,0},{10,2},{12,4},{14,6},{16,24},{18,... | collective-permute-start | bytes 884744 | tf_op jit(solution)/shard_map/ppermute | solution.py:57
  176.3 3.7 %collective-permute-done.35.refs_3_ = bf16[384,768]{1,0:T(8,128)(2,1)S(1)} collective-permute-done((bf16[384,768]{1,0:T(8,128)(2,1)S(1)}, bf16[384,768]{1,0:T(8,128)(2,1)S(1)}, u32[]{:S(2)}, u32[]{:S(2)}) %collective-permute-start.35) | collective-permute-done | bytes 589856 | tf_op jit(solution)/shard_map/ppermute | solution.py:61
  180.0 3.3 %collective-permute-done.34.refs_1_ = bf16[192,1792]{1,0:T(8,128)(2,1)S(1)} collective-permute-done((bf16[192,1792]{1,0:T(8,128)(2,1)S(1)}, bf16[192,1792]{1,0:T(8,128)(2,1)S(1)}, u32[]{:S(2)}, u32[]{:S(2)}) %collective-permute-start.34) | collective-permute-done | bytes 688160 | tf_op jit(solution)/shard_map/ppermute | solution.py:57
  184.8 9.8 %collective-permute-done.32.refs_2_ = bf16[48,3072]{1,0:T(8,128)(2,1)S(1)} collective-permute-done((bf16[48,3072]{1,0:T(8,128)(2,1)S(1)}, bf16[48,3072]{1,0:T(8,128)(2,1)S(1)}, u32[]{:S(2)}, u32[]{:S(2)}) %collective-permute-start.32) | collective-permute-done | bytes 294944 | tf_op jit(solution)/shard_map/ppermute | solution.py:57
  196.4 3.8 %collective-permute-start.39 = (bf16[48,1664]{1,0:T(8,128)(2,1)S(1)}, bf16[48,1664]{1,0:T(8,128)(2,1)S(1)}, u32[]{:S(2)}, u32[]{:S(2)}) collective-permute-start(bf16[48,1664]{1,0:T(8,128)(2,1)S(1)} %get-tuple-element.151), channel_id=1, source_target_pairs={{0,8},{2,10},{4,12},{6,14},{8,0},{10,2},{12,4},{14,6},{16,24},{18,... | collective-permute-start | bytes 479240 | tf_op jit(solution)/shard_map/ppermute | solution.py:57
  205.7 2.0 shard_map.353.refs_14_
  207.7 4.7 %collective-permute-done.40.refs_12_ = bf16[48,1664]{1,0:T(8,128)(2,1)S(1)} collective-permute-done((bf16[48,1664]{1,0:T(8,128)(2,1)S(1)}, bf16[48,1664]{1,0:T(8,128)(2,1)S(1)}, u32[]{:S(2)}, u32[]{:S(2)}) %collective-permute-start.40) | collective-permute-done | bytes 159776 | tf_op jit(solution)/shard_map/ppermute | solution.py:57
  (162 shorter events, 50.6 us)
Async XLA Ops:
  6.5 14.8 %collective-permute-start.2 = (bf16[48,1664]{1,0:T(8,128)(2,1)S(1)}, bf16[48,1664]{1,0:T(8,128)(2,1)S(1)}, u32[]{:S(2)}, u32[]{:S(2)}) collective-permute-start(bf16[48,1664]{1,0:T(8,128)(2,1)S(1)} %shard_map.323.refs_0_), channel_id=1, source_target_pairs={{0,16},{2,18},{4,20},{6,22},{8,24},{10,26},{12,28},{14,30},{16,0},... | collective-permute-start | bytes 479240 | tf_op jit(solution)/shard_map/ppermute | solution.py:57
  9.0 12.2 %collective-permute-start.3 = (bf16[48,1664]{1,0:T(8,128)(2,1)S(1)}, bf16[48,1664]{1,0:T(8,128)(2,1)S(1)}, u32[]{:S(2)}, u32[]{:S(2)}) collective-permute-start(bf16[48,1664]{1,0:T(8,128)(2,1)S(1)} %shard_map.323.refs_0_), channel_id=1, source_target_pairs={{0,24},{2,26},{4,28},{6,30},{8,16},{10,18},{12,20},{14,22},{16,8},... | collective-permute-start | bytes 479240 | tf_op jit(solution)/shard_map/ppermute | solution.py:57
  9.0 18.9 %collective-permute-start = (bf16[256,768]{1,0:T(8,128)(2,1)}, bf16[256,768]{1,0:T(8,128)(2,1)S(1)}, u32[]{:S(2)}, u32[]{:S(2)}) collective-permute-start(bf16[256,768]{1,0:T(8,128)(2,1)} %param.20), channel_id=1, source_target_pairs={{0,1},{1,0},{2,3},{3,2},{4,5},{5,4},{6,7},{7,6},{8,9},{9,8},{10,11... | collective-permute-start | bytes 1179656 | tf_op jit(solution)/shard_map/ppermute | solution.py:61
  21.3 13.7 %collective-permute-start.4 = (bf16[192,896]{1,0:T(8,128)(2,1)S(1)}, bf16[192,896]{1,0:T(8,128)(2,1)S(1)}, u32[]{:S(2)}, u32[]{:S(2)}) collective-permute-start(bf16[192,896]{1,0:T(8,128)(2,1)S(1)} %get-tuple-element.90.refs_0_.refs_2_), channel_id=1, source_target_pairs={{0,1},{1,0},{2,3},{3,2},{4,5},{5,4},{6,7},{7,6},{8,9},{9,8},{10,11... | collective-permute-start | bytes 1032200 | tf_op jit(solution)/shard_map/ppermute | solution.py:61
  22.9 14.3 %collective-permute-start.8 = (bf16[48,3072]{1,0:T(8,128)(2,1)S(1)}, bf16[48,3072]{1,0:T(8,128)(2,1)S(1)}, u32[]{:S(2)}, u32[]{:S(2)}) collective-permute-start(bf16[48,3072]{1,0:T(8,128)(2,1)S(1)} %shard_map.326.refs_0_), channel_id=1, source_target_pairs={{0,8},{2,10},{4,12},{6,14},{8,0},{10,2},{12,4},{14,6},{16,24},{18,... | collective-permute-start | bytes 884744 | tf_op jit(solution)/shard_map/ppermute | solution.py:57
  25.5 23.5 %collective-permute-start.9 = (bf16[48,3072]{1,0:T(8,128)(2,1)S(1)}, bf16[48,3072]{1,0:T(8,128)(2,1)S(1)}, u32[]{:S(2)}, u32[]{:S(2)}) collective-permute-start(bf16[48,3072]{1,0:T(8,128)(2,1)S(1)} %shard_map.326.refs_0_), channel_id=1, source_target_pairs={{0,16},{2,18},{4,20},{6,22},{8,24},{10,26},{12,28},{14,30},{16,0},... | collective-permute-start | bytes 884744 | tf_op jit(solution)/shard_map/ppermute | solution.py:57
  26.6 22.4 %collective-permute-start.10 = (bf16[48,3072]{1,0:T(8,128)(2,1)S(1)}, bf16[48,3072]{1,0:T(8,128)(2,1)S(1)}, u32[]{:S(2)}, u32[]{:S(2)}) collective-permute-start(bf16[48,3072]{1,0:T(8,128)(2,1)S(1)} %shard_map.326.refs_0_), channel_id=1, source_target_pairs={{0,24},{2,26},{4,28},{6,30},{8,16},{10,18},{12,20},{14,22},{16,8},... | collective-permute-start | bytes 884744 | tf_op jit(solution)/shard_map/ppermute | solution.py:57
  35.0 14.0 %collective-permute-start.6 = (bf16[384,768]{1,0:T(8,128)(2,1)S(1)}, bf16[384,768]{1,0:T(8,128)(2,1)S(1)}, u32[]{:S(2)}, u32[]{:S(2)}) collective-permute-start(bf16[384,768]{1,0:T(8,128)(2,1)S(1)} %get-tuple-element.92.refs_0_), channel_id=1, source_target_pairs={{0,1},{1,0},{2,3},{3,2},{4,5},{5,4},{6,7},{7,6},{8,9},{9,8},{10,11... | collective-permute-start | bytes 1769480 | tf_op jit(solution)/shard_map/ppermute | solution.py:61
  35.6 14.2 %collective-permute-start.7 = (bf16[192,1792]{1,0:T(8,128)(2,1)S(1)}, bf16[192,1792]{1,0:T(8,128)(2,1)S(1)}, u32[]{:S(2)}, u32[]{:S(2)}) collective-permute-start(bf16[192,1792]{1,0:T(8,128)(2,1)S(1)} %get-tuple-element.93.refs_1_), channel_id=1, source_target_pairs={{0,4},{2,6},{4,0},{6,2},{8,12},{10,14},{12,8},{14,10},{16,20},{18,... | collective-permute-start | bytes 2064392 | tf_op jit(solution)/shard_map/ppermute | solution.py:57
  50.6 15.3 %collective-permute-start.13 = (bf16[192,1536]{1,0:T(8,128)(2,1)S(1)}, bf16[192,1536]{1,0:T(8,128)(2,1)S(1)}, u32[]{:S(2)}, u32[]{:S(2)}) collective-permute-start(bf16[192,1536]{1,0:T(8,128)(2,1)S(1)} %get-tuple-element.94.refs_4_.refs_0_), channel_id=1, source_target_pairs={{0,1},{1,0},{2,3},{3,2},{4,5},{5,4},{6,7},{7,6},{8,9},{9,8},{10,11... | collective-permute-start | bytes 1769480 | tf_op jit(solution)/shard_map/ppermute | solution.py:61
  52.1 15.0 %collective-permute-start.14 = (bf16[192,1536]{1,0:T(8,128)(2,1)S(1)}, bf16[192,1536]{1,0:T(8,128)(2,1)S(1)}, u32[]{:S(2)}, u32[]{:S(2)}) collective-permute-start(bf16[192,1536]{1,0:T(8,128)(2,1)S(1)} %get-tuple-element.102.refs_1_), channel_id=1, source_target_pairs={{0,4},{2,6},{4,0},{6,2},{8,12},{10,14},{12,8},{14,10},{16,20},{18,... | collective-permute-start | bytes 1769480 | tf_op jit(solution)/shard_map/ppermute | solution.py:57
  67.3 11.1 %collective-permute-start.15 = (bf16[192,3072]{1,0:T(8,128)(2,1)S(1)}, bf16[192,3072]{1,0:T(8,128)(2,1)S(1)}, u32[]{:S(2)}, u32[]{:S(2)}) collective-permute-start(bf16[192,3072]{1,0:T(8,128)(2,1)S(1)} %get-tuple-element.103.refs_5_.refs_1_), channel_id=1, source_target_pairs={{0,2},{2,0},{4,6},{6,4},{8,10},{10,8},{12,14},{14,12},{16,18},{18,... | collective-permute-start | bytes 3538952 | tf_op jit(solution)/shard_map/ppermute | solution.py:57
  67.3 11.1 %collective-permute-start.16 = (bf16[384,1536]{1,0:T(8,128)(2,1)S(1)}, bf16[384,1536]{1,0:T(8,128)(2,1)S(1)}, u32[]{:S(2)}, u32[]{:S(2)}) collective-permute-start(bf16[384,1536]{1,0:T(8,128)(2,1)S(1)} %get-tuple-element.105.refs_3_.refs_1_), channel_id=1, source_target_pairs={{0,2},{2,0},{4,6},{6,4},{8,10},{10,8},{12,14},{14,12},{16,18},{18,... | collective-permute-start | bytes 3538952 | tf_op jit(solution)/shard_map/ppermute | solution.py:57
  67.8 28.0 %collective-permute-start.17 = (bf16[192,3072]{1,0:T(8,128)(2,1)S(1)}, bf16[192,3072]{1,0:T(8,128)(2,1)S(1)}, u32[]{:S(2)}, u32[]{:S(2)}) collective-permute-start(bf16[192,3072]{1,0:T(8,128)(2,1)S(1)} %get-tuple-element.103.refs_5_.refs_1_), channel_id=1, source_target_pairs={{0,4},{2,6},{4,0},{6,2},{8,12},{10,14},{12,8},{14,10},{16,20},{18,... | collective-permute-start | bytes 3538952 | tf_op jit(solution)/shard_map/ppermute | solution.py:57
  69.4 27.7 %collective-permute-start.18 = (bf16[384,1536]{1,0:T(8,128)(2,1)S(1)}, bf16[384,1536]{1,0:T(8,128)(2,1)S(1)}, u32[]{:S(2)}, u32[]{:S(2)}) collective-permute-start(bf16[384,1536]{1,0:T(8,128)(2,1)S(1)} %get-tuple-element.105.refs_3_.refs_1_), channel_id=1, source_target_pairs={{0,1},{1,0},{2,3},{3,2},{4,5},{5,4},{6,7},{7,6},{8,9},{9,8},{10,11... | collective-permute-start | bytes 3538952 | tf_op jit(solution)/shard_map/ppermute | solution.py:61
  109.8 34.3 %collective-permute-start.23 = (bf16[192,3072]{1,0:T(8,128)(2,1)S(1)}, bf16[192,3072]{1,0:T(8,128)(2,1)S(1)}, u32[]{:S(2)}, u32[]{:S(2)}) collective-permute-start(bf16[192,3072]{1,0:T(8,128)(2,1)S(1)} %convolution_convert_fusion), channel_id=1, source_target_pairs={{0,2},{2,0},{4,6},{6,4},{8,10},{10,8},{12,14},{14,12},{16,18},{18,... | collective-permute-start | bytes 3538952 | tf_op jit(solution)/shard_map/ppermute | solution.py:57
  110.5 32.9 %collective-permute-start.24 = (bf16[384,1536]{1,0:T(8,128)(2,1)S(1)}, bf16[384,1536]{1,0:T(8,128)(2,1)S(1)}, u32[]{:S(2)}, u32[]{:S(2)}) collective-permute-start(bf16[384,1536]{1,0:T(8,128)(2,1)S(1)} %convolution_convert_fusion.4), channel_id=1, source_target_pairs={{0,2},{2,0},{4,6},{6,4},{8,10},{10,8},{12,14},{14,12},{16,18},{18,... | collective-permute-start | bytes 3538952 | tf_op jit(solution)/shard_map/ppermute | solution.py:57
  112.4 40.2 %collective-permute-start.26 = (bf16[384,1536]{1,0:T(8,128)(2,1)S(1)}, bf16[384,1536]{1,0:T(8,128)(2,1)S(1)}, u32[]{:S(2)}, u32[]{:S(2)}) collective-permute-start(bf16[384,1536]{1,0:T(8,128)(2,1)S(1)} %shard_map.338.refs_2_), channel_id=1, source_target_pairs={{0,1},{1,0},{2,3},{3,2},{4,5},{5,4},{6,7},{7,6},{8,9},{9,8},{10,11... | collective-permute-start | bytes 3538952 | tf_op jit(solution)/shard_map/ppermute | solution.py:61
  124.8 27.8 %collective-permute-start.25 = (bf16[192,3072]{1,0:T(8,128)(2,1)S(1)}, bf16[192,3072]{1,0:T(8,128)(2,1)S(1)}, u32[]{:S(2)}, u32[]{:S(2)}) collective-permute-start(bf16[192,3072]{1,0:T(8,128)(2,1)S(1)} %shard_map.339.refs_11_), channel_id=1, source_target_pairs={{0,4},{2,6},{4,0},{6,2},{8,12},{10,14},{12,8},{14,10},{16,20},{18,... | collective-permute-start | bytes 3538952 | tf_op jit(solution)/shard_map/ppermute | solution.py:57
  143.3 14.6 %collective-permute-start.29 = (bf16[384,1792]{1,0:T(8,128)(2,1)S(1)}, bf16[384,1792]{1,0:T(8,128)(2,1)S(1)}, u32[]{:S(2)}, u32[]{:S(2)}) collective-permute-start(bf16[384,1792]{1,0:T(8,128)(2,1)S(1)} %get-tuple-element.135), channel_id=1, source_target_pairs={{0,2},{2,0},{4,6},{6,4},{8,10},{10,8},{12,14},{14,12},{16,18},{18,... | collective-permute-start | bytes 4128776 | tf_op jit(solution)/shard_map/ppermute | solution.py:57
  143.4 14.5 %collective-permute-start.30 = (bf16[384,1536]{1,0:T(8,128)(2,1)S(1)}, bf16[384,1536]{1,0:T(8,128)(2,1)S(1)}, u32[]{:S(2)}, u32[]{:S(2)}) collective-permute-start(bf16[384,1536]{1,0:T(8,128)(2,1)S(1)} %get-tuple-element.137), channel_id=1, source_target_pairs={{0,2},{2,0},{4,6},{6,4},{8,10},{10,8},{12,14},{14,12},{16,18},{18,... | collective-permute-start | bytes 3538952 | tf_op jit(solution)/shard_map/ppermute | solution.py:57
  153.1 16.3 %collective-permute-start.27 = (bf16[192,1536]{1,0:T(8,128)(2,1)S(1)}, bf16[192,1536]{1,0:T(8,128)(2,1)S(1)}, u32[]{:S(2)}, u32[]{:S(2)}) collective-permute-start(bf16[192,1536]{1,0:T(8,128)(2,1)S(1)} %get-tuple-element.132), channel_id=1, source_target_pairs={{0,1},{1,0},{2,3},{3,2},{4,5},{5,4},{6,7},{7,6},{8,9},{9,8},{10,11... | collective-permute-start | bytes 1769480 | tf_op jit(solution)/shard_map/ppermute | solution.py:61
  154.7 16.3 %collective-permute-start.28 = (bf16[192,1536]{1,0:T(8,128)(2,1)S(1)}, bf16[192,1536]{1,0:T(8,128)(2,1)S(1)}, u32[]{:S(2)}, u32[]{:S(2)}) collective-permute-start(bf16[192,1536]{1,0:T(8,128)(2,1)S(1)} %get-tuple-element.134), channel_id=1, source_target_pairs={{0,4},{2,6},{4,0},{6,2},{8,12},{10,14},{12,8},{14,10},{16,20},{18,... | collective-permute-start | bytes 1769480 | tf_op jit(solution)/shard_map/ppermute | solution.py:57
  158.4 24.9 %collective-permute-start.34 = (bf16[192,1792]{1,0:T(8,128)(2,1)S(1)}, bf16[192,1792]{1,0:T(8,128)(2,1)S(1)}, u32[]{:S(2)}, u32[]{:S(2)}) collective-permute-start(bf16[192,1792]{1,0:T(8,128)(2,1)S(1)} %get-tuple-element.143), channel_id=1, source_target_pairs={{0,4},{2,6},{4,0},{6,2},{8,12},{10,14},{12,8},{14,10},{16,20},{18,... | collective-permute-start | bytes 2064392 | tf_op jit(solution)/shard_map/ppermute | solution.py:57
  160.0 20.0 %collective-permute-start.35 = (bf16[384,768]{1,0:T(8,128)(2,1)S(1)}, bf16[384,768]{1,0:T(8,128)(2,1)S(1)}, u32[]{:S(2)}, u32[]{:S(2)}) collective-permute-start(bf16[384,768]{1,0:T(8,128)(2,1)S(1)} %get-tuple-element.145), channel_id=1, source_target_pairs={{0,1},{1,0},{2,3},{3,2},{4,5},{5,4},{6,7},{7,6},{8,9},{9,8},{10,11... | collective-permute-start | bytes 1769480 | tf_op jit(solution)/shard_map/ppermute | solution.py:61
  171.2 13.6 %collective-permute-start.31 = (bf16[48,3072]{1,0:T(8,128)(2,1)S(1)}, bf16[48,3072]{1,0:T(8,128)(2,1)S(1)}, u32[]{:S(2)}, u32[]{:S(2)}) collective-permute-start(bf16[48,3072]{1,0:T(8,128)(2,1)S(1)} %get-tuple-element.140), channel_id=1, source_target_pairs={{0,8},{2,10},{4,12},{6,14},{8,0},{10,2},{12,4},{14,6},{16,24},{18,... | collective-permute-start | bytes 884744 | tf_op jit(solution)/shard_map/ppermute | solution.py:57
  173.6 20.9 %collective-permute-start.32 = (bf16[48,3072]{1,0:T(8,128)(2,1)S(1)}, bf16[48,3072]{1,0:T(8,128)(2,1)S(1)}, u32[]{:S(2)}, u32[]{:S(2)}) collective-permute-start(bf16[48,3072]{1,0:T(8,128)(2,1)S(1)} %get-tuple-element.141), channel_id=1, source_target_pairs={{0,16},{2,18},{4,20},{6,22},{8,24},{10,26},{12,28},{14,30},{16,0},... | collective-permute-start | bytes 884744 | tf_op jit(solution)/shard_map/ppermute | solution.py:57
  174.9 19.6 %collective-permute-start.33 = (bf16[48,3072]{1,0:T(8,128)(2,1)S(1)}, bf16[48,3072]{1,0:T(8,128)(2,1)S(1)}, u32[]{:S(2)}, u32[]{:S(2)}) collective-permute-start(bf16[48,3072]{1,0:T(8,128)(2,1)S(1)} %get-tuple-element.142), channel_id=1, source_target_pairs={{0,24},{2,26},{4,28},{6,30},{8,16},{10,18},{12,20},{14,22},{16,8},... | collective-permute-start | bytes 884744 | tf_op jit(solution)/shard_map/ppermute | solution.py:57
  183.7 12.6 %collective-permute-start.37 = (bf16[192,896]{1,0:T(8,128)(2,1)S(1)}, bf16[192,896]{1,0:T(8,128)(2,1)S(1)}, u32[]{:S(2)}, u32[]{:S(2)}) collective-permute-start(bf16[192,896]{1,0:T(8,128)(2,1)S(1)} %get-tuple-element.147), channel_id=1, source_target_pairs={{0,1},{1,0},{2,3},{3,2},{4,5},{5,4},{6,7},{7,6},{8,9},{9,8},{10,11... | collective-permute-start | bytes 1032200 | tf_op jit(solution)/shard_map/ppermute | solution.py:61
  184.3 12.0 %collective-permute-start.38 = (bf16[192,768]{1,0:T(8,128)(2,1)S(1)}, bf16[192,768]{1,0:T(8,128)(2,1)S(1)}, u32[]{:S(2)}, u32[]{:S(2)}) collective-permute-start(bf16[192,768]{1,0:T(8,128)(2,1)S(1)} %get-tuple-element.149), channel_id=1, source_target_pairs={{0,4},{2,6},{4,0},{6,2},{8,12},{10,14},{12,8},{14,10},{16,20},{18,... | collective-permute-start | bytes 884744 | tf_op jit(solution)/shard_map/ppermute | solution.py:57
  196.4 11.2 %collective-permute-start.39 = (bf16[48,1664]{1,0:T(8,128)(2,1)S(1)}, bf16[48,1664]{1,0:T(8,128)(2,1)S(1)}, u32[]{:S(2)}, u32[]{:S(2)}) collective-permute-start(bf16[48,1664]{1,0:T(8,128)(2,1)S(1)} %get-tuple-element.151), channel_id=1, source_target_pairs={{0,8},{2,10},{4,12},{6,14},{8,0},{10,2},{12,4},{14,6},{16,24},{18,... | collective-permute-start | bytes 479240 | tf_op jit(solution)/shard_map/ppermute | solution.py:57
  200.2 12.1 %collective-permute-start.40 = (bf16[48,1664]{1,0:T(8,128)(2,1)S(1)}, bf16[48,1664]{1,0:T(8,128)(2,1)S(1)}, u32[]{:S(2)}, u32[]{:S(2)}) collective-permute-start(bf16[48,1664]{1,0:T(8,128)(2,1)S(1)} %get-tuple-element.152), channel_id=1, source_target_pairs={{0,16},{2,18},{4,20},{6,22},{8,24},{10,26},{12,28},{14,30},{16,0},... | collective-permute-start | bytes 479240 | tf_op jit(solution)/shard_map/ppermute | solution.py:57
  (40 other events, 349.3 us)

commit v10 on v9

--- a/solution.py
+++ b/solution.py
@@ -479,8 +479,10 @@
     rows = y_low[...]
     columns = pieces[0].shape[1]
     step = columns // 8
-    for start in range(0, columns, step):
-        at = slice(start, start + step)
+
+    @pl.loop(0, 8)
+    def _(place):
+        at = pl.ds(pl.multiple_of(place * step, LANES), step)
         pre = dot(rows, stacked(pieces, at)) + bias[:, at]
         cdf = 0.5 + 0.5 * lax.erf(pre * (0.5**0.5))
         activation[:, at] = (pre * cdf).astype(LOW)
@@ -514,10 +516,13 @@
     rows = grad_low[...]
     columns = own.shape[1]
     step = columns // 4
-    for place, pieces in enumerate(((own, far), (own_side, far_side))):
-        for start in range(0, columns, step):
-            to = slice(place * columns + start, place * columns + start + step)
-            grad_act = dot(rows, stacked(pieces, slice(start, start + step)))
+    for side, pieces in enumerate(((own, far), (own_side, far_side))):
+
+        @pl.loop(0, 4)
+        def _(place, side=side, pieces=pieces):
+            to = pl.ds(pl.multiple_of(side * columns + place * step, LANES), step)
+            at = pl.ds(pl.multiple_of(place * step, LANES), step)
+            grad_act = dot(rows, stacked(pieces, at))
             value = (grad_act * slope[:, to]).astype(LOW)
             grad_pre[:, to] = value
             sums[:, to] = jnp.sum(value.astype(F32), axis=0, keepdims=True)

time: 216 us -> 207 us (0.958)
  between operations: 13 us -> 1.52 us
  Pallas kernels: 46.5 us -> 49.2 us
    pallas_call x30, Pallas kernels: 46.5 us -> 49.2 us  [run(): pl.pallas_call(body, grid=grid, out_shape=list(outs), in_specs=list(in_sp...]
  transfers between devices with their start and end apart: 42 -> 42, of which waited for: 16 -> 16; matrix products, arithmetic and copies ran while one was open for 5% -> 5% of each run, Pallas kernels for 20% -> 22%
where the time goes in v10:
time: 207 us; the launch traced here: 206 us
  waiting for transfers between devices  93.9 us (45%)
  Pallas kernels  49.2 us (24%)
  starting transfers between devices  45.8 us (22%)
  matrix products  7.67 us (4%)
  local copies, waits for them, and re-layouts  4.74 us (2%)
  other arithmetic  3.27 us (2%)
    ppermute x32, waiting for transfers between devices, swap_dp(): return lax.ppermute(values, 'dp', [(i, i ^ mask) for i in range(size)])  72.2 us
    pallas_call x30, Pallas kernels, run(): pl.pallas_call(body, grid=grid, out_shape=list(outs), in_specs=list(in_sp...  49.2 us
    ppermute x32, starting transfers between devices, swap_dp(): return lax.ppermute(values, 'dp', [(i, i ^ mask) for i in range(size)])  35.1 us
    ppermute x10, waiting for transfers between devices, swap_tensor(): return lax.ppermute(values, 'tensor', [(0, 1), (1, 0)])  21.7 us
    ppermute x10, starting transfers between devices, swap_tensor(): return lax.ppermute(values, 'tensor', [(0, 1), (1, 0)])  10.7 us
    unnamed x60, local copies, waits for them, and re-layouts  4.74 us
    dot_general x8, matrix products, dot_tn(): lax.dot_general(left, right, (((0,), (0,)), ((), ())), preferred_element_...  4.16 us
  transfers between devices with their start and end apart: 42, of which 16 were waited for; matrix products, arithmetic and copies ran while one was open for 5% of the time, Pallas kernels for 22%

profile of v10, /device:TPU:0, one launch (start us, length us, event | category | flops | bytes accessed | tf_op | source)
XLA Modules:
  0.0 206.2 jit_solution(6267193533201747737)
XLA Ops:
  3.4 3.1 %collective-permute-start.1 = (bf16[48,1664]{1,0:T(8,128)(2,1)S(1)}, bf16[48,1664]{1,0:T(8,128)(2,1)S(1)}, u32[]{:S(2)}, u32[]{:S(2)}) collective-permute-start(bf16[48,1664]{1,0:T(8,128)(2,1)S(1)} %shard_map.323.refs_0_), channel_id=1, source_target_pairs={{0,8},{2,10},{4,12},{6,14},{8,0},{10,2},{12,4},{14,6},{16,24},{18,... | collective-permute-start | bytes 479240 | tf_op jit(solution)/shard_map/ppermute | solution.py:57
  6.5 2.6 %collective-permute-start.2 = (bf16[48,1664]{1,0:T(8,128)(2,1)S(1)}, bf16[48,1664]{1,0:T(8,128)(2,1)S(1)}, u32[]{:S(2)}, u32[]{:S(2)}) collective-permute-start(bf16[48,1664]{1,0:T(8,128)(2,1)S(1)} %shard_map.323.refs_0_), channel_id=1, source_target_pairs={{0,16},{2,18},{4,20},{6,22},{8,24},{10,26},{12,28},{14,30},{16,0},... | collective-permute-start | bytes 479240 | tf_op jit(solution)/shard_map/ppermute | solution.py:57
  9.0 1.7 collective-permute-start
  11.5 1.6 fusion.10
  13.1 8.1 %collective-permute-done.2.refs_2_ = bf16[48,1664]{1,0:T(8,128)(2,1)S(1)} collective-permute-done((bf16[48,1664]{1,0:T(8,128)(2,1)S(1)}, bf16[48,1664]{1,0:T(8,128)(2,1)S(1)}, u32[]{:S(2)}, u32[]{:S(2)}) %collective-permute-start.2) | collective-permute-done | bytes 159776 | tf_op jit(solution)/shard_map/ppermute | solution.py:57
  21.3 1.6 collective-permute-start.4
  22.9 2.6 %collective-permute-start.8 = (bf16[48,3072]{1,0:T(8,128)(2,1)S(1)}, bf16[48,3072]{1,0:T(8,128)(2,1)S(1)}, u32[]{:S(2)}, u32[]{:S(2)}) collective-permute-start(bf16[48,3072]{1,0:T(8,128)(2,1)S(1)} %shard_map.326.refs_0_), channel_id=1, source_target_pairs={{0,8},{2,10},{4,12},{6,14},{8,0},{10,2},{12,4},{14,6},{16,24},{18,... | collective-permute-start | bytes 884744 | tf_op jit(solution)/shard_map/ppermute | solution.py:57
  30.2 4.7 %collective-permute-done.5.refs_3_ = bf16[192,768]{1,0:T(8,128)(2,1)S(1)} collective-permute-done((bf16[192,768]{1,0:T(8,128)(2,1)S(1)}, bf16[192,768]{1,0:T(8,128)(2,1)S(1)}, u32[]{:S(2)}, u32[]{:S(2)}) %collective-permute-start.5) | collective-permute-done | bytes 294944 | tf_op jit(solution)/shard_map/ppermute | solution.py:57
  37.2 11.8 %collective-permute-done.9.refs_2_ = bf16[48,3072]{1,0:T(8,128)(2,1)S(1)} collective-permute-done((bf16[48,3072]{1,0:T(8,128)(2,1)S(1)}, bf16[48,3072]{1,0:T(8,128)(2,1)S(1)}, u32[]{:S(2)}, u32[]{:S(2)}) %collective-permute-start.9) | collective-permute-done | bytes 294944 | tf_op jit(solution)/shard_map/ppermute | solution.py:57
  55.5 2.6 %shard_map.330 = (bf16[256,768]{1,0:T(8,128)(2,1)S(1)}, bf16[512,768]{1,0:T(8,128)(2,1)S(1)}, bf16[512,768]{1,0:T(8,128)(2,1)S(1)}) custom-call(bf16[512,768]{1,0:T(8,128)(2,1)S(1)} %pad_maximum_fusion.refs_4_.refs_0_.refs_1_.refs_2_, bf16[384,1792]{1,0:T(8,128)(2,1)S(1)} %get-tuple-element.95.refs_2_.refs_1_.refs_3_, ...), custom_call_target="tpu_custom_call" | custom-call | flops 1509949440 | bytes 7870464 | tf_op jit(solution)/shard_map/pallas_call | solution.py:142
  58.1 7.8 %collective-permute-done.13.refs_2_ = bf16[192,1536]{1,0:T(8,128)(2,1)S(1)} collective-permute-done((bf16[192,1536]{1,0:T(8,128)(2,1)S(1)}, bf16[192,1536]{1,0:T(8,128)(2,1)S(1)}, u32[]{:S(2)}, u32[]{:S(2)}) %collective-permute-start.13) | collective-permute-done | bytes 589856 | tf_op jit(solution)/shard_map/ppermute | solution.py:61
  69.9 8.2 %shard_map.332.refs_0_.refs_7_ = bf16[256,768]{1,0:T(8,128)(2,1)S(1)} custom-call(s32[1]{0:T(128)} %bitcast.refs_0_, s32[1,3]{1,0:T(1,128)S(1)} %copy-done.25, bf16[256,768]{1,0:T(8,128)(2,1)S(1)} %get-tuple-element.99.refs_4_.refs_2_, bf16[512,768]{1,0:T(8,128)(2,1)S(1)} %get-tuple-element.100.refs_3_, bf16[512,768]{1,0:T(8,128)(2,1)S(1)} %get-tuple-element.101.refs_4_, ...), custom_call_target="tpu_custom_call" | custom-call | flops 905969664 | bytes 2359312 | tf_op jit(solution)/shard_map/pallas_call | solution.py:142
  79.1 16.7 %collective-permute-done.17.refs_0_ = bf16[192,3072]{1,0:T(8,128)(2,1)S(1)} collective-permute-done((bf16[192,3072]{1,0:T(8,128)(2,1)S(1)}, bf16[192,3072]{1,0:T(8,128)(2,1)S(1)}, u32[]{:S(2)}, u32[]{:S(2)}) %collective-permute-start.17) | collective-permute-done | bytes 1179680 | tf_op jit(solution)/shard_map/ppermute | solution.py:57
  98.2 1.7 collective-permute-done.19.refs_4_
  99.9 3.9 %shard_map.335 = (bf16[256,3072]{1,0:T(8,128)(2,1)S(1)}, f32[256,3072]{1,0:T(8,128)S(1)}) custom-call(bf16[256,768]{1,0:T(8,128)(2,1)S(1)} %get-tuple-element.106.refs_2_.refs_0_, bf16[192,3072]{1,0:T(8,128)(2,1)S(1)} %get-tuple-element.103.refs_5_.refs_1_, bf16[192,3072]{1,0:T(8,128)(2,1)S(1)} %get-tuple-element.107.refs_2_, ...), custom_call_target="tpu_custom_call" | custom-call | flops 2415919104 | bytes 9842688 | tf_op jit(solution)/shard_map/pallas_call | solution.py:142
  103.8 3.0 %shard_map.336 = (bf16[256,768]{1,0:T(8,128)(2,1)S(1)}, f32[256,768]{1,0:T(8,128)S(1)}, bf16[256,768]{1,0:T(8,128)(2,1)S(1)}, f32[8,768]{1,0:T(8,128)S(1)}) custom-call(s32[1]{0:T(128)} %bitcast.refs_0_, s32[1,3]{1,0:T(1,128)S(1)} %copy-done.25, bf16[256,3072]{1,0:T(8,128)(2,1)S(1)} %get-tuple-element.109.refs_2_, ...), custom_call_target="tpu_custom_call" | custom-call | flops 1509949440 | bytes 9480208 | tf_op jit(solution)/shard_map/pallas_call | solution.py:142
  107.6 3.4 %shard_map.337 = (bf16[256,3072]{1,0:T(8,128)(2,1)S(1)}, f32[1,3072]{1,0:T(1,128)S(1)}) custom-call(bf16[256,768]{1,0:T(8,128)(2,1)S(1)} %get-tuple-element.113.refs_0_, bf16[384,1536]{1,0:T(8,128)(2,1)S(1)} %get-tuple-element.105.refs_3_.refs_1_, bf16[384,1536]{1,0:T(8,128)(2,1)S(1)} %get-tuple-element.110.refs_4_.refs_2_, ...), custom_call_target="tpu_custom_call" | custom-call | flops 1811939328 | bytes 9842688 | tf_op jit(solution)/shard_map/pallas_call | solution.py:142
  118.2 2.7 %shard_map.340 = (f32[256,768]{1,0:T(8,128)S(1)}, bf16[256,768]{1,0:T(8,128)(2,1)S(1)}, bf16[256,768]{1,0:T(8,128)(2,1)S(1)}, f32[8,768]{1,0:T(8,128)S(1)}) custom-call(bf16[256,3072]{1,0:T(8,128)(2,1)S(1)} %get-tuple-element.115.refs_2_.refs_0_, bf16[192,3072]{1,0:T(8,128)(2,1)S(1)} %get-tuple-element.103.refs_5_.refs_1_, ...), custom_call_target="tpu_custom_call" | custom-call | flops 1811939328 | bytes 11840512 | tf_op jit(solution)/shard_map/pallas_call | solution.py:142
  120.9 10.8 %shard_map.341 = (bf16[256,768]{1,0:T(8,128)(2,1)S(1)}, bf16[512,768]{1,0:T(8,128)(2,1)S(1)}, bf16[512,768]{1,0:T(8,128)(2,1)S(1)}) custom-call(s32[1]{0:T(128)} %bitcast.refs_0_, s32[1,3]{1,0:T(1,128)S(1)} %copy-done.25, bf16[256,768]{1,0:T(8,128)(2,1)S(1)} %get-tuple-element.99.refs_4_.refs_2_, bf16[512,768]{1,0:T(8,128)(2,1)S(1)} %get-tuple-element.100.refs_3_, ...), custom_call_target="tpu_custom_call" | custom-call | flops 1509949440 | bytes 4325392 | tf_op jit(solution)/shard_map/pallas_call | solution.py:142
  131.6 3.1 %shard_map.344 = (bf16[384,1792]{1,0:T(8,128)(2,1)S(1)}, bf16[384,1536]{1,0:T(8,128)(2,1)S(1)}, bf16[384,1792]{1,0:T(8,128)(2,1)S(1)}, bf16[384,1536]{1,0:T(8,128)(2,1)S(1)}) custom-call(s32[1]{0:T(128)} %bitcast.refs_0_, bf16[768,768]{1,0:T(8,128)(2,1)S(1)} %copy-done.7, bf16[512,768]{1,0:T(8,128)(2,1)S(1)} %pad_maximum_fusion.refs_4_.refs_0_.refs_1_.refs_2_, ...), custom_call_target="tpu_custom_call" | custom-call | flops 1811939328 | bytes 9891844 | tf_op jit(solution)/shard_map/pallas_call | solution.py:142
  135.9 7.9 %collective-permute-done.25.refs_1_ = bf16[192,3072]{1,0:T(8,128)(2,1)S(1)} collective-permute-done((bf16[192,3072]{1,0:T(8,128)(2,1)S(1)}, bf16[192,3072]{1,0:T(8,128)(2,1)S(1)}, u32[]{:S(2)}, u32[]{:S(2)}) %collective-permute-start.25) | collective-permute-done | bytes 1179680 | tf_op jit(solution)/shard_map/ppermute | solution.py:57
  144.3 1.6 collective-permute-start.27
  146.4 2.6 %shard_map.346 = (f32[256,768]{1,0:T(8,128)S(1)}, bf16[256,768]{1,0:T(8,128)(2,1)S(1)}) custom-call(bf16[256,768]{1,0:T(8,128)(2,1)S(1)} %get-tuple-element.120.refs_3_.refs_0_, bf16[512,768]{1,0:T(8,128)(2,1)S(1)} %get-tuple-element.121.refs_4_.refs_1_, bf16[512,768]{1,0:T(8,128)(2,1)S(1)} %get-tuple-element.122.refs_5_.refs_2_, ...), custom_call_target="tpu_custom_call" | custom-call | flops 120795955200 | bytes 9043968 | tf_op jit(solution)/shard_map/pallas_call | solution.py:142
  149.6 1.6 collective-permute-start.34
  151.7 8.9 %collective-permute-done.27.refs_1_ = bf16[192,1536]{1,0:T(8,128)(2,1)S(1)} collective-permute-done((bf16[192,1536]{1,0:T(8,128)(2,1)S(1)}, bf16[192,1536]{1,0:T(8,128)(2,1)S(1)}, u32[]{:S(2)}, u32[]{:S(2)}) %collective-permute-start.27) | collective-permute-done | bytes 589856 | tf_op jit(solution)/shard_map/ppermute | solution.py:61
  162.4 2.4 %collective-permute-start.31 = (bf16[48,3072]{1,0:T(8,128)(2,1)S(1)}, bf16[48,3072]{1,0:T(8,128)(2,1)S(1)}, u32[]{:S(2)}, u32[]{:S(2)}) collective-permute-start(bf16[48,3072]{1,0:T(8,128)(2,1)S(1)} %get-tuple-element.140), channel_id=1, source_target_pairs={{0,8},{2,10},{4,12},{6,14},{8,0},{10,2},{12,4},{14,6},{16,24},{18,... | collective-permute-start | bytes 884744 | tf_op jit(solution)/shard_map/ppermute | solution.py:57
  167.5 3.8 %collective-permute-done.35.refs_3_ = bf16[384,768]{1,0:T(8,128)(2,1)S(1)} collective-permute-done((bf16[384,768]{1,0:T(8,128)(2,1)S(1)}, bf16[384,768]{1,0:T(8,128)(2,1)S(1)}, u32[]{:S(2)}, u32[]{:S(2)}) %collective-permute-start.35) | collective-permute-done | bytes 589856 | tf_op jit(solution)/shard_map/ppermute | solution.py:61
  171.2 3.3 %collective-permute-done.34.refs_1_ = bf16[192,1792]{1,0:T(8,128)(2,1)S(1)} collective-permute-done((bf16[192,1792]{1,0:T(8,128)(2,1)S(1)}, bf16[192,1792]{1,0:T(8,128)(2,1)S(1)}, u32[]{:S(2)}, u32[]{:S(2)}) %collective-permute-start.34) | collective-permute-done | bytes 688160 | tf_op jit(solution)/shard_map/ppermute | solution.py:57
  176.0 9.7 %collective-permute-done.32.refs_2_ = bf16[48,3072]{1,0:T(8,128)(2,1)S(1)} collective-permute-done((bf16[48,3072]{1,0:T(8,128)(2,1)S(1)}, bf16[48,3072]{1,0:T(8,128)(2,1)S(1)}, u32[]{:S(2)}, u32[]{:S(2)}) %collective-permute-start.32) | collective-permute-done | bytes 294944 | tf_op jit(solution)/shard_map/ppermute | solution.py:57
  187.6 3.8 %collective-permute-start.39 = (bf16[48,1664]{1,0:T(8,128)(2,1)S(1)}, bf16[48,1664]{1,0:T(8,128)(2,1)S(1)}, u32[]{:S(2)}, u32[]{:S(2)}) collective-permute-start(bf16[48,1664]{1,0:T(8,128)(2,1)S(1)} %get-tuple-element.151), channel_id=1, source_target_pairs={{0,8},{2,10},{4,12},{6,14},{8,0},{10,2},{12,4},{14,6},{16,24},{18,... | collective-permute-start | bytes 479240 | tf_op jit(solution)/shard_map/ppermute | solution.py:57
  196.9 2.0 shard_map.353.refs_14_
  198.9 4.7 %collective-permute-done.40.refs_12_ = bf16[48,1664]{1,0:T(8,128)(2,1)S(1)} collective-permute-done((bf16[48,1664]{1,0:T(8,128)(2,1)S(1)}, bf16[48,1664]{1,0:T(8,128)(2,1)S(1)}, u32[]{:S(2)}, u32[]{:S(2)}) %collective-permute-start.40) | collective-permute-done | bytes 159776 | tf_op jit(solution)/shard_map/ppermute | solution.py:57
  (162 shorter events, 50.7 us)
Async XLA Ops:
  6.5 14.8 %collective-permute-start.2 = (bf16[48,1664]{1,0:T(8,128)(2,1)S(1)}, bf16[48,1664]{1,0:T(8,128)(2,1)S(1)}, u32[]{:S(2)}, u32[]{:S(2)}) collective-permute-start(bf16[48,1664]{1,0:T(8,128)(2,1)S(1)} %shard_map.323.refs_0_), channel_id=1, source_target_pairs={{0,16},{2,18},{4,20},{6,22},{8,24},{10,26},{12,28},{14,30},{16,0},... | collective-permute-start | bytes 479240 | tf_op jit(solution)/shard_map/ppermute | solution.py:57
  9.0 12.2 %collective-permute-start.3 = (bf16[48,1664]{1,0:T(8,128)(2,1)S(1)}, bf16[48,1664]{1,0:T(8,128)(2,1)S(1)}, u32[]{:S(2)}, u32[]{:S(2)}) collective-permute-start(bf16[48,1664]{1,0:T(8,128)(2,1)S(1)} %shard_map.323.refs_0_), channel_id=1, source_target_pairs={{0,24},{2,26},{4,28},{6,30},{8,16},{10,18},{12,20},{14,22},{16,8},... | collective-permute-start | bytes 479240 | tf_op jit(solution)/shard_map/ppermute | solution.py:57
  9.0 18.9 %collective-permute-start = (bf16[256,768]{1,0:T(8,128)(2,1)}, bf16[256,768]{1,0:T(8,128)(2,1)S(1)}, u32[]{:S(2)}, u32[]{:S(2)}) collective-permute-start(bf16[256,768]{1,0:T(8,128)(2,1)} %param.20), channel_id=1, source_target_pairs={{0,1},{1,0},{2,3},{3,2},{4,5},{5,4},{6,7},{7,6},{8,9},{9,8},{10,11... | collective-permute-start | bytes 1179656 | tf_op jit(solution)/shard_map/ppermute | solution.py:61
  21.3 13.7 %collective-permute-start.4 = (bf16[192,896]{1,0:T(8,128)(2,1)S(1)}, bf16[192,896]{1,0:T(8,128)(2,1)S(1)}, u32[]{:S(2)}, u32[]{:S(2)}) collective-permute-start(bf16[192,896]{1,0:T(8,128)(2,1)S(1)} %get-tuple-element.90.refs_0_.refs_2_), channel_id=1, source_target_pairs={{0,1},{1,0},{2,3},{3,2},{4,5},{5,4},{6,7},{7,6},{8,9},{9,8},{10,11... | collective-permute-start | bytes 1032200 | tf_op jit(solution)/shard_map/ppermute | solution.py:61
  22.9 14.3 %collective-permute-start.8 = (bf16[48,3072]{1,0:T(8,128)(2,1)S(1)}, bf16[48,3072]{1,0:T(8,128)(2,1)S(1)}, u32[]{:S(2)}, u32[]{:S(2)}) collective-permute-start(bf16[48,3072]{1,0:T(8,128)(2,1)S(1)} %shard_map.326.refs_0_), channel_id=1, source_target_pairs={{0,8},{2,10},{4,12},{6,14},{8,0},{10,2},{12,4},{14,6},{16,24},{18,... | collective-permute-start | bytes 884744 | tf_op jit(solution)/shard_map/ppermute | solution.py:57
  25.5 23.5 %collective-permute-start.9 = (bf16[48,3072]{1,0:T(8,128)(2,1)S(1)}, bf16[48,3072]{1,0:T(8,128)(2,1)S(1)}, u32[]{:S(2)}, u32[]{:S(2)}) collective-permute-start(bf16[48,3072]{1,0:T(8,128)(2,1)S(1)} %shard_map.326.refs_0_), channel_id=1, source_target_pairs={{0,16},{2,18},{4,20},{6,22},{8,24},{10,26},{12,28},{14,30},{16,0},... | collective-permute-start | bytes 884744 | tf_op jit(solution)/shard_map/ppermute | solution.py:57
  26.6 22.4 %collective-permute-start.10 = (bf16[48,3072]{1,0:T(8,128)(2,1)S(1)}, bf16[48,3072]{1,0:T(8,128)(2,1)S(1)}, u32[]{:S(2)}, u32[]{:S(2)}) collective-permute-start(bf16[48,3072]{1,0:T(8,128)(2,1)S(1)} %shard_map.326.refs_0_), channel_id=1, source_target_pairs={{0,24},{2,26},{4,28},{6,30},{8,16},{10,18},{12,20},{14,22},{16,8},... | collective-permute-start | bytes 884744 | tf_op jit(solution)/shard_map/ppermute | solution.py:57
  35.0 14.0 %collective-permute-start.6 = (bf16[384,768]{1,0:T(8,128)(2,1)S(1)}, bf16[384,768]{1,0:T(8,128)(2,1)S(1)}, u32[]{:S(2)}, u32[]{:S(2)}) collective-permute-start(bf16[384,768]{1,0:T(8,128)(2,1)S(1)} %get-tuple-element.92.refs_0_), channel_id=1, source_target_pairs={{0,1},{1,0},{2,3},{3,2},{4,5},{5,4},{6,7},{7,6},{8,9},{9,8},{10,11... | collective-permute-start | bytes 1769480 | tf_op jit(solution)/shard_map/ppermute | solution.py:61
  35.6 14.2 %collective-permute-start.7 = (bf16[192,1792]{1,0:T(8,128)(2,1)S(1)}, bf16[192,1792]{1,0:T(8,128)(2,1)S(1)}, u32[]{:S(2)}, u32[]{:S(2)}) collective-permute-start(bf16[192,1792]{1,0:T(8,128)(2,1)S(1)} %get-tuple-element.93.refs_1_), channel_id=1, source_target_pairs={{0,4},{2,6},{4,0},{6,2},{8,12},{10,14},{12,8},{14,10},{16,20},{18,... | collective-permute-start | bytes 2064392 | tf_op jit(solution)/shard_map/ppermute | solution.py:57
  50.6 15.3 %collective-permute-start.13 = (bf16[192,1536]{1,0:T(8,128)(2,1)S(1)}, bf16[192,1536]{1,0:T(8,128)(2,1)S(1)}, u32[]{:S(2)}, u32[]{:S(2)}) collective-permute-start(bf16[192,1536]{1,0:T(8,128)(2,1)S(1)} %get-tuple-element.94.refs_4_.refs_0_), channel_id=1, source_target_pairs={{0,1},{1,0},{2,3},{3,2},{4,5},{5,4},{6,7},{7,6},{8,9},{9,8},{10,11... | collective-permute-start | bytes 1769480 | tf_op jit(solution)/shard_map/ppermute | solution.py:61
  52.1 15.0 %collective-permute-start.14 = (bf16[192,1536]{1,0:T(8,128)(2,1)S(1)}, bf16[192,1536]{1,0:T(8,128)(2,1)S(1)}, u32[]{:S(2)}, u32[]{:S(2)}) collective-permute-start(bf16[192,1536]{1,0:T(8,128)(2,1)S(1)} %get-tuple-element.102.refs_1_), channel_id=1, source_target_pairs={{0,4},{2,6},{4,0},{6,2},{8,12},{10,14},{12,8},{14,10},{16,20},{18,... | collective-permute-start | bytes 1769480 | tf_op jit(solution)/shard_map/ppermute | solution.py:57
  67.3 10.9 %collective-permute-start.15 = (bf16[192,3072]{1,0:T(8,128)(2,1)S(1)}, bf16[192,3072]{1,0:T(8,128)(2,1)S(1)}, u32[]{:S(2)}, u32[]{:S(2)}) collective-permute-start(bf16[192,3072]{1,0:T(8,128)(2,1)S(1)} %get-tuple-element.103.refs_5_.refs_1_), channel_id=1, source_target_pairs={{0,2},{2,0},{4,6},{6,4},{8,10},{10,8},{12,14},{14,12},{16,18},{18,... | collective-permute-start | bytes 3538952 | tf_op jit(solution)/shard_map/ppermute | solution.py:57
  67.8 28.0 %collective-permute-start.17 = (bf16[192,3072]{1,0:T(8,128)(2,1)S(1)}, bf16[192,3072]{1,0:T(8,128)(2,1)S(1)}, u32[]{:S(2)}, u32[]{:S(2)}) collective-permute-start(bf16[192,3072]{1,0:T(8,128)(2,1)S(1)} %get-tuple-element.103.refs_5_.refs_1_), channel_id=1, source_target_pairs={{0,4},{2,6},{4,0},{6,2},{8,12},{10,14},{12,8},{14,10},{16,20},{18,... | collective-permute-start | bytes 3538952 | tf_op jit(solution)/shard_map/ppermute | solution.py:57
  69.4 27.7 %collective-permute-start.18 = (bf16[384,1536]{1,0:T(8,128)(2,1)S(1)}, bf16[384,1536]{1,0:T(8,128)(2,1)S(1)}, u32[]{:S(2)}, u32[]{:S(2)}) collective-permute-start(bf16[384,1536]{1,0:T(8,128)(2,1)S(1)} %get-tuple-element.105.refs_3_.refs_1_), channel_id=1, source_target_pairs={{0,1},{1,0},{2,3},{3,2},{4,5},{5,4},{6,7},{7,6},{8,9},{9,8},{10,11... | collective-permute-start | bytes 3538952 | tf_op jit(solution)/shard_map/ppermute | solution.py:61
  112.5 23.1 %collective-permute-start.23 = (bf16[192,3072]{1,0:T(8,128)(2,1)S(1)}, bf16[192,3072]{1,0:T(8,128)(2,1)S(1)}, u32[]{:S(2)}, u32[]{:S(2)}) collective-permute-start(bf16[192,3072]{1,0:T(8,128)(2,1)S(1)} %convolution_convert_fusion), channel_id=1, source_target_pairs={{0,2},{2,0},{4,6},{6,4},{8,10},{10,8},{12,14},{14,12},{16,18},{18,... | collective-permute-start | bytes 3538952 | tf_op jit(solution)/shard_map/ppermute | solution.py:57
  113.2 21.6 %collective-permute-start.24 = (bf16[384,1536]{1,0:T(8,128)(2,1)S(1)}, bf16[384,1536]{1,0:T(8,128)(2,1)S(1)}, u32[]{:S(2)}, u32[]{:S(2)}) collective-permute-start(bf16[384,1536]{1,0:T(8,128)(2,1)S(1)} %convolution_convert_fusion.4), channel_id=1, source_target_pairs={{0,2},{2,0},{4,6},{6,4},{8,10},{10,8},{12,14},{14,12},{16,18},{18,... | collective-permute-start | bytes 3538952 | tf_op jit(solution)/shard_map/ppermute | solution.py:57
  115.0 28.7 %collective-permute-start.26 = (bf16[384,1536]{1,0:T(8,128)(2,1)S(1)}, bf16[384,1536]{1,0:T(8,128)(2,1)S(1)}, u32[]{:S(2)}, u32[]{:S(2)}) collective-permute-start(bf16[384,1536]{1,0:T(8,128)(2,1)S(1)} %shard_map.338.refs_2_), channel_id=1, source_target_pairs={{0,1},{1,0},{2,3},{3,2},{4,5},{5,4},{6,7},{7,6},{8,9},{9,8},{10,11... | collective-permute-start | bytes 3538952 | tf_op jit(solution)/shard_map/ppermute | solution.py:61
  115.9 27.8 %collective-permute-start.25 = (bf16[192,3072]{1,0:T(8,128)(2,1)S(1)}, bf16[192,3072]{1,0:T(8,128)(2,1)S(1)}, u32[]{:S(2)}, u32[]{:S(2)}) collective-permute-start(bf16[192,3072]{1,0:T(8,128)(2,1)S(1)} %shard_map.339.refs_11_), channel_id=1, source_target_pairs={{0,4},{2,6},{4,0},{6,2},{8,12},{10,14},{12,8},{14,10},{16,20},{18,... | collective-permute-start | bytes 3538952 | tf_op jit(solution)/shard_map/ppermute | solution.py:57
  134.7 14.3 %collective-permute-start.29 = (bf16[384,1792]{1,0:T(8,128)(2,1)S(1)}, bf16[384,1792]{1,0:T(8,128)(2,1)S(1)}, u32[]{:S(2)}, u32[]{:S(2)}) collective-permute-start(bf16[384,1792]{1,0:T(8,128)(2,1)S(1)} %get-tuple-element.135), channel_id=1, source_target_pairs={{0,2},{2,0},{4,6},{6,4},{8,10},{10,8},{12,14},{14,12},{16,18},{18,... | collective-permute-start | bytes 4128776 | tf_op jit(solution)/shard_map/ppermute | solution.py:57
  134.8 14.2 %collective-permute-start.30 = (bf16[384,1536]{1,0:T(8,128)(2,1)S(1)}, bf16[384,1536]{1,0:T(8,128)(2,1)S(1)}, u32[]{:S(2)}, u32[]{:S(2)}) collective-permute-start(bf16[384,1536]{1,0:T(8,128)(2,1)S(1)} %get-tuple-element.137), channel_id=1, source_target_pairs={{0,2},{2,0},{4,6},{6,4},{8,10},{10,8},{12,14},{14,12},{16,18},{18,... | collective-permute-start | bytes 3538952 | tf_op jit(solution)/shard_map/ppermute | solution.py:57
  144.3 16.3 %collective-permute-start.27 = (bf16[192,1536]{1,0:T(8,128)(2,1)S(1)}, bf16[192,1536]{1,0:T(8,128)(2,1)S(1)}, u32[]{:S(2)}, u32[]{:S(2)}) collective-permute-start(bf16[192,1536]{1,0:T(8,128)(2,1)S(1)} %get-tuple-element.132), channel_id=1, source_target_pairs={{0,1},{1,0},{2,3},{3,2},{4,5},{5,4},{6,7},{7,6},{8,9},{9,8},{10,11... | collective-permute-start | bytes 1769480 | tf_op jit(solution)/shard_map/ppermute | solution.py:61
  145.9 16.3 %collective-permute-start.28 = (bf16[192,1536]{1,0:T(8,128)(2,1)S(1)}, bf16[192,1536]{1,0:T(8,128)(2,1)S(1)}, u32[]{:S(2)}, u32[]{:S(2)}) collective-permute-start(bf16[192,1536]{1,0:T(8,128)(2,1)S(1)} %get-tuple-element.134), channel_id=1, source_target_pairs={{0,4},{2,6},{4,0},{6,2},{8,12},{10,14},{12,8},{14,10},{16,20},{18,... | collective-permute-start | bytes 1769480 | tf_op jit(solution)/shard_map/ppermute | solution.py:57
  149.6 24.9 %collective-permute-start.34 = (bf16[192,1792]{1,0:T(8,128)(2,1)S(1)}, bf16[192,1792]{1,0:T(8,128)(2,1)S(1)}, u32[]{:S(2)}, u32[]{:S(2)}) collective-permute-start(bf16[192,1792]{1,0:T(8,128)(2,1)S(1)} %get-tuple-element.143), channel_id=1, source_target_pairs={{0,4},{2,6},{4,0},{6,2},{8,12},{10,14},{12,8},{14,10},{16,20},{18,... | collective-permute-start | bytes 2064392 | tf_op jit(solution)/shard_map/ppermute | solution.py:57
  151.2 20.0 %collective-permute-start.35 = (bf16[384,768]{1,0:T(8,128)(2,1)S(1)}, bf16[384,768]{1,0:T(8,128)(2,1)S(1)}, u32[]{:S(2)}, u32[]{:S(2)}) collective-permute-start(bf16[384,768]{1,0:T(8,128)(2,1)S(1)} %get-tuple-element.145), channel_id=1, source_target_pairs={{0,1},{1,0},{2,3},{3,2},{4,5},{5,4},{6,7},{7,6},{8,9},{9,8},{10,11... | collective-permute-start | bytes 1769480 | tf_op jit(solution)/shard_map/ppermute | solution.py:61
  162.4 13.6 %collective-permute-start.31 = (bf16[48,3072]{1,0:T(8,128)(2,1)S(1)}, bf16[48,3072]{1,0:T(8,128)(2,1)S(1)}, u32[]{:S(2)}, u32[]{:S(2)}) collective-permute-start(bf16[48,3072]{1,0:T(8,128)(2,1)S(1)} %get-tuple-element.140), channel_id=1, source_target_pairs={{0,8},{2,10},{4,12},{6,14},{8,0},{10,2},{12,4},{14,6},{16,24},{18,... | collective-permute-start | bytes 884744 | tf_op jit(solution)/shard_map/ppermute | solution.py:57
  164.8 20.9 %collective-permute-start.32 = (bf16[48,3072]{1,0:T(8,128)(2,1)S(1)}, bf16[48,3072]{1,0:T(8,128)(2,1)S(1)}, u32[]{:S(2)}, u32[]{:S(2)}) collective-permute-start(bf16[48,3072]{1,0:T(8,128)(2,1)S(1)} %get-tuple-element.141), channel_id=1, source_target_pairs={{0,16},{2,18},{4,20},{6,22},{8,24},{10,26},{12,28},{14,30},{16,0},... | collective-permute-start | bytes 884744 | tf_op jit(solution)/shard_map/ppermute | solution.py:57
  166.1 19.6 %collective-permute-start.33 = (bf16[48,3072]{1,0:T(8,128)(2,1)S(1)}, bf16[48,3072]{1,0:T(8,128)(2,1)S(1)}, u32[]{:S(2)}, u32[]{:S(2)}) collective-permute-start(bf16[48,3072]{1,0:T(8,128)(2,1)S(1)} %get-tuple-element.142), channel_id=1, source_target_pairs={{0,24},{2,26},{4,28},{6,30},{8,16},{10,18},{12,20},{14,22},{16,8},... | collective-permute-start | bytes 884744 | tf_op jit(solution)/shard_map/ppermute | solution.py:57
  174.9 12.5 %collective-permute-start.37 = (bf16[192,896]{1,0:T(8,128)(2,1)S(1)}, bf16[192,896]{1,0:T(8,128)(2,1)S(1)}, u32[]{:S(2)}, u32[]{:S(2)}) collective-permute-start(bf16[192,896]{1,0:T(8,128)(2,1)S(1)} %get-tuple-element.147), channel_id=1, source_target_pairs={{0,1},{1,0},{2,3},{3,2},{4,5},{5,4},{6,7},{7,6},{8,9},{9,8},{10,11... | collective-permute-start | bytes 1032200 | tf_op jit(solution)/shard_map/ppermute | solution.py:61
  175.5 11.9 %collective-permute-start.38 = (bf16[192,768]{1,0:T(8,128)(2,1)S(1)}, bf16[192,768]{1,0:T(8,128)(2,1)S(1)}, u32[]{:S(2)}, u32[]{:S(2)}) collective-permute-start(bf16[192,768]{1,0:T(8,128)(2,1)S(1)} %get-tuple-element.149), channel_id=1, source_target_pairs={{0,4},{2,6},{4,0},{6,2},{8,12},{10,14},{12,8},{14,10},{16,20},{18,... | collective-permute-start | bytes 884744 | tf_op jit(solution)/shard_map/ppermute | solution.py:57
  187.6 11.3 %collective-permute-start.39 = (bf16[48,1664]{1,0:T(8,128)(2,1)S(1)}, bf16[48,1664]{1,0:T(8,128)(2,1)S(1)}, u32[]{:S(2)}, u32[]{:S(2)}) collective-permute-start(bf16[48,1664]{1,0:T(8,128)(2,1)S(1)} %get-tuple-element.151), channel_id=1, source_target_pairs={{0,8},{2,10},{4,12},{6,14},{8,0},{10,2},{12,4},{14,6},{16,24},{18,... | collective-permute-start | bytes 479240 | tf_op jit(solution)/shard_map/ppermute | solution.py:57
  191.3 12.3 %collective-permute-start.40 = (bf16[48,1664]{1,0:T(8,128)(2,1)S(1)}, bf16[48,1664]{1,0:T(8,128)(2,1)S(1)}, u32[]{:S(2)}, u32[]{:S(2)}) collective-permute-start(bf16[48,1664]{1,0:T(8,128)(2,1)S(1)} %get-tuple-element.152), channel_id=1, source_target_pairs={{0,16},{2,18},{4,20},{6,22},{8,24},{10,26},{12,28},{14,30},{16,0},... | collective-permute-start | bytes 479240 | tf_op jit(solution)/shard_map/ppermute | solution.py:57
  192.7 10.9 %collective-permute-start.41 = (bf16[48,1664]{1,0:T(8,128)(2,1)S(1)}, bf16[48,1664]{1,0:T(8,128)(2,1)S(1)}, u32[]{:S(2)}, u32[]{:S(2)}) collective-permute-start(bf16[48,1664]{1,0:T(8,128)(2,1)S(1)} %get-tuple-element.153), channel_id=1, source_target_pairs={{0,24},{2,26},{4,28},{6,30},{8,16},{10,18},{12,20},{14,22},{16,8},... | collective-permute-start | bytes 479240 | tf_op jit(solution)/shard_map/ppermute | solution.py:57
  (40 other events, 353.1 us)

commit v11 on v9

--- a/solution.py
+++ b/solution.py
@@ -380,15 +380,20 @@
     part = width // 2
     low, high = rows[:, :half], rows[:, half:]
     a_half, b_half = a_own.shape[1] // 2, b_own.shape[1] // 2
-    for side in range(2):
-        cols = slice(side * part, (side + 1) * part)
-        at = slice(side * a_half, side * a_half + part)
+
+    def block(start):
+        return pl.ds(pl.multiple_of(start, LANES), part)
+
+    @pl.loop(0, 2)
+    def _(side):
+        cols = block(side * part)
+        at = block(side * a_half)
         q[:, cols] = (
             dot(low[:own_rows], a_own[:, at]) + dot(high[:own_rows], a_far[:, at]) + bias_q[:, cols]
         ).astype(LOW)
-        at = slice(side * a_half + part, side * a_half + 2 * part)
+        at = block(side * a_half + part)
         k[:, cols] = (dot(low, a_own[:, at]) + dot(high, a_far[:, at])).astype(LOW)
-        at = slice(side * b_half, side * b_half + part)
+        at = block(side * b_half)
         v[:, cols] = (dot(low, b_own[:, at]) + dot(high, b_far[:, at]) + bias_v[:, cols]).astype(
             LOW
         )
@@ -595,15 +600,21 @@
         both = rows[:, at]
         mine = rows[:own_rows, at]
         low = grad_low[:, at]
-        for side in range(2):
-            cols = slice(side * part, (side + 1) * part)
+        lanes = extra[at, :]
+
+        @pl.loop(0, 2)
+        def _(side, to=to, to_b=to_b, both=both, mine=mine, low=low, lanes=lanes):
+            def block(start, size=part):
+                return pl.ds(pl.multiple_of(start, LANES), size)
+
+            cols = block(side * part)
             base = side * a_half
-            to[:, base : base + part] = dot_tn(mine, grad_q[:, cols]).astype(LOW)
-            to[:, base + part : base + 2 * part] = dot_tn(both, grad_k[:, cols]).astype(LOW)
-            to[:, base + 2 * part : base + a_half] = extra[at, :]
+            to[:, block(base)] = dot_tn(mine, grad_q[:, cols]).astype(LOW)
+            to[:, block(base + part)] = dot_tn(both, grad_k[:, cols]).astype(LOW)
+            to[:, block(base + 2 * part, LANES)] = lanes
             base = side * 2 * part
-            to_b[:, base : base + part] = dot_tn(both, grad_v[:, cols]).astype(LOW)
-            to_b[:, base + part : base + 2 * part] = dot_tn(low, attended[:, cols]).astype(LOW)
+            to_b[:, block(base)] = dot_tn(both, grad_v[:, cols]).astype(LOW)
+            to_b[:, block(base + part)] = dot_tn(low, attended[:, cols]).astype(LOW)
 
 
 def close_kernel(rates, rank_ref, *refs):

time: 216 us -> 204 us (0.944)
  between operations: 13 us -> 1.74 us
  transfers between devices with their start and end apart: 42 -> 42, of which waited for: 16 -> 16; matrix products, arithmetic and copies ran while one was open for 5% -> 5% of each run, Pallas kernels for 20% -> 21%
where the time goes in v11:
time: 204 us
  waiting for transfers between devices  92.6 us (45%)
  Pallas kernels  47.9 us (23%)
  starting transfers between devices  45.9 us (22%)
  matrix products  7.68 us (4%)
  local copies, waits for them, and re-layouts  4.74 us (2%)
  other arithmetic  3.27 us (2%)
    ppermute x32, waiting for transfers between devices, swap_dp(): return lax.ppermute(values, 'dp', [(i, i ^ mask) for i in range(size)])  71.1 us
    pallas_call x30, Pallas kernels, run(): pl.pallas_call(body, grid=grid, out_shape=list(outs), in_specs=list(in_sp...  47.8 us
    ppermute x32, starting transfers between devices, swap_dp(): return lax.ppermute(values, 'dp', [(i, i ^ mask) for i in range(size)])  35.2 us
    ppermute x10, waiting for transfers between devices, swap_tensor(): return lax.ppermute(values, 'tensor', [(0, 1), (1, 0)])  21.5 us
    ppermute x10, starting transfers between devices, swap_tensor(): return lax.ppermute(values, 'tensor', [(0, 1), (1, 0)])  10.7 us
    unnamed x60, local copies, waits for them, and re-layouts  4.74 us
    dot_general x8, matrix products, dot_tn(): lax.dot_general(left, right, (((0,), (0,)), ((), ())), preferred_element_...  4.17 us
  transfers between devices with their start and end apart: 42, of which 16 were waited for; matrix products, arithmetic and copies ran while one was open for 5% of the time, Pallas kernels for 21%

profile of v11, /device:TPU:0, one launch (start us, length us, event | category | flops | bytes accessed | tf_op | source)
XLA Modules:
  0.0 203.8 jit_solution(18344431838264390345)
XLA Ops:
  3.4 3.1 %collective-permute-start.1 = (bf16[48,1664]{1,0:T(8,128)(2,1)S(1)}, bf16[48,1664]{1,0:T(8,128)(2,1)S(1)}, u32[]{:S(2)}, u32[]{:S(2)}) collective-permute-start(bf16[48,1664]{1,0:T(8,128)(2,1)S(1)} %shard_map.323.refs_0_), channel_id=1, source_target_pairs={{0,8},{2,10},{4,12},{6,14},{8,0},{10,2},{12,4},{14,6},{16,24},{18,... | collective-permute-start | bytes 479240 | tf_op jit(solution)/shard_map/ppermute | solution.py:57
  6.5 2.6 %collective-permute-start.2 = (bf16[48,1664]{1,0:T(8,128)(2,1)S(1)}, bf16[48,1664]{1,0:T(8,128)(2,1)S(1)}, u32[]{:S(2)}, u32[]{:S(2)}) collective-permute-start(bf16[48,1664]{1,0:T(8,128)(2,1)S(1)} %shard_map.323.refs_0_), channel_id=1, source_target_pairs={{0,16},{2,18},{4,20},{6,22},{8,24},{10,26},{12,28},{14,30},{16,0},... | collective-permute-start | bytes 479240 | tf_op jit(solution)/shard_map/ppermute | solution.py:57
  9.0 1.7 collective-permute-start
  11.5 1.6 fusion.10
  13.1 8.1 %collective-permute-done.2.refs_2_ = bf16[48,1664]{1,0:T(8,128)(2,1)S(1)} collective-permute-done((bf16[48,1664]{1,0:T(8,128)(2,1)S(1)}, bf16[48,1664]{1,0:T(8,128)(2,1)S(1)}, u32[]{:S(2)}, u32[]{:S(2)}) %collective-permute-start.2) | collective-permute-done | bytes 159776 | tf_op jit(solution)/shard_map/ppermute | solution.py:57
  21.3 1.6 collective-permute-start.4
  22.9 2.6 %collective-permute-start.8 = (bf16[48,3072]{1,0:T(8,128)(2,1)S(1)}, bf16[48,3072]{1,0:T(8,128)(2,1)S(1)}, u32[]{:S(2)}, u32[]{:S(2)}) collective-permute-start(bf16[48,3072]{1,0:T(8,128)(2,1)S(1)} %shard_map.326.refs_0_), channel_id=1, source_target_pairs={{0,8},{2,10},{4,12},{6,14},{8,0},{10,2},{12,4},{14,6},{16,24},{18,... | collective-permute-start | bytes 884744 | tf_op jit(solution)/shard_map/ppermute | solution.py:57
  30.2 4.7 %collective-permute-done.5.refs_3_ = bf16[192,768]{1,0:T(8,128)(2,1)S(1)} collective-permute-done((bf16[192,768]{1,0:T(8,128)(2,1)S(1)}, bf16[192,768]{1,0:T(8,128)(2,1)S(1)}, u32[]{:S(2)}, u32[]{:S(2)}) %collective-permute-start.5) | collective-permute-done | bytes 294944 | tf_op jit(solution)/shard_map/ppermute | solution.py:57
  37.2 11.8 %collective-permute-done.9.refs_2_ = bf16[48,3072]{1,0:T(8,128)(2,1)S(1)} collective-permute-done((bf16[48,3072]{1,0:T(8,128)(2,1)S(1)}, bf16[48,3072]{1,0:T(8,128)(2,1)S(1)}, u32[]{:S(2)}, u32[]{:S(2)}) %collective-permute-start.9) | collective-permute-done | bytes 294944 | tf_op jit(solution)/shard_map/ppermute | solution.py:57
  55.5 2.8 %shard_map.330 = (bf16[256,768]{1,0:T(8,128)(2,1)S(1)}, bf16[512,768]{1,0:T(8,128)(2,1)S(1)}, bf16[512,768]{1,0:T(8,128)(2,1)S(1)}) custom-call(bf16[512,768]{1,0:T(8,128)(2,1)S(1)} %pad_maximum_fusion.refs_4_.refs_0_.refs_1_.refs_2_, bf16[384,1792]{1,0:T(8,128)(2,1)S(1)} %get-tuple-element.95.refs_2_.refs_1_.refs_3_, ...), custom_call_target="tpu_custom_call" | custom-call | flops 1509949440 | bytes 7870464 | tf_op jit(solution)/shard_map/pallas_call | solution.py:142
  58.3 7.6 %collective-permute-done.13.refs_2_ = bf16[192,1536]{1,0:T(8,128)(2,1)S(1)} collective-permute-done((bf16[192,1536]{1,0:T(8,128)(2,1)S(1)}, bf16[192,1536]{1,0:T(8,128)(2,1)S(1)}, u32[]{:S(2)}, u32[]{:S(2)}) %collective-permute-start.13) | collective-permute-done | bytes 589856 | tf_op jit(solution)/shard_map/ppermute | solution.py:61
  69.9 8.4 %shard_map.332.refs_0_.refs_7_ = bf16[256,768]{1,0:T(8,128)(2,1)S(1)} custom-call(s32[1]{0:T(128)} %bitcast.refs_0_, s32[1,3]{1,0:T(1,128)S(1)} %copy-done.25, bf16[256,768]{1,0:T(8,128)(2,1)S(1)} %get-tuple-element.99.refs_4_.refs_2_, bf16[512,768]{1,0:T(8,128)(2,1)S(1)} %get-tuple-element.100.refs_3_, bf16[512,768]{1,0:T(8,128)(2,1)S(1)} %get-tuple-element.101.refs_4_, ...), custom_call_target="tpu_custom_call" | custom-call | flops 905969664 | bytes 2359312 | tf_op jit(solution)/shard_map/pallas_call | solution.py:142
  79.3 16.5 %collective-permute-done.17.refs_0_ = bf16[192,3072]{1,0:T(8,128)(2,1)S(1)} collective-permute-done((bf16[192,3072]{1,0:T(8,128)(2,1)S(1)}, bf16[192,3072]{1,0:T(8,128)(2,1)S(1)}, u32[]{:S(2)}, u32[]{:S(2)}) %collective-permute-start.17) | collective-permute-done | bytes 1179680 | tf_op jit(solution)/shard_map/ppermute | solution.py:57
  98.2 1.7 collective-permute-done.19.refs_4_
  99.9 2.8 %shard_map.335 = (bf16[256,3072]{1,0:T(8,128)(2,1)S(1)}, f32[256,3072]{1,0:T(8,128)S(1)}) custom-call(bf16[256,768]{1,0:T(8,128)(2,1)S(1)} %get-tuple-element.106.refs_2_.refs_0_, bf16[192,3072]{1,0:T(8,128)(2,1)S(1)} %get-tuple-element.103.refs_5_.refs_1_, bf16[192,3072]{1,0:T(8,128)(2,1)S(1)} %get-tuple-element.107.refs_2_, ...), custom_call_target="tpu_custom_call" | custom-call | flops 2415919104 | bytes 9842688 | tf_op jit(solution)/shard_map/pallas_call | solution.py:142
  102.7 3.0 %shard_map.336 = (bf16[256,768]{1,0:T(8,128)(2,1)S(1)}, f32[256,768]{1,0:T(8,128)S(1)}, bf16[256,768]{1,0:T(8,128)(2,1)S(1)}, f32[8,768]{1,0:T(8,128)S(1)}) custom-call(s32[1]{0:T(128)} %bitcast.refs_0_, s32[1,3]{1,0:T(1,128)S(1)} %copy-done.25, bf16[256,3072]{1,0:T(8,128)(2,1)S(1)} %get-tuple-element.109.refs_2_, ...), custom_call_target="tpu_custom_call" | custom-call | flops 1509949440 | bytes 9480208 | tf_op jit(solution)/shard_map/pallas_call | solution.py:142
  106.4 1.8 shard_map.337
  115.7 2.7 %shard_map.340 = (f32[256,768]{1,0:T(8,128)S(1)}, bf16[256,768]{1,0:T(8,128)(2,1)S(1)}, bf16[256,768]{1,0:T(8,128)(2,1)S(1)}, f32[8,768]{1,0:T(8,128)S(1)}) custom-call(bf16[256,3072]{1,0:T(8,128)(2,1)S(1)} %get-tuple-element.115.refs_2_.refs_0_, bf16[192,3072]{1,0:T(8,128)(2,1)S(1)} %get-tuple-element.103.refs_5_.refs_1_, ...), custom_call_target="tpu_custom_call" | custom-call | flops 1811939328 | bytes 11840512 | tf_op jit(solution)/shard_map/pallas_call | solution.py:142
  118.4 10.5 %shard_map.341 = (bf16[256,768]{1,0:T(8,128)(2,1)S(1)}, bf16[512,768]{1,0:T(8,128)(2,1)S(1)}, bf16[512,768]{1,0:T(8,128)(2,1)S(1)}) custom-call(s32[1]{0:T(128)} %bitcast.refs_0_, s32[1,3]{1,0:T(1,128)S(1)} %copy-done.25, bf16[256,768]{1,0:T(8,128)(2,1)S(1)} %get-tuple-element.99.refs_4_.refs_2_, bf16[512,768]{1,0:T(8,128)(2,1)S(1)} %get-tuple-element.100.refs_3_, ...), custom_call_target="tpu_custom_call" | custom-call | flops 1509949440 | bytes 4325392 | tf_op jit(solution)/shard_map/pallas_call | solution.py:142
  128.9 4.2 %shard_map.344 = (bf16[384,1792]{1,0:T(8,128)(2,1)S(1)}, bf16[384,1536]{1,0:T(8,128)(2,1)S(1)}, bf16[384,1792]{1,0:T(8,128)(2,1)S(1)}, bf16[384,1536]{1,0:T(8,128)(2,1)S(1)}) custom-call(s32[1]{0:T(128)} %bitcast.refs_0_, bf16[768,768]{1,0:T(8,128)(2,1)S(1)} %copy-done.7, bf16[512,768]{1,0:T(8,128)(2,1)S(1)} %pad_maximum_fusion.refs_4_.refs_0_.refs_1_.refs_2_, ...), custom_call_target="tpu_custom_call" | custom-call | flops 1811939328 | bytes 9891844 | tf_op jit(solution)/shard_map/pallas_call | solution.py:142
  134.3 7.0 %collective-permute-done.25.refs_1_ = bf16[192,3072]{1,0:T(8,128)(2,1)S(1)} collective-permute-done((bf16[192,3072]{1,0:T(8,128)(2,1)S(1)}, bf16[192,3072]{1,0:T(8,128)(2,1)S(1)}, u32[]{:S(2)}, u32[]{:S(2)}) %collective-permute-start.25) | collective-permute-done | bytes 1179680 | tf_op jit(solution)/shard_map/ppermute | solution.py:57
  141.8 1.6 collective-permute-start.27
  143.9 2.6 %shard_map.346 = (f32[256,768]{1,0:T(8,128)S(1)}, bf16[256,768]{1,0:T(8,128)(2,1)S(1)}) custom-call(bf16[256,768]{1,0:T(8,128)(2,1)S(1)} %get-tuple-element.120.refs_3_.refs_0_, bf16[512,768]{1,0:T(8,128)(2,1)S(1)} %get-tuple-element.121.refs_4_.refs_1_, bf16[512,768]{1,0:T(8,128)(2,1)S(1)} %get-tuple-element.122.refs_5_.refs_2_, ...), custom_call_target="tpu_custom_call" | custom-call | flops 120795955200 | bytes 9043968 | tf_op jit(solution)/shard_map/pallas_call | solution.py:142
  147.2 1.6 collective-permute-start.34
  149.3 8.9 %collective-permute-done.27.refs_1_ = bf16[192,1536]{1,0:T(8,128)(2,1)S(1)} collective-permute-done((bf16[192,1536]{1,0:T(8,128)(2,1)S(1)}, bf16[192,1536]{1,0:T(8,128)(2,1)S(1)}, u32[]{:S(2)}, u32[]{:S(2)}) %collective-permute-start.27) | collective-permute-done | bytes 589856 | tf_op jit(solution)/shard_map/ppermute | solution.py:61
  159.9 2.4 %collective-permute-start.31 = (bf16[48,3072]{1,0:T(8,128)(2,1)S(1)}, bf16[48,3072]{1,0:T(8,128)(2,1)S(1)}, u32[]{:S(2)}, u32[]{:S(2)}) collective-permute-start(bf16[48,3072]{1,0:T(8,128)(2,1)S(1)} %get-tuple-element.140), channel_id=1, source_target_pairs={{0,8},{2,10},{4,12},{6,14},{8,0},{10,2},{12,4},{14,6},{16,24},{18,... | collective-permute-start | bytes 884744 | tf_op jit(solution)/shard_map/ppermute | solution.py:57
  165.0 3.7 %collective-permute-done.35.refs_3_ = bf16[384,768]{1,0:T(8,128)(2,1)S(1)} collective-permute-done((bf16[384,768]{1,0:T(8,128)(2,1)S(1)}, bf16[384,768]{1,0:T(8,128)(2,1)S(1)}, u32[]{:S(2)}, u32[]{:S(2)}) %collective-permute-start.35) | collective-permute-done | bytes 589856 | tf_op jit(solution)/shard_map/ppermute | solution.py:61
  168.8 3.3 %collective-permute-done.34.refs_1_ = bf16[192,1792]{1,0:T(8,128)(2,1)S(1)} collective-permute-done((bf16[192,1792]{1,0:T(8,128)(2,1)S(1)}, bf16[192,1792]{1,0:T(8,128)(2,1)S(1)}, u32[]{:S(2)}, u32[]{:S(2)}) %collective-permute-start.34) | collective-permute-done | bytes 688160 | tf_op jit(solution)/shard_map/ppermute | solution.py:57
  173.5 9.7 %collective-permute-done.32.refs_2_ = bf16[48,3072]{1,0:T(8,128)(2,1)S(1)} collective-permute-done((bf16[48,3072]{1,0:T(8,128)(2,1)S(1)}, bf16[48,3072]{1,0:T(8,128)(2,1)S(1)}, u32[]{:S(2)}, u32[]{:S(2)}) %collective-permute-start.32) | collective-permute-done | bytes 294944 | tf_op jit(solution)/shard_map/ppermute | solution.py:57
  185.1 3.8 %collective-permute-start.39 = (bf16[48,1664]{1,0:T(8,128)(2,1)S(1)}, bf16[48,1664]{1,0:T(8,128)(2,1)S(1)}, u32[]{:S(2)}, u32[]{:S(2)}) collective-permute-start(bf16[48,1664]{1,0:T(8,128)(2,1)S(1)} %get-tuple-element.151), channel_id=1, source_target_pairs={{0,8},{2,10},{4,12},{6,14},{8,0},{10,2},{12,4},{14,6},{16,24},{18,... | collective-permute-start | bytes 479240 | tf_op jit(solution)/shard_map/ppermute | solution.py:57
  194.4 2.0 shard_map.353.refs_14_
  196.4 4.8 %collective-permute-done.40.refs_12_ = bf16[48,1664]{1,0:T(8,128)(2,1)S(1)} collective-permute-done((bf16[48,1664]{1,0:T(8,128)(2,1)S(1)}, bf16[48,1664]{1,0:T(8,128)(2,1)S(1)}, u32[]{:S(2)}, u32[]{:S(2)}) %collective-permute-start.40) | collective-permute-done | bytes 159776 | tf_op jit(solution)/shard_map/ppermute | solution.py:57
  (162 shorter events, 50.8 us)
Async XLA Ops:
  6.5 14.8 %collective-permute-start.2 = (bf16[48,1664]{1,0:T(8,128)(2,1)S(1)}, bf16[48,1664]{1,0:T(8,128)(2,1)S(1)}, u32[]{:S(2)}, u32[]{:S(2)}) collective-permute-start(bf16[48,1664]{1,0:T(8,128)(2,1)S(1)} %shard_map.323.refs_0_), channel_id=1, source_target_pairs={{0,16},{2,18},{4,20},{6,22},{8,24},{10,26},{12,28},{14,30},{16,0},... | collective-permute-start | bytes 479240 | tf_op jit(solution)/shard_map/ppermute | solution.py:57
  9.0 12.2 %collective-permute-start.3 = (bf16[48,1664]{1,0:T(8,128)(2,1)S(1)}, bf16[48,1664]{1,0:T(8,128)(2,1)S(1)}, u32[]{:S(2)}, u32[]{:S(2)}) collective-permute-start(bf16[48,1664]{1,0:T(8,128)(2,1)S(1)} %shard_map.323.refs_0_), channel_id=1, source_target_pairs={{0,24},{2,26},{4,28},{6,30},{8,16},{10,18},{12,20},{14,22},{16,8},... | collective-permute-start | bytes 479240 | tf_op jit(solution)/shard_map/ppermute | solution.py:57
  9.0 18.9 %collective-permute-start = (bf16[256,768]{1,0:T(8,128)(2,1)}, bf16[256,768]{1,0:T(8,128)(2,1)S(1)}, u32[]{:S(2)}, u32[]{:S(2)}) collective-permute-start(bf16[256,768]{1,0:T(8,128)(2,1)} %param.20), channel_id=1, source_target_pairs={{0,1},{1,0},{2,3},{3,2},{4,5},{5,4},{6,7},{7,6},{8,9},{9,8},{10,11... | collective-permute-start | bytes 1179656 | tf_op jit(solution)/shard_map/ppermute | solution.py:61
  21.3 13.7 %collective-permute-start.4 = (bf16[192,896]{1,0:T(8,128)(2,1)S(1)}, bf16[192,896]{1,0:T(8,128)(2,1)S(1)}, u32[]{:S(2)}, u32[]{:S(2)}) collective-permute-start(bf16[192,896]{1,0:T(8,128)(2,1)S(1)} %get-tuple-element.90.refs_0_.refs_2_), channel_id=1, source_target_pairs={{0,1},{1,0},{2,3},{3,2},{4,5},{5,4},{6,7},{7,6},{8,9},{9,8},{10,11... | collective-permute-start | bytes 1032200 | tf_op jit(solution)/shard_map/ppermute | solution.py:61
  22.9 14.3 %collective-permute-start.8 = (bf16[48,3072]{1,0:T(8,128)(2,1)S(1)}, bf16[48,3072]{1,0:T(8,128)(2,1)S(1)}, u32[]{:S(2)}, u32[]{:S(2)}) collective-permute-start(bf16[48,3072]{1,0:T(8,128)(2,1)S(1)} %shard_map.326.refs_0_), channel_id=1, source_target_pairs={{0,8},{2,10},{4,12},{6,14},{8,0},{10,2},{12,4},{14,6},{16,24},{18,... | collective-permute-start | bytes 884744 | tf_op jit(solution)/shard_map/ppermute | solution.py:57
  25.5 23.5 %collective-permute-start.9 = (bf16[48,3072]{1,0:T(8,128)(2,1)S(1)}, bf16[48,3072]{1,0:T(8,128)(2,1)S(1)}, u32[]{:S(2)}, u32[]{:S(2)}) collective-permute-start(bf16[48,3072]{1,0:T(8,128)(2,1)S(1)} %shard_map.326.refs_0_), channel_id=1, source_target_pairs={{0,16},{2,18},{4,20},{6,22},{8,24},{10,26},{12,28},{14,30},{16,0},... | collective-permute-start | bytes 884744 | tf_op jit(solution)/shard_map/ppermute | solution.py:57
  26.6 22.4 %collective-permute-start.10 = (bf16[48,3072]{1,0:T(8,128)(2,1)S(1)}, bf16[48,3072]{1,0:T(8,128)(2,1)S(1)}, u32[]{:S(2)}, u32[]{:S(2)}) collective-permute-start(bf16[48,3072]{1,0:T(8,128)(2,1)S(1)} %shard_map.326.refs_0_), channel_id=1, source_target_pairs={{0,24},{2,26},{4,28},{6,30},{8,16},{10,18},{12,20},{14,22},{16,8},... | collective-permute-start | bytes 884744 | tf_op jit(solution)/shard_map/ppermute | solution.py:57
  35.0 14.0 %collective-permute-start.6 = (bf16[384,768]{1,0:T(8,128)(2,1)S(1)}, bf16[384,768]{1,0:T(8,128)(2,1)S(1)}, u32[]{:S(2)}, u32[]{:S(2)}) collective-permute-start(bf16[384,768]{1,0:T(8,128)(2,1)S(1)} %get-tuple-element.92.refs_0_), channel_id=1, source_target_pairs={{0,1},{1,0},{2,3},{3,2},{4,5},{5,4},{6,7},{7,6},{8,9},{9,8},{10,11... | collective-permute-start | bytes 1769480 | tf_op jit(solution)/shard_map/ppermute | solution.py:61
  35.6 14.2 %collective-permute-start.7 = (bf16[192,1792]{1,0:T(8,128)(2,1)S(1)}, bf16[192,1792]{1,0:T(8,128)(2,1)S(1)}, u32[]{:S(2)}, u32[]{:S(2)}) collective-permute-start(bf16[192,1792]{1,0:T(8,128)(2,1)S(1)} %get-tuple-element.93.refs_1_), channel_id=1, source_target_pairs={{0,4},{2,6},{4,0},{6,2},{8,12},{10,14},{12,8},{14,10},{16,20},{18,... | collective-permute-start | bytes 2064392 | tf_op jit(solution)/shard_map/ppermute | solution.py:57
  50.6 15.3 %collective-permute-start.13 = (bf16[192,1536]{1,0:T(8,128)(2,1)S(1)}, bf16[192,1536]{1,0:T(8,128)(2,1)S(1)}, u32[]{:S(2)}, u32[]{:S(2)}) collective-permute-start(bf16[192,1536]{1,0:T(8,128)(2,1)S(1)} %get-tuple-element.94.refs_4_.refs_0_), channel_id=1, source_target_pairs={{0,1},{1,0},{2,3},{3,2},{4,5},{5,4},{6,7},{7,6},{8,9},{9,8},{10,11... | collective-permute-start | bytes 1769480 | tf_op jit(solution)/shard_map/ppermute | solution.py:61
  52.1 15.0 %collective-permute-start.14 = (bf16[192,1536]{1,0:T(8,128)(2,1)S(1)}, bf16[192,1536]{1,0:T(8,128)(2,1)S(1)}, u32[]{:S(2)}, u32[]{:S(2)}) collective-permute-start(bf16[192,1536]{1,0:T(8,128)(2,1)S(1)} %get-tuple-element.102.refs_1_), channel_id=1, source_target_pairs={{0,4},{2,6},{4,0},{6,2},{8,12},{10,14},{12,8},{14,10},{16,20},{18,... | collective-permute-start | bytes 1769480 | tf_op jit(solution)/shard_map/ppermute | solution.py:57
  67.3 11.1 %collective-permute-start.15 = (bf16[192,3072]{1,0:T(8,128)(2,1)S(1)}, bf16[192,3072]{1,0:T(8,128)(2,1)S(1)}, u32[]{:S(2)}, u32[]{:S(2)}) collective-permute-start(bf16[192,3072]{1,0:T(8,128)(2,1)S(1)} %get-tuple-element.103.refs_5_.refs_1_), channel_id=1, source_target_pairs={{0,2},{2,0},{4,6},{6,4},{8,10},{10,8},{12,14},{14,12},{16,18},{18,... | collective-permute-start | bytes 3538952 | tf_op jit(solution)/shard_map/ppermute | solution.py:57
  67.8 28.0 %collective-permute-start.17 = (bf16[192,3072]{1,0:T(8,128)(2,1)S(1)}, bf16[192,3072]{1,0:T(8,128)(2,1)S(1)}, u32[]{:S(2)}, u32[]{:S(2)}) collective-permute-start(bf16[192,3072]{1,0:T(8,128)(2,1)S(1)} %get-tuple-element.103.refs_5_.refs_1_), channel_id=1, source_target_pairs={{0,4},{2,6},{4,0},{6,2},{8,12},{10,14},{12,8},{14,10},{16,20},{18,... | collective-permute-start | bytes 3538952 | tf_op jit(solution)/shard_map/ppermute | solution.py:57
  69.4 27.7 %collective-permute-start.18 = (bf16[384,1536]{1,0:T(8,128)(2,1)S(1)}, bf16[384,1536]{1,0:T(8,128)(2,1)S(1)}, u32[]{:S(2)}, u32[]{:S(2)}) collective-permute-start(bf16[384,1536]{1,0:T(8,128)(2,1)S(1)} %get-tuple-element.105.refs_3_.refs_1_), channel_id=1, source_target_pairs={{0,1},{1,0},{2,3},{3,2},{4,5},{5,4},{6,7},{7,6},{8,9},{9,8},{10,11... | collective-permute-start | bytes 3538952 | tf_op jit(solution)/shard_map/ppermute | solution.py:61
  109.8 24.2 %collective-permute-start.23 = (bf16[192,3072]{1,0:T(8,128)(2,1)S(1)}, bf16[192,3072]{1,0:T(8,128)(2,1)S(1)}, u32[]{:S(2)}, u32[]{:S(2)}) collective-permute-start(bf16[192,3072]{1,0:T(8,128)(2,1)S(1)} %convolution_convert_fusion), channel_id=1, source_target_pairs={{0,2},{2,0},{4,6},{6,4},{8,10},{10,8},{12,14},{14,12},{16,18},{18,... | collective-permute-start | bytes 3538952 | tf_op jit(solution)/shard_map/ppermute | solution.py:57
  110.5 22.7 %collective-permute-start.24 = (bf16[384,1536]{1,0:T(8,128)(2,1)S(1)}, bf16[384,1536]{1,0:T(8,128)(2,1)S(1)}, u32[]{:S(2)}, u32[]{:S(2)}) collective-permute-start(bf16[384,1536]{1,0:T(8,128)(2,1)S(1)} %convolution_convert_fusion.4), channel_id=1, source_target_pairs={{0,2},{2,0},{4,6},{6,4},{8,10},{10,8},{12,14},{14,12},{16,18},{18,... | collective-permute-start | bytes 3538952 | tf_op jit(solution)/shard_map/ppermute | solution.py:57
  112.3 28.9 %collective-permute-start.26 = (bf16[384,1536]{1,0:T(8,128)(2,1)S(1)}, bf16[384,1536]{1,0:T(8,128)(2,1)S(1)}, u32[]{:S(2)}, u32[]{:S(2)}) collective-permute-start(bf16[384,1536]{1,0:T(8,128)(2,1)S(1)} %shard_map.338.refs_2_), channel_id=1, source_target_pairs={{0,1},{1,0},{2,3},{3,2},{4,5},{5,4},{6,7},{7,6},{8,9},{9,8},{10,11... | collective-permute-start | bytes 3538952 | tf_op jit(solution)/shard_map/ppermute | solution.py:61
  113.5 27.8 %collective-permute-start.25 = (bf16[192,3072]{1,0:T(8,128)(2,1)S(1)}, bf16[192,3072]{1,0:T(8,128)(2,1)S(1)}, u32[]{:S(2)}, u32[]{:S(2)}) collective-permute-start(bf16[192,3072]{1,0:T(8,128)(2,1)S(1)} %shard_map.339.refs_11_), channel_id=1, source_target_pairs={{0,4},{2,6},{4,0},{6,2},{8,12},{10,14},{12,8},{14,10},{16,20},{18,... | collective-permute-start | bytes 3538952 | tf_op jit(solution)/shard_map/ppermute | solution.py:57
  133.2 13.4 %collective-permute-start.29 = (bf16[384,1792]{1,0:T(8,128)(2,1)S(1)}, bf16[384,1792]{1,0:T(8,128)(2,1)S(1)}, u32[]{:S(2)}, u32[]{:S(2)}) collective-permute-start(bf16[384,1792]{1,0:T(8,128)(2,1)S(1)} %get-tuple-element.135), channel_id=1, source_target_pairs={{0,2},{2,0},{4,6},{6,4},{8,10},{10,8},{12,14},{14,12},{16,18},{18,... | collective-permute-start | bytes 4128776 | tf_op jit(solution)/shard_map/ppermute | solution.py:57
  133.2 13.3 %collective-permute-start.30 = (bf16[384,1536]{1,0:T(8,128)(2,1)S(1)}, bf16[384,1536]{1,0:T(8,128)(2,1)S(1)}, u32[]{:S(2)}, u32[]{:S(2)}) collective-permute-start(bf16[384,1536]{1,0:T(8,128)(2,1)S(1)} %get-tuple-element.137), channel_id=1, source_target_pairs={{0,2},{2,0},{4,6},{6,4},{8,10},{10,8},{12,14},{14,12},{16,18},{18,... | collective-permute-start | bytes 3538952 | tf_op jit(solution)/shard_map/ppermute | solution.py:57
  141.8 16.3 %collective-permute-start.27 = (bf16[192,1536]{1,0:T(8,128)(2,1)S(1)}, bf16[192,1536]{1,0:T(8,128)(2,1)S(1)}, u32[]{:S(2)}, u32[]{:S(2)}) collective-permute-start(bf16[192,1536]{1,0:T(8,128)(2,1)S(1)} %get-tuple-element.132), channel_id=1, source_target_pairs={{0,1},{1,0},{2,3},{3,2},{4,5},{5,4},{6,7},{7,6},{8,9},{9,8},{10,11... | collective-permute-start | bytes 1769480 | tf_op jit(solution)/shard_map/ppermute | solution.py:61
  143.4 16.3 %collective-permute-start.28 = (bf16[192,1536]{1,0:T(8,128)(2,1)S(1)}, bf16[192,1536]{1,0:T(8,128)(2,1)S(1)}, u32[]{:S(2)}, u32[]{:S(2)}) collective-permute-start(bf16[192,1536]{1,0:T(8,128)(2,1)S(1)} %get-tuple-element.134), channel_id=1, source_target_pairs={{0,4},{2,6},{4,0},{6,2},{8,12},{10,14},{12,8},{14,10},{16,20},{18,... | collective-permute-start | bytes 1769480 | tf_op jit(solution)/shard_map/ppermute | solution.py:57
  147.2 24.9 %collective-permute-start.34 = (bf16[192,1792]{1,0:T(8,128)(2,1)S(1)}, bf16[192,1792]{1,0:T(8,128)(2,1)S(1)}, u32[]{:S(2)}, u32[]{:S(2)}) collective-permute-start(bf16[192,1792]{1,0:T(8,128)(2,1)S(1)} %get-tuple-element.143), channel_id=1, source_target_pairs={{0,4},{2,6},{4,0},{6,2},{8,12},{10,14},{12,8},{14,10},{16,20},{18,... | collective-permute-start | bytes 2064392 | tf_op jit(solution)/shard_map/ppermute | solution.py:57
  148.7 20.0 %collective-permute-start.35 = (bf16[384,768]{1,0:T(8,128)(2,1)S(1)}, bf16[384,768]{1,0:T(8,128)(2,1)S(1)}, u32[]{:S(2)}, u32[]{:S(2)}) collective-permute-start(bf16[384,768]{1,0:T(8,128)(2,1)S(1)} %get-tuple-element.145), channel_id=1, source_target_pairs={{0,1},{1,0},{2,3},{3,2},{4,5},{5,4},{6,7},{7,6},{8,9},{9,8},{10,11... | collective-permute-start | bytes 1769480 | tf_op jit(solution)/shard_map/ppermute | solution.py:61
  159.9 13.6 %collective-permute-start.31 = (bf16[48,3072]{1,0:T(8,128)(2,1)S(1)}, bf16[48,3072]{1,0:T(8,128)(2,1)S(1)}, u32[]{:S(2)}, u32[]{:S(2)}) collective-permute-start(bf16[48,3072]{1,0:T(8,128)(2,1)S(1)} %get-tuple-element.140), channel_id=1, source_target_pairs={{0,8},{2,10},{4,12},{6,14},{8,0},{10,2},{12,4},{14,6},{16,24},{18,... | collective-permute-start | bytes 884744 | tf_op jit(solution)/shard_map/ppermute | solution.py:57
  162.4 20.9 %collective-permute-start.32 = (bf16[48,3072]{1,0:T(8,128)(2,1)S(1)}, bf16[48,3072]{1,0:T(8,128)(2,1)S(1)}, u32[]{:S(2)}, u32[]{:S(2)}) collective-permute-start(bf16[48,3072]{1,0:T(8,128)(2,1)S(1)} %get-tuple-element.141), channel_id=1, source_target_pairs={{0,16},{2,18},{4,20},{6,22},{8,24},{10,26},{12,28},{14,30},{16,0},... | collective-permute-start | bytes 884744 | tf_op jit(solution)/shard_map/ppermute | solution.py:57
  163.6 19.6 %collective-permute-start.33 = (bf16[48,3072]{1,0:T(8,128)(2,1)S(1)}, bf16[48,3072]{1,0:T(8,128)(2,1)S(1)}, u32[]{:S(2)}, u32[]{:S(2)}) collective-permute-start(bf16[48,3072]{1,0:T(8,128)(2,1)S(1)} %get-tuple-element.142), channel_id=1, source_target_pairs={{0,24},{2,26},{4,28},{6,30},{8,16},{10,18},{12,20},{14,22},{16,8},... | collective-permute-start | bytes 884744 | tf_op jit(solution)/shard_map/ppermute | solution.py:57
  172.4 12.5 %collective-permute-start.37 = (bf16[192,896]{1,0:T(8,128)(2,1)S(1)}, bf16[192,896]{1,0:T(8,128)(2,1)S(1)}, u32[]{:S(2)}, u32[]{:S(2)}) collective-permute-start(bf16[192,896]{1,0:T(8,128)(2,1)S(1)} %get-tuple-element.147), channel_id=1, source_target_pairs={{0,1},{1,0},{2,3},{3,2},{4,5},{5,4},{6,7},{7,6},{8,9},{9,8},{10,11... | collective-permute-start | bytes 1032200 | tf_op jit(solution)/shard_map/ppermute | solution.py:61
  173.0 11.9 %collective-permute-start.38 = (bf16[192,768]{1,0:T(8,128)(2,1)S(1)}, bf16[192,768]{1,0:T(8,128)(2,1)S(1)}, u32[]{:S(2)}, u32[]{:S(2)}) collective-permute-start(bf16[192,768]{1,0:T(8,128)(2,1)S(1)} %get-tuple-element.149), channel_id=1, source_target_pairs={{0,4},{2,6},{4,0},{6,2},{8,12},{10,14},{12,8},{14,10},{16,20},{18,... | collective-permute-start | bytes 884744 | tf_op jit(solution)/shard_map/ppermute | solution.py:57
  185.1 11.4 %collective-permute-start.39 = (bf16[48,1664]{1,0:T(8,128)(2,1)S(1)}, bf16[48,1664]{1,0:T(8,128)(2,1)S(1)}, u32[]{:S(2)}, u32[]{:S(2)}) collective-permute-start(bf16[48,1664]{1,0:T(8,128)(2,1)S(1)} %get-tuple-element.151), channel_id=1, source_target_pairs={{0,8},{2,10},{4,12},{6,14},{8,0},{10,2},{12,4},{14,6},{16,24},{18,... | collective-permute-start | bytes 479240 | tf_op jit(solution)/shard_map/ppermute | solution.py:57
  188.8 12.4 %collective-permute-start.40 = (bf16[48,1664]{1,0:T(8,128)(2,1)S(1)}, bf16[48,1664]{1,0:T(8,128)(2,1)S(1)}, u32[]{:S(2)}, u32[]{:S(2)}) collective-permute-start(bf16[48,1664]{1,0:T(8,128)(2,1)S(1)} %get-tuple-element.152), channel_id=1, source_target_pairs={{0,16},{2,18},{4,20},{6,22},{8,24},{10,26},{12,28},{14,30},{16,0},... | collective-permute-start | bytes 479240 | tf_op jit(solution)/shard_map/ppermute | solution.py:57
  190.2 11.0 %collective-permute-start.41 = (bf16[48,1664]{1,0:T(8,128)(2,1)S(1)}, bf16[48,1664]{1,0:T(8,128)(2,1)S(1)}, u32[]{:S(2)}, u32[]{:S(2)}) collective-permute-start(bf16[48,1664]{1,0:T(8,128)(2,1)S(1)} %get-tuple-element.153), channel_id=1, source_target_pairs={{0,24},{2,26},{4,28},{6,30},{8,16},{10,18},{12,20},{14,22},{16,8},... | collective-permute-start | bytes 479240 | tf_op jit(solution)/shard_map/ppermute | solution.py:57
  (40 other events, 351.1 us)
